TPU v7x, 32 devices: a whole 2x2x4 slice. The times are simulated.
32 devices in a mesh: site: 4 (over x, core), sec: 8 (over z, y).
Axes of the slice: x: 2, y: 2, z: 4, core: 2. Of those that a mesh axis runs over, the one named last changes fastest.
Arguments:
- left_iso: bfloat16 [4, 4, 8, 128, 128], P('site', None, 'sec'), may hold values from -0.03125 to 0.03125
- right_iso: bfloat16 [4, 4, 8, 128, 128], P('site', None, 'sec'), may hold values from -0.03125 to 0.03125
- centre: bfloat16 [4, 8, 128, 128], P('site', 'sec'), may hold values from -6 to 6
- left_env: bfloat16 [4, 42, 8, 128, 128], P('site', None, 'sec'), may hold values from -6 to 6
- right_env: bfloat16 [4, 42, 8, 128, 128], P('site', None, 'sec'), may hold values from -6 to 6
- mpo: bfloat16 [4, 42, 42, 4, 4], P('site'), may hold values from -1 to 1
- pattern: int32 [4, 42, 42], P('site'), may hold values from 0 to 1, as said below
Outputs:
- new_left: bfloat16 [4, 4, 8, 128, 128], P('site', None, 'sec')
- energy: float32 [4], P('site')
Inputs may be any that keep to these rules, and one draw needn't show every extreme that they name: At every site n, pattern[n][0][0] is 1 and every other entry of row 0 and of column 0 is 0.
All inputs are finite; a program needn't handle non-finite values.
Results may differ from a plain program's by a relative error of at most 0.015.
Values may be sent and summed in bfloat16 or wider, within the bound.
No kernel may reach another device: no remote copies, remote signals or barrier semaphores. Data moves between devices by JAX's collectives and lax.ppermute only.
A program may use at most 128 MiB of HBM per device.

v0:
```python
import functools

import jax
import jax.numpy as jnp
import numpy as np
from jax import lax
from jax.experimental import pallas as pl
from jax.experimental.pallas import tpu as pltpu
from jax.sharding import PartitionSpec as P

ENV_STEPS = 2
POLAR = 6

TINY = 1e-06
HIGHEST = lax.Precision.HIGHEST
CHARGE_STEPS = (0, 1, -1, 2, -2)
CLASSES = len(CHARGE_STEPS)
BOTH = ("site", "sec")
VMEM_LIMIT = 24 * 1024 * 1024
PIECES = 2


class Places:
    def __init__(self, sites, secs):
        self.sites, self.secs = sites, secs
        self.half = secs // 2
        self.up = (self.half + 1) // 2

    def home(self, site, sector):
        return (site % self.sites) * self.secs + sector % self.secs

    def position(self, place):
        back = self.half - 1 + self.up - place
        if isinstance(place, int):
            return place if place < self.up else back
        return jnp.where(place < self.up, place, back)

    def slot(self, chain, sector):
        chain, sector = chain % self.sites, sector % self.secs
        place = chain % 2 * self.half + self.position(sector // 2)
        return (chain // 2 * 2 + sector % 2) * self.secs + place

    def pairs(self, source, target):
        return [
            (source(chain, sector), target(chain, sector))
            for chain in range(self.sites)
            for sector in range(self.secs)
        ]

    def fetch(self, x, site_by=0, sec_by=0):
        return lax.ppermute(
            x, BOTH, self.pairs(lambda g, k: self.home(g + site_by, k + sec_by), self.slot)
        )

    def send_home(self, x, site_by, sec_by):
        return lax.ppermute(
            x, BOTH, self.pairs(self.slot, lambda g, k: self.home(g + site_by, k + sec_by))
        )

    def ahead(self, x, by, chain_by=0):
        return lax.ppermute(
            x, BOTH, self.pairs(lambda g, k: self.slot(g + chain_by, k + by), self.slot)
        )

    def partner(self, x, bit):
        return lax.ppermute(x, BOTH, self.pairs(lambda g, k: self.slot(g, k ^ bit), self.slot))

    def my_chain(self):
        return lax.axis_index("site") // 2 * 2 + lax.axis_index("sec") // self.half

    def my_sector(self):
        position = self.position(lax.axis_index("sec") % self.half)
        return 2 * position + lax.axis_index("site") % 2

    def collect(self, values):
        sector = self.my_sector()
        table = values
        bit = 1
        while bit < self.secs:
            other = self.partner(table, bit)
            first = (sector & bit) == 0
            table = jnp.where(
                first, jnp.concatenate([table, other]), jnp.concatenate([other, table])
            )
            bit *= 2
        return table


ROWS = 8
PARTS = 2


def label_groups(channels, states, sectors, sign):
    groups = {}
    for state in range(states):
        for channel in range(channels):
            label = (state + sign * CHARGE_STEPS[channel % CLASSES]) % sectors
            groups.setdefault(label, []).append((state, channel))
    return [groups[label] for label in sorted(groups)]


def even(count):
    return count + count % 2


def spread_matrix(groups, channels, states):
    rows = []
    for group in groups:
        block = np.zeros((even(len(group)), ROWS, states * channels), np.float32)
        for index, (state, channel) in enumerate(group):
            block[index, :, state * channels + channel] = 1
        rows.append(block.reshape(-1, states * channels))
    return np.concatenate(rows)


def expand_kernel(sizes, weight_ref, spread_ref, out_ref):
    start = 0
    for size in sizes:
        spread = spread_ref[pl.ds(start, size), :]
        picked = jnp.dot(spread, weight_ref[...], preferred_element_type=jnp.float32)
        full = lax.dot_general(
            picked.astype(jnp.bfloat16),
            spread,
            (((1,), (1,)), ((), ())),
            preferred_element_type=jnp.float32,
        )
        row = lax.broadcasted_iota(jnp.int32, full.shape, 0)
        column = lax.broadcasted_iota(jnp.int32, full.shape, 1)
        same = lax.rem(row, ROWS) == lax.rem(column, ROWS)
        out_ref[pl.ds(start, size), pl.ds(0, size)] = jnp.where(same, full, 0.0).astype(
            jnp.bfloat16
        )
        start += size


def mix_channels(groups, channels, weight_ref, mixed_ref, write, offset, height):
    def step(index, carry):
        first = pl.multiple_of(index * 2 * ROWS, 2 * ROWS)
        start = 0
        for group in groups:
            size = even(len(group)) * ROWS
            parts = []
            for state, channel in group:
                rows = (state * channels + channel) * height + first
                halves = [
                    mixed_ref[pl.ds(pl.multiple_of(rows + half * ROWS, ROWS), ROWS), :]
                    for half in range(2)
                ]
                parts.append(jnp.concatenate(halves, axis=1))
            if len(group) % 2:
                parts.append(parts[0])
            operand = jnp.concatenate(parts, axis=0).astype(jnp.bfloat16)
            product = jnp.dot(
                weight_ref[pl.ds(start, size), pl.ds(0, size)],
                operand,
                preferred_element_type=jnp.float32,
            )
            block = product.shape[1] // 2
            for number, pair in enumerate(group):
                rows = product[number * ROWS : (number + 1) * ROWS]
                both = jnp.concatenate([rows[:, :block], rows[:, block:]], axis=0)
                write(*pair, pl.multiple_of(offset + first, 2 * ROWS), both.astype(jnp.bfloat16))
            start += size
        return carry

    lax.fori_loop(0, height // (2 * ROWS), step, 0)


def by_parts(block, body):
    height = block // PARTS

    def one(part, carry):
        body(pl.multiple_of(part * height, height), height)
        return carry

    lax.fori_loop(0, PARTS, one, 0)


def into(gathered_ref, channels, block):
    def write(state, channel, first, rows):
        start = (state * channels + channel) * block
        gathered_ref[pl.ds(pl.multiple_of(start + first, 2 * ROWS), 2 * ROWS), :] = rows

    return write


def batches(items, most):
    pieces = -(-len(items) // most)
    size = -(-len(items) // pieces)
    return [items[start : start + size] for start in range(0, len(items), size)]


def rows_of(chunks, channel, offset, height):
    size = chunks[0].shape[0]
    return chunks[channel // size][channel % size, pl.ds(offset, height), :]


def channel_of(chunks, channel):
    size = chunks[0].shape[0]
    return chunks[channel // size][channel % size]


def put_channel(chunks, channel, value):
    size = chunks[0].shape[0]
    chunks[channel // size][channel % size] = value


def count_channels(chunks):
    return sum(chunk.shape[0] for chunk in chunks)


def mix_left(env, tensors, mixed_ref, offset, height):
    channels, block = count_channels(env), env[0].shape[1]
    for cls in range(CLASSES):
        right = jnp.concatenate(tensors[cls], axis=1)
        for batch in batches(list(range(cls, channels, CLASSES)), 5):
            rows = jnp.concatenate(
                [rows_of(env, channel, offset, height) for channel in batch], axis=0
            )
            product = jnp.dot(rows, right, preferred_element_type=jnp.float32)
            for number, channel in enumerate(batch):
                for t in range(len(tensors[cls])):
                    mixed_ref[pl.ds((t * channels + channel) * height, height), :] = product[
                        number * height : (number + 1) * height, t * block : (t + 1) * block
                    ]


def left_kernel(groups, states, pieces, *refs):
    env, (tensor_ref, weight_ref) = refs[:pieces], refs[pieces : pieces + 2]
    outs, mixed_ref = refs[pieces + 2 : -1], refs[-1]
    channels, block = count_channels(env), env[0].shape[1]

    def write(state, channel, first, rows):
        size = channels // pieces
        out_ref = outs[state * pieces + channel // size]
        out_ref[channel % size, pl.ds(first, 2 * ROWS), :] = rows

    def body(offset, height):
        tensors = [[tensor_ref[cls, t] for t in range(states)] for cls in range(CLASSES)]
        mix_left(env, tensors, mixed_ref, offset, height)
        mix_channels(groups, channels, weight_ref, mixed_ref, write, offset, height)

    by_parts(block, body)


def left_close_kernel(iso_ref, gathered_ref, moved_ref, out_ref, square_ref):
    channels, block, _ = gathered_ref.shape
    square = jnp.zeros((ROWS, block), jnp.float32)
    for batch in batches(list(range(channels)), 2):
        right = jnp.concatenate([gathered_ref[channel] for channel in batch], axis=1)
        product = lax.dot_general(
            iso_ref[...], right, (((0,), (0,)), ((), ())), preferred_element_type=jnp.float32
        )
        for number, channel in enumerate(batch):
            part = product[:, number * block : (number + 1) * block]
            part = part + moved_ref[channel].astype(jnp.float32)
            out_ref[channel] = part.astype(jnp.bfloat16)
            square = square + jnp.sum((part * part).reshape(-1, ROWS, block), axis=0)
    square_ref[...] = square


def right_kernel(groups, states, pieces, *refs):
    envs = [refs[t * pieces : (t + 1) * pieces] for t in range(states)]
    refs = refs[states * pieces :]
    own_ref, tensor_ref, weight_ref = refs[:3]
    outs, (square_ref, mixed_ref, gathered_ref) = refs[3 : 3 + pieces], refs[3 + pieces :]
    channels, block = count_channels(envs[0]), envs[0][0].shape[1]
    zero = jnp.zeros((block, block), jnp.bfloat16)
    write = into(gathered_ref, channels, block)

    def body(offset, height):
        for pair in batches(list(range(states)), 2):
            own = jnp.concatenate(
                [
                    jnp.concatenate([own_ref[t] if t == other else zero for other in pair], axis=1)
                    for t in pair
                ],
                axis=0,
            )
            for batch in batches(list(range(channels)), 6):
                rows = jnp.concatenate(
                    [
                        jnp.concatenate(
                            [rows_of(envs[t], channel, offset, height) for channel in batch], axis=0
                        )
                        for t in pair
                    ],
                    axis=1,
                )
                product = lax.dot_general(
                    rows, own, (((1,), (1,)), ((), ())), preferred_element_type=jnp.float32
                )
                for number, t in enumerate(pair):
                    start = (t * channels + batch[0]) * height
                    mixed_ref[pl.ds(start, len(batch) * height), :] = product[
                        :, number * block : (number + 1) * block
                    ]
        mix_channels(groups, channels, weight_ref, mixed_ref, write, offset, height)

    by_parts(block, body)
    square = jnp.zeros((ROWS, block), jnp.float32)
    for cls in range(CLASSES):
        left = jnp.concatenate([tensor_ref[cls, s] for s in range(states)], axis=1)
        for batch in batches(list(range(cls, channels, CLASSES)), 2):
            right = jnp.concatenate(
                [
                    jnp.concatenate(
                        [
                            gathered_ref[pl.ds((s * channels + channel) * block, block), :]
                            for s in range(states)
                        ],
                        axis=0,
                    )
                    for channel in batch
                ],
                axis=1,
            )
            product = jnp.dot(left, right, preferred_element_type=jnp.float32)
            for number, channel in enumerate(batch):
                part = product[:, number * block : (number + 1) * block]
                put_channel(outs, channel, part.astype(jnp.bfloat16))
                square = square + jnp.sum((part * part).reshape(-1, ROWS, block), axis=0)
    square_ref[...] = square


ENV_LANE = 5
LANES = 128


def quotient(table, entry_count):
    def total(x):
        return jnp.sum(x, axis=0, keepdims=True)

    squares = [
        total(table[:, lane : lane + 1]) for lane in range(ENV_LANE, ENV_LANE + 2 * ENV_STEPS + 1)
    ]
    scale = jnp.ones((1, 1), jnp.float32)
    for side in range(2):
        side_scale = jnp.ones((1, 1), jnp.float32)
        for square in squares[side * ENV_STEPS : (side + 1) * ENV_STEPS]:
            side_scale = side_scale * lax.rsqrt(side_scale * side_scale * square / entry_count + TINY)
        scale = scale * side_scale
    a, b, e, c, unit = (table[:, lane : lane + 1] for lane in range(ENV_LANE))
    a, e, unit = scale * a, scale * e, scale * unit
    c = unit * unit * c
    whole_a, whole_b = total(a), total(b)
    energy = whole_a / (whole_b + TINY)
    off = e - energy
    residual_sq = total(c + 2.0 * off * (a - e * b) + off * off * b)
    factor = 0.5 * jnp.sqrt(whole_b / (residual_sq + TINY))
    square = whole_b - 2.0 * factor * (whole_a - energy * whole_b) + factor * factor * residual_sq
    return scale, energy, factor, square, squares[2 * ENV_STEPS]


def updated(vector, image, scale, energy, factor):
    return vector - factor * (scale * image - energy * vector)


def sum_all(x):
    return jnp.sum(jnp.sum(x, axis=0, keepdims=True), axis=1, keepdims=True)


def operator_front_kernel(groups, states, pieces, renew, entry_count, *refs):
    env, refs = refs[:pieces], refs[pieces:]
    others = CLASSES - 1
    weight_ref, vector_ref, rolled = refs[0], refs[1], refs[2 : 2 + others]
    rest = refs[2 + others :]
    if renew:
        image_ref, moved, table_ref = rest[0], rest[1 : 1 + others], rest[1 + others]
        rest = rest[2 + others :]
        scale, energy, factor, _, _ = quotient(table_ref[...], entry_count)
    gathered_ref, new_ref, tensor_ref, mixed_ref = rest
    channels, block = count_channels(env), env[0].shape[1]
    for t in range(states):
        vector = vector_ref[t]
        if renew:
            vector = updated(vector, image_ref[t], scale, energy, factor)
        new_ref[t] = vector
        tensor_ref[0, t] = vector.astype(jnp.bfloat16)
        for cls in range(1, CLASSES):
            vector = rolled[cls - 1][t]
            if renew:
                image = moved[cls - 1][t].astype(jnp.float32)
                vector = updated(vector.astype(jnp.float32), image, scale, energy, factor)
            tensor_ref[cls, t] = vector.astype(jnp.bfloat16)
    write = into(gathered_ref, channels, block)

    def body(offset, height):
        tensors = [[tensor_ref[cls, t] for t in range(states)] for cls in range(CLASSES)]
        mix_left(env, tensors, mixed_ref, offset, height)
        mix_channels(groups, channels, weight_ref, mixed_ref, write, offset, height)

    by_parts(block, body)


def operator_back_kernel(states, pieces, *refs):
    rights = [refs[t * pieces : (t + 1) * pieces] for t in range(states)]
    refs = refs[states * pieces :]
    squares, refs = refs[: 2 * ENV_STEPS + 1], refs[2 * ENV_STEPS + 1 :]
    gathered_ref, vector_ref, image_ref, half_ref, sums_ref = refs
    channels, block = count_channels(rights[0]), rights[0][0].shape[1]
    a = jnp.zeros((1, 1), jnp.float32)
    b = jnp.zeros((1, 1), jnp.float32)
    for s in range(states):
        total = jnp.zeros((block, block), jnp.float32)
        for batch in batches(list(range(channels)), 6):
            left = jnp.concatenate(
                [
                    gathered_ref[pl.ds((s * channels + channel) * block, block), :]
                    for channel in batch
                ],
                axis=1,
            )
            right = jnp.concatenate([channel_of(rights[s], channel) for channel in batch], axis=0)
            total = total + jnp.dot(left, right, preferred_element_type=jnp.float32)
        image_ref[s] = total
        half_ref[s] = total.astype(jnp.bfloat16)
        vector = vector_ref[s]
        a = a + sum_all(vector * total)
        b = b + sum_all(vector * vector)
    e = jnp.where(b > 0, a / jnp.where(b > 0, b, 1.0), 0.0)
    residual = image_ref[...].reshape(states * block, block) - e * vector_ref[...].reshape(
        states * block, block
    )
    unit = jnp.max(jnp.max(jnp.abs(residual), axis=0, keepdims=True), axis=1, keepdims=True)
    unit = jnp.where(unit > 0, unit, 1.0)
    residual = residual / unit
    lane = lax.broadcasted_iota(jnp.int32, sums_ref.shape, 1)
    sums = jnp.zeros(sums_ref.shape, jnp.float32)
    values = (a, b, e, sum_all(residual * residual), unit, *(sum_all(x[...]) for x in squares))
    for place, value in enumerate(values):
        sums = jnp.where(lane == place, value, sums)
    sums_ref[...] = sums


def operator_whole_kernel(groups, states, pieces, entry_count, counts, *refs):
    front, refs = refs[: counts[0]], refs[counts[0] :]
    back, refs = refs[: counts[1]], refs[counts[1] :]
    image_ref, half_ref, sums_ref, new_ref, gathered_ref, tensor_ref, mixed_ref = refs
    operator_front_kernel(
        groups, states, pieces, True, entry_count, *front, gathered_ref, new_ref, tensor_ref, mixed_ref
    )
    operator_back_kernel(
        states, pieces, *back, gathered_ref, new_ref, image_ref, half_ref, sums_ref
    )


def polar_kernel(entry_count, both_ref, table_ref, centre_ref, out_ref, energy_ref):
    states, _, block, _ = both_ref.shape
    rows = lax.broadcasted_iota(jnp.int32, (block, block), 0)
    columns = lax.broadcasted_iota(jnp.int32, (block, block), 1)
    unit = (rows == columns).astype(jnp.float32)

    def product(x, y, contract=((1,), (0,))):
        return lax.dot_general(
            x, y, (contract, ((), ())), precision=HIGHEST, preferred_element_type=jnp.float32
        )

    scale, energy, factor, square, centre_sq = quotient(table_ref[...], entry_count)
    energy_ref[...] = jnp.broadcast_to(energy, energy_ref.shape)
    vector = updated(
        both_ref[:, 0].reshape(states * block, block),
        both_ref[:, 1].reshape(states * block, block),
        scale,
        energy,
        factor,
    ) * lax.rsqrt(square + TINY)
    centre = centre_ref[...].astype(jnp.float32) * lax.rsqrt(centre_sq + TINY)
    grams = [product(x, x, ((0,), (0,))) for x in (vector, centre)]
    totals = [unit, unit]
    for step in range(POLAR):
        factors = [1.5 * unit - 0.5 * gram for gram in grams]
        totals = [
            factor if step == 0 else product(total, factor)
            for total, factor in zip(totals, factors)
        ]
        if step < POLAR - 1:
            grams = [
                product(product(factor, gram), factor) for gram, factor in zip(grams, factors)
            ]
    closing = product(totals[0], product(centre, totals[1]), ((1,), (1,)))
    out_ref[...] = product(vector, closing).reshape(states, block, block).astype(jnp.bfloat16)


def call(kernel, out_shape, scratch_shapes, flops, operands):
    return pl.pallas_call(
        kernel,
        out_shape=out_shape,
        scratch_shapes=scratch_shapes,
        compiler_params=pltpu.CompilerParams(vmem_limit_bytes=VMEM_LIMIT),
        cost_estimate=pl.CostEstimate(
            flops=flops,
            bytes_accessed=sum(int(np.prod(x.shape)) * x.dtype.itemsize for x in operands),
            transcendentals=0,
        ),
    )(*operands)


def float_out(*shape):
    return jax.ShapeDtypeStruct(shape, jnp.float32)


def half_out(*shape):
    return jax.ShapeDtypeStruct(shape, jnp.bfloat16)


def work(states, channels, block):
    return 4 * states * channels * block**3 + 2 * (states * channels * block) ** 2


def expanded(weight, groups, channels, states):
    spread = spread_matrix(groups, channels, states)
    sizes = tuple(even(len(group)) * ROWS for group in groups)
    return call(
        functools.partial(expand_kernel, sizes),
        half_out(spread.shape[0], -(-max(sizes) // 128) * 128),
        [],
        2 * spread.size * spread.shape[0],
        (weight, jnp.asarray(spread, jnp.bfloat16)),
    )


def left_front(env, tensors, weight, groups):
    channels, block = count_channels(env), env[0].shape[1]
    states, pieces = tensors.shape[1], len(env)
    outs = call(
        functools.partial(left_kernel, groups, states, pieces),
        [half_out(channels // pieces, block, block)] * (states * pieces),
        [pltpu.VMEM((states * channels * block // PARTS, block), jnp.float32)],
        work(states, channels, block),
        (*env, tensors, weight),
    )
    return [outs[s * pieces : (s + 1) * pieces] for s in range(states)]


def left_close(iso, gathered, moved):
    channels, block, _ = gathered.shape
    return call(
        left_close_kernel,
        (half_out(channels, block, block), float_out(ROWS, block)),
        [],
        2 * channels * block**3,
        (iso, gathered, moved),
    )


def right_whole(envs, own, tensors, weight, groups):
    channels, block = count_channels(envs[0]), envs[0][0].shape[1]
    states, pieces = len(envs), len(envs[0])
    outs = call(
        functools.partial(right_kernel, groups, states, pieces),
        [half_out(channels // pieces, block, block)] * pieces + [float_out(ROWS, block)],
        [
            pltpu.VMEM((states * channels * block // PARTS, block), jnp.float32),
            pltpu.VMEM((states * channels * block, block), jnp.bfloat16),
        ],
        work(states, channels, block),
        (*(chunk for env in envs for chunk in env), own, tensors, weight),
    )
    return outs[:pieces], outs[pieces]


def front_scratch(states, channels, block):
    return [
        pltpu.VMEM((CLASSES, states, block, block), jnp.bfloat16),
        pltpu.VMEM((states * channels * block // PARTS, block), jnp.float32),
    ]


def back_outs(states, block):
    return (
        float_out(states, block, block),
        half_out(states, block, block),
        float_out(1, LANES),
    )


def operator_front(env, weight, groups, entry_count, vector, rolled):
    channels, block = count_channels(env), env[0].shape[1]
    states, pieces = vector.shape[0], len(env)
    return call(
        functools.partial(operator_front_kernel, groups, states, pieces, False, entry_count),
        (half_out(states * channels * block, block), float_out(states, block, block)),
        front_scratch(states, channels, block),
        work(states, channels, block),
        (*env, weight, vector, *rolled),
    )


def operator_back(rights, squares, gathered, vector):
    channels, block = count_channels(rights[0]), rights[0][0].shape[1]
    states, pieces = len(rights), len(rights[0])
    return call(
        functools.partial(operator_back_kernel, states, pieces),
        back_outs(states, block),
        [],
        2 * states * channels * block**3,
        (*(chunk for right in rights for chunk in right), *squares, gathered, vector),
    )


def operator_whole(env, weight, groups, entry_count, vector, rolled, news, rights, squares):
    channels, block = count_channels(env), env[0].shape[1]
    states, pieces = vector.shape[0], len(env)
    front = (*env, weight, vector, *rolled, *news)
    back = (*(chunk for right in rights for chunk in right), *squares)
    counts = (len(front), len(back))
    return call(
        functools.partial(operator_whole_kernel, groups, states, pieces, entry_count, counts),
        (*back_outs(states, block), float_out(states, block, block)),
        [
            pltpu.VMEM((states * channels * block, block), jnp.bfloat16),
            *front_scratch(states, channels, block),
        ],
        work(states, channels, block) + 2 * states * channels * block**3,
        (*front, *back),
    )


def polar(both, table, centre, entry_count):
    states, _, block, _ = both.shape
    return call(
        functools.partial(polar_kernel, entry_count),
        (half_out(states, block, block), float_out(1, LANES)),
        [],
        600 * block**3,
        (both, table, centre),
    )


def charge_mask(channels, states, sectors):
    charge = np.array([CHARGE_STEPS[channel % CLASSES] for channel in range(channels)])
    state = np.arange(states)
    balance = (
        charge[:, None, None, None]
        + state[None, None, None, :]
        - state[None, None, :, None]
        - charge[None, :, None, None]
    )
    return jnp.asarray((balance % sectors == 0).astype(np.float32)).astype(jnp.bfloat16)


def weight_matrices(mpo, pattern, sectors):
    channels, _, states, _ = mpo.shape
    allowed = charge_mask(channels, states, sectors)
    weights = mpo * pattern[:, :, None, None].astype(jnp.bfloat16) * allowed
    size = states * channels
    left = jnp.transpose(weights, (2, 1, 3, 0)).reshape(size, size)
    right = jnp.transpose(weights, (2, 0, 3, 1)).reshape(size, size)
    return jnp.stack([left, right])


def other_classes_of(places, x):
    one, minus = places.ahead(x, 1), places.ahead(x, -1)
    return one, minus, places.ahead(one, 1), places.ahead(minus, -1)


def classes_of(places, x):
    return jnp.stack([x, *other_classes_of(places, x)])


def other_classes_at_once(places, x):
    return tuple(places.ahead(x, charge) for charge in CHARGE_STEPS[1:])


def after(first, then):
    return lax.optimization_barrier((first, then))


def local(left_iso, right_iso, centre, left_env, right_env, mpo, pattern):
    sites, secs = lax.axis_size("site"), lax.axis_size("sec")
    places = Places(sites, secs)
    left_iso, right_iso, centre = left_iso[0, :, 0], right_iso[0, :, 0], centre[0, 0]
    states, block, _ = left_iso.shape
    channels = mpo.shape[1]
    entry_count = left_env.size * secs
    left_groups = label_groups(channels, states, secs, 1)
    right_groups = label_groups(channels, states, secs, -1)

    pieces = PIECES if channels % PIECES == 0 else 1

    def ahead(env, by, chain_by=0):
        return [places.ahead(chunk, by, chain_by) for chunk in env]

    both_isos = places.fetch(jnp.concatenate([left_iso, right_iso]))
    left_isos, right_isos = [both_isos[:states]], [both_isos[states:]]
    for step in range(1, ENV_STEPS):
        left_isos.append(places.fetch(left_iso, step))
        right_isos.append(places.fetch(right_iso, -step))
    own_tensors = places.fetch(jnp.concatenate([left_iso, centre[None]]), ENV_STEPS)
    (left_isos, right_isos, own_tensors), envs = after(
        (left_isos, right_isos, own_tensors),
        jnp.concatenate([right_env[0, :, 0], left_env[0, :, 0]]),
    )
    envs = jnp.split(places.fetch(envs), 2 * pieces)
    right, left = envs[:pieces], envs[pieces:]
    rolled = [
        classes_of(places, jnp.concatenate([left_isos[step], right_isos[step]]))
        for step in range(ENV_STEPS)
    ]
    own_iso, own_centre = own_tensors[:states], own_tensors[states]
    centres = [own_centre] + [places.ahead(own_centre, s) for s in range(1, states)]

    gathered_weights = lax.all_gather(weight_matrices(mpo[0], pattern[0], secs), "site")
    chain = places.my_chain()

    def weight_of(site_by, kind):
        weight = lax.dynamic_index_in_dim(
            gathered_weights, (chain + site_by) % sites, 0, False
        )[kind]
        return expanded(weight, (left_groups, right_groups)[kind], channels, states)

    weights = (
        [weight_of(step, 0) for step in range(ENV_STEPS + 1)],
        [weight_of(-step, 1) for step in range(ENV_STEPS)],
    )
    vector = jnp.einsum(
        "sxy,syz->sxz", own_iso, jnp.stack(centres), preferred_element_type=jnp.float32
    )
    rolled_vector = other_classes_of(places, vector.astype(jnp.bfloat16))
    (right, left), (rolled, rolled_vector, weights) = after(
        (right, left), (rolled, rolled_vector, weights)
    )
    centre_float = own_centre.astype(jnp.float32)
    centre_square = jnp.sum((centre_float * centre_float).reshape(-1, ROWS, block), axis=0)

    left_squares, right_squares = [], []
    for step in range(ENV_STEPS):
        envs = [right]
        for t in range(1, states):
            envs.append(ahead(envs[-1], 1))
        right, square = right_whole(
            envs,
            right_isos[step],
            rolled[step][:, states:],
            weights[1][step],
            right_groups,
        )
        right_squares.append(square)

        gathered = left_front(left, rolled[step][:, :states], weights[0][step], left_groups)
        moved = [None] * pieces
        for s in reversed(range(1, states)):
            for piece in range(pieces):
                part = jnp.einsum(
                    "xy,vxz->vyz",
                    left_isos[step][s],
                    gathered[s][piece],
                    preferred_element_type=jnp.float32,
                )
                if moved[piece] is not None:
                    part = part + moved[piece].astype(jnp.float32)
                moved[piece] = places.ahead(part.astype(jnp.bfloat16), -1)
        closed = [
            left_close(left_isos[step][0], gathered[0][piece], moved[piece])
            for piece in range(pieces)
        ]
        left = [env for env, _ in closed]
        left_squares.append(sum(square for _, square in closed))

    if (2 * ENV_STEPS) % sites:
        right = ahead(right, 0, 2 * ENV_STEPS)
        right_squares = ahead(right_squares, 0, 2 * ENV_STEPS)
    squares = left_squares + right_squares + [centre_square]
    rights = [right]
    for s in range(1, states):
        rights.append(ahead(rights[-1], 1))
    weight = weights[0][ENV_STEPS]
    gathered, vector = operator_front(
        left, weight, left_groups, entry_count, vector, rolled_vector
    )
    image, half_image, own_sums = operator_back(rights, squares, gathered, vector)
    table = places.collect(own_sums)
    news = (image, *other_classes_at_once(places, half_image), table)
    image, _, own_sums, vector = operator_whole(
        left, weight, left_groups, entry_count, vector, rolled_vector, news, rights, squares
    )
    table = places.collect(own_sums)

    both = jnp.stack([vector, image], axis=1)
    columns = jnp.stack([both[0]] + [places.ahead(both[s], -s) for s in range(1, states)])
    column_left, energy = polar(columns, table, own_centre, entry_count)
    new_left = jnp.stack(
        [places.send_home(column_left[s], ENV_STEPS, -s) for s in range(states)]
    )
    energy = places.send_home(energy, ENV_STEPS, 0)
    return new_left[None, :, None], energy[0, :1]


def solution(mesh):
    placed = (
        P("site", None, "sec", None, None),
        P("site", None, "sec", None, None),
        P("site", "sec", None, None),
        P("site", None, "sec", None, None),
        P("site", None, "sec", None, None),
        P("site", None, None, None, None),
        P("site", None, None),
    )
    return jax.shard_map(
        local,
        mesh=mesh,
        in_specs=placed,
        out_specs=(P("site", None, "sec", None, None), P("site")),
        check_vma=False,
    )
```

profile of v0, /device:TPU:0, one launch (start us, length us, event | category | flops | bytes accessed | tf_op | source)
XLA Modules:
  0.0 329.8 jit_solution(4380904072931740028)
XLA Ops:
  0.6 5.0 %collective-permute-start.1 = (bf16[4,128,128]{2,1,0:T(8,128)(2,1)}, bf16[4,128,128]{2,1,0:T(8,128)(2,1)S(1)}, u32[]{:S(2)}, u32[]{:S(2)}) collective-permute-start(bf16[4,128,128]{2,1,0:T(8,128)(2,1)} %bitcast.201), channel_id=1, source_target_pairs={{8,0},{9,8},{10,1},{11,9},{12,3},{13,11},{14,2},{15,10},{16,4},{17... | collective-permute-start | bytes 393224 | tf_op jit(solution)/shard_map/ppermute | solution.py:51
  5.7 4.4 %collective-permute-start.2 = (bf16[4,128,128]{2,1,0:T(8,128)(2,1)}, bf16[4,128,128]{2,1,0:T(8,128)(2,1)S(1)}, u32[]{:S(2)}, u32[]{:S(2)}) collective-permute-start(bf16[4,128,128]{2,1,0:T(8,128)(2,1)} %bitcast.204), channel_id=1, source_target_pairs={{24,0},{25,8},{26,1},{27,9},{28,3},{29,11},{30,2},{31,10},{0,4},{1... | collective-permute-start | bytes 393224 | tf_op jit(solution)/shard_map/ppermute | solution.py:51
  15.9 9.2 %all-gather = bf16[8,168,168]{2,1,0:T(8,128)(2,1)S(1)} all-gather(bf16[2,168,168]{2,1,0:T(8,128)(2,1)S(1)} %pad_maximum_fusion.3), channel_id=2, replica_groups=mesh['site'=4,'sec'=8] {'site'}, dimensions={0}, use_global_device_ids=true | all-gather | bytes 564480 | tf_op jit(solution)/shard_map/all_gather | solution.py:704
  32.1 3.2 collective-permute-start.13
  37.0 5.8 %collective-permute-start.10 = (bf16[8,128,128]{2,1,0:T(8,128)(2,1)S(1)}, bf16[8,128,128]{2,1,0:T(8,128)(2,1)S(1)}, u32[]{:S(2)}, u32[]{:S(2)}) collective-permute-start(bf16[8,128,128]{2,1,0:T(8,128)(2,1)S(1)} %constant_dynamic-update-slice_fusion.2), channel_id=1, source_target_pairs={{10,0},{0,8},{8,1},{1,9},{9,3},{3,11},{11,2},{2,10},{14,4},{4,12},... | collective-permute-start | bytes 786440 | tf_op jit(solution)/shard_map/ppermute | solution.py:61
  44.3 8.0 %collective-permute-done.16.refs_4_ = bf16[4,128,128]{2,1,0:T(8,128)(2,1)S(1)} collective-permute-done((bf16[4,128,128]{2,1,0:T(8,128)(2,1)S(1)}, bf16[4,128,128]{2,1,0:T(8,128)(2,1)S(1)}, u32[]{:S(2)}, u32[]{:S(2)}) %collective-permute-start.16) | collective-permute-done | bytes 131104 | tf_op jit(solution)/shard_map/ppermute | solution.py:61
  52.4 23.7 %collective-permute-start.6 = (bf16[8,128,128]{2,1,0:T(8,128)(2,1)S(1)}, bf16[8,128,128]{2,1,0:T(8,128)(2,1)S(1)}, u32[]{:S(2)}, u32[]{:S(2)}) collective-permute-start(bf16[8,128,128]{2,1,0:T(8,128)(2,1)S(1)} %constant_dynamic-update-slice_fusion), channel_id=1, source_target_pairs={{10,0},{0,8},{8,1},{1,9},{9,3},{3,11},{11,2},{2,10},{14,4},{4,12},... | collective-permute-start | bytes 786440 | tf_op jit(solution)/shard_map/ppermute | solution.py:61
  76.7 1.5 collective-permute-start.11
  78.2 2.8 collective-permute-start.12
  82.1 2.2 collective-permute-start.7
  84.3 2.6 collective-permute-start.8
  88.2 21.5 %collective-permute-done.8 = bf16[8,128,128]{2,1,0:T(8,128)(2,1)S(1)} collective-permute-done((bf16[8,128,128]{2,1,0:T(8,128)(2,1)S(1)}, bf16[8,128,128]{2,1,0:T(8,128)(2,1)S(1)}, u32[]{:S(2)}, u32[]{:S(2)}) %collective-permute-start.8) | collective-permute-done | bytes 262176 | tf_op jit(solution)/shard_map/ppermute | solution.py:61
  110.1 3.6 %collective-permute-start.33 = (bf16[21,128,128]{2,1,0:T(8,128)(2,1)S(1)}, bf16[21,128,128]{2,1,0:T(8,128)(2,1)S(1)}, u32[]{:S(2)}, u32[]{:S(2)}) collective-permute-start(bf16[21,128,128]{2,1,0:T(8,128)(2,1)S(1)} %get-tuple-element.102.refs_1_), channel_id=1, source_target_pairs={{8,0},{1,8},{9,1},{3,9},{11,3},{2,11},{10,2},{0,10},{12,4},{5,12},... | collective-permute-start | bytes 2064392 | tf_op jit(solution)/shard_map/ppermute | solution.py:61
  113.8 5.2 %shard_map.145 = (bf16[21,128,128]{2,1,0:T(8,128)(2,1)S(1)}, bf16[21,128,128]{2,1,0:T(8,128)(2,1)S(1)}, bf16[21,128,128]{2,1,0:T(8,128)(2,1)S(1)}, bf16[21,128,1...) custom-call(bf16[21,128,128]{2,1,0:T(8,128)(2,1)S(1)} %get-tuple-ele, ...), custom_call_target="tpu_custom_call" | custom-call | flops 2334130176 | bytes 3076096 | tf_op jit(solution)/shard_map/pallas_call | solution.py:486
  119.0 1.4 collective-permute-start.34
  120.4 5.5 %collective-permute-done.33.refs_3_ = bf16[21,128,128]{2,1,0:T(8,128)(2,1)S(1)} collective-permute-done((bf16[21,128,128]{2,1,0:T(8,128)(2,1)S(1)}, bf16[21,128,128]{2,1,0:T(8,128)(2,1)S(1)}, u32[]{:S(2)}, u32[]{:S(2)}) %collective-permute-start.33) | collective-permute-done | bytes 688160 | tf_op jit(solution)/shard_map/ppermute | solution.py:61
  125.9 1.9 collective-permute-start.35
  128.7 4.6 %collective-permute-done.34.refs_4_ = bf16[21,128,128]{2,1,0:T(8,128)(2,1)S(1)} collective-permute-done((bf16[21,128,128]{2,1,0:T(8,128)(2,1)S(1)}, bf16[21,128,128]{2,1,0:T(8,128)(2,1)S(1)}, u32[]{:S(2)}, u32[]{:S(2)}) %collective-permute-start.34) | collective-permute-done | bytes 688160 | tf_op jit(solution)/shard_map/ppermute | solution.py:61
  133.3 2.2 collective-permute-start.36
  135.5 5.2 %collective-permute-done.35.refs_5_ = bf16[21,128,128]{2,1,0:T(8,128)(2,1)S(1)} collective-permute-done((bf16[21,128,128]{2,1,0:T(8,128)(2,1)S(1)}, bf16[21,128,128]{2,1,0:T(8,128)(2,1)S(1)}, u32[]{:S(2)}, u32[]{:S(2)}) %collective-permute-start.35) | collective-permute-done | bytes 688160 | tf_op jit(solution)/shard_map/ppermute | solution.py:61
  140.6 2.2 collective-permute-start.37
  143.5 2.5 collective-permute-done.20
  146.4 1.6 collective-permute-done.36.refs_6_
  148.0 7.4 %collective-permute-done.37.refs_7_ = bf16[21,128,128]{2,1,0:T(8,128)(2,1)S(1)} collective-permute-done((bf16[21,128,128]{2,1,0:T(8,128)(2,1)S(1)}, bf16[21,128,128]{2,1,0:T(8,128)(2,1)S(1)}, u32[]{:S(2)}, u32[]{:S(2)}) %collective-permute-start.37) | collective-permute-done | bytes 688160 | tf_op jit(solution)/shard_map/ppermute | solution.py:61
  155.4 6.3 %shard_map.152 = (bf16[21,128,128]{2,1,0:T(8,128)(2,1)S(1)}, bf16[21,128,128]{2,1,0:T(8,128)(2,1)S(1)}, f32[8,128]{1,0:T(8,128)S(1)}) custom-call(bf16[21,128,128]{2,1,0:T(8,128)(2,1)S(1)} %get-tuple-element.101.refs_0_, bf16[21,128,128]{2,1,0:T(8,128)(2,1)S(1)} %get-tuple-element.102.refs_1_, bf16[21,128,128]{2,1,0:T(8,128)(2,1)S(1)} %collective-permute-done.32.refs_2_, ...), custom_call_target="tpu_custom_call" | custom-call | flops 2334130176 | bytes 7335936 | tf_op jit(solution)/shard_map/pallas_call | solution.py:486
  161.7 2.3 collective-permute-start.38
  164.0 1.4 collective-permute-start.39
  166.3 6.1 %collective-permute-done.38.refs_2_ = bf16[21,128,128]{2,1,0:T(8,128)(2,1)S(1)} collective-permute-done((bf16[21,128,128]{2,1,0:T(8,128)(2,1)S(1)}, bf16[21,128,128]{2,1,0:T(8,128)(2,1)S(1)}, u32[]{:S(2)}, u32[]{:S(2)}) %collective-permute-start.38) | collective-permute-done | bytes 688160 | tf_op jit(solution)/shard_map/ppermute | solution.py:61
  172.4 2.2 collective-permute-start.40
  174.6 5.2 %collective-permute-done.39.refs_3_ = bf16[21,128,128]{2,1,0:T(8,128)(2,1)S(1)} collective-permute-done((bf16[21,128,128]{2,1,0:T(8,128)(2,1)S(1)}, bf16[21,128,128]{2,1,0:T(8,128)(2,1)S(1)}, u32[]{:S(2)}, u32[]{:S(2)}) %collective-permute-start.39) | collective-permute-done | bytes 688160 | tf_op jit(solution)/shard_map/ppermute | solution.py:61
  179.8 2.2 collective-permute-start.41
  184.2 5.2 %shard_map.148 = (bf16[21,128,128]{2,1,0:T(8,128)(2,1)S(1)}, bf16[21,128,128]{2,1,0:T(8,128)(2,1)S(1)}, bf16[21,128,128]{2,1,0:T(8,128)(2,1)S(1)}, bf16[21,128,1...) custom-call(bf16[21,128,128]{2,1,0:T(8,128)(2,1)S(1)} %get-tuple-ele, ...), custom_call_target="tpu_custom_call" | custom-call | flops 2334130176 | bytes 3076096 | tf_op jit(solution)/shard_map/pallas_call | solution.py:486
  189.4 5.1 %collective-permute-done.41.refs_5_ = bf16[21,128,128]{2,1,0:T(8,128)(2,1)S(1)} collective-permute-done((bf16[21,128,128]{2,1,0:T(8,128)(2,1)S(1)}, bf16[21,128,128]{2,1,0:T(8,128)(2,1)S(1)}, u32[]{:S(2)}, u32[]{:S(2)}) %collective-permute-start.41) | collective-permute-done | bytes 688160 | tf_op jit(solution)/shard_map/ppermute | solution.py:61
  194.5 1.9 collective-permute-start.43
  197.4 4.5 %collective-permute-done.42.refs_6_ = bf16[21,128,128]{2,1,0:T(8,128)(2,1)S(1)} collective-permute-done((bf16[21,128,128]{2,1,0:T(8,128)(2,1)S(1)}, bf16[21,128,128]{2,1,0:T(8,128)(2,1)S(1)}, u32[]{:S(2)}, u32[]{:S(2)}) %collective-permute-start.42) | collective-permute-done | bytes 688160 | tf_op jit(solution)/shard_map/ppermute | solution.py:61
  201.9 7.4 %collective-permute-done.43.refs_7_ = bf16[21,128,128]{2,1,0:T(8,128)(2,1)S(1)} collective-permute-done((bf16[21,128,128]{2,1,0:T(8,128)(2,1)S(1)}, bf16[21,128,128]{2,1,0:T(8,128)(2,1)S(1)}, u32[]{:S(2)}, u32[]{:S(2)}) %collective-permute-start.43) | collective-permute-done | bytes 688160 | tf_op jit(solution)/shard_map/ppermute | solution.py:61
  209.3 6.3 %shard_map.153 = (bf16[21,128,128]{2,1,0:T(8,128)(2,1)S(1)}, bf16[21,128,128]{2,1,0:T(8,128)(2,1)S(1)}, f32[8,128]{1,0:T(8,128)S(1)}) custom-call(bf16[21,128,128]{2,1,0:T(8,128)(2,1)S(1)} %get-tuple-element.104.refs_0_, bf16[21,128,128]{2,1,0:T(8,128)(2,1)S(1)} %get-tuple-element.105.refs_1_, bf16[21,128,128]{2,1,0:T(8,128)(2,1)S(1)} %collective-permute-done.38.refs_2_, ...), custom_call_target="tpu_custom_call" | custom-call | flops 2334130176 | bytes 7335936 | tf_op jit(solution)/shard_map/pallas_call | solution.py:486
  215.6 2.3 collective-permute-start.44
  220.0 6.4 %collective-permute-done.44.refs_2_.refs_16_ = bf16[21,128,128]{2,1,0:T(8,128)(2,1)S(1)} collective-permute-done((bf16[21,128,128]{2,1,0:T(8,128)(2,1)S(1)}, bf16[21,128,128]{2,1,0:T(8,128)(2,1)S(1)}, u32[]{:S(2)}, u32[]{:S(2)}) %collective-permute-start.44) | collective-permute-done | bytes 688160 | tf_op jit(solution)/shard_map/ppermute | solution.py:61
  226.3 2.2 collective-permute-start.46
  228.5 5.2 %collective-permute-done.45.refs_3_.refs_17_ = bf16[21,128,128]{2,1,0:T(8,128)(2,1)S(1)} collective-permute-done((bf16[21,128,128]{2,1,0:T(8,128)(2,1)S(1)}, bf16[21,128,128]{2,1,0:T(8,128)(2,1)S(1)}, u32[]{:S(2)}, u32[]{:S(2)}) %collective-permute-start.45) | collective-permute-done | bytes 688160 | tf_op jit(solution)/shard_map/ppermute | solution.py:61
  233.7 2.2 collective-permute-start.47
  235.9 1.3 fusion.5
  237.4 1.3 fusion.7
  238.7 2.4 collective-permute-done.46.refs_4_.refs_18_
  241.1 2.2 collective-permute-start.48
  243.3 5.2 %collective-permute-done.47.refs_5_.refs_19_ = bf16[21,128,128]{2,1,0:T(8,128)(2,1)} collective-permute-done((bf16[21,128,128]{2,1,0:T(8,128)(2,1)S(1)}, bf16[21,128,128]{2,1,0:T(8,128)(2,1)}, u32[]{:S(2)}, u32[]{:S(2)}) %collective-permute-start.47) | collective-permute-done | bytes 688160 | tf_op jit(solution)/shard_map/ppermute | solution.py:61
  248.4 2.2 collective-permute-start.49
  252.7 2.5 collective-permute-done.28.moved_ref
  255.7 5.2 %shard_map.151 = (bf16[21504,128]{1,0:T(8,128)(2,1)S(1)}, f32[4,128,128]{2,1,0:T(8,128)S(1)}) custom-call(bf16[21,128,128]{2,1,0:T(8,128)(2,1)S(1)} %get-tuple-element.89.refs_0_, bf16[21,128,128]{2,1,0:T(8,128)(2,1)S(1)} %get-tuple-element.94.refs_1_, bf16[1360,384]{1,0:T(8,128)(2,1)S(1)} %copy-done.27, f32[4,128,128]{2,1,0:T(8,128)S(1)} %copy-done.25, ...), custom_call_target="tpu_custom_call" | custom-call | flops 2334130176 | bytes 3207168 | tf_op jit(solution)/shard_map/pallas_call | solution.py:486
  260.9 2.4 collective-permute-done.49.refs_7_.refs_21_
  263.3 3.7 %shard_map.154 = (f32[4,128,128]{2,1,0:T(8,128)S(1)}, bf16[4,128,128]{2,1,0:T(8,128)(2,1)S(1)}, f32[1,128]{1,0:T(1,128)S(1)}) custom-call(bf16[21,128,128]{2,1,0:T(8,128)(2,1)S(1)} %get-tuple-element.107.refs_0_.refs_14_, bf16[21,128,128]{2,1,0:T(8,128)(2,1)S(1)} %copy-done.1, bf16[21,128,128]{2,1,0:T(8,128)(2,1)S(1)} %copy-done.3, ...), custom_call_target="tpu_custom_call" | custom-call | flops 704643072 | bytes 11292672 | tf_op jit(solution)/shard_map/pallas_call | solution.py:486
  268.9 4.6 %collective-permute-start.50 = (bf16[4,128,128]{2,1,0:T(8,128)(2,1)}, bf16[4,128,128]{2,1,0:T(8,128)(2,1)}, u32[]{:S(2)}, u32[]{:S(2)}) collective-permute-start(bf16[4,128,128]{2,1,0:T(8,128)(2,1)} %copy-done.22), channel_id=1, source_target_pairs={{8,0},{1,8},{9,1},{3,9},{11,3},{2,11},{10,2},{0,10},{12,4},{5,12},... | collective-permute-start | bytes 393224 | tf_op jit(solution)/shard_map/ppermute | solution.py:61
  275.6 1.4 collective-permute-start.56
  276.9 3.2 collective-permute-done.56
  287.1 10.1 %shard_map.155 = (f32[4,128,128]{2,1,0:T(8,128)S(1)}, bf16[4,128,128]{2,1,0:T(8,128)(2,1)}, f32[1,128]{1,0:T(1,128)S(1)}, f32[4,128,128]{2,1,0:T(8,128)S(1)}) custom-call(bf16[21,128,128]{2,1,0:T(8,128)(2,1)S(1)} %copy-done.9, bf16[21,128,128]{2,1,0:T(8,128)(2,1)S(1)} %copy-done.7, bf16[1360,384]{1,0:T(8,128)(2,1)S(1)} %copy-done.28, ...), custom_call_target="tpu_custom_call" | custom-call | flops 3038773248 | bytes 9523200 | tf_op jit(solution)/shard_map/pallas_call | solution.py:486
  298.3 1.5 collective-permute-start.61
  300.5 1.5 collective-permute-start.59
  302.0 1.5 collective-permute-start.62
  303.5 3.0 collective-permute-done.62
  306.6 4.8 %shard_map.156 = (bf16[4,128,128]{2,1,0:T(8,128)(2,1)S(1)}, f32[1,128]{1,0:T(1,128)S(1)}) custom-call(f32[4,2,128,128]{3,2,1,0:T(8,128)S(1)} %pad_maximum_fusion.1.both_ref, f32[8,128]{1,0:T(8,128)S(1)} %maximum_select_fusion.1.table_ref, bf16[128,128]{1,0:T(8,128)(2,1)S(1)} %get-tuple-element.152.centre_ref), custom_call_target="tpu_custom_call" | custom-call | flops 1258291200 | bytes 561152 | tf_op jit(solution)/shard_map/pallas_call | solution.py:486
  312.7 9.7 %collective-permute-start.64 = (bf16[128,128]{1,0:T(8,128)(2,1)S(1)}, bf16[128,128]{1,0:T(8,128)(2,1)S(1)}, u32[]{:S(2)}, u32[]{:S(2)}) collective-permute-start(bf16[128,128]{1,0:T(8,128)(2,1)S(1)} %get-tuple-element.156), channel_id=1, source_target_pairs={{0,23},{8,16},{1,17},{9,18},{3,19},{11,20},{2,21},{10,22},{4,31},{... | collective-permute-start | bytes 98312 | tf_op jit(solution)/shard_map/ppermute | solution.py:56
  323.7 1.4 collective-permute-start.67
  325.0 2.2 collective-permute-done.67
  (217 shorter events, 46.4 us)
Async XLA Ops:
  0.6 31.4 %collective-permute-start.1 = (bf16[4,128,128]{2,1,0:T(8,128)(2,1)}, bf16[4,128,128]{2,1,0:T(8,128)(2,1)S(1)}, u32[]{:S(2)}, u32[]{:S(2)}) collective-permute-start(bf16[4,128,128]{2,1,0:T(8,128)(2,1)} %bitcast.201), channel_id=1, source_target_pairs={{8,0},{9,8},{10,1},{11,9},{12,3},{13,11},{14,2},{15,10},{16,4},{17... | collective-permute-start | bytes 393224 | tf_op jit(solution)/shard_map/ppermute | solution.py:51
  5.7 26.4 %collective-permute-start.2 = (bf16[4,128,128]{2,1,0:T(8,128)(2,1)}, bf16[4,128,128]{2,1,0:T(8,128)(2,1)S(1)}, u32[]{:S(2)}, u32[]{:S(2)}) collective-permute-start(bf16[4,128,128]{2,1,0:T(8,128)(2,1)} %bitcast.204), channel_id=1, source_target_pairs={{24,0},{25,8},{26,1},{27,9},{28,3},{29,11},{30,2},{31,10},{0,4},{1... | collective-permute-start | bytes 393224 | tf_op jit(solution)/shard_map/ppermute | solution.py:51
  11.1 20.9 %collective-permute-start = (bf16[8,128,128]{2,1,0:T(8,128)(2,1)S(1)}, bf16[8,128,128]{2,1,0:T(8,128)(2,1)S(1)}, u32[]{:S(2)}, u32[]{:S(2)}) collective-permute-start(bf16[8,128,128]{2,1,0:T(8,128)(2,1)S(1)} %pad_maximum_fusion.2), channel_id=1, source_target_pairs={{0,0},{1,8},{2,1},{3,9},{4,3},{5,11},{6,2},{7,10},{8,4},{9,12},{10... | collective-permute-start | bytes 786440 | tf_op jit(solution)/shard_map/ppermute | solution.py:51
  12.7 19.3 %collective-permute-start.3 = (bf16[5,128,128]{2,1,0:T(8,128)(2,1)S(1)}, bf16[5,128,128]{2,1,0:T(8,128)(2,1)S(1)}, u32[]{:S(2)}, u32[]{:S(2)}) collective-permute-start(bf16[5,128,128]{2,1,0:T(8,128)(2,1)S(1)} %pad_maximum_fusion.4), channel_id=1, source_target_pairs={{16,0},{17,8},{18,1},{19,9},{20,3},{21,11},{22,2},{23,10},{24,4},{... | collective-permute-start | bytes 491528 | tf_op jit(solution)/shard_map/ppermute | solution.py:51
  32.1 5.0 %collective-permute-start.13 = (bf16[128,128]{1,0:T(8,128)(2,1)S(1)}, bf16[128,128]{1,0:T(8,128)(2,1)S(1)}, u32[]{:S(2)}, u32[]{:S(2)}) collective-permute-start(bf16[128,128]{1,0:T(8,128)(2,1)S(1)} %get-tuple-element.152.centre_ref), channel_id=1, source_target_pairs={{8,0},{1,8},{9,1},{3,9},{11,3},{2,11},{10,2},{0,10},{12,4},{5,12},... | collective-permute-start | bytes 98312 | tf_op jit(solution)/shard_map/ppermute | solution.py:61
  35.3 7.6 %collective-permute-start.14 = (bf16[128,128]{1,0:T(8,128)(2,1)S(1)}, bf16[128,128]{1,0:T(8,128)(2,1)S(1)}, u32[]{:S(2)}, u32[]{:S(2)}) collective-permute-start(bf16[128,128]{1,0:T(8,128)(2,1)S(1)} %get-tuple-element.152.centre_ref), channel_id=1, source_target_pairs={{1,0},{9,8},{3,1},{11,9},{2,3},{10,11},{0,2},{8,10},{5,4},{13,12},... | collective-permute-start | bytes 98312 | tf_op jit(solution)/shard_map/ppermute | solution.py:61
  35.7 7.2 %collective-permute-start.15 = (bf16[128,128]{1,0:T(8,128)(2,1)S(1)}, bf16[128,128]{1,0:T(8,128)(2,1)S(1)}, u32[]{:S(2)}, u32[]{:S(2)}) collective-permute-start(bf16[128,128]{1,0:T(8,128)(2,1)S(1)} %get-tuple-element.152.centre_ref), channel_id=1, source_target_pairs={{9,0},{3,8},{11,1},{2,9},{10,3},{0,11},{8,2},{1,10},{13,4},{7,12},... | collective-permute-start | bytes 98312 | tf_op jit(solution)/shard_map/ppermute | solution.py:61
  35.8 8.0 %collective-permute-start.9 = (bf16[8,128,128]{2,1,0:T(8,128)(2,1)S(1)}, bf16[8,128,128]{2,1,0:T(8,128)(2,1)S(1)}, u32[]{:S(2)}, u32[]{:S(2)}) collective-permute-start(bf16[8,128,128]{2,1,0:T(8,128)(2,1)S(1)} %constant_dynamic-update-slice_fusion.2), channel_id=1, source_target_pairs={{8,0},{1,8},{9,1},{3,9},{11,3},{2,11},{10,2},{0,10},{12,4},{5,12},... | collective-permute-start | bytes 786440 | tf_op jit(solution)/shard_map/ppermute | solution.py:61
  35.9 73.8 %collective-permute-start.4 = (bf16[84,128,128]{2,1,0:T(8,128)(2,1)S(1)}, bf16[84,128,128]{2,1,0:T(8,128)(2,1)S(1)}, u32[]{:S(2)}, u32[]{:S(2)}) collective-permute-start(bf16[84,128,128]{2,1,0:T(8,128)(2,1)S(1)} %pad_maximum_fusion), channel_id=1, source_target_pairs={{0,0},{1,8},{2,1},{3,9},{4,3},{5,11},{6,2},{7,10},{8,4},{9,12},{10... | collective-permute-start | bytes 8257544 | tf_op jit(solution)/shard_map/ppermute | solution.py:51
  37.0 39.1 %collective-permute-start.10 = (bf16[8,128,128]{2,1,0:T(8,128)(2,1)S(1)}, bf16[8,128,128]{2,1,0:T(8,128)(2,1)S(1)}, u32[]{:S(2)}, u32[]{:S(2)}) collective-permute-start(bf16[8,128,128]{2,1,0:T(8,128)(2,1)S(1)} %constant_dynamic-update-slice_fusion.2), channel_id=1, source_target_pairs={{10,0},{0,8},{8,1},{1,9},{9,3},{3,11},{11,2},{2,10},{14,4},{4,12},... | collective-permute-start | bytes 786440 | tf_op jit(solution)/shard_map/ppermute | solution.py:61
  42.9 33.8 %collective-permute-start.5 = (bf16[8,128,128]{2,1,0:T(8,128)(2,1)S(1)}, bf16[8,128,128]{2,1,0:T(8,128)(2,1)S(1)}, u32[]{:S(2)}, u32[]{:S(2)}) collective-permute-start(bf16[8,128,128]{2,1,0:T(8,128)(2,1)S(1)} %constant_dynamic-update-slice_fusion), channel_id=1, source_target_pairs={{8,0},{1,8},{9,1},{3,9},{11,3},{2,11},{10,2},{0,10},{12,4},{5,12},... | collective-permute-start | bytes 786440 | tf_op jit(solution)/shard_map/ppermute | solution.py:61
  43.8 8.6 %collective-permute-start.16 = (bf16[4,128,128]{2,1,0:T(8,128)(2,1)S(1)}, bf16[4,128,128]{2,1,0:T(8,128)(2,1)S(1)}, u32[]{:S(2)}, u32[]{:S(2)}) collective-permute-start(bf16[4,128,128]{2,1,0:T(8,128)(2,1)S(1)} %get-tuple-element.157), channel_id=1, source_target_pairs={{8,0},{1,8},{9,1},{3,9},{11,3},{2,11},{10,2},{0,10},{12,4},{5,12},... | collective-permute-start | bytes 393224 | tf_op jit(solution)/shard_map/ppermute | solution.py:61
  43.8 32.3 %collective-permute-start.17 = (bf16[4,128,128]{2,1,0:T(8,128)(2,1)S(1)}, bf16[4,128,128]{2,1,0:T(8,128)(2,1)S(1)}, u32[]{:S(2)}, u32[]{:S(2)}) collective-permute-start(bf16[4,128,128]{2,1,0:T(8,128)(2,1)S(1)} %get-tuple-element.157), channel_id=1, source_target_pairs={{10,0},{0,8},{8,1},{1,9},{9,3},{3,11},{11,2},{2,10},{14,4},{4,12},... | collective-permute-start | bytes 393224 | tf_op jit(solution)/shard_map/ppermute | solution.py:61
  52.4 25.8 %collective-permute-start.6 = (bf16[8,128,128]{2,1,0:T(8,128)(2,1)S(1)}, bf16[8,128,128]{2,1,0:T(8,128)(2,1)S(1)}, u32[]{:S(2)}, u32[]{:S(2)}) collective-permute-start(bf16[8,128,128]{2,1,0:T(8,128)(2,1)S(1)} %constant_dynamic-update-slice_fusion), channel_id=1, source_target_pairs={{10,0},{0,8},{8,1},{1,9},{9,3},{3,11},{11,2},{2,10},{14,4},{4,12},... | collective-permute-start | bytes 786440 | tf_op jit(solution)/shard_map/ppermute | solution.py:61
  76.1 33.9 %collective-permute-start.18 = (bf16[4,128,128]{2,1,0:T(8,128)(2,1)S(1)}, bf16[4,128,128]{2,1,0:T(8,128)(2,1)S(1)}, u32[]{:S(2)}, u32[]{:S(2)}) collective-permute-start(bf16[4,128,128]{2,1,0:T(8,128)(2,1)S(1)} %collective-permute-done.16.refs_4_), channel_id=1, source_target_pairs={{8,0},{1,8},{9,1},{3,9},{11,3},{2,11},{10,2},{0,10},{12,4},{5,12},... | collective-permute-start | bytes 393224 | tf_op jit(solution)/shard_map/ppermute | solution.py:61
  76.1 33.9 %collective-permute-start.19 = (bf16[4,128,128]{2,1,0:T(8,128)(2,1)S(1)}, bf16[4,128,128]{2,1,0:T(8,128)(2,1)S(1)}, u32[]{:S(2)}, u32[]{:S(2)}) collective-permute-start(bf16[4,128,128]{2,1,0:T(8,128)(2,1)S(1)} %collective-permute-done.17.refs_5_), channel_id=1, source_target_pairs={{10,0},{0,8},{8,1},{1,9},{9,3},{3,11},{11,2},{2,10},{14,4},{4,12},... | collective-permute-start | bytes 393224 | tf_op jit(solution)/shard_map/ppermute | solution.py:61
  76.7 5.4 %collective-permute-start.11 = (bf16[8,128,128]{2,1,0:T(8,128)(2,1)S(1)}, bf16[8,128,128]{2,1,0:T(8,128)(2,1)S(1)}, u32[]{:S(2)}, u32[]{:S(2)}) collective-permute-start(bf16[8,128,128]{2,1,0:T(8,128)(2,1)S(1)} %collective-permute-done.9), channel_id=1, source_target_pairs={{8,0},{1,8},{9,1},{3,9},{11,3},{2,11},{10,2},{0,10},{12,4},{5,12},... | collective-permute-start | bytes 786440 | tf_op jit(solution)/shard_map/ppermute | solution.py:61
  78.2 6.1 %collective-permute-start.12 = (bf16[8,128,128]{2,1,0:T(8,128)(2,1)S(1)}, bf16[8,128,128]{2,1,0:T(8,128)(2,1)S(1)}, u32[]{:S(2)}, u32[]{:S(2)}) collective-permute-start(bf16[8,128,128]{2,1,0:T(8,128)(2,1)S(1)} %collective-permute-done.10), channel_id=1, source_target_pairs={{10,0},{0,8},{8,1},{1,9},{9,3},{3,11},{11,2},{2,10},{14,4},{4,12},... | collective-permute-start | bytes 786440 | tf_op jit(solution)/shard_map/ppermute | solution.py:61
  82.1 6.1 %collective-permute-start.7 = (bf16[8,128,128]{2,1,0:T(8,128)(2,1)S(1)}, bf16[8,128,128]{2,1,0:T(8,128)(2,1)S(1)}, u32[]{:S(2)}, u32[]{:S(2)}) collective-permute-start(bf16[8,128,128]{2,1,0:T(8,128)(2,1)S(1)} %collective-permute-done.5), channel_id=1, source_target_pairs={{8,0},{1,8},{9,1},{3,9},{11,3},{2,11},{10,2},{0,10},{12,4},{5,12},... | collective-permute-start | bytes 786440 | tf_op jit(solution)/shard_map/ppermute | solution.py:61
  84.3 25.4 %collective-permute-start.8 = (bf16[8,128,128]{2,1,0:T(8,128)(2,1)S(1)}, bf16[8,128,128]{2,1,0:T(8,128)(2,1)S(1)}, u32[]{:S(2)}, u32[]{:S(2)}) collective-permute-start(bf16[8,128,128]{2,1,0:T(8,128)(2,1)S(1)} %collective-permute-done.6), channel_id=1, source_target_pairs={{10,0},{0,8},{8,1},{1,9},{9,3},{3,11},{11,2},{2,10},{14,4},{4,12},... | collective-permute-start | bytes 786440 | tf_op jit(solution)/shard_map/ppermute | solution.py:61
  110.0 9.0 %collective-permute-start.32 = (bf16[21,128,128]{2,1,0:T(8,128)(2,1)S(1)}, bf16[21,128,128]{2,1,0:T(8,128)(2,1)S(1)}, u32[]{:S(2)}, u32[]{:S(2)}) collective-permute-start(bf16[21,128,128]{2,1,0:T(8,128)(2,1)S(1)} %get-tuple-element.101.refs_0_), channel_id=1, source_target_pairs={{8,0},{1,8},{9,1},{3,9},{11,3},{2,11},{10,2},{0,10},{12,4},{5,12},... | collective-permute-start | bytes 2064392 | tf_op jit(solution)/shard_map/ppermute | solution.py:61
  110.1 15.8 %collective-permute-start.33 = (bf16[21,128,128]{2,1,0:T(8,128)(2,1)S(1)}, bf16[21,128,128]{2,1,0:T(8,128)(2,1)S(1)}, u32[]{:S(2)}, u32[]{:S(2)}) collective-permute-start(bf16[21,128,128]{2,1,0:T(8,128)(2,1)S(1)} %get-tuple-element.102.refs_1_), channel_id=1, source_target_pairs={{8,0},{1,8},{9,1},{3,9},{11,3},{2,11},{10,2},{0,10},{12,4},{5,12},... | collective-permute-start | bytes 2064392 | tf_op jit(solution)/shard_map/ppermute | solution.py:61
  119.0 14.2 %collective-permute-start.34 = (bf16[21,128,128]{2,1,0:T(8,128)(2,1)S(1)}, bf16[21,128,128]{2,1,0:T(8,128)(2,1)S(1)}, u32[]{:S(2)}, u32[]{:S(2)}) collective-permute-start(bf16[21,128,128]{2,1,0:T(8,128)(2,1)S(1)} %collective-permute-done.32.refs_2_), channel_id=1, source_target_pairs={{8,0},{1,8},{9,1},{3,9},{11,3},{2,11},{10,2},{0,10},{12,4},{5,12},... | collective-permute-start | bytes 2064392 | tf_op jit(solution)/shard_map/ppermute | solution.py:61
  125.9 14.7 %collective-permute-start.35 = (bf16[21,128,128]{2,1,0:T(8,128)(2,1)S(1)}, bf16[21,128,128]{2,1,0:T(8,128)(2,1)S(1)}, u32[]{:S(2)}, u32[]{:S(2)}) collective-permute-start(bf16[21,128,128]{2,1,0:T(8,128)(2,1)S(1)} %collective-permute-done.33.refs_3_), channel_id=1, source_target_pairs={{8,0},{1,8},{9,1},{3,9},{11,3},{2,11},{10,2},{0,10},{12,4},{5,12},... | collective-permute-start | bytes 2064392 | tf_op jit(solution)/shard_map/ppermute | solution.py:61
  128.2 14.7 %collective-permute-start.23 = (bf16[21,128,128]{2,1,0:T(8,128)(2,1)S(1)}, bf16[21,128,128]{2,1,0:T(8,128)(2,1)S(1)}, u32[]{:S(2)}, u32[]{:S(2)}) collective-permute-start(bf16[21,128,128]{2,1,0:T(8,128)(2,1)S(1)} %fusion.9), channel_id=1, source_target_pairs={{10,0},{0,8},{8,1},{1,9},{9,3},{3,11},{11,2},{2,10},{14,4},{4,12},... | collective-permute-start | bytes 2064392 | tf_op jit(solution)/shard_map/ppermute | solution.py:61
  128.6 17.3 %collective-permute-start.20 = (bf16[21,128,128]{2,1,0:T(8,128)(2,1)S(1)}, bf16[21,128,128]{2,1,0:T(8,128)(2,1)S(1)}, u32[]{:S(2)}, u32[]{:S(2)}) collective-permute-start(bf16[21,128,128]{2,1,0:T(8,128)(2,1)S(1)} %fusion.8), channel_id=1, source_target_pairs={{10,0},{0,8},{8,1},{1,9},{9,3},{3,11},{11,2},{2,10},{14,4},{4,12},... | collective-permute-start | bytes 2064392 | tf_op jit(solution)/shard_map/ppermute | solution.py:61
  133.3 14.7 %collective-permute-start.36 = (bf16[21,128,128]{2,1,0:T(8,128)(2,1)S(1)}, bf16[21,128,128]{2,1,0:T(8,128)(2,1)S(1)}, u32[]{:S(2)}, u32[]{:S(2)}) collective-permute-start(bf16[21,128,128]{2,1,0:T(8,128)(2,1)S(1)} %collective-permute-done.34.refs_4_), channel_id=1, source_target_pairs={{8,0},{1,8},{9,1},{3,9},{11,3},{2,11},{10,2},{0,10},{12,4},{5,12},... | collective-permute-start | bytes 2064392 | tf_op jit(solution)/shard_map/ppermute | solution.py:61
  140.6 14.7 %collective-permute-start.37 = (bf16[21,128,128]{2,1,0:T(8,128)(2,1)S(1)}, bf16[21,128,128]{2,1,0:T(8,128)(2,1)S(1)}, u32[]{:S(2)}, u32[]{:S(2)}) collective-permute-start(bf16[21,128,128]{2,1,0:T(8,128)(2,1)S(1)} %collective-permute-done.35.refs_5_), channel_id=1, source_target_pairs={{8,0},{1,8},{9,1},{3,9},{11,3},{2,11},{10,2},{0,10},{12,4},{5,12},... | collective-permute-start | bytes 2064392 | tf_op jit(solution)/shard_map/ppermute | solution.py:61
  143.2 22.2 %collective-permute-start.24 = (bf16[21,128,128]{2,1,0:T(8,128)(2,1)S(1)}, bf16[21,128,128]{2,1,0:T(8,128)(2,1)S(1)}, u32[]{:S(2)}, u32[]{:S(2)}) collective-permute-start(bf16[21,128,128]{2,1,0:T(8,128)(2,1)S(1)} %add_convert_fusion.1), channel_id=1, source_target_pairs={{10,0},{0,8},{8,1},{1,9},{9,3},{3,11},{11,2},{2,10},{14,4},{4,12},... | collective-permute-start | bytes 2064392 | tf_op jit(solution)/shard_map/ppermute | solution.py:61
  146.4 19.5 %collective-permute-start.21 = (bf16[21,128,128]{2,1,0:T(8,128)(2,1)S(1)}, bf16[21,128,128]{2,1,0:T(8,128)(2,1)S(1)}, u32[]{:S(2)}, u32[]{:S(2)}) collective-permute-start(bf16[21,128,128]{2,1,0:T(8,128)(2,1)S(1)} %add_convert_fusion.3), channel_id=1, source_target_pairs={{10,0},{0,8},{8,1},{1,9},{9,3},{3,11},{11,2},{2,10},{14,4},{4,12},... | collective-permute-start | bytes 2064392 | tf_op jit(solution)/shard_map/ppermute | solution.py:61
  161.7 10.7 %collective-permute-start.38 = (bf16[21,128,128]{2,1,0:T(8,128)(2,1)S(1)}, bf16[21,128,128]{2,1,0:T(8,128)(2,1)S(1)}, u32[]{:S(2)}, u32[]{:S(2)}) collective-permute-start(bf16[21,128,128]{2,1,0:T(8,128)(2,1)S(1)} %get-tuple-element.104.refs_0_), channel_id=1, source_target_pairs={{8,0},{1,8},{9,1},{3,9},{11,3},{2,11},{10,2},{0,10},{12,4},{5,12},... | collective-permute-start | bytes 2064392 | tf_op jit(solution)/shard_map/ppermute | solution.py:61
  164.0 15.8 %collective-permute-start.39 = (bf16[21,128,128]{2,1,0:T(8,128)(2,1)S(1)}, bf16[21,128,128]{2,1,0:T(8,128)(2,1)S(1)}, u32[]{:S(2)}, u32[]{:S(2)}) collective-permute-start(bf16[21,128,128]{2,1,0:T(8,128)(2,1)S(1)} %get-tuple-element.105.refs_1_), channel_id=1, source_target_pairs={{8,0},{1,8},{9,1},{3,9},{11,3},{2,11},{10,2},{0,10},{12,4},{5,12},... | collective-permute-start | bytes 2064392 | tf_op jit(solution)/shard_map/ppermute | solution.py:61
  165.8 16.3 %collective-permute-start.25 = (bf16[21,128,128]{2,1,0:T(8,128)(2,1)S(1)}, bf16[21,128,128]{2,1,0:T(8,128)(2,1)S(1)}, u32[]{:S(2)}, u32[]{:S(2)}) collective-permute-start(bf16[21,128,128]{2,1,0:T(8,128)(2,1)S(1)} %add_convert_fusion), channel_id=1, source_target_pairs={{10,0},{0,8},{8,1},{1,9},{9,3},{3,11},{11,2},{2,10},{14,4},{4,12},... | collective-permute-start | bytes 2064392 | tf_op jit(solution)/shard_map/ppermute | solution.py:61
  166.3 17.5 %collective-permute-start.22 = (bf16[21,128,128]{2,1,0:T(8,128)(2,1)S(1)}, bf16[21,128,128]{2,1,0:T(8,128)(2,1)S(1)}, u32[]{:S(2)}, u32[]{:S(2)}) collective-permute-start(bf16[21,128,128]{2,1,0:T(8,128)(2,1)S(1)} %add_convert_fusion.2), channel_id=1, source_target_pairs={{10,0},{0,8},{8,1},{1,9},{9,3},{3,11},{11,2},{2,10},{14,4},{4,12},... | collective-permute-start | bytes 2064392 | tf_op jit(solution)/shard_map/ppermute | solution.py:61
  172.4 17.0 %collective-permute-start.40 = (bf16[21,128,128]{2,1,0:T(8,128)(2,1)S(1)}, bf16[21,128,128]{2,1,0:T(8,128)(2,1)S(1)}, u32[]{:S(2)}, u32[]{:S(2)}) collective-permute-start(bf16[21,128,128]{2,1,0:T(8,128)(2,1)S(1)} %collective-permute-done.38.refs_2_), channel_id=1, source_target_pairs={{8,0},{1,8},{9,1},{3,9},{11,3},{2,11},{10,2},{0,10},{12,4},{5,12},... | collective-permute-start | bytes 2064392 | tf_op jit(solution)/shard_map/ppermute | solution.py:61
  179.8 14.7 %collective-permute-start.41 = (bf16[21,128,128]{2,1,0:T(8,128)(2,1)S(1)}, bf16[21,128,128]{2,1,0:T(8,128)(2,1)S(1)}, u32[]{:S(2)}, u32[]{:S(2)}) collective-permute-start(bf16[21,128,128]{2,1,0:T(8,128)(2,1)S(1)} %collective-permute-done.39.refs_3_), channel_id=1, source_target_pairs={{8,0},{1,8},{9,1},{3,9},{11,3},{2,11},{10,2},{0,10},{12,4},{5,12},... | collective-permute-start | bytes 2064392 | tf_op jit(solution)/shard_map/ppermute | solution.py:61
  189.4 12.5 %collective-permute-start.42 = (bf16[21,128,128]{2,1,0:T(8,128)(2,1)S(1)}, bf16[21,128,128]{2,1,0:T(8,128)(2,1)S(1)}, u32[]{:S(2)}, u32[]{:S(2)}) collective-permute-start(bf16[21,128,128]{2,1,0:T(8,128)(2,1)S(1)} %collective-permute-done.40.refs_4_), channel_id=1, source_target_pairs={{8,0},{1,8},{9,1},{3,9},{11,3},{2,11},{10,2},{0,10},{12,4},{5,12},... | collective-permute-start | bytes 2064392 | tf_op jit(solution)/shard_map/ppermute | solution.py:61
  194.5 14.7 %collective-permute-start.43 = (bf16[21,128,128]{2,1,0:T(8,128)(2,1)S(1)}, bf16[21,128,128]{2,1,0:T(8,128)(2,1)S(1)}, u32[]{:S(2)}, u32[]{:S(2)}) collective-permute-start(bf16[21,128,128]{2,1,0:T(8,128)(2,1)S(1)} %collective-permute-done.41.refs_5_), channel_id=1, source_target_pairs={{8,0},{1,8},{9,1},{3,9},{11,3},{2,11},{10,2},{0,10},{12,4},{5,12},... | collective-permute-start | bytes 2064392 | tf_op jit(solution)/shard_map/ppermute | solution.py:61
  196.8 22.2 %collective-permute-start.29 = (bf16[21,128,128]{2,1,0:T(8,128)(2,1)S(1)}, bf16[21,128,128]{2,1,0:T(8,128)(2,1)S(1)}, u32[]{:S(2)}, u32[]{:S(2)}) collective-permute-start(bf16[21,128,128]{2,1,0:T(8,128)(2,1)S(1)} %fusion.11), channel_id=1, source_target_pairs={{10,0},{0,8},{8,1},{1,9},{9,3},{3,11},{11,2},{2,10},{14,4},{4,12},... | collective-permute-start | bytes 2064392 | tf_op jit(solution)/shard_map/ppermute | solution.py:61
  197.3 22.2 %collective-permute-start.26 = (bf16[21,128,128]{2,1,0:T(8,128)(2,1)S(1)}, bf16[21,128,128]{2,1,0:T(8,128)(2,1)S(1)}, u32[]{:S(2)}, u32[]{:S(2)}) collective-permute-start(bf16[21,128,128]{2,1,0:T(8,128)(2,1)S(1)} %fusion.10), channel_id=1, source_target_pairs={{10,0},{0,8},{8,1},{1,9},{9,3},{3,11},{11,2},{2,10},{14,4},{4,12},... | collective-permute-start | bytes 2064392 | tf_op jit(solution)/shard_map/ppermute | solution.py:61
  215.6 10.7 %collective-permute-start.44 = (bf16[21,128,128]{2,1,0:T(8,128)(2,1)S(1)}, bf16[21,128,128]{2,1,0:T(8,128)(2,1)S(1)}, u32[]{:S(2)}, u32[]{:S(2)}) collective-permute-start(bf16[21,128,128]{2,1,0:T(8,128)(2,1)S(1)} %get-tuple-element.107.refs_0_.refs_14_), channel_id=1, source_target_pairs={{8,0},{1,8},{9,1},{3,9},{11,3},{2,11},{10,2},{0,10},{12,4},{5,12},... | collective-permute-start | bytes 2064392 | tf_op jit(solution)/shard_map/ppermute | solution.py:61
  217.9 15.8 %collective-permute-start.45 = (bf16[21,128,128]{2,1,0:T(8,128)(2,1)S(1)}, bf16[21,128,128]{2,1,0:T(8,128)(2,1)S(1)}, u32[]{:S(2)}, u32[]{:S(2)}) collective-permute-start(bf16[21,128,128]{2,1,0:T(8,128)(2,1)S(1)} %get-tuple-element.108.refs_1_.refs_15_), channel_id=1, source_target_pairs={{8,0},{1,8},{9,1},{3,9},{11,3},{2,11},{10,2},{0,10},{12,4},{5,12},... | collective-permute-start | bytes 2064392 | tf_op jit(solution)/shard_map/ppermute | solution.py:61
  219.4 16.5 %collective-permute-start.30 = (bf16[21,128,128]{2,1,0:T(8,128)(2,1)S(1)}, bf16[21,128,128]{2,1,0:T(8,128)(2,1)S(1)}, u32[]{:S(2)}, u32[]{:S(2)}) collective-permute-start(bf16[21,128,128]{2,1,0:T(8,128)(2,1)S(1)} %fusion.4), channel_id=1, source_target_pairs={{10,0},{0,8},{8,1},{1,9},{9,3},{3,11},{11,2},{2,10},{14,4},{4,12},... | collective-permute-start | bytes 2064392 | tf_op jit(solution)/shard_map/ppermute | solution.py:61
  219.9 17.5 %collective-permute-start.27 = (bf16[21,128,128]{2,1,0:T(8,128)(2,1)S(1)}, bf16[21,128,128]{2,1,0:T(8,128)(2,1)S(1)}, u32[]{:S(2)}, u32[]{:S(2)}) collective-permute-start(bf16[21,128,128]{2,1,0:T(8,128)(2,1)S(1)} %fusion.6), channel_id=1, source_target_pairs={{10,0},{0,8},{8,1},{1,9},{9,3},{3,11},{11,2},{2,10},{14,4},{4,12},... | collective-permute-start | bytes 2064392 | tf_op jit(solution)/shard_map/ppermute | solution.py:61
  226.3 14.7 %collective-permute-start.46 = (bf16[21,128,128]{2,1,0:T(8,128)(2,1)S(1)}, bf16[21,128,128]{2,1,0:T(8,128)(2,1)}, u32[]{:S(2)}, u32[]{:S(2)}) collective-permute-start(bf16[21,128,128]{2,1,0:T(8,128)(2,1)S(1)} %collective-permute-done.44.refs_2_.refs_16_), channel_id=1, source_target_pairs={{8,0},{1,8},{9,1},{3,9},{11,3},{2,11},{10,2},{0,10},{12,4},{5,12},... | collective-permute-start | bytes 2064392 | tf_op jit(solution)/shard_map/ppermute | solution.py:61
  233.7 14.7 %collective-permute-start.47 = (bf16[21,128,128]{2,1,0:T(8,128)(2,1)S(1)}, bf16[21,128,128]{2,1,0:T(8,128)(2,1)}, u32[]{:S(2)}, u32[]{:S(2)}) collective-permute-start(bf16[21,128,128]{2,1,0:T(8,128)(2,1)S(1)} %collective-permute-done.45.refs_3_.refs_17_), channel_id=1, source_target_pairs={{8,0},{1,8},{9,1},{3,9},{11,3},{2,11},{10,2},{0,10},{12,4},{5,12},... | collective-permute-start | bytes 2064392 | tf_op jit(solution)/shard_map/ppermute | solution.py:61
  237.2 15.0 %collective-permute-start.31 = (bf16[21,128,128]{2,1,0:T(8,128)(2,1)}, bf16[21,128,128]{2,1,0:T(8,128)(2,1)S(1)}, u32[]{:S(2)}, u32[]{:S(2)}) collective-permute-start(bf16[21,128,128]{2,1,0:T(8,128)(2,1)} %fusion.5), channel_id=1, source_target_pairs={{10,0},{0,8},{8,1},{1,9},{9,3},{3,11},{11,2},{2,10},{14,4},{4,12},... | collective-permute-start | bytes 2064392 | tf_op jit(solution)/shard_map/ppermute | solution.py:61
  238.7 16.5 %collective-permute-start.28 = (bf16[21,128,128]{2,1,0:T(8,128)(2,1)}, bf16[21,128,128]{2,1,0:T(8,128)(2,1)S(1)}, u32[]{:S(2)}, u32[]{:S(2)}) collective-permute-start(bf16[21,128,128]{2,1,0:T(8,128)(2,1)} %fusion.7), channel_id=1, source_target_pairs={{10,0},{0,8},{8,1},{1,9},{9,3},{3,11},{11,2},{2,10},{14,4},{4,12},... | collective-permute-start | bytes 2064392 | tf_op jit(solution)/shard_map/ppermute | solution.py:61
  241.1 19.9 %collective-permute-start.48 = (bf16[21,128,128]{2,1,0:T(8,128)(2,1)}, bf16[21,128,128]{2,1,0:T(8,128)(2,1)}, u32[]{:S(2)}, u32[]{:S(2)}) collective-permute-start(bf16[21,128,128]{2,1,0:T(8,128)(2,1)} %collective-permute-done.46.refs_4_.refs_18_), channel_id=1, source_target_pairs={{8,0},{1,8},{9,1},{3,9},{11,3},{2,11},{10,2},{0,10},{12,4},{5,12},... | collective-permute-start | bytes 2064392 | tf_op jit(solution)/shard_map/ppermute | solution.py:61
  248.4 14.9 %collective-permute-start.49 = (bf16[21,128,128]{2,1,0:T(8,128)(2,1)}, bf16[21,128,128]{2,1,0:T(8,128)(2,1)}, u32[]{:S(2)}, u32[]{:S(2)}) collective-permute-start(bf16[21,128,128]{2,1,0:T(8,128)(2,1)} %collective-permute-done.47.refs_5_.refs_19_), channel_id=1, source_target_pairs={{8,0},{1,8},{9,1},{3,9},{11,3},{2,11},{10,2},{0,10},{12,4},{5,12},... | collective-permute-start | bytes 2064392 | tf_op jit(solution)/shard_map/ppermute | solution.py:61
  268.9 6.7 %collective-permute-start.55 = (f32[2,128]{1,0:T(2,128)S(1)}, f32[2,128]{1,0:T(2,128)S(1)}, u32[]{:S(2)}, u32[]{:S(2)}) collective-permute-start(f32[2,128]{1,0:T(2,128)S(1)} %maximum_select_fusion.4), channel_id=1, source_target_pairs={{1,0},{9,8},{0,1},{8,9},{2,3},{10,11},{3,2},{11,10},{5,4},{13,12},... | collective-permute-start | bytes 3080 | tf_op jit(solution)/shard_map/ppermute | solution.py:66
  268.9 11.2 %collective-permute-start.50 = (bf16[4,128,128]{2,1,0:T(8,128)(2,1)}, bf16[4,128,128]{2,1,0:T(8,128)(2,1)}, u32[]{:S(2)}, u32[]{:S(2)}) collective-permute-start(bf16[4,128,128]{2,1,0:T(8,128)(2,1)} %copy-done.22), channel_id=1, source_target_pairs={{8,0},{1,8},{9,1},{3,9},{11,3},{2,11},{10,2},{0,10},{12,4},{5,12},... | collective-permute-start | bytes 393224 | tf_op jit(solution)/shard_map/ppermute | solution.py:61
  273.5 6.6 %collective-permute-start.51 = (bf16[4,128,128]{2,1,0:T(8,128)(2,1)}, bf16[4,128,128]{2,1,0:T(8,128)(2,1)}, u32[]{:S(2)}, u32[]{:S(2)}) collective-permute-start(bf16[4,128,128]{2,1,0:T(8,128)(2,1)} %copy-done.22), channel_id=1, source_target_pairs={{10,0},{0,8},{8,1},{1,9},{9,3},{3,11},{11,2},{2,10},{14,4},{4,12},... | collective-permute-start | bytes 393224 | tf_op jit(solution)/shard_map/ppermute | solution.py:61
  273.5 6.6 %collective-permute-start.52 = (bf16[4,128,128]{2,1,0:T(8,128)(2,1)}, bf16[4,128,128]{2,1,0:T(8,128)(2,1)}, u32[]{:S(2)}, u32[]{:S(2)}) collective-permute-start(bf16[4,128,128]{2,1,0:T(8,128)(2,1)} %copy-done.22), channel_id=1, source_target_pairs={{1,0},{9,8},{3,1},{11,9},{2,3},{10,11},{0,2},{8,10},{5,4},{13,12},... | collective-permute-start | bytes 393224 | tf_op jit(solution)/shard_map/ppermute | solution.py:61
  274.3 6.6 %collective-permute-start.53 = (bf16[4,128,128]{2,1,0:T(8,128)(2,1)}, bf16[4,128,128]{2,1,0:T(8,128)(2,1)}, u32[]{:S(2)}, u32[]{:S(2)}) collective-permute-start(bf16[4,128,128]{2,1,0:T(8,128)(2,1)} %copy-done.22), channel_id=1, source_target_pairs={{2,0},{10,8},{0,1},{8,9},{1,3},{9,11},{3,2},{11,10},{6,4},{14,12},... | collective-permute-start | bytes 393224 | tf_op jit(solution)/shard_map/ppermute | solution.py:61
  275.6 4.5 %collective-permute-start.56 = (f32[4,128]{1,0:T(4,128)S(1)}, f32[4,128]{1,0:T(4,128)S(1)}, u32[]{:S(2)}, u32[]{:S(2)}) collective-permute-start(f32[4,128]{1,0:T(4,128)S(1)} %maximum_select_fusion.2), channel_id=1, source_target_pairs={{3,0},{11,8},{2,1},{10,9},{0,3},{8,11},{1,2},{9,10},{7,4},{15,12},... | collective-permute-start | bytes 6152 | tf_op jit(solution)/shard_map/ppermute | solution.py:66
  299.9 6.7 %collective-permute-start.57 = (f32[2,128,128]{2,1,0:T(8,128)S(1)}, f32[2,128,128]{2,1,0:T(8,128)S(1)}, u32[]{:S(2)}, u32[]{:S(2)}) collective-permute-start(f32[2,128,128]{2,1,0:T(8,128)S(1)} %get-tuple-element.144), channel_id=1, source_target_pairs={{10,0},{0,8},{8,1},{1,9},{9,3},{3,11},{11,2},{2,10},{14,4},{4,12},... | collective-permute-start | bytes 393224 | tf_op jit(solution)/shard_map/ppermute | solution.py:61
  299.9 6.7 %collective-permute-start.58 = (f32[2,128,128]{2,1,0:T(8,128)S(1)}, f32[2,128,128]{2,1,0:T(8,128)S(1)}, u32[]{:S(2)}, u32[]{:S(2)}) collective-permute-start(f32[2,128,128]{2,1,0:T(8,128)S(1)} %get-tuple-element.146), channel_id=1, source_target_pairs={{2,0},{10,8},{0,1},{8,9},{1,3},{9,11},{3,2},{11,10},{6,4},{14,12},... | collective-permute-start | bytes 393224 | tf_op jit(solution)/shard_map/ppermute | solution.py:61
  300.5 6.1 %collective-permute-start.59 = (f32[2,128,128]{2,1,0:T(8,128)S(1)}, f32[2,128,128]{2,1,0:T(8,128)S(1)}, u32[]{:S(2)}, u32[]{:S(2)}) collective-permute-start(f32[2,128,128]{2,1,0:T(8,128)S(1)} %get-tuple-element.145), channel_id=1, source_target_pairs={{11,0},{2,8},{10,1},{0,9},{8,3},{1,11},{9,2},{3,10},{15,4},{6,12},... | collective-permute-start | bytes 393224 | tf_op jit(solution)/shard_map/ppermute | solution.py:61
  302.0 4.5 %collective-permute-start.62 = (f32[4,128]{1,0:T(4,128)S(1)}, f32[4,128]{1,0:T(4,128)S(1)}, u32[]{:S(2)}, u32[]{:S(2)}) collective-permute-start(f32[4,128]{1,0:T(4,128)S(1)} %maximum_select_fusion.3), channel_id=1, source_target_pairs={{3,0},{11,8},{2,1},{10,9},{0,3},{8,11},{1,2},{9,10},{7,4},{15,12},... | collective-permute-start | bytes 6152 | tf_op jit(solution)/shard_map/ppermute | solution.py:66
  311.4 15.8 %collective-permute-start.63 = (bf16[128,128]{1,0:T(8,128)(2,1)S(1)}, bf16[128,128]{1,0:T(8,128)(2,1)S(1)}, u32[]{:S(2)}, u32[]{:S(2)}) collective-permute-start(bf16[128,128]{1,0:T(8,128)(2,1)S(1)} %get-tuple-element.153), channel_id=1, source_target_pairs={{0,16},{8,17},{1,18},{9,19},{3,20},{11,21},{2,22},{10,23},{4,24},{... | collective-permute-start | bytes 98312 | tf_op jit(solution)/shard_map/ppermute | solution.py:56
  312.7 14.5 %collective-permute-start.64 = (bf16[128,128]{1,0:T(8,128)(2,1)S(1)}, bf16[128,128]{1,0:T(8,128)(2,1)S(1)}, u32[]{:S(2)}, u32[]{:S(2)}) collective-permute-start(bf16[128,128]{1,0:T(8,128)(2,1)S(1)} %get-tuple-element.156), channel_id=1, source_target_pairs={{0,23},{8,16},{1,17},{9,18},{3,19},{11,20},{2,21},{10,22},{4,31},{... | collective-permute-start | bytes 98312 | tf_op jit(solution)/shard_map/ppermute | solution.py:56
  322.4 5.0 %collective-permute-start.65 = (bf16[128,128]{1,0:T(8,128)(2,1)S(1)}, bf16[128,128]{1,0:T(8,128)(2,1)S(1)}, u32[]{:S(2)}, u32[]{:S(2)}) collective-permute-start(bf16[128,128]{1,0:T(8,128)(2,1)S(1)} %get-tuple-element.155), channel_id=1, source_target_pairs={{0,22},{8,23},{1,16},{9,17},{3,18},{11,19},{2,20},{10,21},{4,30},{... | collective-permute-start | bytes 98312 | tf_op jit(solution)/shard_map/ppermute | solution.py:56
  323.6 4.3 %collective-permute-start.66 = (bf16[128,128]{1,0:T(8,128)(2,1)S(1)}, bf16[128,128]{1,0:T(8,128)(2,1)S(1)}, u32[]{:S(2)}, u32[]{:S(2)}) collective-permute-start(bf16[128,128]{1,0:T(8,128)(2,1)S(1)} %get-tuple-element.154), channel_id=1, source_target_pairs={{0,21},{8,22},{1,23},{9,16},{3,17},{11,18},{2,19},{10,20},{4,29},{... | collective-permute-start | bytes 98312 | tf_op jit(solution)/shard_map/ppermute | solution.py:56
  (38 other events, 447.0 us)
where the time goes:
time: 334 us; the launch traced here: 330 us
  waiting for transfers between devices  124 us (37%)
  starting transfers between devices  116 us (35%)
  Pallas kernels  53.5 us (16%)
  local copies, waits for them, and re-layouts  10.6 us (3%)
  blocking collectives  9.24 us (3%)
  matrix products  7.34 us (2%)
  other arithmetic  5.67 us (2%)
    ppermute x52, waiting for transfers between devices, ahead(): lax.ppermute(x, BOTH, self.pairs(lambda g, k: self.slot(g + chain_by, k +...  113 us
    ppermute x52, starting transfers between devices, ahead(): lax.ppermute(x, BOTH, self.pairs(lambda g, k: self.slot(g + chain_by, k +...  86.6 us
    pallas_call x17, Pallas kernels, call(): pl.pallas_call(kernel, out_shape=out_shape, scratch_shapes=scratch_shapes...  53.5 us
    ppermute x5, starting transfers between devices, send_home(): lax.ppermute(x, BOTH, self.pairs(self.slot, lambda g, k: self.home(g + si...  13.6 us
    ppermute x5, starting transfers between devices, fetch(): lax.ppermute(x, BOTH, self.pairs(lambda g, k: self.home(g + site_by, k +...  11.5 us
    all_gather x1, blocking collectives, local(): lax.all_gather(weight_matrices(mpo[0], pattern[0], secs), 'site')  9.24 us
    unnamed x79, local copies, waits for them, and re-layouts  8.53 us
    ppermute x6, waiting for transfers between devices, partner(): lax.ppermute(x, BOTH, self.pairs(lambda g, k: self.slot(g, k ^ bit), self...  8.36 us
  transfers between devices with their start and end apart: 68, of which 32 were waited for; matrix products, arithmetic and copies ran while one was open for 4% of the time, Pallas kernels for 11%

commit v1 on v0

--- a/solution.py
+++ b/solution.py
@@ -16,7 +16,7 @@
 CHARGE_STEPS = (0, 1, -1, 2, -2)
 CLASSES = len(CHARGE_STEPS)
 BOTH = ("site", "sec")
-VMEM_LIMIT = 24 * 1024 * 1024
+VMEM_LIMIT = 20 * 1024 * 1024
 PIECES = 2
 
 
@@ -445,7 +445,12 @@
     )
 
 
-def polar_kernel(entry_count, both_ref, table_ref, centre_ref, out_ref, energy_ref):
+def energy_kernel(entry_count, table_ref, out_ref):
+    energy = quotient(table_ref[...], entry_count)[1]
+    out_ref[...] = jnp.broadcast_to(energy, out_ref.shape)
+
+
+def polar_kernel(entry_count, both_ref, table_ref, centre_ref, out_ref):
     states, _, block, _ = both_ref.shape
     rows = lax.broadcasted_iota(jnp.int32, (block, block), 0)
     columns = lax.broadcasted_iota(jnp.int32, (block, block), 1)
@@ -457,7 +462,6 @@
         )
 
     scale, energy, factor, square, centre_sq = quotient(table_ref[...], entry_count)
-    energy_ref[...] = jnp.broadcast_to(energy, energy_ref.shape)
     vector = updated(
         both_ref[:, 0].reshape(states * block, block),
         both_ref[:, 1].reshape(states * block, block),
@@ -621,10 +625,16 @@
     states, _, block, _ = both.shape
     return call(
         functools.partial(polar_kernel, entry_count),
-        (half_out(states, block, block), float_out(1, LANES)),
+        half_out(states, block, block),
         [],
         600 * block**3,
         (both, table, centre),
+    )
+
+
+def energy_of(table, entry_count):
+    return call(
+        functools.partial(energy_kernel, entry_count), float_out(1, LANES), [], 0, (table,)
     )
 
 
@@ -682,18 +692,16 @@
     def ahead(env, by, chain_by=0):
         return [places.ahead(chunk, by, chain_by) for chunk in env]
 
-    both_isos = places.fetch(jnp.concatenate([left_iso, right_iso]))
-    left_isos, right_isos = [both_isos[:states]], [both_isos[states:]]
+    first = places.fetch(jnp.concatenate([right_env[0, :, 0], left_iso, right_iso]))
+    left_isos = [first[channels : channels + states]]
+    right_isos = [first[channels + states :]]
     for step in range(1, ENV_STEPS):
         left_isos.append(places.fetch(left_iso, step))
         right_isos.append(places.fetch(right_iso, -step))
     own_tensors = places.fetch(jnp.concatenate([left_iso, centre[None]]), ENV_STEPS)
-    (left_isos, right_isos, own_tensors), envs = after(
-        (left_isos, right_isos, own_tensors),
-        jnp.concatenate([right_env[0, :, 0], left_env[0, :, 0]]),
-    )
-    envs = jnp.split(places.fetch(envs), 2 * pieces)
-    right, left = envs[:pieces], envs[pieces:]
+    right = jnp.split(first[:channels], pieces)
+    right, left_env = after(right, left_env)
+    left = jnp.split(places.fetch(left_env[0, :, 0]), pieces)
     rolled = [
         classes_of(places, jnp.concatenate([left_isos[step], right_isos[step]]))
         for step in range(ENV_STEPS)
@@ -718,8 +726,8 @@
         "sxy,syz->sxz", own_iso, jnp.stack(centres), preferred_element_type=jnp.float32
     )
     rolled_vector = other_classes_of(places, vector.astype(jnp.bfloat16))
-    (right, left), (rolled, rolled_vector, weights) = after(
-        (right, left), (rolled, rolled_vector, weights)
+    right, (rolled[1:], rolled_vector, weights) = after(
+        right, (rolled[1:], rolled_vector, weights)
     )
     centre_float = own_centre.astype(jnp.float32)
     centre_square = jnp.sum((centre_float * centre_float).reshape(-1, ROWS, block), axis=0)
@@ -728,6 +736,8 @@
     for step in range(ENV_STEPS):
         envs = [right]
         for t in range(1, states):
+            if step == 0 and t == states - 1:
+                left, envs[-1] = after(left, envs[-1])
             envs.append(ahead(envs[-1], 1))
         right, square = right_whole(
             envs,
@@ -779,11 +789,13 @@
 
     both = jnp.stack([vector, image], axis=1)
     columns = jnp.stack([both[0]] + [places.ahead(both[s], -s) for s in range(1, states)])
-    column_left, energy = polar(columns, table, own_centre, entry_count)
+    home_table = places.send_home(table, ENV_STEPS, 0)
+    home_table, columns = after(home_table, columns)
+    column_left = polar(columns, table, own_centre, entry_count)
     new_left = jnp.stack(
         [places.send_home(column_left[s], ENV_STEPS, -s) for s in range(states)]
     )
-    energy = places.send_home(energy, ENV_STEPS, 0)
+    energy = energy_of(home_table, entry_count)
     return new_left[None, :, None], energy[0, :1]
 
 

time: 334 us -> 322 us (0.964)
  starting transfers between devices: 116 us -> 107 us
  waiting for transfers between devices: 124 us -> 116 us
  local copies, waits for them, and re-layouts: 10.6 us -> 15.2 us
  matrix products: 7.34 us -> 11.8 us
    ppermute x52, starting transfers between devices: 86.6 us -> 65.3 us  [ahead(): lax.ppermute(x, BOTH, self.pairs(lambda g, k: self.slot(g + chain_by, k +...]
    ppermute x5, starting transfers between devices: 11.5 us -> 24.7 us  [fetch(): lax.ppermute(x, BOTH, self.pairs(lambda g, k: self.home(g + site_by, k +...]
    ppermute x52, waiting for transfers between devices: 113 us -> 102 us  [ahead(): lax.ppermute(x, BOTH, self.pairs(lambda g, k: self.slot(g + chain_by, k +...]
    dot_general x12, matrix products: 6.43 us -> 11 us  [local(): jnp.einsum('xy,vxz->vyz', left_isos[step][s], gathered[s][piece], preferr...]
    ppermute x5, starting transfers between devices: 13.6 us -> 9.99 us  [send_home(): lax.ppermute(x, BOTH, self.pairs(self.slot, lambda g, k: self.home(g + si...]
    pallas_call x17 -> x18, Pallas kernels: 53.5 us -> 54.2 us  [call(): pl.pallas_call(kernel, out_shape=out_shape, scratch_shapes=scratch_shapes...]
    unnamed x79 -> x82, local copies, waits for them, and re-layouts: 8.53 us -> 9.16 us
  transfers between devices with their start and end apart: 68 -> 68, of which waited for: 32 -> 29; matrix products, arithmetic and copies ran while one was open for 4% -> 7% of each run, Pallas kernels for 11% -> 10%
where the time goes in v1:
time: 322 us; the launch traced here: 320 us
  waiting for transfers between devices  116 us (36%)
  starting transfers between devices  107 us (33%)
  Pallas kernels  54.2 us (17%)
  local copies, waits for them, and re-layouts  15.2 us (5%)
  matrix products  11.8 us (4%)
  blocking collectives  8.06 us (3%)
  other arithmetic  5.59 us (2%)
    ppermute x52, waiting for transfers between devices, ahead(): lax.ppermute(x, BOTH, self.pairs(lambda g, k: self.slot(g + chain_by, k +...  102 us
    ppermute x52, starting transfers between devices, ahead(): lax.ppermute(x, BOTH, self.pairs(lambda g, k: self.slot(g + chain_by, k +...  65.3 us
    pallas_call x18, Pallas kernels, call(): pl.pallas_call(kernel, out_shape=out_shape, scratch_shapes=scratch_shapes...  54.2 us
    ppermute x5, starting transfers between devices, fetch(): lax.ppermute(x, BOTH, self.pairs(lambda g, k: self.home(g + site_by, k +...  24.7 us
    dot_general x12, matrix products, local(): jnp.einsum('xy,vxz->vyz', left_isos[step][s], gathered[s][piece], preferr...  11 us
    ppermute x5, starting transfers between devices, send_home(): lax.ppermute(x, BOTH, self.pairs(self.slot, lambda g, k: self.home(g + si...  9.99 us
    ppermute x6, waiting for transfers between devices, partner(): lax.ppermute(x, BOTH, self.pairs(lambda g, k: self.slot(g, k ^ bit), self...  9.52 us
    unnamed x82, local copies, waits for them, and re-layouts  9.16 us
  transfers between devices with their start and end apart: 68, of which 29 were waited for; matrix products, arithmetic and copies ran while one was open for 7% of the time, Pallas kernels for 10%

profile of v1, /device:TPU:0, one launch (start us, length us, event | category | flops | bytes accessed | tf_op | source)
XLA Modules:
  0.0 319.6 jit_solution(5272149839634143477)
XLA Ops:
  0.6 5.0 %collective-permute-start = (bf16[4,128,128]{2,1,0:T(8,128)(2,1)}, bf16[4,128,128]{2,1,0:T(8,128)(2,1)S(1)}, u32[]{:S(2)}, u32[]{:S(2)}) collective-permute-start(bf16[4,128,128]{2,1,0:T(8,128)(2,1)} %bitcast.194), channel_id=1, source_target_pairs={{8,0},{9,8},{10,1},{11,9},{12,3},{13,11},{14,2},{15,10},{16,4},{17... | collective-permute-start | bytes 393224 | tf_op jit(solution)/shard_map/ppermute | solution.py:51
  5.7 4.4 %collective-permute-start.3 = (bf16[4,128,128]{2,1,0:T(8,128)(2,1)}, bf16[4,128,128]{2,1,0:T(8,128)(2,1)S(1)}, u32[]{:S(2)}, u32[]{:S(2)}) collective-permute-start(bf16[4,128,128]{2,1,0:T(8,128)(2,1)} %bitcast.197), channel_id=1, source_target_pairs={{24,0},{25,8},{26,1},{27,9},{28,3},{29,11},{30,2},{31,10},{0,4},{1... | collective-permute-start | bytes 393224 | tf_op jit(solution)/shard_map/ppermute | solution.py:51
  11.6 2.9 pad_maximum_fusion
  14.5 13.9 %collective-permute-start.1 = (bf16[50,128,128]{2,1,0:T(8,128)(2,1)}, bf16[50,128,128]{2,1,0:T(8,128)(2,1)}, u32[]{:S(2)}, u32[]{:S(2)}) collective-permute-start(bf16[50,128,128]{2,1,0:T(8,128)(2,1)} %pad_maximum_fusion), channel_id=1, source_target_pairs={{0,0},{1,8},{2,1},{3,9},{4,3},{5,11},{6,2},{7,10},{8,4},{9,12},{10... | collective-permute-start | bytes 4915208 | tf_op jit(solution)/shard_map/ppermute | solution.py:51
  29.3 8.1 %all-gather = bf16[8,168,168]{2,1,0:T(8,128)(2,1)S(1)} all-gather(bf16[2,168,168]{2,1,0:T(8,128)(2,1)S(1)} %pad_maximum_fusion.2), channel_id=2, replica_groups=mesh['site'=4,'sec'=8] {'site'}, dimensions={0}, use_global_device_ids=true | all-gather | bytes 564480 | tf_op jit(solution)/shard_map/all_gather | solution.py:712
  44.5 2.6 collective-permute-done.11
  50.4 2.6 collective-permute-done.13.refs_5_
  53.1 2.9 collective-permute-start.14
  56.0 3.7 %collective-permute-start.6 = (bf16[8,128,128]{2,1,0:T(8,128)(2,1)S(1)}, bf16[8,128,128]{2,1,0:T(8,128)(2,1)S(1)}, u32[]{:S(2)}, u32[]{:S(2)}) collective-permute-start(bf16[8,128,128]{2,1,0:T(8,128)(2,1)S(1)} %collective-permute-done.4), channel_id=1, source_target_pairs={{8,0},{1,8},{9,1},{3,9},{11,3},{2,11},{10,2},{0,10},{12,4},{5,12},... | collective-permute-start | bytes 786440 | tf_op jit(solution)/shard_map/ppermute | solution.py:61
  59.7 3.8 %collective-permute-done.6 = bf16[8,128,128]{2,1,0:T(8,128)(2,1)S(1)} collective-permute-done((bf16[8,128,128]{2,1,0:T(8,128)(2,1)S(1)}, bf16[8,128,128]{2,1,0:T(8,128)(2,1)S(1)}, u32[]{:S(2)}, u32[]{:S(2)}) %collective-permute-start.6) | collective-permute-done | bytes 262176 | tf_op jit(solution)/shard_map/ppermute | solution.py:61
  64.7 2.2 collective-permute-start.20
  68.5 1.7 collective-permute-start.16
  73.3 4.0 %collective-permute-start.22 = (bf16[8,128,128]{2,1,0:T(8,128)(2,1)S(1)}, bf16[8,128,128]{2,1,0:T(8,128)(2,1)S(1)}, u32[]{:S(2)}, u32[]{:S(2)}) collective-permute-start(bf16[8,128,128]{2,1,0:T(8,128)(2,1)S(1)} %collective-permute-done.20), channel_id=1, source_target_pairs={{8,0},{1,8},{9,1},{3,9},{11,3},{2,11},{10,2},{0,10},{12,4},{5,12},... | collective-permute-start | bytes 786440 | tf_op jit(solution)/shard_map/ppermute | solution.py:61
  77.3 26.3 %collective-permute-done.22 = bf16[8,128,128]{2,1,0:T(8,128)(2,1)S(1)} collective-permute-done((bf16[8,128,128]{2,1,0:T(8,128)(2,1)S(1)}, bf16[8,128,128]{2,1,0:T(8,128)(2,1)S(1)}, u32[]{:S(2)}, u32[]{:S(2)}) %collective-permute-start.22) | collective-permute-done | bytes 262176 | tf_op jit(solution)/shard_map/ppermute | solution.py:61
  103.6 2.0 collective-permute-start.17
  106.0 8.0 %collective-permute-done.17.refs_4_ = bf16[21,128,128]{2,1,0:T(8,128)(2,1)S(1)} collective-permute-done((bf16[21,128,128]{2,1,0:T(8,128)(2,1)S(1)}, bf16[21,128,128]{2,1,0:T(8,128)(2,1)S(1)}, u32[]{:S(2)}, u32[]{:S(2)}) %collective-permute-start.17) | collective-permute-done | bytes 688160 | tf_op jit(solution)/shard_map/ppermute | solution.py:61
  114.0 7.4 %collective-permute-done.19.refs_5_ = bf16[21,128,128]{2,1,0:T(8,128)(2,1)S(1)} collective-permute-done((bf16[21,128,128]{2,1,0:T(8,128)(2,1)S(1)}, bf16[21,128,128]{2,1,0:T(8,128)(2,1)S(1)}, u32[]{:S(2)}, u32[]{:S(2)}) %collective-permute-start.19) | collective-permute-done | bytes 688160 | tf_op jit(solution)/shard_map/ppermute | solution.py:61
  121.4 5.2 %shard_map.145 = (bf16[21,128,128]{2,1,0:T(8,128)(2,1)S(1)}, bf16[21,128,128]{2,1,0:T(8,128)(2,1)S(1)}, bf16[21,128,128]{2,1,0:T(8,128)(2,1)S(1)}, bf16[21,128,1...) custom-call(bf16[21,128,128]{2,1,0:T(8,128)(2,1)S(1)} %get-tuple-ele, ...), custom_call_target="tpu_custom_call" | custom-call | flops 2334130176 | bytes 3076096 | tf_op jit(solution)/shard_map/pallas_call | solution.py:490
  127.8 2.0 collective-permute-start.27
  132.4 5.9 %collective-permute-done.27 = bf16[21,128,128]{2,1,0:T(8,128)(2,1)S(1)} collective-permute-done((bf16[21,128,128]{2,1,0:T(8,128)(2,1)S(1)}, bf16[21,128,128]{2,1,0:T(8,128)(2,1)S(1)}, u32[]{:S(2)}, u32[]{:S(2)}) %collective-permute-start.27) | collective-permute-done | bytes 688160 | tf_op jit(solution)/shard_map/ppermute | solution.py:61
  139.8 5.9 %collective-permute-done.37.refs_7_ = bf16[21,128,128]{2,1,0:T(8,128)(2,1)S(1)} collective-permute-done((bf16[21,128,128]{2,1,0:T(8,128)(2,1)S(1)}, bf16[21,128,128]{2,1,0:T(8,128)(2,1)S(1)}, u32[]{:S(2)}, u32[]{:S(2)}) %collective-permute-start.37) | collective-permute-done | bytes 688160 | tf_op jit(solution)/shard_map/ppermute | solution.py:61
  145.6 6.3 %shard_map.152 = (bf16[21,128,128]{2,1,0:T(8,128)(2,1)S(1)}, bf16[21,128,128]{2,1,0:T(8,128)(2,1)S(1)}, f32[8,128]{1,0:T(8,128)S(1)}) custom-call(bf16[21,128,128]{2,1,0:T(8,128)(2,1)S(1)} %get-tuple-element.64.refs_0_, bf16[21,128,128]{2,1,0:T(8,128)(2,1)S(1)} %get-tuple-element.65.refs_1_, bf16[21,128,128]{2,1,0:T(8,128)(2,1)S(1)} %collective-permute-done.16.refs_2_, ...), custom_call_target="tpu_custom_call" | custom-call | flops 2334130176 | bytes 7335936 | tf_op jit(solution)/shard_map/pallas_call | solution.py:490
  151.9 2.2 collective-permute-start.38
  155.3 1.7 collective-permute-start.25
  158.3 1.7 collective-permute-start.29
  160.0 2.7 collective-permute-done.38.refs_2_
  162.6 2.2 collective-permute-start.40
  167.8 2.2 collective-permute-done.39.refs_3_
  170.0 2.2 collective-permute-start.41
  173.1 4.3 %collective-permute-done.40.refs_4_ = bf16[21,128,128]{2,1,0:T(8,128)(2,1)S(1)} collective-permute-done((bf16[21,128,128]{2,1,0:T(8,128)(2,1)S(1)}, bf16[21,128,128]{2,1,0:T(8,128)(2,1)S(1)}, u32[]{:S(2)}, u32[]{:S(2)}) %collective-permute-start.40) | collective-permute-done | bytes 688160 | tf_op jit(solution)/shard_map/ppermute | solution.py:61
  177.4 2.2 collective-permute-start.42
  180.9 5.2 %shard_map.148 = (bf16[21,128,128]{2,1,0:T(8,128)(2,1)S(1)}, bf16[21,128,128]{2,1,0:T(8,128)(2,1)S(1)}, bf16[21,128,128]{2,1,0:T(8,128)(2,1)S(1)}, bf16[21,128,1...) custom-call(bf16[21,128,128]{2,1,0:T(8,128)(2,1)S(1)} %get-tuple-ele, ...), custom_call_target="tpu_custom_call" | custom-call | flops 2334130176 | bytes 3076096 | tf_op jit(solution)/shard_map/pallas_call | solution.py:490
  187.1 1.7 collective-permute-start.33
  189.1 1.8 collective-permute-start.30
  192.1 7.4 %collective-permute-done.43.refs_7_ = bf16[21,128,128]{2,1,0:T(8,128)(2,1)S(1)} collective-permute-done((bf16[21,128,128]{2,1,0:T(8,128)(2,1)S(1)}, bf16[21,128,128]{2,1,0:T(8,128)(2,1)S(1)}, u32[]{:S(2)}, u32[]{:S(2)}) %collective-permute-start.43) | collective-permute-done | bytes 688160 | tf_op jit(solution)/shard_map/ppermute | solution.py:61
  199.5 6.3 %shard_map.153 = (bf16[21,128,128]{2,1,0:T(8,128)(2,1)S(1)}, bf16[21,128,128]{2,1,0:T(8,128)(2,1)S(1)}, f32[8,128]{1,0:T(8,128)S(1)}) custom-call(bf16[21,128,128]{2,1,0:T(8,128)(2,1)S(1)} %get-tuple-element.100.refs_0_, bf16[21,128,128]{2,1,0:T(8,128)(2,1)S(1)} %get-tuple-element.101.refs_1_, bf16[21,128,128]{2,1,0:T(8,128)(2,1)S(1)} %collective-permute-done.38.refs_2_, ...), custom_call_target="tpu_custom_call" | custom-call | flops 2334130176 | bytes 7335936 | tf_op jit(solution)/shard_map/pallas_call | solution.py:490
  205.9 2.3 collective-permute-start.44
  208.6 1.7 collective-permute-start.34
  210.7 1.8 collective-permute-start.31
  212.4 4.1 %collective-permute-done.44.refs_2_.refs_16_ = bf16[21,128,128]{2,1,0:T(8,128)(2,1)S(1)} collective-permute-done((bf16[21,128,128]{2,1,0:T(8,128)(2,1)S(1)}, bf16[21,128,128]{2,1,0:T(8,128)(2,1)S(1)}, u32[]{:S(2)}, u32[]{:S(2)}) %collective-permute-start.44) | collective-permute-done | bytes 688160 | tf_op jit(solution)/shard_map/ppermute | solution.py:61
  216.6 2.2 collective-permute-start.46
  218.8 5.2 %collective-permute-done.45.refs_3_.refs_17_ = bf16[21,128,128]{2,1,0:T(8,128)(2,1)S(1)} collective-permute-done((bf16[21,128,128]{2,1,0:T(8,128)(2,1)S(1)}, bf16[21,128,128]{2,1,0:T(8,128)(2,1)S(1)}, u32[]{:S(2)}, u32[]{:S(2)}) %collective-permute-start.45) | collective-permute-done | bytes 688160 | tf_op jit(solution)/shard_map/ppermute | solution.py:61
  223.9 2.2 collective-permute-start.47
  230.0 1.7 collective-permute-start.32
  231.8 1.7 collective-permute-start.48
  233.5 5.2 %collective-permute-done.47.refs_5_.refs_19_ = bf16[21,128,128]{2,1,0:T(8,128)(2,1)} collective-permute-done((bf16[21,128,128]{2,1,0:T(8,128)(2,1)S(1)}, bf16[21,128,128]{2,1,0:T(8,128)(2,1)}, u32[]{:S(2)}, u32[]{:S(2)}) %collective-permute-start.47) | collective-permute-done | bytes 688160 | tf_op jit(solution)/shard_map/ppermute | solution.py:61
  238.7 2.2 collective-permute-start.49
  242.9 2.5 collective-permute-done.32.moved_ref
  245.9 5.2 %shard_map.151 = (bf16[21504,128]{1,0:T(8,128)(2,1)S(1)}, f32[4,128,128]{2,1,0:T(8,128)S(1)}) custom-call(bf16[21,128,128]{2,1,0:T(8,128)(2,1)S(1)} %get-tuple-element.85.refs_0_, bf16[21,128,128]{2,1,0:T(8,128)(2,1)S(1)} %get-tuple-element.90.refs_1_, bf16[1360,384]{1,0:T(8,128)(2,1)S(1)} %copy-done.27, f32[4,128,128]{2,1,0:T(8,128)S(1)} %copy-done.25, ...), custom_call_target="tpu_custom_call" | custom-call | flops 2334130176 | bytes 3207168 | tf_op jit(solution)/shard_map/pallas_call | solution.py:490
  251.2 2.3 collective-permute-done.49.refs_7_.refs_21_
  253.6 3.7 %shard_map.154 = (f32[4,128,128]{2,1,0:T(8,128)S(1)}, bf16[4,128,128]{2,1,0:T(8,128)(2,1)S(1)}, f32[1,128]{1,0:T(1,128)S(1)}) custom-call(bf16[21,128,128]{2,1,0:T(8,128)(2,1)S(1)} %get-tuple-element.103.refs_0_.refs_14_, bf16[21,128,128]{2,1,0:T(8,128)(2,1)S(1)} %copy-done.1, bf16[21,128,128]{2,1,0:T(8,128)(2,1)S(1)} %copy-done.3, ...), custom_call_target="tpu_custom_call" | custom-call | flops 704643072 | bytes 11292672 | tf_op jit(solution)/shard_map/pallas_call | solution.py:490
  258.0 3.5 %collective-permute-start.54 = (f32[1,128]{1,0:T(1,128)S(1)}, f32[1,128]{1,0:T(1,128)S(1)}, u32[]{:S(2)}, u32[]{:S(2)}) collective-permute-start(f32[1,128]{1,0:T(1,128)S(1)} %get-tuple-element.114), channel_id=1, source_target_pairs={{8,0},{0,8},{9,1},{1,9},{11,3},{3,11},{10,2},{2,10},{12,4},{4,12},... | collective-permute-start | bytes 1544 | tf_op jit(solution)/shard_map/ppermute | solution.py:66
  262.3 1.7 collective-permute-start.55
  264.4 1.7 collective-permute-start.52
  266.1 1.7 collective-permute-start.50
  267.9 4.5 %collective-permute-done.56 = f32[4,128]{1,0:T(4,128)S(1)} collective-permute-done((f32[4,128]{1,0:T(4,128)S(1)}, f32[4,128]{1,0:T(4,128)S(1)}, u32[]{:S(2)}, u32[]{:S(2)}) %collective-permute-start.56) | collective-permute-done | bytes 2080 | tf_op jit(solution)/shard_map/ppermute | solution.py:66
  278.6 10.1 %shard_map.155 = (f32[4,128,128]{2,1,0:T(8,128)S(1)}, bf16[4,128,128]{2,1,0:T(8,128)(2,1)}, f32[1,128]{1,0:T(1,128)S(1)}, f32[4,128,128]{2,1,0:T(8,128)S(1)}) custom-call(bf16[21,128,128]{2,1,0:T(8,128)(2,1)S(1)} %copy-done.9, bf16[21,128,128]{2,1,0:T(8,128)(2,1)S(1)} %copy-done.7, bf16[1360,384]{1,0:T(8,128)(2,1)S(1)} %copy-done.28, ...), custom_call_target="tpu_custom_call" | custom-call | flops 3038773248 | bytes 9523200 | tf_op jit(solution)/shard_map/pallas_call | solution.py:490
  291.8 2.0 collective-permute-start.62
  295.2 3.1 collective-permute-done.59
  300.3 2.0 collective-permute-done.60.table_ref
  302.3 4.8 %shard_map.156 = bf16[4,128,128]{2,1,0:T(8,128)(2,1)S(1)} custom-call(f32[4,2,128,128]{3,2,1,0:T(8,128)S(1)} %pad_maximum_fusion.1.both_ref, f32[8,128]{1,0:T(8,128)S(1)} %maximum_select_fusion.1.table_ref, bf16[128,128]{1,0:T(8,128)(2,1)S(1)} %get-tuple-element.146.centre_ref), custom_call_target="tpu_custom_call" | custom-call | flops 1258291200 | bytes 561152 | tf_op jit(solution)/shard_map/pallas_call | solution.py:490
  307.8 5.7 %collective-permute-start.67 = (bf16[128,128]{1,0:T(8,128)(2,1)S(1)}, bf16[128,128]{1,0:T(8,128)(2,1)S(1)}, u32[]{:S(2)}, u32[]{:S(2)}) collective-permute-start(bf16[128,128]{1,0:T(8,128)(2,1)S(1)} %get-tuple-element.148), channel_id=1, source_target_pairs={{0,21},{8,22},{1,23},{9,16},{3,17},{11,18},{2,19},{10,20},{4,29},{... | collective-permute-start | bytes 98312 | tf_op jit(solution)/shard_map/ppermute | solution.py:56
  314.4 1.6 collective-permute-start.65
  316.7 2.2 collective-permute-done.66
  (221 shorter events, 59.1 us)
Async XLA Ops:
  0.6 43.0 %collective-permute-start = (bf16[4,128,128]{2,1,0:T(8,128)(2,1)}, bf16[4,128,128]{2,1,0:T(8,128)(2,1)S(1)}, u32[]{:S(2)}, u32[]{:S(2)}) collective-permute-start(bf16[4,128,128]{2,1,0:T(8,128)(2,1)} %bitcast.194), channel_id=1, source_target_pairs={{8,0},{9,8},{10,1},{11,9},{12,3},{13,11},{14,2},{15,10},{16,4},{17... | collective-permute-start | bytes 393224 | tf_op jit(solution)/shard_map/ppermute | solution.py:51
  5.7 38.2 %collective-permute-start.3 = (bf16[4,128,128]{2,1,0:T(8,128)(2,1)}, bf16[4,128,128]{2,1,0:T(8,128)(2,1)S(1)}, u32[]{:S(2)}, u32[]{:S(2)}) collective-permute-start(bf16[4,128,128]{2,1,0:T(8,128)(2,1)} %bitcast.197), channel_id=1, source_target_pairs={{24,0},{25,8},{26,1},{27,9},{28,3},{29,11},{30,2},{31,10},{0,4},{1... | collective-permute-start | bytes 393224 | tf_op jit(solution)/shard_map/ppermute | solution.py:51
  11.0 32.6 %collective-permute-start.8 = (bf16[5,128,128]{2,1,0:T(8,128)(2,1)S(1)}, bf16[5,128,128]{2,1,0:T(8,128)(2,1)S(1)}, u32[]{:S(2)}, u32[]{:S(2)}) collective-permute-start(bf16[5,128,128]{2,1,0:T(8,128)(2,1)S(1)} %pad_maximum_fusion.3), channel_id=1, source_target_pairs={{16,0},{17,8},{18,1},{19,9},{20,3},{21,11},{22,2},{23,10},{24,4},{... | collective-permute-start | bytes 491528 | tf_op jit(solution)/shard_map/ppermute | solution.py:51
  14.5 49.2 %collective-permute-start.1 = (bf16[50,128,128]{2,1,0:T(8,128)(2,1)}, bf16[50,128,128]{2,1,0:T(8,128)(2,1)}, u32[]{:S(2)}, u32[]{:S(2)}) collective-permute-start(bf16[50,128,128]{2,1,0:T(8,128)(2,1)} %pad_maximum_fusion), channel_id=1, source_target_pairs={{0,0},{1,8},{2,1},{3,9},{4,3},{5,11},{6,2},{7,10},{8,4},{9,12},{10... | collective-permute-start | bytes 4915208 | tf_op jit(solution)/shard_map/ppermute | solution.py:51
  43.7 4.0 %collective-permute-start.10 = (bf16[128,128]{1,0:T(8,128)(2,1)S(1)}, bf16[128,128]{1,0:T(8,128)(2,1)S(1)}, u32[]{:S(2)}, u32[]{:S(2)}) collective-permute-start(bf16[128,128]{1,0:T(8,128)(2,1)S(1)} %get-tuple-element.146.centre_ref), channel_id=1, source_target_pairs={{1,0},{9,8},{3,1},{11,9},{2,3},{10,11},{0,2},{8,10},{5,4},{13,12},... | collective-permute-start | bytes 98312 | tf_op jit(solution)/shard_map/ppermute | solution.py:61
  43.8 4.0 %collective-permute-start.9 = (bf16[128,128]{1,0:T(8,128)(2,1)S(1)}, bf16[128,128]{1,0:T(8,128)(2,1)S(1)}, u32[]{:S(2)}, u32[]{:S(2)}) collective-permute-start(bf16[128,128]{1,0:T(8,128)(2,1)S(1)} %get-tuple-element.146.centre_ref), channel_id=1, source_target_pairs={{8,0},{1,8},{9,1},{3,9},{11,3},{2,11},{10,2},{0,10},{12,4},{5,12},... | collective-permute-start | bytes 98312 | tf_op jit(solution)/shard_map/ppermute | solution.py:61
  43.9 12.1 %collective-permute-start.5 = (bf16[8,128,128]{2,1,0:T(8,128)(2,1)S(1)}, bf16[8,128,128]{2,1,0:T(8,128)(2,1)S(1)}, u32[]{:S(2)}, u32[]{:S(2)}) collective-permute-start(bf16[8,128,128]{2,1,0:T(8,128)(2,1)S(1)} %constant_dynamic-update-slice_fusion), channel_id=1, source_target_pairs={{10,0},{0,8},{8,1},{1,9},{9,3},{3,11},{11,2},{2,10},{14,4},{4,12},... | collective-permute-start | bytes 786440 | tf_op jit(solution)/shard_map/ppermute | solution.py:61
  47.1 8.9 %collective-permute-start.4 = (bf16[8,128,128]{2,1,0:T(8,128)(2,1)S(1)}, bf16[8,128,128]{2,1,0:T(8,128)(2,1)S(1)}, u32[]{:S(2)}, u32[]{:S(2)}) collective-permute-start(bf16[8,128,128]{2,1,0:T(8,128)(2,1)S(1)} %constant_dynamic-update-slice_fusion), channel_id=1, source_target_pairs={{8,0},{1,8},{9,1},{3,9},{11,3},{2,11},{10,2},{0,10},{12,4},{5,12},... | collective-permute-start | bytes 786440 | tf_op jit(solution)/shard_map/ppermute | solution.py:61
  48.7 4.4 %collective-permute-start.13 = (bf16[4,128,128]{2,1,0:T(8,128)(2,1)S(1)}, bf16[4,128,128]{2,1,0:T(8,128)(2,1)S(1)}, u32[]{:S(2)}, u32[]{:S(2)}) collective-permute-start(bf16[4,128,128]{2,1,0:T(8,128)(2,1)S(1)} %get-tuple-element.151), channel_id=1, source_target_pairs={{10,0},{0,8},{8,1},{1,9},{9,3},{3,11},{11,2},{2,10},{14,4},{4,12},... | collective-permute-start | bytes 393224 | tf_op jit(solution)/shard_map/ppermute | solution.py:61
  53.1 15.4 %collective-permute-start.15 = (bf16[4,128,128]{2,1,0:T(8,128)(2,1)S(1)}, bf16[4,128,128]{2,1,0:T(8,128)(2,1)S(1)}, u32[]{:S(2)}, u32[]{:S(2)}) collective-permute-start(bf16[4,128,128]{2,1,0:T(8,128)(2,1)S(1)} %collective-permute-done.13.refs_5_), channel_id=1, source_target_pairs={{10,0},{0,8},{8,1},{1,9},{9,3},{3,11},{11,2},{2,10},{14,4},{4,12},... | collective-permute-start | bytes 393224 | tf_op jit(solution)/shard_map/ppermute | solution.py:61
  53.1 15.4 %collective-permute-start.14 = (bf16[4,128,128]{2,1,0:T(8,128)(2,1)S(1)}, bf16[4,128,128]{2,1,0:T(8,128)(2,1)S(1)}, u32[]{:S(2)}, u32[]{:S(2)}) collective-permute-start(bf16[4,128,128]{2,1,0:T(8,128)(2,1)S(1)} %collective-permute-done.12.refs_4_), channel_id=1, source_target_pairs={{8,0},{1,8},{9,1},{3,9},{11,3},{2,11},{10,2},{0,10},{12,4},{5,12},... | collective-permute-start | bytes 393224 | tf_op jit(solution)/shard_map/ppermute | solution.py:61
  56.0 7.7 %collective-permute-start.7 = (bf16[8,128,128]{2,1,0:T(8,128)(2,1)S(1)}, bf16[8,128,128]{2,1,0:T(8,128)(2,1)S(1)}, u32[]{:S(2)}, u32[]{:S(2)}) collective-permute-start(bf16[8,128,128]{2,1,0:T(8,128)(2,1)S(1)} %collective-permute-done.5), channel_id=1, source_target_pairs={{10,0},{0,8},{8,1},{1,9},{9,3},{3,11},{11,2},{2,10},{14,4},{4,12},... | collective-permute-start | bytes 786440 | tf_op jit(solution)/shard_map/ppermute | solution.py:61
  56.0 7.5 %collective-permute-start.6 = (bf16[8,128,128]{2,1,0:T(8,128)(2,1)S(1)}, bf16[8,128,128]{2,1,0:T(8,128)(2,1)S(1)}, u32[]{:S(2)}, u32[]{:S(2)}) collective-permute-start(bf16[8,128,128]{2,1,0:T(8,128)(2,1)S(1)} %collective-permute-done.4), channel_id=1, source_target_pairs={{8,0},{1,8},{9,1},{3,9},{11,3},{2,11},{10,2},{0,10},{12,4},{5,12},... | collective-permute-start | bytes 786440 | tf_op jit(solution)/shard_map/ppermute | solution.py:61
  64.7 8.6 %collective-permute-start.20 = (bf16[8,128,128]{2,1,0:T(8,128)(2,1)S(1)}, bf16[8,128,128]{2,1,0:T(8,128)(2,1)S(1)}, u32[]{:S(2)}, u32[]{:S(2)}) collective-permute-start(bf16[8,128,128]{2,1,0:T(8,128)(2,1)S(1)} %concatenate.64), channel_id=1, source_target_pairs={{8,0},{1,8},{9,1},{3,9},{11,3},{2,11},{10,2},{0,10},{12,4},{5,12},... | collective-permute-start | bytes 786440 | tf_op jit(solution)/shard_map/ppermute | solution.py:61
  66.9 10.4 %collective-permute-start.21 = (bf16[8,128,128]{2,1,0:T(8,128)(2,1)S(1)}, bf16[8,128,128]{2,1,0:T(8,128)(2,1)S(1)}, u32[]{:S(2)}, u32[]{:S(2)}) collective-permute-start(bf16[8,128,128]{2,1,0:T(8,128)(2,1)S(1)} %concatenate.64), channel_id=1, source_target_pairs={{10,0},{0,8},{8,1},{1,9},{9,3},{3,11},{11,2},{2,10},{14,4},{4,12},... | collective-permute-start | bytes 786440 | tf_op jit(solution)/shard_map/ppermute | solution.py:61
  68.5 35.2 %collective-permute-start.16 = (bf16[21,128,128]{2,1,0:T(8,128)(2,1)S(1)}, bf16[21,128,128]{2,1,0:T(8,128)(2,1)S(1)}, u32[]{:S(2)}, u32[]{:S(2)}) collective-permute-start(bf16[21,128,128]{2,1,0:T(8,128)(2,1)S(1)} %get-tuple-element.64.refs_0_), channel_id=1, source_target_pairs={{8,0},{1,8},{9,1},{3,9},{11,3},{2,11},{10,2},{0,10},{12,4},{5,12},... | collective-permute-start | bytes 2064392 | tf_op jit(solution)/shard_map/ppermute | solution.py:61
  70.2 35.4 %collective-permute-start.18 = (bf16[21,128,128]{2,1,0:T(8,128)(2,1)S(1)}, bf16[21,128,128]{2,1,0:T(8,128)(2,1)S(1)}, u32[]{:S(2)}, u32[]{:S(2)}) collective-permute-start(bf16[21,128,128]{2,1,0:T(8,128)(2,1)S(1)} %get-tuple-element.65.refs_1_), channel_id=1, source_target_pairs={{8,0},{1,8},{9,1},{3,9},{11,3},{2,11},{10,2},{0,10},{12,4},{5,12},... | collective-permute-start | bytes 2064392 | tf_op jit(solution)/shard_map/ppermute | solution.py:61
  71.5 34.4 %collective-permute-start.2 = (bf16[42,128,128]{2,1,0:T(8,128)(2,1)S(1)}, bf16[42,128,128]{2,1,0:T(8,128)(2,1)S(1)}, u32[]{:S(2)}, u32[]{:S(2)}) collective-permute-start(bf16[42,128,128]{2,1,0:T(8,128)(2,1)S(1)} %bitcast.209), channel_id=1, source_target_pairs={{0,0},{1,8},{2,1},{3,9},{4,3},{5,11},{6,2},{7,10},{8,4},{9,12},{10... | collective-permute-start | bytes 4128776 | tf_op jit(solution)/shard_map/ppermute | solution.py:51
  73.3 30.3 %collective-permute-start.22 = (bf16[8,128,128]{2,1,0:T(8,128)(2,1)S(1)}, bf16[8,128,128]{2,1,0:T(8,128)(2,1)S(1)}, u32[]{:S(2)}, u32[]{:S(2)}) collective-permute-start(bf16[8,128,128]{2,1,0:T(8,128)(2,1)S(1)} %collective-permute-done.20), channel_id=1, source_target_pairs={{8,0},{1,8},{9,1},{3,9},{11,3},{2,11},{10,2},{0,10},{12,4},{5,12},... | collective-permute-start | bytes 786440 | tf_op jit(solution)/shard_map/ppermute | solution.py:61
  77.2 28.4 %collective-permute-start.23 = (bf16[8,128,128]{2,1,0:T(8,128)(2,1)S(1)}, bf16[8,128,128]{2,1,0:T(8,128)(2,1)S(1)}, u32[]{:S(2)}, u32[]{:S(2)}) collective-permute-start(bf16[8,128,128]{2,1,0:T(8,128)(2,1)S(1)} %collective-permute-done.21), channel_id=1, source_target_pairs={{10,0},{0,8},{8,1},{1,9},{9,3},{3,11},{11,2},{2,10},{14,4},{4,12},... | collective-permute-start | bytes 786440 | tf_op jit(solution)/shard_map/ppermute | solution.py:61
  103.6 10.4 %collective-permute-start.17 = (bf16[21,128,128]{2,1,0:T(8,128)(2,1)S(1)}, bf16[21,128,128]{2,1,0:T(8,128)(2,1)S(1)}, u32[]{:S(2)}, u32[]{:S(2)}) collective-permute-start(bf16[21,128,128]{2,1,0:T(8,128)(2,1)S(1)} %collective-permute-done.16.refs_2_), channel_id=1, source_target_pairs={{8,0},{1,8},{9,1},{3,9},{11,3},{2,11},{10,2},{0,10},{12,4},{5,12},... | collective-permute-start | bytes 2064392 | tf_op jit(solution)/shard_map/ppermute | solution.py:61
  105.6 15.8 %collective-permute-start.19 = (bf16[21,128,128]{2,1,0:T(8,128)(2,1)S(1)}, bf16[21,128,128]{2,1,0:T(8,128)(2,1)S(1)}, u32[]{:S(2)}, u32[]{:S(2)}) collective-permute-start(bf16[21,128,128]{2,1,0:T(8,128)(2,1)S(1)} %collective-permute-done.18.refs_3_), channel_id=1, source_target_pairs={{8,0},{1,8},{9,1},{3,9},{11,3},{2,11},{10,2},{0,10},{12,4},{5,12},... | collective-permute-start | bytes 2064392 | tf_op jit(solution)/shard_map/ppermute | solution.py:61
  127.8 10.6 %collective-permute-start.27 = (bf16[21,128,128]{2,1,0:T(8,128)(2,1)S(1)}, bf16[21,128,128]{2,1,0:T(8,128)(2,1)S(1)}, u32[]{:S(2)}, u32[]{:S(2)}) collective-permute-start(bf16[21,128,128]{2,1,0:T(8,128)(2,1)S(1)} %fusion.17), channel_id=1, source_target_pairs={{10,0},{0,8},{8,1},{1,9},{9,3},{3,11},{11,2},{2,10},{14,4},{4,12},... | collective-permute-start | bytes 2064392 | tf_op jit(solution)/shard_map/ppermute | solution.py:61
  129.7 10.0 %collective-permute-start.36 = (bf16[21,128,128]{2,1,0:T(8,128)(2,1)S(1)}, bf16[21,128,128]{2,1,0:T(8,128)(2,1)S(1)}, u32[]{:S(2)}, u32[]{:S(2)}) collective-permute-start(bf16[21,128,128]{2,1,0:T(8,128)(2,1)S(1)} %collective-permute-done.17.refs_4_), channel_id=1, source_target_pairs={{8,0},{1,8},{9,1},{3,9},{11,3},{2,11},{10,2},{0,10},{12,4},{5,12},... | collective-permute-start | bytes 2064392 | tf_op jit(solution)/shard_map/ppermute | solution.py:61
  129.8 15.8 %collective-permute-start.37 = (bf16[21,128,128]{2,1,0:T(8,128)(2,1)S(1)}, bf16[21,128,128]{2,1,0:T(8,128)(2,1)S(1)}, u32[]{:S(2)}, u32[]{:S(2)}) collective-permute-start(bf16[21,128,128]{2,1,0:T(8,128)(2,1)S(1)} %collective-permute-done.19.refs_5_), channel_id=1, source_target_pairs={{8,0},{1,8},{9,1},{3,9},{11,3},{2,11},{10,2},{0,10},{12,4},{5,12},... | collective-permute-start | bytes 2064392 | tf_op jit(solution)/shard_map/ppermute | solution.py:61
  131.4 22.8 %collective-permute-start.24 = (bf16[21,128,128]{2,1,0:T(8,128)(2,1)S(1)}, bf16[21,128,128]{2,1,0:T(8,128)(2,1)S(1)}, u32[]{:S(2)}, u32[]{:S(2)}) collective-permute-start(bf16[21,128,128]{2,1,0:T(8,128)(2,1)S(1)} %fusion.16), channel_id=1, source_target_pairs={{10,0},{0,8},{8,1},{1,9},{9,3},{3,11},{11,2},{2,10},{14,4},{4,12},... | collective-permute-start | bytes 2064392 | tf_op jit(solution)/shard_map/ppermute | solution.py:61
  139.5 17.6 %collective-permute-start.28 = (bf16[21,128,128]{2,1,0:T(8,128)(2,1)S(1)}, bf16[21,128,128]{2,1,0:T(8,128)(2,1)S(1)}, u32[]{:S(2)}, u32[]{:S(2)}) collective-permute-start(bf16[21,128,128]{2,1,0:T(8,128)(2,1)S(1)} %fusion.12), channel_id=1, source_target_pairs={{10,0},{0,8},{8,1},{1,9},{9,3},{3,11},{11,2},{2,10},{14,4},{4,12},... | collective-permute-start | bytes 2064392 | tf_op jit(solution)/shard_map/ppermute | solution.py:61
  151.9 10.7 %collective-permute-start.38 = (bf16[21,128,128]{2,1,0:T(8,128)(2,1)S(1)}, bf16[21,128,128]{2,1,0:T(8,128)(2,1)S(1)}, u32[]{:S(2)}, u32[]{:S(2)}) collective-permute-start(bf16[21,128,128]{2,1,0:T(8,128)(2,1)S(1)} %get-tuple-element.100.refs_0_), channel_id=1, source_target_pairs={{8,0},{1,8},{9,1},{3,9},{11,3},{2,11},{10,2},{0,10},{12,4},{5,12},... | collective-permute-start | bytes 2064392 | tf_op jit(solution)/shard_map/ppermute | solution.py:61
  155.3 10.4 %collective-permute-start.25 = (bf16[21,128,128]{2,1,0:T(8,128)(2,1)S(1)}, bf16[21,128,128]{2,1,0:T(8,128)(2,1)S(1)}, u32[]{:S(2)}, u32[]{:S(2)}) collective-permute-start(bf16[21,128,128]{2,1,0:T(8,128)(2,1)S(1)} %fusion.14), channel_id=1, source_target_pairs={{10,0},{0,8},{8,1},{1,9},{9,3},{3,11},{11,2},{2,10},{14,4},{4,12},... | collective-permute-start | bytes 2064392 | tf_op jit(solution)/shard_map/ppermute | solution.py:61
  157.0 13.0 %collective-permute-start.39 = (bf16[21,128,128]{2,1,0:T(8,128)(2,1)S(1)}, bf16[21,128,128]{2,1,0:T(8,128)(2,1)S(1)}, u32[]{:S(2)}, u32[]{:S(2)}) collective-permute-start(bf16[21,128,128]{2,1,0:T(8,128)(2,1)S(1)} %get-tuple-element.101.refs_1_), channel_id=1, source_target_pairs={{8,0},{1,8},{9,1},{3,9},{11,3},{2,11},{10,2},{0,10},{12,4},{5,12},... | collective-permute-start | bytes 2064392 | tf_op jit(solution)/shard_map/ppermute | solution.py:61
  158.3 21.3 %collective-permute-start.29 = (bf16[21,128,128]{2,1,0:T(8,128)(2,1)S(1)}, bf16[21,128,128]{2,1,0:T(8,128)(2,1)S(1)}, u32[]{:S(2)}, u32[]{:S(2)}) collective-permute-start(bf16[21,128,128]{2,1,0:T(8,128)(2,1)S(1)} %fusion.13), channel_id=1, source_target_pairs={{10,0},{0,8},{8,1},{1,9},{9,3},{3,11},{11,2},{2,10},{14,4},{4,12},... | collective-permute-start | bytes 2064392 | tf_op jit(solution)/shard_map/ppermute | solution.py:61
  162.6 14.7 %collective-permute-start.40 = (bf16[21,128,128]{2,1,0:T(8,128)(2,1)S(1)}, bf16[21,128,128]{2,1,0:T(8,128)(2,1)S(1)}, u32[]{:S(2)}, u32[]{:S(2)}) collective-permute-start(bf16[21,128,128]{2,1,0:T(8,128)(2,1)S(1)} %collective-permute-done.38.refs_2_), channel_id=1, source_target_pairs={{8,0},{1,8},{9,1},{3,9},{11,3},{2,11},{10,2},{0,10},{12,4},{5,12},... | collective-permute-start | bytes 2064392 | tf_op jit(solution)/shard_map/ppermute | solution.py:61
  166.9 13.6 %collective-permute-start.26 = (bf16[21,128,128]{2,1,0:T(8,128)(2,1)S(1)}, bf16[21,128,128]{2,1,0:T(8,128)(2,1)S(1)}, u32[]{:S(2)}, u32[]{:S(2)}) collective-permute-start(bf16[21,128,128]{2,1,0:T(8,128)(2,1)S(1)} %fusion.15), channel_id=1, source_target_pairs={{10,0},{0,8},{8,1},{1,9},{9,3},{3,11},{11,2},{2,10},{14,4},{4,12},... | collective-permute-start | bytes 2064392 | tf_op jit(solution)/shard_map/ppermute | solution.py:61
  170.0 16.1 %collective-permute-start.41 = (bf16[21,128,128]{2,1,0:T(8,128)(2,1)S(1)}, bf16[21,128,128]{2,1,0:T(8,128)(2,1)S(1)}, u32[]{:S(2)}, u32[]{:S(2)}) collective-permute-start(bf16[21,128,128]{2,1,0:T(8,128)(2,1)S(1)} %collective-permute-done.39.refs_3_), channel_id=1, source_target_pairs={{8,0},{1,8},{9,1},{3,9},{11,3},{2,11},{10,2},{0,10},{12,4},{5,12},... | collective-permute-start | bytes 2064392 | tf_op jit(solution)/shard_map/ppermute | solution.py:61
  177.4 14.7 %collective-permute-start.42 = (bf16[21,128,128]{2,1,0:T(8,128)(2,1)S(1)}, bf16[21,128,128]{2,1,0:T(8,128)(2,1)S(1)}, u32[]{:S(2)}, u32[]{:S(2)}) collective-permute-start(bf16[21,128,128]{2,1,0:T(8,128)(2,1)S(1)} %collective-permute-done.40.refs_4_), channel_id=1, source_target_pairs={{8,0},{1,8},{9,1},{3,9},{11,3},{2,11},{10,2},{0,10},{12,4},{5,12},... | collective-permute-start | bytes 2064392 | tf_op jit(solution)/shard_map/ppermute | solution.py:61
  186.1 13.4 %collective-permute-start.43 = (bf16[21,128,128]{2,1,0:T(8,128)(2,1)S(1)}, bf16[21,128,128]{2,1,0:T(8,128)(2,1)S(1)}, u32[]{:S(2)}, u32[]{:S(2)}) collective-permute-start(bf16[21,128,128]{2,1,0:T(8,128)(2,1)S(1)} %collective-permute-done.41.refs_5_), channel_id=1, source_target_pairs={{8,0},{1,8},{9,1},{3,9},{11,3},{2,11},{10,2},{0,10},{12,4},{5,12},... | collective-permute-start | bytes 2064392 | tf_op jit(solution)/shard_map/ppermute | solution.py:61
  187.1 21.1 %collective-permute-start.33 = (bf16[21,128,128]{2,1,0:T(8,128)(2,1)S(1)}, bf16[21,128,128]{2,1,0:T(8,128)(2,1)S(1)}, u32[]{:S(2)}, u32[]{:S(2)}) collective-permute-start(bf16[21,128,128]{2,1,0:T(8,128)(2,1)S(1)} %fusion.19), channel_id=1, source_target_pairs={{10,0},{0,8},{8,1},{1,9},{9,3},{3,11},{11,2},{2,10},{14,4},{4,12},... | collective-permute-start | bytes 2064392 | tf_op jit(solution)/shard_map/ppermute | solution.py:61
  189.1 21.1 %collective-permute-start.30 = (bf16[21,128,128]{2,1,0:T(8,128)(2,1)S(1)}, bf16[21,128,128]{2,1,0:T(8,128)(2,1)S(1)}, u32[]{:S(2)}, u32[]{:S(2)}) collective-permute-start(bf16[21,128,128]{2,1,0:T(8,128)(2,1)S(1)} %fusion.18), channel_id=1, source_target_pairs={{10,0},{0,8},{8,1},{1,9},{9,3},{3,11},{11,2},{2,10},{14,4},{4,12},... | collective-permute-start | bytes 2064392 | tf_op jit(solution)/shard_map/ppermute | solution.py:61
  205.9 10.7 %collective-permute-start.44 = (bf16[21,128,128]{2,1,0:T(8,128)(2,1)S(1)}, bf16[21,128,128]{2,1,0:T(8,128)(2,1)S(1)}, u32[]{:S(2)}, u32[]{:S(2)}) collective-permute-start(bf16[21,128,128]{2,1,0:T(8,128)(2,1)S(1)} %get-tuple-element.103.refs_0_.refs_14_), channel_id=1, source_target_pairs={{8,0},{1,8},{9,1},{3,9},{11,3},{2,11},{10,2},{0,10},{12,4},{5,12},... | collective-permute-start | bytes 2064392 | tf_op jit(solution)/shard_map/ppermute | solution.py:61
  208.1 15.8 %collective-permute-start.45 = (bf16[21,128,128]{2,1,0:T(8,128)(2,1)S(1)}, bf16[21,128,128]{2,1,0:T(8,128)(2,1)S(1)}, u32[]{:S(2)}, u32[]{:S(2)}) collective-permute-start(bf16[21,128,128]{2,1,0:T(8,128)(2,1)S(1)} %get-tuple-element.104.refs_1_.refs_15_), channel_id=1, source_target_pairs={{8,0},{1,8},{9,1},{3,9},{11,3},{2,11},{10,2},{0,10},{12,4},{5,12},... | collective-permute-start | bytes 2064392 | tf_op jit(solution)/shard_map/ppermute | solution.py:61
  208.6 17.6 %collective-permute-start.34 = (bf16[21,128,128]{2,1,0:T(8,128)(2,1)S(1)}, bf16[21,128,128]{2,1,0:T(8,128)(2,1)S(1)}, u32[]{:S(2)}, u32[]{:S(2)}) collective-permute-start(bf16[21,128,128]{2,1,0:T(8,128)(2,1)S(1)} %fusion.8), channel_id=1, source_target_pairs={{10,0},{0,8},{8,1},{1,9},{9,3},{3,11},{11,2},{2,10},{14,4},{4,12},... | collective-permute-start | bytes 2064392 | tf_op jit(solution)/shard_map/ppermute | solution.py:61
  210.7 18.1 %collective-permute-start.31 = (bf16[21,128,128]{2,1,0:T(8,128)(2,1)S(1)}, bf16[21,128,128]{2,1,0:T(8,128)(2,1)S(1)}, u32[]{:S(2)}, u32[]{:S(2)}) collective-permute-start(bf16[21,128,128]{2,1,0:T(8,128)(2,1)S(1)} %fusion.10), channel_id=1, source_target_pairs={{10,0},{0,8},{8,1},{1,9},{9,3},{3,11},{11,2},{2,10},{14,4},{4,12},... | collective-permute-start | bytes 2064392 | tf_op jit(solution)/shard_map/ppermute | solution.py:61
  216.6 15.2 %collective-permute-start.46 = (bf16[21,128,128]{2,1,0:T(8,128)(2,1)S(1)}, bf16[21,128,128]{2,1,0:T(8,128)(2,1)}, u32[]{:S(2)}, u32[]{:S(2)}) collective-permute-start(bf16[21,128,128]{2,1,0:T(8,128)(2,1)S(1)} %collective-permute-done.44.refs_2_.refs_16_), channel_id=1, source_target_pairs={{8,0},{1,8},{9,1},{3,9},{11,3},{2,11},{10,2},{0,10},{12,4},{5,12},... | collective-permute-start | bytes 2064392 | tf_op jit(solution)/shard_map/ppermute | solution.py:61
  223.9 14.7 %collective-permute-start.47 = (bf16[21,128,128]{2,1,0:T(8,128)(2,1)S(1)}, bf16[21,128,128]{2,1,0:T(8,128)(2,1)}, u32[]{:S(2)}, u32[]{:S(2)}) collective-permute-start(bf16[21,128,128]{2,1,0:T(8,128)(2,1)S(1)} %collective-permute-done.45.refs_3_.refs_17_), channel_id=1, source_target_pairs={{8,0},{1,8},{9,1},{3,9},{11,3},{2,11},{10,2},{0,10},{12,4},{5,12},... | collective-permute-start | bytes 2064392 | tf_op jit(solution)/shard_map/ppermute | solution.py:61
  227.5 15.0 %collective-permute-start.35 = (bf16[21,128,128]{2,1,0:T(8,128)(2,1)}, bf16[21,128,128]{2,1,0:T(8,128)(2,1)S(1)}, u32[]{:S(2)}, u32[]{:S(2)}) collective-permute-start(bf16[21,128,128]{2,1,0:T(8,128)(2,1)} %fusion.9), channel_id=1, source_target_pairs={{10,0},{0,8},{8,1},{1,9},{9,3},{3,11},{11,2},{2,10},{14,4},{4,12},... | collective-permute-start | bytes 2064392 | tf_op jit(solution)/shard_map/ppermute | solution.py:61
  230.0 15.4 %collective-permute-start.32 = (bf16[21,128,128]{2,1,0:T(8,128)(2,1)}, bf16[21,128,128]{2,1,0:T(8,128)(2,1)S(1)}, u32[]{:S(2)}, u32[]{:S(2)}) collective-permute-start(bf16[21,128,128]{2,1,0:T(8,128)(2,1)} %fusion.11), channel_id=1, source_target_pairs={{10,0},{0,8},{8,1},{1,9},{9,3},{3,11},{11,2},{2,10},{14,4},{4,12},... | collective-permute-start | bytes 2064392 | tf_op jit(solution)/shard_map/ppermute | solution.py:61
  231.8 19.4 %collective-permute-start.48 = (bf16[21,128,128]{2,1,0:T(8,128)(2,1)}, bf16[21,128,128]{2,1,0:T(8,128)(2,1)}, u32[]{:S(2)}, u32[]{:S(2)}) collective-permute-start(bf16[21,128,128]{2,1,0:T(8,128)(2,1)} %collective-permute-done.46.refs_4_.refs_18_), channel_id=1, source_target_pairs={{8,0},{1,8},{9,1},{3,9},{11,3},{2,11},{10,2},{0,10},{12,4},{5,12},... | collective-permute-start | bytes 2064392 | tf_op jit(solution)/shard_map/ppermute | solution.py:61
  238.7 14.9 %collective-permute-start.49 = (bf16[21,128,128]{2,1,0:T(8,128)(2,1)}, bf16[21,128,128]{2,1,0:T(8,128)(2,1)}, u32[]{:S(2)}, u32[]{:S(2)}) collective-permute-start(bf16[21,128,128]{2,1,0:T(8,128)(2,1)} %collective-permute-done.47.refs_5_.refs_19_), channel_id=1, source_target_pairs={{8,0},{1,8},{9,1},{3,9},{11,3},{2,11},{10,2},{0,10},{12,4},{5,12},... | collective-permute-start | bytes 2064392 | tf_op jit(solution)/shard_map/ppermute | solution.py:61
  258.0 4.3 %collective-permute-start.54 = (f32[1,128]{1,0:T(1,128)S(1)}, f32[1,128]{1,0:T(1,128)S(1)}, u32[]{:S(2)}, u32[]{:S(2)}) collective-permute-start(f32[1,128]{1,0:T(1,128)S(1)} %get-tuple-element.114), channel_id=1, source_target_pairs={{8,0},{0,8},{9,1},{1,9},{11,3},{3,11},{10,2},{2,10},{12,4},{4,12},... | collective-permute-start | bytes 1544 | tf_op jit(solution)/shard_map/ppermute | solution.py:66
  262.3 5.5 %collective-permute-start.55 = (f32[2,128]{1,0:T(2,128)S(1)}, f32[2,128]{1,0:T(2,128)S(1)}, u32[]{:S(2)}, u32[]{:S(2)}) collective-permute-start(f32[2,128]{1,0:T(2,128)S(1)} %maximum_select_fusion.4), channel_id=1, source_target_pairs={{1,0},{9,8},{0,1},{8,9},{2,3},{10,11},{3,2},{11,10},{5,4},{13,12},... | collective-permute-start | bytes 3080 | tf_op jit(solution)/shard_map/ppermute | solution.py:66
  264.0 8.3 %collective-permute-start.53 = (bf16[4,128,128]{2,1,0:T(8,128)(2,1)}, bf16[4,128,128]{2,1,0:T(8,128)(2,1)}, u32[]{:S(2)}, u32[]{:S(2)}) collective-permute-start(bf16[4,128,128]{2,1,0:T(8,128)(2,1)} %copy-done.22), channel_id=1, source_target_pairs={{2,0},{10,8},{0,1},{8,9},{1,3},{9,11},{3,2},{11,10},{6,4},{14,12},... | collective-permute-start | bytes 393224 | tf_op jit(solution)/shard_map/ppermute | solution.py:61
  264.4 8.0 %collective-permute-start.52 = (bf16[4,128,128]{2,1,0:T(8,128)(2,1)}, bf16[4,128,128]{2,1,0:T(8,128)(2,1)}, u32[]{:S(2)}, u32[]{:S(2)}) collective-permute-start(bf16[4,128,128]{2,1,0:T(8,128)(2,1)} %copy-done.22), channel_id=1, source_target_pairs={{1,0},{9,8},{3,1},{11,9},{2,3},{10,11},{0,2},{8,10},{5,4},{13,12},... | collective-permute-start | bytes 393224 | tf_op jit(solution)/shard_map/ppermute | solution.py:61
  266.1 6.3 %collective-permute-start.51 = (bf16[4,128,128]{2,1,0:T(8,128)(2,1)}, bf16[4,128,128]{2,1,0:T(8,128)(2,1)}, u32[]{:S(2)}, u32[]{:S(2)}) collective-permute-start(bf16[4,128,128]{2,1,0:T(8,128)(2,1)} %copy-done.22), channel_id=1, source_target_pairs={{10,0},{0,8},{8,1},{1,9},{9,3},{3,11},{11,2},{2,10},{14,4},{4,12},... | collective-permute-start | bytes 393224 | tf_op jit(solution)/shard_map/ppermute | solution.py:61
  266.1 6.3 %collective-permute-start.50 = (bf16[4,128,128]{2,1,0:T(8,128)(2,1)}, bf16[4,128,128]{2,1,0:T(8,128)(2,1)}, u32[]{:S(2)}, u32[]{:S(2)}) collective-permute-start(bf16[4,128,128]{2,1,0:T(8,128)(2,1)} %copy-done.22), channel_id=1, source_target_pairs={{8,0},{1,8},{9,1},{3,9},{11,3},{2,11},{10,2},{0,10},{12,4},{5,12},... | collective-permute-start | bytes 393224 | tf_op jit(solution)/shard_map/ppermute | solution.py:61
  267.8 4.5 %collective-permute-start.56 = (f32[4,128]{1,0:T(4,128)S(1)}, f32[4,128]{1,0:T(4,128)S(1)}, u32[]{:S(2)}, u32[]{:S(2)}) collective-permute-start(f32[4,128]{1,0:T(4,128)S(1)} %maximum_select_fusion.2), channel_id=1, source_target_pairs={{3,0},{11,8},{2,1},{10,9},{0,3},{8,11},{1,2},{9,10},{7,4},{15,12},... | collective-permute-start | bytes 6152 | tf_op jit(solution)/shard_map/ppermute | solution.py:66
  289.7 4.0 %collective-permute-start.58 = (f32[2,128]{1,0:T(2,128)S(1)}, f32[2,128]{1,0:T(2,128)S(1)}, u32[]{:S(2)}, u32[]{:S(2)}) collective-permute-start(f32[2,128]{1,0:T(2,128)S(1)} %maximum_select_fusion.5), channel_id=1, source_target_pairs={{1,0},{9,8},{0,1},{8,9},{2,3},{10,11},{3,2},{11,10},{5,4},{13,12},... | collective-permute-start | bytes 3080 | tf_op jit(solution)/shard_map/ppermute | solution.py:66
  290.2 9.2 %collective-permute-start.61 = (f32[2,128,128]{2,1,0:T(8,128)S(1)}, f32[2,128,128]{2,1,0:T(8,128)S(1)}, u32[]{:S(2)}, u32[]{:S(2)}) collective-permute-start(f32[2,128,128]{2,1,0:T(8,128)S(1)} %get-tuple-element.140), channel_id=1, source_target_pairs={{10,0},{0,8},{8,1},{1,9},{9,3},{3,11},{11,2},{2,10},{14,4},{4,12},... | collective-permute-start | bytes 393224 | tf_op jit(solution)/shard_map/ppermute | solution.py:61
  290.2 9.2 %collective-permute-start.63 = (f32[2,128,128]{2,1,0:T(8,128)S(1)}, f32[2,128,128]{2,1,0:T(8,128)S(1)}, u32[]{:S(2)}, u32[]{:S(2)}) collective-permute-start(f32[2,128,128]{2,1,0:T(8,128)S(1)} %get-tuple-element.141), channel_id=1, source_target_pairs={{11,0},{2,8},{10,1},{0,9},{8,3},{1,11},{9,2},{3,10},{15,4},{6,12},... | collective-permute-start | bytes 393224 | tf_op jit(solution)/shard_map/ppermute | solution.py:61
  291.8 8.5 %collective-permute-start.62 = (f32[2,128,128]{2,1,0:T(8,128)S(1)}, f32[2,128,128]{2,1,0:T(8,128)S(1)}, u32[]{:S(2)}, u32[]{:S(2)}) collective-permute-start(f32[2,128,128]{2,1,0:T(8,128)S(1)} %get-tuple-element.142), channel_id=1, source_target_pairs={{2,0},{10,8},{0,1},{8,9},{1,3},{9,11},{3,2},{11,10},{6,4},{14,12},... | collective-permute-start | bytes 393224 | tf_op jit(solution)/shard_map/ppermute | solution.py:61
  293.8 4.5 %collective-permute-start.59 = (f32[4,128]{1,0:T(4,128)S(1)}, f32[4,128]{1,0:T(4,128)S(1)}, u32[]{:S(2)}, u32[]{:S(2)}) collective-permute-start(f32[4,128]{1,0:T(4,128)S(1)} %maximum_select_fusion.3), channel_id=1, source_target_pairs={{3,0},{11,8},{2,1},{10,9},{0,3},{8,11},{1,2},{9,10},{7,4},{15,12},... | collective-permute-start | bytes 6152 | tf_op jit(solution)/shard_map/ppermute | solution.py:66
  307.0 9.7 %collective-permute-start.64 = (bf16[128,128]{1,0:T(8,128)(2,1)S(1)}, bf16[128,128]{1,0:T(8,128)(2,1)S(1)}, u32[]{:S(2)}, u32[]{:S(2)}) collective-permute-start(bf16[128,128]{1,0:T(8,128)(2,1)S(1)} %get-tuple-element.147), channel_id=1, source_target_pairs={{0,16},{8,17},{1,18},{9,19},{3,20},{11,21},{2,22},{10,23},{4,24},{... | collective-permute-start | bytes 98312 | tf_op jit(solution)/shard_map/ppermute | solution.py:56
  307.8 8.9 %collective-permute-start.67 = (bf16[128,128]{1,0:T(8,128)(2,1)S(1)}, bf16[128,128]{1,0:T(8,128)(2,1)S(1)}, u32[]{:S(2)}, u32[]{:S(2)}) collective-permute-start(bf16[128,128]{1,0:T(8,128)(2,1)S(1)} %get-tuple-element.148), channel_id=1, source_target_pairs={{0,21},{8,22},{1,23},{9,16},{3,17},{11,18},{2,19},{10,20},{4,29},{... | collective-permute-start | bytes 98312 | tf_op jit(solution)/shard_map/ppermute | solution.py:56
  313.5 5.4 %collective-permute-start.66 = (bf16[128,128]{1,0:T(8,128)(2,1)S(1)}, bf16[128,128]{1,0:T(8,128)(2,1)S(1)}, u32[]{:S(2)}, u32[]{:S(2)}) collective-permute-start(bf16[128,128]{1,0:T(8,128)(2,1)S(1)} %get-tuple-element.149), channel_id=1, source_target_pairs={{0,22},{8,23},{1,16},{9,17},{3,18},{11,19},{2,20},{10,21},{4,30},{... | collective-permute-start | bytes 98312 | tf_op jit(solution)/shard_map/ppermute | solution.py:56
  314.4 4.5 %collective-permute-start.65 = (bf16[128,128]{1,0:T(8,128)(2,1)S(1)}, bf16[128,128]{1,0:T(8,128)(2,1)S(1)}, u32[]{:S(2)}, u32[]{:S(2)}) collective-permute-start(bf16[128,128]{1,0:T(8,128)(2,1)S(1)} %get-tuple-element.150), channel_id=1, source_target_pairs={{0,23},{8,16},{1,17},{9,18},{3,19},{11,20},{2,21},{10,22},{4,31},{... | collective-permute-start | bytes 98312 | tf_op jit(solution)/shard_map/ppermute | solution.py:56
  (40 other events, 458.6 us)

commit v2 on v1

--- a/solution.py
+++ b/solution.py
@@ -61,6 +61,22 @@
         return lax.ppermute(
             x, BOTH, self.pairs(lambda g, k: self.slot(g + chain_by, k + by), self.slot)
         )
+
+    def from_sector(self, x, source):
+        return lax.ppermute(x, BOTH, self.pairs(lambda g, k: self.slot(g, source(k)), self.slot))
+
+    def gather_ahead(self, x, count):
+        if count != 3 or self.secs != 8:
+            found = [x]
+            for _ in range(count):
+                found.append(self.ahead(found[-1], 1))
+            return found
+        one = self.ahead(x, 1)
+        onward = self.from_sector(x, lambda k: k - 2 if k % 2 == 0 else k)
+        three = self.from_sector(onward, lambda k: k + 3 if k % 2 == 0 else k - 3)
+        even = lax.axis_index("site") % 2 == 0
+        two = self.partner(jnp.where(even, three, one), 1)
+        return [x, one, two, three]
 
     def partner(self, x, bit):
         return lax.ppermute(x, BOTH, self.pairs(lambda g, k: self.slot(g, k ^ bit), self.slot))
@@ -692,16 +708,14 @@
     def ahead(env, by, chain_by=0):
         return [places.ahead(chunk, by, chain_by) for chunk in env]
 
-    first = places.fetch(jnp.concatenate([right_env[0, :, 0], left_iso, right_iso]))
-    left_isos = [first[channels : channels + states]]
-    right_isos = [first[channels + states :]]
+    right = places.fetch(right_env[0, :, 0])
+    left = places.fetch(left_env[0, :, 0])
+    both_isos = places.fetch(jnp.concatenate([left_iso, right_iso]))
+    left_isos, right_isos = [both_isos[:states]], [both_isos[states:]]
     for step in range(1, ENV_STEPS):
         left_isos.append(places.fetch(left_iso, step))
         right_isos.append(places.fetch(right_iso, -step))
     own_tensors = places.fetch(jnp.concatenate([left_iso, centre[None]]), ENV_STEPS)
-    right = jnp.split(first[:channels], pieces)
-    right, left_env = after(right, left_env)
-    left = jnp.split(places.fetch(left_env[0, :, 0]), pieces)
     rolled = [
         classes_of(places, jnp.concatenate([left_isos[step], right_isos[step]]))
         for step in range(ENV_STEPS)
@@ -726,9 +740,10 @@
         "sxy,syz->sxz", own_iso, jnp.stack(centres), preferred_element_type=jnp.float32
     )
     rolled_vector = other_classes_of(places, vector.astype(jnp.bfloat16))
-    right, (rolled[1:], rolled_vector, weights) = after(
-        right, (rolled[1:], rolled_vector, weights)
-    )
+    (right, left), (rolled, rolled_vector, weights) = after(
+        (right, left), (rolled, rolled_vector, weights)
+    )
+    right, left = jnp.split(right, pieces), jnp.split(left, pieces)
     centre_float = own_centre.astype(jnp.float32)
     centre_square = jnp.sum((centre_float * centre_float).reshape(-1, ROWS, block), axis=0)
 
@@ -736,8 +751,6 @@
     for step in range(ENV_STEPS):
         envs = [right]
         for t in range(1, states):
-            if step == 0 and t == states - 1:
-                left, envs[-1] = after(left, envs[-1])
             envs.append(ahead(envs[-1], 1))
         right, square = right_whole(
             envs,
@@ -772,9 +785,8 @@
         right = ahead(right, 0, 2 * ENV_STEPS)
         right_squares = ahead(right_squares, 0, 2 * ENV_STEPS)
     squares = left_squares + right_squares + [centre_square]
-    rights = [right]
-    for s in range(1, states):
-        rights.append(ahead(rights[-1], 1))
+    rights = [places.gather_ahead(chunk, states - 1) for chunk in right]
+    rights = [[chunks[s] for chunks in rights] for s in range(states)]
     weight = weights[0][ENV_STEPS]
     gathered, vector = operator_front(
         left, weight, left_groups, entry_count, vector, rolled_vector

time: 322 us -> 351 us (1.090)
  waiting for transfers between devices: 116 us -> 131 us
  starting transfers between devices: 107 us -> 118 us
    ppermute x0 -> x4, waiting for transfers between devices: none -> 11.7 us  [from_sector(): lax.ppermute(x, BOTH, self.pairs(lambda g, k: self.slot(g, source(k)), se...]
    ppermute x52 -> x48, starting transfers between devices: 65.3 us -> 70.7 us  [ahead(): lax.ppermute(x, BOTH, self.pairs(lambda g, k: self.slot(g + chain_by, k +...]
    ppermute x0 -> x4, starting transfers between devices: none -> 5.2 us  [from_sector(): lax.ppermute(x, BOTH, self.pairs(lambda g, k: self.slot(g, source(k)), se...]
    ppermute x5 -> x6, starting transfers between devices: 24.7 us -> 23.3 us  [fetch(): lax.ppermute(x, BOTH, self.pairs(lambda g, k: self.home(g + site_by, k +...]
    ppermute x52 -> x48, waiting for transfers between devices: 102 us -> 104 us  [ahead(): lax.ppermute(x, BOTH, self.pairs(lambda g, k: self.slot(g + chain_by, k +...]
    ppermute x6 -> x8, waiting for transfers between devices: 9.52 us -> 9.16 us  [partner(): lax.ppermute(x, BOTH, self.pairs(lambda g, k: self.slot(g, k ^ bit), self...]
    ppermute x6 -> x8, starting transfers between devices: 7.12 us -> 6.89 us  [partner(): lax.ppermute(x, BOTH, self.pairs(lambda g, k: self.slot(g, k ^ bit), self...]
    unnamed x82 -> x72, local copies, waits for them, and re-layouts: 9.16 us -> 9.23 us
  transfers between devices with their start and end apart: 68 -> 71, of which waited for: 29 -> 35; matrix products, arithmetic and copies ran while one was open for 7% -> 6% of each run, Pallas kernels for 10% -> 11%
where the time goes in v2:
time: 351 us; the launch traced here: 347 us
  waiting for transfers between devices  131 us (37%)
  starting transfers between devices  118 us (34%)
  Pallas kernels  57.4 us (16%)
  local copies, waits for them, and re-layouts  12.6 us (4%)
  matrix products  10.7 us (3%)
  blocking collectives  8.06 us (2%)
  other arithmetic  7.3 us (2%)
    ppermute x48, waiting for transfers between devices, ahead(): lax.ppermute(x, BOTH, self.pairs(lambda g, k: self.slot(g + chain_by, k +...  104 us
    ppermute x48, starting transfers between devices, ahead(): lax.ppermute(x, BOTH, self.pairs(lambda g, k: self.slot(g + chain_by, k +...  70.7 us
    pallas_call x18, Pallas kernels, call(): pl.pallas_call(kernel, out_shape=out_shape, scratch_shapes=scratch_shapes...  57.4 us
    ppermute x6, starting transfers between devices, fetch(): lax.ppermute(x, BOTH, self.pairs(lambda g, k: self.home(g + site_by, k +...  23.3 us
    ppermute x5, starting transfers between devices, send_home(): lax.ppermute(x, BOTH, self.pairs(self.slot, lambda g, k: self.home(g + si...  12 us
    ppermute x4, waiting for transfers between devices, from_sector(): lax.ppermute(x, BOTH, self.pairs(lambda g, k: self.slot(g, source(k)), se...  11.7 us
    dot_general x12, matrix products, local(): jnp.einsum('xy,vxz->vyz', left_isos[step][s], gathered[s][piece], preferr...  9.81 us
    unnamed x72, local copies, waits for them, and re-layouts  9.23 us
  transfers between devices with their start and end apart: 71, of which 35 were waited for; matrix products, arithmetic and copies ran while one was open for 6% of the time, Pallas kernels for 11%

profile of v2, /device:TPU:0, one launch (start us, length us, event | category | flops | bytes accessed | tf_op | source)
XLA Modules:
  0.0 346.6 jit_solution(11559074584086106848)
XLA Ops:
  0.6 5.0 %collective-permute-start = (bf16[4,128,128]{2,1,0:T(8,128)(2,1)}, bf16[4,128,128]{2,1,0:T(8,128)(2,1)S(1)}, u32[]{:S(2)}, u32[]{:S(2)}) collective-permute-start(bf16[4,128,128]{2,1,0:T(8,128)(2,1)} %bitcast.193), channel_id=1, source_target_pairs={{8,0},{9,8},{10,1},{11,9},{12,3},{13,11},{14,2},{15,10},{16,4},{17... | collective-permute-start | bytes 393224 | tf_op jit(solution)/shard_map/ppermute | solution.py:51
  5.7 4.4 %collective-permute-start.8 = (bf16[4,128,128]{2,1,0:T(8,128)(2,1)}, bf16[4,128,128]{2,1,0:T(8,128)(2,1)S(1)}, u32[]{:S(2)}, u32[]{:S(2)}) collective-permute-start(bf16[4,128,128]{2,1,0:T(8,128)(2,1)} %bitcast.196), channel_id=1, source_target_pairs={{24,0},{25,8},{26,1},{27,9},{28,3},{29,11},{30,2},{31,10},{0,4},{1... | collective-permute-start | bytes 393224 | tf_op jit(solution)/shard_map/ppermute | solution.py:51
  13.3 11.9 %collective-permute-start.2 = (bf16[42,128,128]{2,1,0:T(8,128)(2,1)}, bf16[42,128,128]{2,1,0:T(8,128)(2,1)}, u32[]{:S(2)}, u32[]{:S(2)}) collective-permute-start(bf16[42,128,128]{2,1,0:T(8,128)(2,1)} %bitcast.208), channel_id=1, source_target_pairs={{0,0},{1,8},{2,1},{3,9},{4,3},{5,11},{6,2},{7,10},{8,4},{9,12},{10... | collective-permute-start | bytes 4128776 | tf_op jit(solution)/shard_map/ppermute | solution.py:51
  27.8 8.1 %all-gather = bf16[8,168,168]{2,1,0:T(8,128)(2,1)S(1)} all-gather(bf16[2,168,168]{2,1,0:T(8,128)(2,1)S(1)} %pad_maximum_fusion.2), channel_id=2, replica_groups=mesh['site'=4,'sec'=8] {'site'}, dimensions={0}, use_global_device_ids=true | all-gather | bytes 564480 | tf_op jit(solution)/shard_map/all_gather | solution.py:726
  42.3 1.6 collective-permute-done.14
  44.7 2.0 collective-permute-done.15
  46.7 21.9 %collective-permute-start.9 = (bf16[8,128,128]{2,1,0:T(8,128)(2,1)S(1)}, bf16[8,128,128]{2,1,0:T(8,128)(2,1)S(1)}, u32[]{:S(2)}, u32[]{:S(2)}) collective-permute-start(bf16[8,128,128]{2,1,0:T(8,128)(2,1)S(1)} %constant_dynamic-update-slice_fusion), channel_id=1, source_target_pairs={{8,0},{1,8},{9,1},{3,9},{11,3},{2,11},{10,2},{0,10},{12,4},{5,12},... | collective-permute-start | bytes 786440 | tf_op jit(solution)/shard_map/ppermute | solution.py:61
  69.5 2.1 collective-permute-start.17
  72.5 2.2 collective-permute-start.4
  74.7 2.8 collective-permute-done.10
  78.6 2.2 collective-permute-start.11
  80.8 5.3 %collective-permute-done.5 = bf16[8,128,128]{2,1,0:T(8,128)(2,1)S(1)} collective-permute-done((bf16[8,128,128]{2,1,0:T(8,128)(2,1)S(1)}, bf16[8,128,128]{2,1,0:T(8,128)(2,1)S(1)}, u32[]{:S(2)}, u32[]{:S(2)}) %collective-permute-start.5) | collective-permute-done | bytes 262176 | tf_op jit(solution)/shard_map/ppermute | solution.py:61
  86.2 1.8 collective-permute-start.6
  88.1 6.7 %collective-permute-done.12 = bf16[8,128,128]{2,1,0:T(8,128)(2,1)S(1)} collective-permute-done((bf16[8,128,128]{2,1,0:T(8,128)(2,1)S(1)}, bf16[8,128,128]{2,1,0:T(8,128)(2,1)S(1)}, u32[]{:S(2)}, u32[]{:S(2)}) %collective-permute-start.12) | collective-permute-done | bytes 262176 | tf_op jit(solution)/shard_map/ppermute | solution.py:61
  94.9 1.7 collective-permute-done.18.refs_5_
  97.1 3.5 %collective-permute-done.7 = bf16[8,128,128]{2,1,0:T(8,128)(2,1)S(1)} collective-permute-done((bf16[8,128,128]{2,1,0:T(8,128)(2,1)S(1)}, bf16[8,128,128]{2,1,0:T(8,128)(2,1)S(1)}, u32[]{:S(2)}, u32[]{:S(2)}) %collective-permute-start.7) | collective-permute-done | bytes 262176 | tf_op jit(solution)/shard_map/ppermute | solution.py:61
  104.0 5.1 %shard_map.145 = (bf16[21,128,128]{2,1,0:T(8,128)(2,1)S(1)}, bf16[21,128,128]{2,1,0:T(8,128)(2,1)S(1)}, bf16[21,128,128]{2,1,0:T(8,128)(2,1)S(1)}, bf16[21,128,1...) custom-call(bf16[21,128,128]{2,1,0:T(8,128)(2,1)S(1)} %get-tuple-ele, ...), custom_call_target="tpu_custom_call" | custom-call | flops 2334130176 | bytes 3076096 | tf_op jit(solution)/shard_map/pallas_call | solution.py:506
  109.1 3.0 collective-permute-done.33.refs_2_
  112.1 1.9 collective-permute-start.35
  114.0 5.5 %collective-permute-done.34.refs_3_ = bf16[21,128,128]{2,1,0:T(8,128)(2,1)S(1)} collective-permute-done((bf16[21,128,128]{2,1,0:T(8,128)(2,1)S(1)}, bf16[21,128,128]{2,1,0:T(8,128)(2,1)S(1)}, u32[]{:S(2)}, u32[]{:S(2)}) %collective-permute-start.34) | collective-permute-done | bytes 688160 | tf_op jit(solution)/shard_map/ppermute | solution.py:61
  119.5 1.9 collective-permute-start.36
  123.8 3.1 collective-permute-done.35.refs_4_
  126.9 2.2 collective-permute-start.37
  129.1 5.2 %collective-permute-done.36.refs_5_ = bf16[21,128,128]{2,1,0:T(8,128)(2,1)S(1)} collective-permute-done((bf16[21,128,128]{2,1,0:T(8,128)(2,1)S(1)}, bf16[21,128,128]{2,1,0:T(8,128)(2,1)S(1)}, u32[]{:S(2)}, u32[]{:S(2)}) %collective-permute-start.36) | collective-permute-done | bytes 688160 | tf_op jit(solution)/shard_map/ppermute | solution.py:61
  134.2 2.2 collective-permute-start.38
  136.9 2.7 collective-permute-done.21
  141.6 7.4 %collective-permute-done.38.refs_7_ = bf16[21,128,128]{2,1,0:T(8,128)(2,1)S(1)} collective-permute-done((bf16[21,128,128]{2,1,0:T(8,128)(2,1)S(1)}, bf16[21,128,128]{2,1,0:T(8,128)(2,1)S(1)}, u32[]{:S(2)}, u32[]{:S(2)}) %collective-permute-start.38) | collective-permute-done | bytes 688160 | tf_op jit(solution)/shard_map/ppermute | solution.py:61
  149.0 6.3 %shard_map.152 = (bf16[21,128,128]{2,1,0:T(8,128)(2,1)S(1)}, bf16[21,128,128]{2,1,0:T(8,128)(2,1)S(1)}, f32[8,128]{1,0:T(8,128)S(1)}) custom-call(bf16[21,128,128]{2,1,0:T(8,128)(2,1)S(1)} %get-tuple-element.115.refs_0_, bf16[21,128,128]{2,1,0:T(8,128)(2,1)S(1)} %get-tuple-element.114.refs_1_, bf16[21,128,128]{2,1,0:T(8,128)(2,1)S(1)} %collective-permute-done.33.refs_2_, ...), custom_call_target="tpu_custom_call" | custom-call | flops 2334130176 | bytes 7335936 | tf_op jit(solution)/shard_map/pallas_call | solution.py:506
  155.3 2.2 collective-permute-start.39
  160.0 6.0 %collective-permute-done.39.refs_2_ = bf16[21,128,128]{2,1,0:T(8,128)(2,1)S(1)} collective-permute-done((bf16[21,128,128]{2,1,0:T(8,128)(2,1)S(1)}, bf16[21,128,128]{2,1,0:T(8,128)(2,1)S(1)}, u32[]{:S(2)}, u32[]{:S(2)}) %collective-permute-start.39) | collective-permute-done | bytes 688160 | tf_op jit(solution)/shard_map/ppermute | solution.py:61
  166.0 2.2 collective-permute-start.41
  168.2 5.2 %collective-permute-done.40.refs_3_ = bf16[21,128,128]{2,1,0:T(8,128)(2,1)S(1)} collective-permute-done((bf16[21,128,128]{2,1,0:T(8,128)(2,1)S(1)}, bf16[21,128,128]{2,1,0:T(8,128)(2,1)S(1)}, u32[]{:S(2)}, u32[]{:S(2)}) %collective-permute-start.40) | collective-permute-done | bytes 688160 | tf_op jit(solution)/shard_map/ppermute | solution.py:61
  173.4 1.9 collective-permute-start.42
  176.2 5.2 %shard_map.148 = (bf16[21,128,128]{2,1,0:T(8,128)(2,1)S(1)}, bf16[21,128,128]{2,1,0:T(8,128)(2,1)S(1)}, bf16[21,128,128]{2,1,0:T(8,128)(2,1)S(1)}, bf16[21,128,1...) custom-call(bf16[21,128,128]{2,1,0:T(8,128)(2,1)S(1)} %get-tuple-ele, ...), custom_call_target="tpu_custom_call" | custom-call | flops 2334130176 | bytes 3076096 | tf_op jit(solution)/shard_map/pallas_call | solution.py:506
  182.6 5.5 %collective-permute-done.42.refs_5_ = bf16[21,128,128]{2,1,0:T(8,128)(2,1)S(1)} collective-permute-done((bf16[21,128,128]{2,1,0:T(8,128)(2,1)S(1)}, bf16[21,128,128]{2,1,0:T(8,128)(2,1)S(1)}, u32[]{:S(2)}, u32[]{:S(2)}) %collective-permute-start.42) | collective-permute-done | bytes 688160 | tf_op jit(solution)/shard_map/ppermute | solution.py:61
  188.1 1.9 collective-permute-start.44
  192.5 3.0 collective-permute-done.43.refs_6_
  195.5 7.4 %collective-permute-done.44.refs_7_ = bf16[21,128,128]{2,1,0:T(8,128)(2,1)S(1)} collective-permute-done((bf16[21,128,128]{2,1,0:T(8,128)(2,1)S(1)}, bf16[21,128,128]{2,1,0:T(8,128)(2,1)S(1)}, u32[]{:S(2)}, u32[]{:S(2)}) %collective-permute-start.44) | collective-permute-done | bytes 688160 | tf_op jit(solution)/shard_map/ppermute | solution.py:61
  202.9 7.3 %shard_map.153 = (bf16[21,128,128]{2,1,0:T(8,128)(2,1)}, bf16[21,128,128]{2,1,0:T(8,128)(2,1)}, f32[8,128]{1,0:T(8,128)S(1)}) custom-call(bf16[21,128,128]{2,1,0:T(8,128)(2,1)S(1)} %get-tuple-element.88.refs_0_, bf16[21,128,128]{2,1,0:T(8,128)(2,1)S(1)} %get-tuple-element.89.refs_1_, bf16[21,128,128]{2,1,0:T(8,128)(2,1)S(1)} %collective-permute-done.39.refs_2_, ...), custom_call_target="tpu_custom_call" | custom-call | flops 2334130176 | bytes 7335936 | tf_op jit(solution)/shard_map/pallas_call | solution.py:506
  210.2 3.3 collective-permute-start.50
  213.9 5.5 %collective-permute-start.31 = (bf16[21,128,128]{2,1,0:T(8,128)(2,1)S(1)}, bf16[21,128,128]{2,1,0:T(8,128)(2,1)}, u32[]{:S(2)}, u32[]{:S(2)}) collective-permute-start(bf16[21,128,128]{2,1,0:T(8,128)(2,1)S(1)} %fusion.8), channel_id=1, source_target_pairs={{10,0},{0,8},{8,1},{1,9},{9,3},{3,11},{11,2},{2,10},{14,4},{4,12},... | collective-permute-start | bytes 2064392 | tf_op jit(solution)/shard_map/ppermute | solution.py:61
  219.3 1.9 collective-permute-start.47
  222.5 4.9 %collective-permute-start.28 = (bf16[21,128,128]{2,1,0:T(8,128)(2,1)}, bf16[21,128,128]{2,1,0:T(8,128)(2,1)}, u32[]{:S(2)}, u32[]{:S(2)}) collective-permute-start(bf16[21,128,128]{2,1,0:T(8,128)(2,1)} %fusion.10), channel_id=1, source_target_pairs={{10,0},{0,8},{8,1},{1,9},{9,3},{3,11},{11,2},{2,10},{14,4},{4,12},... | collective-permute-start | bytes 2064392 | tf_op jit(solution)/shard_map/ppermute | solution.py:61
  227.6 8.1 %collective-permute-done.31 = bf16[21,128,128]{2,1,0:T(8,128)(2,1)} collective-permute-done((bf16[21,128,128]{2,1,0:T(8,128)(2,1)S(1)}, bf16[21,128,128]{2,1,0:T(8,128)(2,1)}, u32[]{:S(2)}, u32[]{:S(2)}) %collective-permute-start.31) | collective-permute-done | bytes 688160 | tf_op jit(solution)/shard_map/ppermute | solution.py:61
  235.7 4.6 %collective-permute-done.47 = bf16[21,128,128]{2,1,0:T(8,128)(2,1)} collective-permute-done((bf16[21,128,128]{2,1,0:T(8,128)(2,1)}, bf16[21,128,128]{2,1,0:T(8,128)(2,1)}, u32[]{:S(2)}, u32[]{:S(2)}) %collective-permute-start.47) | collective-permute-done | bytes 688160 | tf_op jit(solution)/shard_map/ppermute | solution.py:66
  240.3 2.6 fusion.9
  242.9 7.6 %collective-permute-done.28 = bf16[21,128,128]{2,1,0:T(8,128)(2,1)} collective-permute-done((bf16[21,128,128]{2,1,0:T(8,128)(2,1)}, bf16[21,128,128]{2,1,0:T(8,128)(2,1)}, u32[]{:S(2)}, u32[]{:S(2)}) %collective-permute-start.28) | collective-permute-done | bytes 688160 | tf_op jit(solution)/shard_map/ppermute | solution.py:61
  250.5 2.6 fusion.11
  255.5 2.8 collective-permute-done.45.refs_2_.refs_16_
  258.3 7.1 %collective-permute-done.48.refs_6_.refs_20_ = bf16[21,128,128]{2,1,0:T(8,128)(2,1)S(1)} collective-permute-done((bf16[21,128,128]{2,1,0:T(8,128)(2,1)}, bf16[21,128,128]{2,1,0:T(8,128)(2,1)S(1)}, u32[]{:S(2)}, u32[]{:S(2)}) %collective-permute-start.48) | collective-permute-done | bytes 688160 | tf_op jit(solution)/shard_map/ppermute | solution.py:66
  270.2 1.6 shard_map.150
  271.8 3.1 collective-permute-done.29.moved_ref
  276.5 5.2 %shard_map.151 = (bf16[21504,128]{1,0:T(8,128)(2,1)S(1)}, f32[4,128,128]{2,1,0:T(8,128)S(1)}) custom-call(bf16[21,128,128]{2,1,0:T(8,128)(2,1)S(1)} %get-tuple-element.74.refs_0_, bf16[21,128,128]{2,1,0:T(8,128)(2,1)S(1)} %get-tuple-element.79.refs_1_, bf16[1360,384]{1,0:T(8,128)(2,1)S(1)} %copy-done.25, f32[4,128,128]{2,1,0:T(8,128)S(1)} %copy-done.23, ...), custom_call_target="tpu_custom_call" | custom-call | flops 2334130176 | bytes 3207168 | tf_op jit(solution)/shard_map/pallas_call | solution.py:506
  281.8 3.7 %shard_map.154 = (f32[4,128,128]{2,1,0:T(8,128)S(1)}, bf16[4,128,128]{2,1,0:T(8,128)(2,1)S(1)}, f32[1,128]{1,0:T(1,128)S(1)}) custom-call(bf16[21,128,128]{2,1,0:T(8,128)(2,1)} %get-tuple-element.91.refs_0_.refs_14_, bf16[21,128,128]{2,1,0:T(8,128)(2,1)} %get-tuple-element.92.refs_1_.refs_15_, ...), custom_call_target="tpu_custom_call" | custom-call | flops 704643072 | bytes 11292672 | tf_op jit(solution)/shard_map/pallas_call | solution.py:506
  289.3 2.0 collective-permute-start.56
  292.4 3.9 %collective-permute-done.59 = f32[4,128]{1,0:T(4,128)S(1)} collective-permute-done((f32[4,128]{1,0:T(4,128)S(1)}, f32[4,128]{1,0:T(4,128)S(1)}, u32[]{:S(2)}, u32[]{:S(2)}) %collective-permute-start.59) | collective-permute-done | bytes 2080 | tf_op jit(solution)/shard_map/ppermute | solution.py:82
  302.5 10.0 %shard_map.155 = (f32[4,128,128]{2,1,0:T(8,128)S(1)}, bf16[4,128,128]{2,1,0:T(8,128)(2,1)}, f32[1,128]{1,0:T(1,128)S(1)}, f32[4,128,128]{2,1,0:T(8,128)S(1)}) custom-call(bf16[21,128,128]{2,1,0:T(8,128)(2,1)S(1)} %copy-done.7, bf16[21,128,128]{2,1,0:T(8,128)(2,1)S(1)} %copy-done.5, bf16[1360,384]{1,0:T(8,128)(2,1)S(1)} %copy-done.26, ...), custom_call_target="tpu_custom_call" | custom-call | flops 3038773248 | bytes 9523200 | tf_op jit(solution)/shard_map/pallas_call | solution.py:506
  318.9 3.0 collective-permute-done.62
  323.5 2.4 collective-permute-done.63.table_ref
  325.9 4.8 %shard_map.156 = bf16[4,128,128]{2,1,0:T(8,128)(2,1)S(1)} custom-call(f32[4,2,128,128]{3,2,1,0:T(8,128)S(1)} %pad_maximum_fusion.both_ref, f32[8,128]{1,0:T(8,128)S(1)} %maximum_select_fusion.1.table_ref, bf16[128,128]{1,0:T(8,128)(2,1)S(1)} %get-tuple-element.134.centre_ref), custom_call_target="tpu_custom_call" | custom-call | flops 1258291200 | bytes 561152 | tf_op jit(solution)/shard_map/pallas_call | solution.py:506
  331.9 7.0 %collective-permute-start.68 = (bf16[128,128]{1,0:T(8,128)(2,1)S(1)}, bf16[128,128]{1,0:T(8,128)(2,1)S(1)}, u32[]{:S(2)}, u32[]{:S(2)}) collective-permute-start(bf16[128,128]{1,0:T(8,128)(2,1)S(1)} %get-tuple-element.138), channel_id=1, source_target_pairs={{0,23},{8,16},{1,17},{9,18},{3,19},{11,20},{2,21},{10,22},{4,31},{... | collective-permute-start | bytes 98312 | tf_op jit(solution)/shard_map/ppermute | solution.py:56
  338.9 2.4 collective-permute-start.69
  342.0 1.6 collective-permute-done.69
  343.7 2.2 collective-permute-done.70
  (218 shorter events, 63.7 us)
Async XLA Ops:
  0.6 41.4 %collective-permute-start = (bf16[4,128,128]{2,1,0:T(8,128)(2,1)}, bf16[4,128,128]{2,1,0:T(8,128)(2,1)S(1)}, u32[]{:S(2)}, u32[]{:S(2)}) collective-permute-start(bf16[4,128,128]{2,1,0:T(8,128)(2,1)} %bitcast.193), channel_id=1, source_target_pairs={{8,0},{9,8},{10,1},{11,9},{12,3},{13,11},{14,2},{15,10},{16,4},{17... | collective-permute-start | bytes 393224 | tf_op jit(solution)/shard_map/ppermute | solution.py:51
  5.7 36.4 %collective-permute-start.8 = (bf16[4,128,128]{2,1,0:T(8,128)(2,1)}, bf16[4,128,128]{2,1,0:T(8,128)(2,1)S(1)}, u32[]{:S(2)}, u32[]{:S(2)}) collective-permute-start(bf16[4,128,128]{2,1,0:T(8,128)(2,1)} %bitcast.196), channel_id=1, source_target_pairs={{24,0},{25,8},{26,1},{27,9},{28,3},{29,11},{30,2},{31,10},{0,4},{1... | collective-permute-start | bytes 393224 | tf_op jit(solution)/shard_map/ppermute | solution.py:51
  11.1 58.4 %collective-permute-start.1 = (bf16[8,128,128]{2,1,0:T(8,128)(2,1)S(1)}, bf16[8,128,128]{2,1,0:T(8,128)(2,1)S(1)}, u32[]{:S(2)}, u32[]{:S(2)}) collective-permute-start(bf16[8,128,128]{2,1,0:T(8,128)(2,1)S(1)} %pad_maximum_fusion.1), channel_id=1, source_target_pairs={{0,0},{1,8},{2,1},{3,9},{4,3},{5,11},{6,2},{7,10},{8,4},{9,12},{10... | collective-permute-start | bytes 786440 | tf_op jit(solution)/shard_map/ppermute | solution.py:51
  12.7 29.4 %collective-permute-start.13 = (bf16[5,128,128]{2,1,0:T(8,128)(2,1)S(1)}, bf16[5,128,128]{2,1,0:T(8,128)(2,1)S(1)}, u32[]{:S(2)}, u32[]{:S(2)}) collective-permute-start(bf16[5,128,128]{2,1,0:T(8,128)(2,1)S(1)} %pad_maximum_fusion.3), channel_id=1, source_target_pairs={{16,0},{17,8},{18,1},{19,9},{20,3},{21,11},{22,2},{23,10},{24,4},{... | collective-permute-start | bytes 491528 | tf_op jit(solution)/shard_map/ppermute | solution.py:51
  13.3 88.7 %collective-permute-start.2 = (bf16[42,128,128]{2,1,0:T(8,128)(2,1)}, bf16[42,128,128]{2,1,0:T(8,128)(2,1)}, u32[]{:S(2)}, u32[]{:S(2)}) collective-permute-start(bf16[42,128,128]{2,1,0:T(8,128)(2,1)} %bitcast.208), channel_id=1, source_target_pairs={{0,0},{1,8},{2,1},{3,9},{4,3},{5,11},{6,2},{7,10},{8,4},{9,12},{10... | collective-permute-start | bytes 4128776 | tf_op jit(solution)/shard_map/ppermute | solution.py:51
  42.2 4.5 %collective-permute-start.15 = (bf16[128,128]{1,0:T(8,128)(2,1)S(1)}, bf16[128,128]{1,0:T(8,128)(2,1)S(1)}, u32[]{:S(2)}, u32[]{:S(2)}) collective-permute-start(bf16[128,128]{1,0:T(8,128)(2,1)S(1)} %get-tuple-element.134.centre_ref), channel_id=1, source_target_pairs={{1,0},{9,8},{3,1},{11,9},{2,3},{10,11},{0,2},{8,10},{5,4},{13,12},... | collective-permute-start | bytes 98312 | tf_op jit(solution)/shard_map/ppermute | solution.py:61
  42.3 26.4 %collective-permute-start.16 = (bf16[128,128]{1,0:T(8,128)(2,1)S(1)}, bf16[128,128]{1,0:T(8,128)(2,1)S(1)}, u32[]{:S(2)}, u32[]{:S(2)}) collective-permute-start(bf16[128,128]{1,0:T(8,128)(2,1)S(1)} %get-tuple-element.134.centre_ref), channel_id=1, source_target_pairs={{9,0},{3,8},{11,1},{2,9},{10,3},{0,11},{8,2},{1,10},{13,4},{7,12},... | collective-permute-start | bytes 98312 | tf_op jit(solution)/shard_map/ppermute | solution.py:61
  44.0 58.1 %collective-permute-start.3 = (bf16[42,128,128]{2,1,0:T(8,128)(2,1)S(1)}, bf16[42,128,128]{2,1,0:T(8,128)(2,1)S(1)}, u32[]{:S(2)}, u32[]{:S(2)}) collective-permute-start(bf16[42,128,128]{2,1,0:T(8,128)(2,1)S(1)} %bitcast.209), channel_id=1, source_target_pairs={{0,0},{1,8},{2,1},{3,9},{4,3},{5,11},{6,2},{7,10},{8,4},{9,12},{10... | collective-permute-start | bytes 4128776 | tf_op jit(solution)/shard_map/ppermute | solution.py:51
  46.7 25.8 %collective-permute-start.9 = (bf16[8,128,128]{2,1,0:T(8,128)(2,1)S(1)}, bf16[8,128,128]{2,1,0:T(8,128)(2,1)S(1)}, u32[]{:S(2)}, u32[]{:S(2)}) collective-permute-start(bf16[8,128,128]{2,1,0:T(8,128)(2,1)S(1)} %constant_dynamic-update-slice_fusion), channel_id=1, source_target_pairs={{8,0},{1,8},{9,1},{3,9},{11,3},{2,11},{10,2},{0,10},{12,4},{5,12},... | collective-permute-start | bytes 786440 | tf_op jit(solution)/shard_map/ppermute | solution.py:61
  68.6 8.9 %collective-permute-start.10 = (bf16[8,128,128]{2,1,0:T(8,128)(2,1)S(1)}, bf16[8,128,128]{2,1,0:T(8,128)(2,1)S(1)}, u32[]{:S(2)}, u32[]{:S(2)}) collective-permute-start(bf16[8,128,128]{2,1,0:T(8,128)(2,1)S(1)} %constant_dynamic-update-slice_fusion), channel_id=1, source_target_pairs={{10,0},{0,8},{8,1},{1,9},{9,3},{3,11},{11,2},{2,10},{14,4},{4,12},... | collective-permute-start | bytes 786440 | tf_op jit(solution)/shard_map/ppermute | solution.py:61
  69.5 18.5 %collective-permute-start.17 = (bf16[4,128,128]{2,1,0:T(8,128)(2,1)S(1)}, bf16[4,128,128]{2,1,0:T(8,128)(2,1)S(1)}, u32[]{:S(2)}, u32[]{:S(2)}) collective-permute-start(bf16[4,128,128]{2,1,0:T(8,128)(2,1)S(1)} %get-tuple-element.139), channel_id=1, source_target_pairs={{8,0},{1,8},{9,1},{3,9},{11,3},{2,11},{10,2},{0,10},{12,4},{5,12},... | collective-permute-start | bytes 393224 | tf_op jit(solution)/shard_map/ppermute | solution.py:61
  72.5 6.1 %collective-permute-start.4 = (bf16[8,128,128]{2,1,0:T(8,128)(2,1)S(1)}, bf16[8,128,128]{2,1,0:T(8,128)(2,1)S(1)}, u32[]{:S(2)}, u32[]{:S(2)}) collective-permute-start(bf16[8,128,128]{2,1,0:T(8,128)(2,1)S(1)} %collective-permute-done.1), channel_id=1, source_target_pairs={{8,0},{1,8},{9,1},{3,9},{11,3},{2,11},{10,2},{0,10},{12,4},{5,12},... | collective-permute-start | bytes 786440 | tf_op jit(solution)/shard_map/ppermute | solution.py:61
  77.5 8.7 %collective-permute-start.5 = (bf16[8,128,128]{2,1,0:T(8,128)(2,1)S(1)}, bf16[8,128,128]{2,1,0:T(8,128)(2,1)S(1)}, u32[]{:S(2)}, u32[]{:S(2)}) collective-permute-start(bf16[8,128,128]{2,1,0:T(8,128)(2,1)S(1)} %collective-permute-done.1), channel_id=1, source_target_pairs={{10,0},{0,8},{8,1},{1,9},{9,3},{3,11},{11,2},{2,10},{14,4},{4,12},... | collective-permute-start | bytes 786440 | tf_op jit(solution)/shard_map/ppermute | solution.py:61
  78.6 7.6 %collective-permute-start.11 = (bf16[8,128,128]{2,1,0:T(8,128)(2,1)S(1)}, bf16[8,128,128]{2,1,0:T(8,128)(2,1)S(1)}, u32[]{:S(2)}, u32[]{:S(2)}) collective-permute-start(bf16[8,128,128]{2,1,0:T(8,128)(2,1)S(1)} %collective-permute-done.9), channel_id=1, source_target_pairs={{8,0},{1,8},{9,1},{3,9},{11,3},{2,11},{10,2},{0,10},{12,4},{5,12},... | collective-permute-start | bytes 786440 | tf_op jit(solution)/shard_map/ppermute | solution.py:61
  86.2 8.7 %collective-permute-start.12 = (bf16[8,128,128]{2,1,0:T(8,128)(2,1)S(1)}, bf16[8,128,128]{2,1,0:T(8,128)(2,1)S(1)}, u32[]{:S(2)}, u32[]{:S(2)}) collective-permute-start(bf16[8,128,128]{2,1,0:T(8,128)(2,1)S(1)} %collective-permute-done.10), channel_id=1, source_target_pairs={{10,0},{0,8},{8,1},{1,9},{9,3},{3,11},{11,2},{2,10},{14,4},{4,12},... | collective-permute-start | bytes 786440 | tf_op jit(solution)/shard_map/ppermute | solution.py:61
  86.2 10.5 %collective-permute-start.6 = (bf16[8,128,128]{2,1,0:T(8,128)(2,1)S(1)}, bf16[8,128,128]{2,1,0:T(8,128)(2,1)S(1)}, u32[]{:S(2)}, u32[]{:S(2)}) collective-permute-start(bf16[8,128,128]{2,1,0:T(8,128)(2,1)S(1)} %collective-permute-done.4), channel_id=1, source_target_pairs={{8,0},{1,8},{9,1},{3,9},{11,3},{2,11},{10,2},{0,10},{12,4},{5,12},... | collective-permute-start | bytes 786440 | tf_op jit(solution)/shard_map/ppermute | solution.py:61
  88.1 8.5 %collective-permute-start.18 = (bf16[4,128,128]{2,1,0:T(8,128)(2,1)S(1)}, bf16[4,128,128]{2,1,0:T(8,128)(2,1)S(1)}, u32[]{:S(2)}, u32[]{:S(2)}) collective-permute-start(bf16[4,128,128]{2,1,0:T(8,128)(2,1)S(1)} %get-tuple-element.139), channel_id=1, source_target_pairs={{10,0},{0,8},{8,1},{1,9},{9,3},{3,11},{11,2},{2,10},{14,4},{4,12},... | collective-permute-start | bytes 393224 | tf_op jit(solution)/shard_map/ppermute | solution.py:61
  94.8 5.8 %collective-permute-start.7 = (bf16[8,128,128]{2,1,0:T(8,128)(2,1)S(1)}, bf16[8,128,128]{2,1,0:T(8,128)(2,1)S(1)}, u32[]{:S(2)}, u32[]{:S(2)}) collective-permute-start(bf16[8,128,128]{2,1,0:T(8,128)(2,1)S(1)} %collective-permute-done.5), channel_id=1, source_target_pairs={{10,0},{0,8},{8,1},{1,9},{9,3},{3,11},{11,2},{2,10},{14,4},{4,12},... | collective-permute-start | bytes 786440 | tf_op jit(solution)/shard_map/ppermute | solution.py:61
  96.7 5.3 %collective-permute-start.20 = (bf16[4,128,128]{2,1,0:T(8,128)(2,1)S(1)}, bf16[4,128,128]{2,1,0:T(8,128)(2,1)S(1)}, u32[]{:S(2)}, u32[]{:S(2)}) collective-permute-start(bf16[4,128,128]{2,1,0:T(8,128)(2,1)S(1)} %collective-permute-done.18.refs_5_), channel_id=1, source_target_pairs={{10,0},{0,8},{8,1},{1,9},{9,3},{3,11},{11,2},{2,10},{14,4},{4,12},... | collective-permute-start | bytes 393224 | tf_op jit(solution)/shard_map/ppermute | solution.py:61
  103.6 8.5 %collective-permute-start.33 = (bf16[21,128,128]{2,1,0:T(8,128)(2,1)S(1)}, bf16[21,128,128]{2,1,0:T(8,128)(2,1)S(1)}, u32[]{:S(2)}, u32[]{:S(2)}) collective-permute-start(bf16[21,128,128]{2,1,0:T(8,128)(2,1)S(1)} %get-tuple-element.115.refs_0_), channel_id=1, source_target_pairs={{8,0},{1,8},{9,1},{3,9},{11,3},{2,11},{10,2},{0,10},{12,4},{5,12},... | collective-permute-start | bytes 2064392 | tf_op jit(solution)/shard_map/ppermute | solution.py:61
  103.7 15.8 %collective-permute-start.34 = (bf16[21,128,128]{2,1,0:T(8,128)(2,1)S(1)}, bf16[21,128,128]{2,1,0:T(8,128)(2,1)S(1)}, u32[]{:S(2)}, u32[]{:S(2)}) collective-permute-start(bf16[21,128,128]{2,1,0:T(8,128)(2,1)S(1)} %get-tuple-element.114.refs_1_), channel_id=1, source_target_pairs={{8,0},{1,8},{9,1},{3,9},{11,3},{2,11},{10,2},{0,10},{12,4},{5,12},... | collective-permute-start | bytes 2064392 | tf_op jit(solution)/shard_map/ppermute | solution.py:61
  112.1 14.7 %collective-permute-start.35 = (bf16[21,128,128]{2,1,0:T(8,128)(2,1)S(1)}, bf16[21,128,128]{2,1,0:T(8,128)(2,1)S(1)}, u32[]{:S(2)}, u32[]{:S(2)}) collective-permute-start(bf16[21,128,128]{2,1,0:T(8,128)(2,1)S(1)} %collective-permute-done.33.refs_2_), channel_id=1, source_target_pairs={{8,0},{1,8},{9,1},{3,9},{11,3},{2,11},{10,2},{0,10},{12,4},{5,12},... | collective-permute-start | bytes 2064392 | tf_op jit(solution)/shard_map/ppermute | solution.py:61
  119.5 14.7 %collective-permute-start.36 = (bf16[21,128,128]{2,1,0:T(8,128)(2,1)S(1)}, bf16[21,128,128]{2,1,0:T(8,128)(2,1)S(1)}, u32[]{:S(2)}, u32[]{:S(2)}) collective-permute-start(bf16[21,128,128]{2,1,0:T(8,128)(2,1)S(1)} %collective-permute-done.34.refs_3_), channel_id=1, source_target_pairs={{8,0},{1,8},{9,1},{3,9},{11,3},{2,11},{10,2},{0,10},{12,4},{5,12},... | collective-permute-start | bytes 2064392 | tf_op jit(solution)/shard_map/ppermute | solution.py:61
  121.8 14.7 %collective-permute-start.24 = (bf16[21,128,128]{2,1,0:T(8,128)(2,1)S(1)}, bf16[21,128,128]{2,1,0:T(8,128)(2,1)S(1)}, u32[]{:S(2)}, u32[]{:S(2)}) collective-permute-start(bf16[21,128,128]{2,1,0:T(8,128)(2,1)S(1)} %fusion.17), channel_id=1, source_target_pairs={{10,0},{0,8},{8,1},{1,9},{9,3},{3,11},{11,2},{2,10},{14,4},{4,12},... | collective-permute-start | bytes 2064392 | tf_op jit(solution)/shard_map/ppermute | solution.py:61
  122.2 17.3 %collective-permute-start.21 = (bf16[21,128,128]{2,1,0:T(8,128)(2,1)S(1)}, bf16[21,128,128]{2,1,0:T(8,128)(2,1)S(1)}, u32[]{:S(2)}, u32[]{:S(2)}) collective-permute-start(bf16[21,128,128]{2,1,0:T(8,128)(2,1)S(1)} %fusion.16), channel_id=1, source_target_pairs={{10,0},{0,8},{8,1},{1,9},{9,3},{3,11},{11,2},{2,10},{14,4},{4,12},... | collective-permute-start | bytes 2064392 | tf_op jit(solution)/shard_map/ppermute | solution.py:61
  126.9 14.7 %collective-permute-start.37 = (bf16[21,128,128]{2,1,0:T(8,128)(2,1)S(1)}, bf16[21,128,128]{2,1,0:T(8,128)(2,1)S(1)}, u32[]{:S(2)}, u32[]{:S(2)}) collective-permute-start(bf16[21,128,128]{2,1,0:T(8,128)(2,1)S(1)} %collective-permute-done.35.refs_4_), channel_id=1, source_target_pairs={{8,0},{1,8},{9,1},{3,9},{11,3},{2,11},{10,2},{0,10},{12,4},{5,12},... | collective-permute-start | bytes 2064392 | tf_op jit(solution)/shard_map/ppermute | solution.py:61
  134.2 14.7 %collective-permute-start.38 = (bf16[21,128,128]{2,1,0:T(8,128)(2,1)S(1)}, bf16[21,128,128]{2,1,0:T(8,128)(2,1)S(1)}, u32[]{:S(2)}, u32[]{:S(2)}) collective-permute-start(bf16[21,128,128]{2,1,0:T(8,128)(2,1)S(1)} %collective-permute-done.36.refs_5_), channel_id=1, source_target_pairs={{8,0},{1,8},{9,1},{3,9},{11,3},{2,11},{10,2},{0,10},{12,4},{5,12},... | collective-permute-start | bytes 2064392 | tf_op jit(solution)/shard_map/ppermute | solution.py:61
  136.8 20.8 %collective-permute-start.25 = (bf16[21,128,128]{2,1,0:T(8,128)(2,1)S(1)}, bf16[21,128,128]{2,1,0:T(8,128)(2,1)S(1)}, u32[]{:S(2)}, u32[]{:S(2)}) collective-permute-start(bf16[21,128,128]{2,1,0:T(8,128)(2,1)S(1)} %fusion.12), channel_id=1, source_target_pairs={{10,0},{0,8},{8,1},{1,9},{9,3},{3,11},{11,2},{2,10},{14,4},{4,12},... | collective-permute-start | bytes 2064392 | tf_op jit(solution)/shard_map/ppermute | solution.py:61
  140.0 18.5 %collective-permute-start.22 = (bf16[21,128,128]{2,1,0:T(8,128)(2,1)S(1)}, bf16[21,128,128]{2,1,0:T(8,128)(2,1)S(1)}, u32[]{:S(2)}, u32[]{:S(2)}) collective-permute-start(bf16[21,128,128]{2,1,0:T(8,128)(2,1)S(1)} %fusion.14), channel_id=1, source_target_pairs={{10,0},{0,8},{8,1},{1,9},{9,3},{3,11},{11,2},{2,10},{14,4},{4,12},... | collective-permute-start | bytes 2064392 | tf_op jit(solution)/shard_map/ppermute | solution.py:61
  155.3 10.7 %collective-permute-start.39 = (bf16[21,128,128]{2,1,0:T(8,128)(2,1)S(1)}, bf16[21,128,128]{2,1,0:T(8,128)(2,1)S(1)}, u32[]{:S(2)}, u32[]{:S(2)}) collective-permute-start(bf16[21,128,128]{2,1,0:T(8,128)(2,1)S(1)} %get-tuple-element.88.refs_0_), channel_id=1, source_target_pairs={{8,0},{1,8},{9,1},{3,9},{11,3},{2,11},{10,2},{0,10},{12,4},{5,12},... | collective-permute-start | bytes 2064392 | tf_op jit(solution)/shard_map/ppermute | solution.py:61
  157.5 15.8 %collective-permute-start.40 = (bf16[21,128,128]{2,1,0:T(8,128)(2,1)S(1)}, bf16[21,128,128]{2,1,0:T(8,128)(2,1)S(1)}, u32[]{:S(2)}, u32[]{:S(2)}) collective-permute-start(bf16[21,128,128]{2,1,0:T(8,128)(2,1)S(1)} %get-tuple-element.89.refs_1_), channel_id=1, source_target_pairs={{8,0},{1,8},{9,1},{3,9},{11,3},{2,11},{10,2},{0,10},{12,4},{5,12},... | collective-permute-start | bytes 2064392 | tf_op jit(solution)/shard_map/ppermute | solution.py:61
  158.0 17.4 %collective-permute-start.26 = (bf16[21,128,128]{2,1,0:T(8,128)(2,1)S(1)}, bf16[21,128,128]{2,1,0:T(8,128)(2,1)S(1)}, u32[]{:S(2)}, u32[]{:S(2)}) collective-permute-start(bf16[21,128,128]{2,1,0:T(8,128)(2,1)S(1)} %fusion.13), channel_id=1, source_target_pairs={{10,0},{0,8},{8,1},{1,9},{9,3},{3,11},{11,2},{2,10},{14,4},{4,12},... | collective-permute-start | bytes 2064392 | tf_op jit(solution)/shard_map/ppermute | solution.py:61
  158.9 16.9 %collective-permute-start.23 = (bf16[21,128,128]{2,1,0:T(8,128)(2,1)S(1)}, bf16[21,128,128]{2,1,0:T(8,128)(2,1)S(1)}, u32[]{:S(2)}, u32[]{:S(2)}) collective-permute-start(bf16[21,128,128]{2,1,0:T(8,128)(2,1)S(1)} %fusion.15), channel_id=1, source_target_pairs={{10,0},{0,8},{8,1},{1,9},{9,3},{3,11},{11,2},{2,10},{14,4},{4,12},... | collective-permute-start | bytes 2064392 | tf_op jit(solution)/shard_map/ppermute | solution.py:61
  166.0 15.5 %collective-permute-start.41 = (bf16[21,128,128]{2,1,0:T(8,128)(2,1)S(1)}, bf16[21,128,128]{2,1,0:T(8,128)(2,1)S(1)}, u32[]{:S(2)}, u32[]{:S(2)}) collective-permute-start(bf16[21,128,128]{2,1,0:T(8,128)(2,1)S(1)} %collective-permute-done.39.refs_2_), channel_id=1, source_target_pairs={{8,0},{1,8},{9,1},{3,9},{11,3},{2,11},{10,2},{0,10},{12,4},{5,12},... | collective-permute-start | bytes 2064392 | tf_op jit(solution)/shard_map/ppermute | solution.py:61
  173.4 14.7 %collective-permute-start.42 = (bf16[21,128,128]{2,1,0:T(8,128)(2,1)S(1)}, bf16[21,128,128]{2,1,0:T(8,128)(2,1)S(1)}, u32[]{:S(2)}, u32[]{:S(2)}) collective-permute-start(bf16[21,128,128]{2,1,0:T(8,128)(2,1)S(1)} %collective-permute-done.40.refs_3_), channel_id=1, source_target_pairs={{8,0},{1,8},{9,1},{3,9},{11,3},{2,11},{10,2},{0,10},{12,4},{5,12},... | collective-permute-start | bytes 2064392 | tf_op jit(solution)/shard_map/ppermute | solution.py:61
  181.5 14.0 %collective-permute-start.43 = (bf16[21,128,128]{2,1,0:T(8,128)(2,1)S(1)}, bf16[21,128,128]{2,1,0:T(8,128)(2,1)S(1)}, u32[]{:S(2)}, u32[]{:S(2)}) collective-permute-start(bf16[21,128,128]{2,1,0:T(8,128)(2,1)S(1)} %collective-permute-done.41.refs_4_), channel_id=1, source_target_pairs={{8,0},{1,8},{9,1},{3,9},{11,3},{2,11},{10,2},{0,10},{12,4},{5,12},... | collective-permute-start | bytes 2064392 | tf_op jit(solution)/shard_map/ppermute | solution.py:61
  188.1 14.7 %collective-permute-start.44 = (bf16[21,128,128]{2,1,0:T(8,128)(2,1)S(1)}, bf16[21,128,128]{2,1,0:T(8,128)(2,1)S(1)}, u32[]{:S(2)}, u32[]{:S(2)}) collective-permute-start(bf16[21,128,128]{2,1,0:T(8,128)(2,1)S(1)} %collective-permute-done.42.refs_5_), channel_id=1, source_target_pairs={{8,0},{1,8},{9,1},{3,9},{11,3},{2,11},{10,2},{0,10},{12,4},{5,12},... | collective-permute-start | bytes 2064392 | tf_op jit(solution)/shard_map/ppermute | solution.py:61
  190.4 23.0 %collective-permute-start.30 = (bf16[21,128,128]{2,1,0:T(8,128)(2,1)S(1)}, bf16[21,128,128]{2,1,0:T(8,128)(2,1)S(1)}, u32[]{:S(2)}, u32[]{:S(2)}) collective-permute-start(bf16[21,128,128]{2,1,0:T(8,128)(2,1)S(1)} %fusion.19), channel_id=1, source_target_pairs={{10,0},{0,8},{8,1},{1,9},{9,3},{3,11},{11,2},{2,10},{14,4},{4,12},... | collective-permute-start | bytes 2064392 | tf_op jit(solution)/shard_map/ppermute | solution.py:61
  190.9 30.4 %collective-permute-start.27 = (bf16[21,128,128]{2,1,0:T(8,128)(2,1)S(1)}, bf16[21,128,128]{2,1,0:T(8,128)(2,1)S(1)}, u32[]{:S(2)}, u32[]{:S(2)}) collective-permute-start(bf16[21,128,128]{2,1,0:T(8,128)(2,1)S(1)} %fusion.18), channel_id=1, source_target_pairs={{10,0},{0,8},{8,1},{1,9},{9,3},{3,11},{11,2},{2,10},{14,4},{4,12},... | collective-permute-start | bytes 2064392 | tf_op jit(solution)/shard_map/ppermute | solution.py:61
  210.2 17.4 %collective-permute-start.50 = (bf16[21,128,128]{2,1,0:T(8,128)(2,1)}, bf16[21,128,128]{2,1,0:T(8,128)(2,1)}, u32[]{:S(2)}, u32[]{:S(2)}) collective-permute-start(bf16[21,128,128]{2,1,0:T(8,128)(2,1)} %get-tuple-element.92.refs_1_.refs_15_), channel_id=1, source_target_pairs={{2,0},{8,8},{0,1},{9,9},{1,3},{11,11},{3,2},{10,10},{6,4},{12,12},... | collective-permute-start | bytes 2064392 | tf_op jit(solution)/shard_map/ppermute | solution.py:66
  213.9 21.9 %collective-permute-start.31 = (bf16[21,128,128]{2,1,0:T(8,128)(2,1)S(1)}, bf16[21,128,128]{2,1,0:T(8,128)(2,1)}, u32[]{:S(2)}, u32[]{:S(2)}) collective-permute-start(bf16[21,128,128]{2,1,0:T(8,128)(2,1)S(1)} %fusion.8), channel_id=1, source_target_pairs={{10,0},{0,8},{8,1},{1,9},{9,3},{3,11},{11,2},{2,10},{14,4},{4,12},... | collective-permute-start | bytes 2064392 | tf_op jit(solution)/shard_map/ppermute | solution.py:61
  219.3 21.0 %collective-permute-start.47 = (bf16[21,128,128]{2,1,0:T(8,128)(2,1)}, bf16[21,128,128]{2,1,0:T(8,128)(2,1)}, u32[]{:S(2)}, u32[]{:S(2)}) collective-permute-start(bf16[21,128,128]{2,1,0:T(8,128)(2,1)} %get-tuple-element.91.refs_0_.refs_14_), channel_id=1, source_target_pairs={{2,0},{8,8},{0,1},{9,9},{1,3},{11,11},{3,2},{10,10},{6,4},{12,12},... | collective-permute-start | bytes 2064392 | tf_op jit(solution)/shard_map/ppermute | solution.py:66
  222.5 28.0 %collective-permute-start.28 = (bf16[21,128,128]{2,1,0:T(8,128)(2,1)}, bf16[21,128,128]{2,1,0:T(8,128)(2,1)}, u32[]{:S(2)}, u32[]{:S(2)}) collective-permute-start(bf16[21,128,128]{2,1,0:T(8,128)(2,1)} %fusion.10), channel_id=1, source_target_pairs={{10,0},{0,8},{8,1},{1,9},{9,3},{3,11},{11,2},{2,10},{14,4},{4,12},... | collective-permute-start | bytes 2064392 | tf_op jit(solution)/shard_map/ppermute | solution.py:61
  227.4 25.7 %collective-permute-start.46 = (bf16[21,128,128]{2,1,0:T(8,128)(2,1)}, bf16[21,128,128]{2,1,0:T(8,128)(2,1)S(1)}, u32[]{:S(2)}, u32[]{:S(2)}) collective-permute-start(bf16[21,128,128]{2,1,0:T(8,128)(2,1)} %get-tuple-element.92.refs_1_.refs_15_), channel_id=1, source_target_pairs={{8,0},{1,8},{9,1},{3,9},{11,3},{2,11},{10,2},{0,10},{12,4},{5,12},... | collective-permute-start | bytes 2064392 | tf_op jit(solution)/shard_map/ppermute | solution.py:61
  227.6 26.9 %collective-permute-start.51 = (bf16[21,128,128]{2,1,0:T(8,128)(2,1)}, bf16[21,128,128]{2,1,0:T(8,128)(2,1)S(1)}, u32[]{:S(2)}, u32[]{:S(2)}) collective-permute-start(bf16[21,128,128]{2,1,0:T(8,128)(2,1)} %collective-permute-done.50), channel_id=1, source_target_pairs={{9,0},{2,8},{11,1},{0,9},{10,3},{1,11},{8,2},{3,10},{13,4},{6,12},... | collective-permute-start | bytes 2064392 | tf_op jit(solution)/shard_map/ppermute | solution.py:66
  235.7 22.6 %collective-permute-start.45 = (bf16[21,128,128]{2,1,0:T(8,128)(2,1)}, bf16[21,128,128]{2,1,0:T(8,128)(2,1)S(1)}, u32[]{:S(2)}, u32[]{:S(2)}) collective-permute-start(bf16[21,128,128]{2,1,0:T(8,128)(2,1)} %get-tuple-element.91.refs_0_.refs_14_), channel_id=1, source_target_pairs={{8,0},{1,8},{9,1},{3,9},{11,3},{2,11},{10,2},{0,10},{12,4},{5,12},... | collective-permute-start | bytes 2064392 | tf_op jit(solution)/shard_map/ppermute | solution.py:61
  240.3 25.0 %collective-permute-start.48 = (bf16[21,128,128]{2,1,0:T(8,128)(2,1)}, bf16[21,128,128]{2,1,0:T(8,128)(2,1)S(1)}, u32[]{:S(2)}, u32[]{:S(2)}) collective-permute-start(bf16[21,128,128]{2,1,0:T(8,128)(2,1)} %collective-permute-done.47), channel_id=1, source_target_pairs={{9,0},{2,8},{11,1},{0,9},{10,3},{1,11},{8,2},{3,10},{13,4},{6,12},... | collective-permute-start | bytes 2064392 | tf_op jit(solution)/shard_map/ppermute | solution.py:66
  250.5 18.6 %collective-permute-start.32 = (bf16[21,128,128]{2,1,0:T(8,128)(2,1)}, bf16[21,128,128]{2,1,0:T(8,128)(2,1)}, u32[]{:S(2)}, u32[]{:S(2)}) collective-permute-start(bf16[21,128,128]{2,1,0:T(8,128)(2,1)} %fusion.9), channel_id=1, source_target_pairs={{10,0},{0,8},{8,1},{1,9},{9,3},{3,11},{11,2},{2,10},{14,4},{4,12},... | collective-permute-start | bytes 2064392 | tf_op jit(solution)/shard_map/ppermute | solution.py:61
  253.0 21.9 %collective-permute-start.29 = (bf16[21,128,128]{2,1,0:T(8,128)(2,1)}, bf16[21,128,128]{2,1,0:T(8,128)(2,1)}, u32[]{:S(2)}, u32[]{:S(2)}) collective-permute-start(bf16[21,128,128]{2,1,0:T(8,128)(2,1)} %fusion.11), channel_id=1, source_target_pairs={{10,0},{0,8},{8,1},{1,9},{9,3},{3,11},{11,2},{2,10},{14,4},{4,12},... | collective-permute-start | bytes 2064392 | tf_op jit(solution)/shard_map/ppermute | solution.py:61
  255.5 26.2 %collective-permute-start.52 = (bf16[21,128,128]{2,1,0:T(8,128)(2,1)}, bf16[21,128,128]{2,1,0:T(8,128)(2,1)}, u32[]{:S(2)}, u32[]{:S(2)}) collective-permute-start(bf16[21,128,128]{2,1,0:T(8,128)(2,1)} %broadcast_select_fusion), channel_id=1, source_target_pairs={{8,0},{0,8},{9,1},{1,9},{11,3},{3,11},{10,2},{2,10},{12,4},{4,12},... | collective-permute-start | bytes 2064392 | tf_op jit(solution)/shard_map/ppermute | solution.py:82
  266.3 15.5 %collective-permute-start.49 = (bf16[21,128,128]{2,1,0:T(8,128)(2,1)}, bf16[21,128,128]{2,1,0:T(8,128)(2,1)}, u32[]{:S(2)}, u32[]{:S(2)}) collective-permute-start(bf16[21,128,128]{2,1,0:T(8,128)(2,1)} %broadcast_select_fusion.1), channel_id=1, source_target_pairs={{8,0},{0,8},{9,1},{1,9},{11,3},{3,11},{10,2},{2,10},{12,4},{4,12},... | collective-permute-start | bytes 2064392 | tf_op jit(solution)/shard_map/ppermute | solution.py:82
  288.7 7.6 %collective-permute-start.53 = (bf16[4,128,128]{2,1,0:T(8,128)(2,1)}, bf16[4,128,128]{2,1,0:T(8,128)(2,1)}, u32[]{:S(2)}, u32[]{:S(2)}) collective-permute-start(bf16[4,128,128]{2,1,0:T(8,128)(2,1)} %copy-done.20), channel_id=1, source_target_pairs={{8,0},{1,8},{9,1},{3,9},{11,3},{2,11},{10,2},{0,10},{12,4},{5,12},... | collective-permute-start | bytes 393224 | tf_op jit(solution)/shard_map/ppermute | solution.py:61
  288.7 7.6 %collective-permute-start.54 = (bf16[4,128,128]{2,1,0:T(8,128)(2,1)}, bf16[4,128,128]{2,1,0:T(8,128)(2,1)}, u32[]{:S(2)}, u32[]{:S(2)}) collective-permute-start(bf16[4,128,128]{2,1,0:T(8,128)(2,1)} %copy-done.20), channel_id=1, source_target_pairs={{10,0},{0,8},{8,1},{1,9},{9,3},{3,11},{11,2},{2,10},{14,4},{4,12},... | collective-permute-start | bytes 393224 | tf_op jit(solution)/shard_map/ppermute | solution.py:61
  289.3 7.1 %collective-permute-start.55 = (bf16[4,128,128]{2,1,0:T(8,128)(2,1)}, bf16[4,128,128]{2,1,0:T(8,128)(2,1)}, u32[]{:S(2)}, u32[]{:S(2)}) collective-permute-start(bf16[4,128,128]{2,1,0:T(8,128)(2,1)} %copy-done.20), channel_id=1, source_target_pairs={{1,0},{9,8},{3,1},{11,9},{2,3},{10,11},{0,2},{8,10},{5,4},{13,12},... | collective-permute-start | bytes 393224 | tf_op jit(solution)/shard_map/ppermute | solution.py:61
  289.3 7.1 %collective-permute-start.56 = (bf16[4,128,128]{2,1,0:T(8,128)(2,1)}, bf16[4,128,128]{2,1,0:T(8,128)(2,1)}, u32[]{:S(2)}, u32[]{:S(2)}) collective-permute-start(bf16[4,128,128]{2,1,0:T(8,128)(2,1)} %copy-done.20), channel_id=1, source_target_pairs={{2,0},{10,8},{0,1},{8,9},{1,3},{9,11},{3,2},{11,10},{6,4},{14,12},... | collective-permute-start | bytes 393224 | tf_op jit(solution)/shard_map/ppermute | solution.py:61
  291.3 5.0 %collective-permute-start.59 = (f32[4,128]{1,0:T(4,128)S(1)}, f32[4,128]{1,0:T(4,128)S(1)}, u32[]{:S(2)}, u32[]{:S(2)}) collective-permute-start(f32[4,128]{1,0:T(4,128)S(1)} %maximum_select_fusion.2), channel_id=1, source_target_pairs={{3,0},{11,8},{2,1},{10,9},{0,3},{8,11},{1,2},{9,10},{7,4},{15,12},... | collective-permute-start | bytes 6152 | tf_op jit(solution)/shard_map/ppermute | solution.py:82
  315.3 8.1 %collective-permute-start.64 = (f32[2,128,128]{2,1,0:T(8,128)S(1)}, f32[2,128,128]{2,1,0:T(8,128)S(1)}, u32[]{:S(2)}, u32[]{:S(2)}) collective-permute-start(f32[2,128,128]{2,1,0:T(8,128)S(1)} %get-tuple-element.128), channel_id=1, source_target_pairs={{10,0},{0,8},{8,1},{1,9},{9,3},{3,11},{11,2},{2,10},{14,4},{4,12},... | collective-permute-start | bytes 393224 | tf_op jit(solution)/shard_map/ppermute | solution.py:61
  315.3 8.1 %collective-permute-start.65 = (f32[2,128,128]{2,1,0:T(8,128)S(1)}, f32[2,128,128]{2,1,0:T(8,128)S(1)}, u32[]{:S(2)}, u32[]{:S(2)}) collective-permute-start(f32[2,128,128]{2,1,0:T(8,128)S(1)} %get-tuple-element.130), channel_id=1, source_target_pairs={{2,0},{10,8},{0,1},{8,9},{1,3},{9,11},{3,2},{11,10},{6,4},{14,12},... | collective-permute-start | bytes 393224 | tf_op jit(solution)/shard_map/ppermute | solution.py:61
  315.9 7.5 %collective-permute-start.66 = (f32[2,128,128]{2,1,0:T(8,128)S(1)}, f32[2,128,128]{2,1,0:T(8,128)S(1)}, u32[]{:S(2)}, u32[]{:S(2)}) collective-permute-start(f32[2,128,128]{2,1,0:T(8,128)S(1)} %get-tuple-element.129), channel_id=1, source_target_pairs={{11,0},{2,8},{10,1},{0,9},{8,3},{1,11},{9,2},{3,10},{15,4},{6,12},... | collective-permute-start | bytes 393224 | tf_op jit(solution)/shard_map/ppermute | solution.py:61
  317.4 4.5 %collective-permute-start.62 = (f32[4,128]{1,0:T(4,128)S(1)}, f32[4,128]{1,0:T(4,128)S(1)}, u32[]{:S(2)}, u32[]{:S(2)}) collective-permute-start(f32[4,128]{1,0:T(4,128)S(1)} %maximum_select_fusion.3), channel_id=1, source_target_pairs={{3,0},{11,8},{2,1},{10,9},{0,3},{8,11},{1,2},{9,10},{7,4},{15,12},... | collective-permute-start | bytes 6152 | tf_op jit(solution)/shard_map/ppermute | solution.py:82
  330.7 11.3 %collective-permute-start.67 = (bf16[128,128]{1,0:T(8,128)(2,1)S(1)}, bf16[128,128]{1,0:T(8,128)(2,1)S(1)}, u32[]{:S(2)}, u32[]{:S(2)}) collective-permute-start(bf16[128,128]{1,0:T(8,128)(2,1)S(1)} %get-tuple-element.135), channel_id=1, source_target_pairs={{0,16},{8,17},{1,18},{9,19},{3,20},{11,21},{2,22},{10,23},{4,24},{... | collective-permute-start | bytes 98312 | tf_op jit(solution)/shard_map/ppermute | solution.py:56
  331.9 10.2 %collective-permute-start.68 = (bf16[128,128]{1,0:T(8,128)(2,1)S(1)}, bf16[128,128]{1,0:T(8,128)(2,1)S(1)}, u32[]{:S(2)}, u32[]{:S(2)}) collective-permute-start(bf16[128,128]{1,0:T(8,128)(2,1)S(1)} %get-tuple-element.138), channel_id=1, source_target_pairs={{0,23},{8,16},{1,17},{9,18},{3,19},{11,20},{2,21},{10,22},{4,31},{... | collective-permute-start | bytes 98312 | tf_op jit(solution)/shard_map/ppermute | solution.py:56
  338.9 4.8 %collective-permute-start.69 = (bf16[128,128]{1,0:T(8,128)(2,1)S(1)}, bf16[128,128]{1,0:T(8,128)(2,1)S(1)}, u32[]{:S(2)}, u32[]{:S(2)}) collective-permute-start(bf16[128,128]{1,0:T(8,128)(2,1)S(1)} %get-tuple-element.137), channel_id=1, source_target_pairs={{0,22},{8,23},{1,16},{9,17},{3,18},{11,19},{2,20},{10,21},{4,30},{... | collective-permute-start | bytes 98312 | tf_op jit(solution)/shard_map/ppermute | solution.py:56
  341.3 4.6 %collective-permute-start.70 = (bf16[128,128]{1,0:T(8,128)(2,1)S(1)}, bf16[128,128]{1,0:T(8,128)(2,1)S(1)}, u32[]{:S(2)}, u32[]{:S(2)}) collective-permute-start(bf16[128,128]{1,0:T(8,128)(2,1)S(1)} %get-tuple-element.136), channel_id=1, source_target_pairs={{0,21},{8,22},{1,23},{9,16},{3,17},{11,18},{2,19},{10,20},{4,29},{... | collective-permute-start | bytes 98312 | tf_op jit(solution)/shard_map/ppermute | solution.py:56
  (38 other events, 275.8 us)

commit v3 on v1

--- a/solution.py
+++ b/solution.py
@@ -360,68 +360,38 @@
     return jnp.sum(jnp.sum(x, axis=0, keepdims=True), axis=1, keepdims=True)
 
 
-def operator_front_kernel(groups, states, pieces, renew, entry_count, *refs):
+def operator_front_kernel(groups, states, pieces, *refs):
     env, refs = refs[:pieces], refs[pieces:]
-    others = CLASSES - 1
-    weight_ref, vector_ref, rolled = refs[0], refs[1], refs[2 : 2 + others]
-    rest = refs[2 + others :]
-    if renew:
-        image_ref, moved, table_ref = rest[0], rest[1 : 1 + others], rest[1 + others]
-        rest = rest[2 + others :]
-        scale, energy, factor, _, _ = quotient(table_ref[...], entry_count)
-    gathered_ref, new_ref, tensor_ref, mixed_ref = rest
+    weight_ref, classes, refs = refs[0], refs[1 : 1 + CLASSES], refs[1 + CLASSES :]
+    gathered_ref, mixed_ref = refs
     channels, block = count_channels(env), env[0].shape[1]
-    for t in range(states):
-        vector = vector_ref[t]
-        if renew:
-            vector = updated(vector, image_ref[t], scale, energy, factor)
-        new_ref[t] = vector
-        tensor_ref[0, t] = vector.astype(jnp.bfloat16)
-        for cls in range(1, CLASSES):
-            vector = rolled[cls - 1][t]
-            if renew:
-                image = moved[cls - 1][t].astype(jnp.float32)
-                vector = updated(vector.astype(jnp.float32), image, scale, energy, factor)
-            tensor_ref[cls, t] = vector.astype(jnp.bfloat16)
     write = into(gathered_ref, channels, block)
 
     def body(offset, height):
-        tensors = [[tensor_ref[cls, t] for t in range(states)] for cls in range(CLASSES)]
+        tensors = [[classes[cls][t] for t in range(states)] for cls in range(CLASSES)]
         mix_left(env, tensors, mixed_ref, offset, height)
         mix_channels(groups, channels, weight_ref, mixed_ref, write, offset, height)
 
     by_parts(block, body)
 
 
-def operator_back_kernel(states, pieces, *refs):
-    rights = [refs[t * pieces : (t + 1) * pieces] for t in range(states)]
-    refs = refs[states * pieces :]
-    squares, refs = refs[: 2 * ENV_STEPS + 1], refs[2 * ENV_STEPS + 1 :]
-    gathered_ref, vector_ref, image_ref, half_ref, sums_ref = refs
+def products(rights, gathered_ref, s):
     channels, block = count_channels(rights[0]), rights[0][0].shape[1]
-    a = jnp.zeros((1, 1), jnp.float32)
-    b = jnp.zeros((1, 1), jnp.float32)
-    for s in range(states):
-        total = jnp.zeros((block, block), jnp.float32)
-        for batch in batches(list(range(channels)), 6):
-            left = jnp.concatenate(
-                [
-                    gathered_ref[pl.ds((s * channels + channel) * block, block), :]
-                    for channel in batch
-                ],
-                axis=1,
-            )
-            right = jnp.concatenate([channel_of(rights[s], channel) for channel in batch], axis=0)
-            total = total + jnp.dot(left, right, preferred_element_type=jnp.float32)
-        image_ref[s] = total
-        half_ref[s] = total.astype(jnp.bfloat16)
-        vector = vector_ref[s]
-        a = a + sum_all(vector * total)
-        b = b + sum_all(vector * vector)
+    total = jnp.zeros((block, block), jnp.float32)
+    for batch in batches(list(range(channels)), 6):
+        left = jnp.concatenate(
+            [gathered_ref[pl.ds((s * channels + channel) * block, block), :] for channel in batch],
+            axis=1,
+        )
+        right = jnp.concatenate([channel_of(rights[s], channel) for channel in batch], axis=0)
+        total = total + jnp.dot(left, right, preferred_element_type=jnp.float32)
+    return total
+
+
+def write_sums(vector, image, squares, sums_ref):
+    a, b = sum_all(vector * image), sum_all(vector * vector)
     e = jnp.where(b > 0, a / jnp.where(b > 0, b, 1.0), 0.0)
-    residual = image_ref[...].reshape(states * block, block) - e * vector_ref[...].reshape(
-        states * block, block
-    )
+    residual = image - e * vector
     unit = jnp.max(jnp.max(jnp.abs(residual), axis=0, keepdims=True), axis=1, keepdims=True)
     unit = jnp.where(unit > 0, unit, 1.0)
     residual = residual / unit
@@ -433,16 +403,67 @@
     sums_ref[...] = sums
 
 
-def operator_whole_kernel(groups, states, pieces, entry_count, counts, *refs):
-    front, refs = refs[: counts[0]], refs[counts[0] :]
-    back, refs = refs[: counts[1]], refs[counts[1] :]
-    image_ref, half_ref, sums_ref, new_ref, gathered_ref, tensor_ref, mixed_ref = refs
-    operator_front_kernel(
-        groups, states, pieces, True, entry_count, *front, gathered_ref, new_ref, tensor_ref, mixed_ref
-    )
-    operator_back_kernel(
-        states, pieces, *back, gathered_ref, new_ref, image_ref, half_ref, sums_ref
-    )
+def flat(ref):
+    states, block, _ = ref.shape
+    return ref[...].reshape(states * block, block)
+
+
+UNIT_ROWS = 16
+
+
+def power_above(x):
+    top = jnp.max(jnp.max(jnp.abs(x), axis=0, keepdims=True), axis=1, keepdims=True)
+    steps = jnp.ceil(jnp.log(jnp.where(top > 0, top, 1.0)) * (1 / np.log(2)))
+    return jnp.exp(steps * np.log(2)).astype(jnp.bfloat16).astype(jnp.float32)
+
+
+def operator_back_kernel(states, pieces, *refs):
+    rights = [refs[t * pieces : (t + 1) * pieces] for t in range(states)]
+    refs = refs[states * pieces :]
+    squares, refs = refs[: 2 * ENV_STEPS + 1], refs[2 * ENV_STEPS + 1 :]
+    gathered_ref, vector_ref, image_ref, half_ref, sums_ref = refs
+    for s in range(states):
+        image_ref[s] = products(rights, gathered_ref, s)
+    image = flat(image_ref)
+    unit = power_above(image)
+    half_ref[: image.shape[0]] = (image / unit).astype(jnp.bfloat16)
+    half_ref[image.shape[0] :] = jnp.broadcast_to(unit, (UNIT_ROWS, LANES)).astype(jnp.bfloat16)
+    write_sums(flat(vector_ref), image, squares, sums_ref)
+
+
+def operator_whole_kernel(groups, states, pieces, front_count, *refs):
+    front, refs = refs[:front_count], refs[front_count:]
+    env_and_weight, sent = front[:-CLASSES], front[-CLASSES:]
+    rights = [refs[t * pieces : (t + 1) * pieces] for t in range(states)]
+    image_ref, unit_ref, gathered_ref, tensor_ref, mixed_ref = refs[states * pieces :]
+    block = image_ref.shape[1]
+    units = [
+        x[pl.ds(states * block, UNIT_ROWS), :].astype(jnp.float32)[:1, :1] for x in sent
+    ]
+    unit = functools.reduce(jnp.maximum, units)
+    unit_ref[...] = jnp.broadcast_to(unit, unit_ref.shape)
+    for cls in range(CLASSES):
+        for t in range(states):
+            tensor = sent[cls][pl.ds(t * block, block), :].astype(jnp.float32)
+            tensor_ref[cls, t] = (tensor * (units[cls] / unit)).astype(jnp.bfloat16)
+    classes = [tensor_ref.at[cls] for cls in range(CLASSES)]
+    operator_front_kernel(groups, states, pieces, *env_and_weight, *classes, gathered_ref, mixed_ref)
+    for s in range(states):
+        image_ref[s] = products(rights, gathered_ref, s)
+
+
+def renew_kernel(entry_count, *refs):
+    table_ref, vector_ref, image_ref, second_ref, unit_ref = refs[:5]
+    squares, (both_ref, sums_ref) = refs[5:-2], refs[-2:]
+    states, block, _ = vector_ref.shape
+    scale, energy, factor, _, _ = quotient(table_ref[...], entry_count)
+    vector, image = flat(vector_ref), flat(image_ref)
+    part = factor * (scale * unit_ref[:, :1])
+    new_image = (1.0 + factor * energy) * image - part * flat(second_ref)
+    new = updated(vector, image, scale, energy, factor)
+    both_ref[:, 0] = new.reshape(states, block, block)
+    both_ref[:, 1] = new_image.reshape(states, block, block)
+    write_sums(new, new_image, squares, sums_ref)
 
 
 def energy_kernel(entry_count, table_ref, out_ref):
@@ -565,29 +586,18 @@
 
 
 def front_scratch(states, channels, block):
-    return [
-        pltpu.VMEM((CLASSES, states, block, block), jnp.bfloat16),
-        pltpu.VMEM((states * channels * block // PARTS, block), jnp.float32),
-    ]
-
-
-def back_outs(states, block):
-    return (
-        float_out(states, block, block),
-        half_out(states, block, block),
-        float_out(1, LANES),
-    )
-
-
-def operator_front(env, weight, groups, entry_count, vector, rolled):
+    return [pltpu.VMEM((states * channels * block // PARTS, block), jnp.float32)]
+
+
+def operator_front(env, weight, groups, classes):
     channels, block = count_channels(env), env[0].shape[1]
-    states, pieces = vector.shape[0], len(env)
+    states, pieces = classes[0].shape[0], len(env)
     return call(
-        functools.partial(operator_front_kernel, groups, states, pieces, False, entry_count),
-        (half_out(states * channels * block, block), float_out(states, block, block)),
+        functools.partial(operator_front_kernel, groups, states, pieces),
+        half_out(states * channels * block, block),
         front_scratch(states, channels, block),
         work(states, channels, block),
-        (*env, weight, vector, *rolled),
+        (*env, weight, *classes),
     )
 
 
@@ -596,28 +606,42 @@
     states, pieces = len(rights), len(rights[0])
     return call(
         functools.partial(operator_back_kernel, states, pieces),
-        back_outs(states, block),
+        (
+            float_out(states, block, block),
+            half_out(states * block + UNIT_ROWS, block),
+            float_out(1, LANES),
+        ),
         [],
         2 * states * channels * block**3,
         (*(chunk for right in rights for chunk in right), *squares, gathered, vector),
     )
 
 
-def operator_whole(env, weight, groups, entry_count, vector, rolled, news, rights, squares):
+def operator_whole(env, weight, groups, classes, rights):
     channels, block = count_channels(env), env[0].shape[1]
-    states, pieces = vector.shape[0], len(env)
-    front = (*env, weight, vector, *rolled, *news)
-    back = (*(chunk for right in rights for chunk in right), *squares)
-    counts = (len(front), len(back))
+    states, pieces = len(rights), len(env)
+    front = (*env, weight, *classes)
     return call(
-        functools.partial(operator_whole_kernel, groups, states, pieces, entry_count, counts),
-        (*back_outs(states, block), float_out(states, block, block)),
+        functools.partial(operator_whole_kernel, groups, states, pieces, len(front)),
+        (float_out(states, block, block), float_out(1, LANES)),
         [
             pltpu.VMEM((states * channels * block, block), jnp.bfloat16),
+            pltpu.VMEM((CLASSES, states, block, block), jnp.bfloat16),
             *front_scratch(states, channels, block),
         ],
         work(states, channels, block) + 2 * states * channels * block**3,
-        (*front, *back),
+        (*front, *(chunk for right in rights for chunk in right)),
+    )
+
+
+def renewed(table, vector, image, second, unit, squares, entry_count):
+    states, block, _ = vector.shape
+    return call(
+        functools.partial(renew_kernel, entry_count),
+        (float_out(states, 2, block, block), float_out(1, LANES)),
+        [],
+        0,
+        (table, vector, image, second, unit, *squares),
     )
 
 
@@ -725,10 +749,9 @@
     vector = jnp.einsum(
         "sxy,syz->sxz", own_iso, jnp.stack(centres), preferred_element_type=jnp.float32
     )
-    rolled_vector = other_classes_of(places, vector.astype(jnp.bfloat16))
-    right, (rolled[1:], rolled_vector, weights) = after(
-        right, (rolled[1:], rolled_vector, weights)
-    )
+    half_vector = vector.astype(jnp.bfloat16)
+    rolled_vector = (half_vector, *other_classes_of(places, half_vector))
+    right, (vector, weights) = after(right, (vector, weights))
     centre_float = own_centre.astype(jnp.float32)
     centre_square = jnp.sum((centre_float * centre_float).reshape(-1, ROWS, block), axis=0)
 
@@ -739,6 +762,8 @@
             if step == 0 and t == states - 1:
                 left, envs[-1] = after(left, envs[-1])
             envs.append(ahead(envs[-1], 1))
+        if step == 0:
+            (rolled, rolled_vector), envs = after((rolled, rolled_vector), envs)
         right, square = right_whole(
             envs,
             right_isos[step],
@@ -776,18 +801,14 @@
     for s in range(1, states):
         rights.append(ahead(rights[-1], 1))
     weight = weights[0][ENV_STEPS]
-    gathered, vector = operator_front(
-        left, weight, left_groups, entry_count, vector, rolled_vector
-    )
-    image, half_image, own_sums = operator_back(rights, squares, gathered, vector)
+    gathered = operator_front(left, weight, left_groups, rolled_vector)
+    image, sent, own_sums = operator_back(rights, squares, gathered, vector)
+    rolled_image = (sent, *other_classes_at_once(places, sent))
+    second, unit = operator_whole(left, weight, left_groups, rolled_image, rights)
     table = places.collect(own_sums)
-    news = (image, *other_classes_at_once(places, half_image), table)
-    image, _, own_sums, vector = operator_whole(
-        left, weight, left_groups, entry_count, vector, rolled_vector, news, rights, squares
-    )
+    both, own_sums = renewed(table, vector, image, second, unit, squares, entry_count)
     table = places.collect(own_sums)
 
-    both = jnp.stack([vector, image], axis=1)
     columns = jnp.stack([both[0]] + [places.ahead(both[s], -s) for s in range(1, states)])
     home_table = places.send_home(table, ENV_STEPS, 0)
     home_table, columns = after(home_table, columns)

time: 322 us -> 311 us (0.966)
  waiting for transfers between devices: 116 us -> 107 us
  local copies, waits for them, and re-layouts: 15.2 us -> 11.9 us
    ppermute x52, waiting for transfers between devices: 102 us -> 93.4 us  [ahead(): lax.ppermute(x, BOTH, self.pairs(lambda g, k: self.slot(g + chain_by, k +...]
    unnamed x82 -> x70, local copies, waits for them, and re-layouts: 9.16 us -> 5.82 us
    pallas_call x18 -> x19, Pallas kernels: 54.2 us -> 54 us  [call(): pl.pallas_call(kernel, out_shape=out_shape, scratch_shapes=scratch_shapes...]
where the time goes in v3:
time: 311 us; the launch traced here: 309 us
  starting transfers between devices  109 us (35%)
  waiting for transfers between devices  107 us (34%)
  Pallas kernels  54 us (17%)
  local copies, waits for them, and re-layouts  11.9 us (4%)
  matrix products  11.1 us (4%)
  blocking collectives  8.06 us (3%)
  other arithmetic  5.6 us (2%)
    ppermute x52, waiting for transfers between devices, ahead(): lax.ppermute(x, BOTH, self.pairs(lambda g, k: self.slot(g + chain_by, k +...  93.4 us
    ppermute x52, starting transfers between devices, ahead(): lax.ppermute(x, BOTH, self.pairs(lambda g, k: self.slot(g + chain_by, k +...  65.9 us
    pallas_call x19, Pallas kernels, call(): pl.pallas_call(kernel, out_shape=out_shape, scratch_shapes=scratch_shapes...  54 us
    ppermute x5, starting transfers between devices, fetch(): lax.ppermute(x, BOTH, self.pairs(lambda g, k: self.home(g + site_by, k +...  24.7 us
    dot_general x12, matrix products, local(): jnp.einsum('xy,vxz->vyz', left_isos[step][s], gathered[s][piece], preferr...  10.9 us
    ppermute x5, starting transfers between devices, send_home(): lax.ppermute(x, BOTH, self.pairs(self.slot, lambda g, k: self.home(g + si...  10.9 us
    ppermute x6, waiting for transfers between devices, partner(): lax.ppermute(x, BOTH, self.pairs(lambda g, k: self.slot(g, k ^ bit), self...  9.76 us
    all_gather x1, blocking collectives, local(): lax.all_gather(weight_matrices(mpo[0], pattern[0], secs), 'site')  8.06 us
  transfers between devices with their start and end apart: 68, of which 29 were waited for; matrix products, arithmetic and copies ran while one was open for 7% of the time, Pallas kernels for 10%

profile of v3, /device:TPU:0, one launch (start us, length us, event | category | flops | bytes accessed | tf_op | source)
XLA Modules:
  0.0 308.8 jit_solution(8783335500164557605)
XLA Ops:
  0.6 5.0 %collective-permute-start.5 = (bf16[4,128,128]{2,1,0:T(8,128)(2,1)}, bf16[4,128,128]{2,1,0:T(8,128)(2,1)S(1)}, u32[]{:S(2)}, u32[]{:S(2)}) collective-permute-start(bf16[4,128,128]{2,1,0:T(8,128)(2,1)} %bitcast.190), channel_id=1, source_target_pairs={{8,0},{9,8},{10,1},{11,9},{12,3},{13,11},{14,2},{15,10},{16,4},{17... | collective-permute-start | bytes 393224 | tf_op jit(solution)/shard_map/ppermute | solution.py:51
  5.7 4.4 %collective-permute-start.6 = (bf16[4,128,128]{2,1,0:T(8,128)(2,1)}, bf16[4,128,128]{2,1,0:T(8,128)(2,1)S(1)}, u32[]{:S(2)}, u32[]{:S(2)}) collective-permute-start(bf16[4,128,128]{2,1,0:T(8,128)(2,1)} %bitcast.193), channel_id=1, source_target_pairs={{24,0},{25,8},{26,1},{27,9},{28,3},{29,11},{30,2},{31,10},{0,4},{1... | collective-permute-start | bytes 393224 | tf_op jit(solution)/shard_map/ppermute | solution.py:51
  11.6 2.9 pad_maximum_fusion
  14.6 13.9 %collective-permute-start = (bf16[50,128,128]{2,1,0:T(8,128)(2,1)}, bf16[50,128,128]{2,1,0:T(8,128)(2,1)}, u32[]{:S(2)}, u32[]{:S(2)}) collective-permute-start(bf16[50,128,128]{2,1,0:T(8,128)(2,1)} %pad_maximum_fusion), channel_id=1, source_target_pairs={{0,0},{1,8},{2,1},{3,9},{4,3},{5,11},{6,2},{7,10},{8,4},{9,12},{10... | collective-permute-start | bytes 4915208 | tf_op jit(solution)/shard_map/ppermute | solution.py:51
  29.5 8.1 %all-gather = bf16[8,168,168]{2,1,0:T(8,128)(2,1)S(1)} all-gather(bf16[2,168,168]{2,1,0:T(8,128)(2,1)S(1)} %pad_maximum_fusion.2), channel_id=2, replica_groups=mesh['site'=4,'sec'=8] {'site'}, dimensions={0}, use_global_device_ids=true | all-gather | bytes 564480 | tf_op jit(solution)/shard_map/all_gather | solution.py:736
  45.8 1.5 collective-permute-done.14
  47.4 4.2 %collective-permute-done.13 = bf16[128,128]{1,0:T(8,128)(2,1)S(1)} collective-permute-done((bf16[128,128]{1,0:T(8,128)(2,1)S(1)}, bf16[128,128]{1,0:T(8,128)(2,1)S(1)}, u32[]{:S(2)}, u32[]{:S(2)}) %collective-permute-start.13) | collective-permute-done | bytes 32800 | tf_op jit(solution)/shard_map/ppermute | solution.py:61
  52.3 1.8 collective-permute-start.9
  54.1 1.4 fusion.32
  56.4 7.9 %collective-permute-start.19 = (bf16[21,128,128]{2,1,0:T(8,128)(2,1)S(1)}, bf16[21,128,128]{2,1,0:T(8,128)(2,1)S(1)}, u32[]{:S(2)}, u32[]{:S(2)}) collective-permute-start(bf16[21,128,128]{2,1,0:T(8,128)(2,1)S(1)} %get-tuple-element.78.refs_0_), channel_id=1, source_target_pairs={{8,0},{1,8},{9,1},{3,9},{11,3},{2,11},{10,2},{0,10},{12,4},{5,12},... | collective-permute-start | bytes 2064392 | tf_op jit(solution)/shard_map/ppermute | solution.py:61
  67.3 12.9 %collective-permute-done.19.refs_2_ = bf16[21,128,128]{2,1,0:T(8,128)(2,1)S(1)} collective-permute-done((bf16[21,128,128]{2,1,0:T(8,128)(2,1)S(1)}, bf16[21,128,128]{2,1,0:T(8,128)(2,1)S(1)}, u32[]{:S(2)}, u32[]{:S(2)}) %collective-permute-start.19) | collective-permute-done | bytes 688160 | tf_op jit(solution)/shard_map/ppermute | solution.py:61
  80.2 1.9 collective-permute-start.22
  82.1 8.3 %collective-permute-done.20.refs_3_ = bf16[21,128,128]{2,1,0:T(8,128)(2,1)S(1)} collective-permute-done((bf16[21,128,128]{2,1,0:T(8,128)(2,1)S(1)}, bf16[21,128,128]{2,1,0:T(8,128)(2,1)S(1)}, u32[]{:S(2)}, u32[]{:S(2)}) %collective-permute-start.20) | collective-permute-done | bytes 688160 | tf_op jit(solution)/shard_map/ppermute | solution.py:61
  90.4 1.9 collective-permute-start.23
  93.4 1.8 collective-permute-start.3
  95.4 3.8 %collective-permute-done.2 = bf16[8,128,128]{2,1,0:T(8,128)(2,1)S(1)} collective-permute-done((bf16[8,128,128]{2,1,0:T(8,128)(2,1)S(1)}, bf16[8,128,128]{2,1,0:T(8,128)(2,1)S(1)}, u32[]{:S(2)}, u32[]{:S(2)}) %collective-permute-start.2) | collective-permute-done | bytes 262176 | tf_op jit(solution)/shard_map/ppermute | solution.py:61
  100.6 7.4 %collective-permute-done.23.refs_5_ = bf16[21,128,128]{2,1,0:T(8,128)(2,1)S(1)} collective-permute-done((bf16[21,128,128]{2,1,0:T(8,128)(2,1)S(1)}, bf16[21,128,128]{2,1,0:T(8,128)(2,1)S(1)}, u32[]{:S(2)}, u32[]{:S(2)}) %collective-permute-start.23) | collective-permute-done | bytes 688160 | tf_op jit(solution)/shard_map/ppermute | solution.py:61
  107.9 1.9 collective-permute-start.24
  109.9 1.6 collective-permute-start.25
  112.2 2.0 collective-permute-start.17
  114.2 2.5 collective-permute-done.18.refs_7_
  116.7 11.6 %collective-permute-done.17.refs_6_ = bf16[4,128,128]{2,1,0:T(8,128)(2,1)S(1)} collective-permute-done((bf16[4,128,128]{2,1,0:T(8,128)(2,1)S(1)}, bf16[4,128,128]{2,1,0:T(8,128)(2,1)S(1)}, u32[]{:S(2)}, u32[]{:S(2)}) %collective-permute-start.17) | collective-permute-done | bytes 131104 | tf_op jit(solution)/shard_map/ppermute | solution.py:61
  128.5 5.2 %shard_map.147 = (bf16[21,128,128]{2,1,0:T(8,128)(2,1)S(1)}, bf16[21,128,128]{2,1,0:T(8,128)(2,1)S(1)}, bf16[21,128,128]{2,1,0:T(8,128)(2,1)S(1)}, bf16[21,128,1...) custom-call(bf16[21,128,128]{2,1,0:T(8,128)(2,1)S(1)} %get-tuple-ele, ...), custom_call_target="tpu_custom_call" | custom-call | flops 2334130176 | bytes 3076096 | tf_op jit(solution)/shard_map/pallas_call | solution.py:511
  137.2 6.3 %shard_map.145 = (bf16[21,128,128]{2,1,0:T(8,128)(2,1)S(1)}, bf16[21,128,128]{2,1,0:T(8,128)(2,1)S(1)}, f32[8,128]{1,0:T(8,128)S(1)}) custom-call(bf16[21,128,128]{2,1,0:T(8,128)(2,1)S(1)} %get-tuple-element.78.refs_0_, bf16[21,128,128]{2,1,0:T(8,128)(2,1)S(1)} %get-tuple-element.79.refs_1_, bf16[21,128,128]{2,1,0:T(8,128)(2,1)S(1)} %collective-permute-done.19.refs_2_, ...), custom_call_target="tpu_custom_call" | custom-call | flops 2334130176 | bytes 7335936 | tf_op jit(solution)/shard_map/pallas_call | solution.py:511
  143.6 2.0 collective-permute-start.26
  145.5 1.6 collective-permute-start.27
  149.0 3.8 %collective-permute-done.38 = bf16[21,128,128]{2,1,0:T(8,128)(2,1)S(1)} collective-permute-done((bf16[21,128,128]{2,1,0:T(8,128)(2,1)S(1)}, bf16[21,128,128]{2,1,0:T(8,128)(2,1)S(1)}, u32[]{:S(2)}, u32[]{:S(2)}) %collective-permute-start.38) | collective-permute-done | bytes 688160 | tf_op jit(solution)/shard_map/ppermute | solution.py:61
  154.0 2.2 collective-permute-start.28
  156.2 5.2 %collective-permute-done.27.refs_3_ = bf16[21,128,128]{2,1,0:T(8,128)(2,1)S(1)} collective-permute-done((bf16[21,128,128]{2,1,0:T(8,128)(2,1)S(1)}, bf16[21,128,128]{2,1,0:T(8,128)(2,1)S(1)}, u32[]{:S(2)}, u32[]{:S(2)}) %collective-permute-start.27) | collective-permute-done | bytes 688160 | tf_op jit(solution)/shard_map/ppermute | solution.py:61
  161.4 2.2 collective-permute-start.29
  164.7 2.2 collective-permute-start.43
  171.4 4.6 %collective-permute-done.29.refs_5_ = bf16[21,128,128]{2,1,0:T(8,128)(2,1)S(1)} collective-permute-done((bf16[21,128,128]{2,1,0:T(8,128)(2,1)S(1)}, bf16[21,128,128]{2,1,0:T(8,128)(2,1)S(1)}, u32[]{:S(2)}, u32[]{:S(2)}) %collective-permute-start.29) | collective-permute-done | bytes 688160 | tf_op jit(solution)/shard_map/ppermute | solution.py:61
  176.1 2.2 collective-permute-start.31
  178.7 3.8 %collective-permute-done.40.moved_ref = bf16[21,128,128]{2,1,0:T(8,128)(2,1)S(1)} collective-permute-done((bf16[21,128,128]{2,1,0:T(8,128)(2,1)S(1)}, bf16[21,128,128]{2,1,0:T(8,128)(2,1)S(1)}, u32[]{:S(2)}, u32[]{:S(2)}) %collective-permute-start.40) | collective-permute-done | bytes 688160 | tf_op jit(solution)/shard_map/ppermute | solution.py:61
  182.9 5.2 %shard_map.150 = (bf16[21,128,128]{2,1,0:T(8,128)(2,1)S(1)}, bf16[21,128,128]{2,1,0:T(8,128)(2,1)S(1)}, bf16[21,128,128]{2,1,0:T(8,128)(2,1)S(1)}, bf16[21,128,1...) custom-call(bf16[21,128,128]{2,1,0:T(8,128)(2,1)S(1)} %get-tuple-ele, ...), custom_call_target="tpu_custom_call" | custom-call | flops 2334130176 | bytes 3076096 | tf_op jit(solution)/shard_map/pallas_call | solution.py:511
  188.5 1.5 collective-permute-start.47
  190.4 2.5 collective-permute-start.44
  192.9 6.3 %shard_map.146 = (bf16[21,128,128]{2,1,0:T(8,128)(2,1)S(1)}, bf16[21,128,128]{2,1,0:T(8,128)(2,1)S(1)}, f32[8,128]{1,0:T(8,128)S(1)}) custom-call(bf16[21,128,128]{2,1,0:T(8,128)(2,1)S(1)} %get-tuple-element.88.refs_0_, bf16[21,128,128]{2,1,0:T(8,128)(2,1)S(1)} %get-tuple-element.89.refs_1_, bf16[21,128,128]{2,1,0:T(8,128)(2,1)S(1)} %collective-permute-done.26.refs_2_, ...), custom_call_target="tpu_custom_call" | custom-call | flops 2334130176 | bytes 7335936 | tf_op jit(solution)/shard_map/pallas_call | solution.py:511
  199.3 1.4 collective-permute-start.33
  202.1 4.2 %collective-permute-done.44 = bf16[21,128,128]{2,1,0:T(8,128)(2,1)S(1)} collective-permute-done((bf16[21,128,128]{2,1,0:T(8,128)(2,1)S(1)}, bf16[21,128,128]{2,1,0:T(8,128)(2,1)S(1)}, u32[]{:S(2)}, u32[]{:S(2)}) %collective-permute-start.44) | collective-permute-done | bytes 688160 | tf_op jit(solution)/shard_map/ppermute | solution.py:61
  206.7 1.5 collective-permute-start.45
  208.2 1.8 collective-permute-start.34
  210.0 5.2 %collective-permute-done.33.refs_3_.refs_11_ = bf16[21,128,128]{2,1,0:T(8,128)(2,1)S(1)} collective-permute-done((bf16[21,128,128]{2,1,0:T(8,128)(2,1)S(1)}, bf16[21,128,128]{2,1,0:T(8,128)(2,1)S(1)}, u32[]{:S(2)}, u32[]{:S(2)}) %collective-permute-start.33) | collective-permute-done | bytes 688160 | tf_op jit(solution)/shard_map/ppermute | solution.py:61
  215.2 2.2 collective-permute-start.35
  218.7 2.3 collective-permute-start.49
  222.3 1.6 collective-permute-start.46
  224.5 5.4 %collective-permute-done.35.refs_5_.refs_13_ = bf16[21,128,128]{2,1,0:T(8,128)(2,1)} collective-permute-done((bf16[21,128,128]{2,1,0:T(8,128)(2,1)S(1)}, bf16[21,128,128]{2,1,0:T(8,128)(2,1)}, u32[]{:S(2)}, u32[]{:S(2)}) %collective-permute-start.35) | collective-permute-done | bytes 688160 | tf_op jit(solution)/shard_map/ppermute | solution.py:61
  229.9 2.2 collective-permute-start.37
  234.1 2.5 collective-permute-done.46.moved_ref
  237.1 5.2 %shard_map.153.refs_13_ = bf16[21504,128]{1,0:T(8,128)(2,1)S(1)} custom-call(bf16[21,128,128]{2,1,0:T(8,128)(2,1)S(1)} %get-tuple-element.122.refs_0_, bf16[21,128,128]{2,1,0:T(8,128)(2,1)S(1)} %get-tuple-element.123.refs_1_, bf16[1360,384]{1,0:T(8,128)(2,1)S(1)} %copy-done.21, bf16[4,128,128]{2,1,0:T(8,128)(2,1)S(1)} %get-tuple-element.125.refs_3_, ...), custom_call_target="tpu_custom_call" | custom-call | flops 2334130176 | bytes 3076096 | tf_op jit(solution)/shard_map/pallas_call | solution.py:511
  242.3 2.4 collective-permute-done.37.refs_7_.refs_15_
  244.8 3.8 %shard_map.154 = (f32[4,128,128]{2,1,0:T(8,128)S(1)}, bf16[528,128]{1,0:T(8,128)(2,1)S(1)}, f32[1,128]{1,0:T(1,128)S(1)}) custom-call(bf16[21,128,128]{2,1,0:T(8,128)(2,1)S(1)} %copy-done.1, bf16[21,128,128]{2,1,0:T(8,128)(2,1)S(1)} %copy-done.3, bf16[21,128,128]{2,1,0:T(8,128)(2,1)S(1)} %copy-done.5, bf16[21,128,128]{2,1,0:T(8,128)(2,1)S(1)} %copy-done.7, ...), custom_call_target="tpu_custom_call" | custom-call | flops 704643072 | bytes 11292672 | tf_op jit(solution)/shard_map/pallas_call | solution.py:511
  248.5 4.2 %collective-permute-start.50 = (f32[1,128]{1,0:T(1,128)S(1)}, f32[1,128]{1,0:T(1,128)S(1)}, u32[]{:S(2)}, u32[]{:S(2)}) collective-permute-start(f32[1,128]{1,0:T(1,128)S(1)} %get-tuple-element.131), channel_id=1, source_target_pairs={{8,0},{0,8},{9,1},{1,9},{11,3},{3,11},{10,2},{2,10},{12,4},{4,12},... | collective-permute-start | bytes 1544 | tf_op jit(solution)/shard_map/ppermute | solution.py:66
  253.6 1.8 collective-permute-start.51
  255.6 1.8 collective-permute-start.55
  257.4 1.7 collective-permute-start.53
  259.2 4.5 %collective-permute-done.52 = f32[4,128]{1,0:T(4,128)S(1)} collective-permute-done((f32[4,128]{1,0:T(4,128)S(1)}, f32[4,128]{1,0:T(4,128)S(1)}, u32[]{:S(2)}, u32[]{:S(2)}) %collective-permute-start.52) | collective-permute-done | bytes 2080 | tf_op jit(solution)/shard_map/ppermute | solution.py:66
  267.1 8.9 %shard_map.155 = (f32[4,128,128]{2,1,0:T(8,128)S(1)}, f32[1,128]{1,0:T(1,128)S(1)}) custom-call(bf16[21,128,128]{2,1,0:T(8,128)(2,1)S(1)} %copy-done.11, bf16[21,128,128]{2,1,0:T(8,128)(2,1)S(1)} %copy-done.9, bf16[1360,384]{1,0:T(8,128)(2,1)S(1)} %copy-done.22, bf16[528,128]{1,0:T(8,128)(2,1)S(1)} %get-tuple-element.133.refs_3_, ...), custom_call_target="tpu_custom_call" | custom-call | flops 3038773248 | bytes 8601600 | tf_op jit(solution)/shard_map/pallas_call | solution.py:511
  283.2 3.1 %collective-permute-done.59 = f32[4,128]{1,0:T(4,128)S(1)} collective-permute-done((f32[4,128]{1,0:T(4,128)S(1)}, f32[4,128]{1,0:T(4,128)S(1)}, u32[]{:S(2)}, u32[]{:S(2)}) %collective-permute-start.59) | collective-permute-done | bytes 2080 | tf_op jit(solution)/shard_map/ppermute | solution.py:66
  287.3 1.5 collective-permute-done.61
  290.2 4.8 %shard_map.157 = bf16[4,128,128]{2,1,0:T(8,128)(2,1)S(1)} custom-call(f32[4,2,128,128]{3,2,1,0:T(8,128)S(1)} %pad_maximum_fusion.1.both_ref, f32[8,128]{1,0:T(8,128)S(1)} %maximum_select_fusion.1.table_ref, bf16[128,128]{1,0:T(8,128)(2,1)S(1)} %get-tuple-element.166.centre_ref), custom_call_target="tpu_custom_call" | custom-call | flops 1258291200 | bytes 561152 | tf_op jit(solution)/shard_map/pallas_call | solution.py:511
  295.8 7.3 %collective-permute-start.67 = (bf16[128,128]{1,0:T(8,128)(2,1)S(1)}, bf16[128,128]{1,0:T(8,128)(2,1)S(1)}, u32[]{:S(2)}, u32[]{:S(2)}) collective-permute-start(bf16[128,128]{1,0:T(8,128)(2,1)S(1)} %get-tuple-element.168), channel_id=1, source_target_pairs={{0,21},{8,22},{1,23},{9,16},{3,17},{11,18},{2,19},{10,20},{4,29},{... | collective-permute-start | bytes 98312 | tf_op jit(solution)/shard_map/ppermute | solution.py:56
  303.1 1.8 collective-permute-start.65
  305.6 2.4 collective-permute-done.66
  (210 shorter events, 56.2 us)
Async XLA Ops:
  0.6 43.2 %collective-permute-start.5 = (bf16[4,128,128]{2,1,0:T(8,128)(2,1)}, bf16[4,128,128]{2,1,0:T(8,128)(2,1)S(1)}, u32[]{:S(2)}, u32[]{:S(2)}) collective-permute-start(bf16[4,128,128]{2,1,0:T(8,128)(2,1)} %bitcast.190), channel_id=1, source_target_pairs={{8,0},{9,8},{10,1},{11,9},{12,3},{13,11},{14,2},{15,10},{16,4},{17... | collective-permute-start | bytes 393224 | tf_op jit(solution)/shard_map/ppermute | solution.py:51
  5.7 38.3 %collective-permute-start.6 = (bf16[4,128,128]{2,1,0:T(8,128)(2,1)}, bf16[4,128,128]{2,1,0:T(8,128)(2,1)S(1)}, u32[]{:S(2)}, u32[]{:S(2)}) collective-permute-start(bf16[4,128,128]{2,1,0:T(8,128)(2,1)} %bitcast.193), channel_id=1, source_target_pairs={{24,0},{25,8},{26,1},{27,9},{28,3},{29,11},{30,2},{31,10},{0,4},{1... | collective-permute-start | bytes 393224 | tf_op jit(solution)/shard_map/ppermute | solution.py:51
  11.0 32.9 %collective-permute-start.11 = (bf16[5,128,128]{2,1,0:T(8,128)(2,1)S(1)}, bf16[5,128,128]{2,1,0:T(8,128)(2,1)S(1)}, u32[]{:S(2)}, u32[]{:S(2)}) collective-permute-start(bf16[5,128,128]{2,1,0:T(8,128)(2,1)S(1)} %pad_maximum_fusion.3), channel_id=1, source_target_pairs={{16,0},{17,8},{18,1},{19,9},{20,3},{21,11},{22,2},{23,10},{24,4},{... | collective-permute-start | bytes 491528 | tf_op jit(solution)/shard_map/ppermute | solution.py:51
  14.6 39.5 %collective-permute-start = (bf16[50,128,128]{2,1,0:T(8,128)(2,1)}, bf16[50,128,128]{2,1,0:T(8,128)(2,1)}, u32[]{:S(2)}, u32[]{:S(2)}) collective-permute-start(bf16[50,128,128]{2,1,0:T(8,128)(2,1)} %pad_maximum_fusion), channel_id=1, source_target_pairs={{0,0},{1,8},{2,1},{3,9},{4,3},{5,11},{6,2},{7,10},{8,4},{9,12},{10... | collective-permute-start | bytes 4915208 | tf_op jit(solution)/shard_map/ppermute | solution.py:51
  44.0 7.8 %collective-permute-start.8 = (bf16[8,128,128]{2,1,0:T(8,128)(2,1)S(1)}, bf16[8,128,128]{2,1,0:T(8,128)(2,1)S(1)}, u32[]{:S(2)}, u32[]{:S(2)}) collective-permute-start(bf16[8,128,128]{2,1,0:T(8,128)(2,1)S(1)} %constant_dynamic-update-slice_fusion), channel_id=1, source_target_pairs={{10,0},{0,8},{8,1},{1,9},{9,3},{3,11},{11,2},{2,10},{14,4},{4,12},... | collective-permute-start | bytes 786440 | tf_op jit(solution)/shard_map/ppermute | solution.py:61
  44.4 7.9 %collective-permute-start.7 = (bf16[8,128,128]{2,1,0:T(8,128)(2,1)S(1)}, bf16[8,128,128]{2,1,0:T(8,128)(2,1)S(1)}, u32[]{:S(2)}, u32[]{:S(2)}) collective-permute-start(bf16[8,128,128]{2,1,0:T(8,128)(2,1)S(1)} %constant_dynamic-update-slice_fusion), channel_id=1, source_target_pairs={{8,0},{1,8},{9,1},{3,9},{11,3},{2,11},{10,2},{0,10},{12,4},{5,12},... | collective-permute-start | bytes 786440 | tf_op jit(solution)/shard_map/ppermute | solution.py:61
  45.8 5.8 %collective-permute-start.13 = (bf16[128,128]{1,0:T(8,128)(2,1)S(1)}, bf16[128,128]{1,0:T(8,128)(2,1)S(1)}, u32[]{:S(2)}, u32[]{:S(2)}) collective-permute-start(bf16[128,128]{1,0:T(8,128)(2,1)S(1)} %get-tuple-element.166.centre_ref), channel_id=1, source_target_pairs={{1,0},{9,8},{3,1},{11,9},{2,3},{10,11},{0,2},{8,10},{5,4},{13,12},... | collective-permute-start | bytes 98312 | tf_op jit(solution)/shard_map/ppermute | solution.py:61
  47.3 4.3 %collective-permute-start.12 = (bf16[128,128]{1,0:T(8,128)(2,1)S(1)}, bf16[128,128]{1,0:T(8,128)(2,1)S(1)}, u32[]{:S(2)}, u32[]{:S(2)}) collective-permute-start(bf16[128,128]{1,0:T(8,128)(2,1)S(1)} %get-tuple-element.166.centre_ref), channel_id=1, source_target_pairs={{8,0},{1,8},{9,1},{3,9},{11,3},{2,11},{10,2},{0,10},{12,4},{5,12},... | collective-permute-start | bytes 98312 | tf_op jit(solution)/shard_map/ppermute | solution.py:61
  51.8 14.1 %collective-permute-start.10 = (bf16[8,128,128]{2,1,0:T(8,128)(2,1)S(1)}, bf16[8,128,128]{2,1,0:T(8,128)(2,1)S(1)}, u32[]{:S(2)}, u32[]{:S(2)}) collective-permute-start(bf16[8,128,128]{2,1,0:T(8,128)(2,1)S(1)} %collective-permute-done.8), channel_id=1, source_target_pairs={{10,0},{0,8},{8,1},{1,9},{9,3},{3,11},{11,2},{2,10},{14,4},{4,12},... | collective-permute-start | bytes 786440 | tf_op jit(solution)/shard_map/ppermute | solution.py:61
  52.3 12.1 %collective-permute-start.9 = (bf16[8,128,128]{2,1,0:T(8,128)(2,1)S(1)}, bf16[8,128,128]{2,1,0:T(8,128)(2,1)S(1)}, u32[]{:S(2)}, u32[]{:S(2)}) collective-permute-start(bf16[8,128,128]{2,1,0:T(8,128)(2,1)S(1)} %collective-permute-done.7), channel_id=1, source_target_pairs={{8,0},{1,8},{9,1},{3,9},{11,3},{2,11},{10,2},{0,10},{12,4},{5,12},... | collective-permute-start | bytes 786440 | tf_op jit(solution)/shard_map/ppermute | solution.py:61
  55.5 37.8 %collective-permute-start.21 = (bf16[42,128,128]{2,1,0:T(8,128)(2,1)S(1)}, bf16[42,128,128]{2,1,0:T(8,128)(2,1)S(1)}, u32[]{:S(2)}, u32[]{:S(2)}) collective-permute-start(bf16[42,128,128]{2,1,0:T(8,128)(2,1)S(1)} %bitcast.205), channel_id=1, source_target_pairs={{0,0},{1,8},{2,1},{3,9},{4,3},{5,11},{6,2},{7,10},{8,4},{9,12},{10... | collective-permute-start | bytes 4128776 | tf_op jit(solution)/shard_map/ppermute | solution.py:51
  56.4 23.8 %collective-permute-start.19 = (bf16[21,128,128]{2,1,0:T(8,128)(2,1)S(1)}, bf16[21,128,128]{2,1,0:T(8,128)(2,1)S(1)}, u32[]{:S(2)}, u32[]{:S(2)}) collective-permute-start(bf16[21,128,128]{2,1,0:T(8,128)(2,1)S(1)} %get-tuple-element.78.refs_0_), channel_id=1, source_target_pairs={{8,0},{1,8},{9,1},{3,9},{11,3},{2,11},{10,2},{0,10},{12,4},{5,12},... | collective-permute-start | bytes 2064392 | tf_op jit(solution)/shard_map/ppermute | solution.py:61
  64.3 26.1 %collective-permute-start.20 = (bf16[21,128,128]{2,1,0:T(8,128)(2,1)S(1)}, bf16[21,128,128]{2,1,0:T(8,128)(2,1)S(1)}, u32[]{:S(2)}, u32[]{:S(2)}) collective-permute-start(bf16[21,128,128]{2,1,0:T(8,128)(2,1)S(1)} %get-tuple-element.79.refs_1_), channel_id=1, source_target_pairs={{8,0},{1,8},{9,1},{3,9},{11,3},{2,11},{10,2},{0,10},{12,4},{5,12},... | collective-permute-start | bytes 2064392 | tf_op jit(solution)/shard_map/ppermute | solution.py:61
  64.4 45.4 %collective-permute-start.16 = (bf16[4,128,128]{2,1,0:T(8,128)(2,1)S(1)}, bf16[4,128,128]{2,1,0:T(8,128)(2,1)S(1)}, u32[]{:S(2)}, u32[]{:S(2)}) collective-permute-start(bf16[4,128,128]{2,1,0:T(8,128)(2,1)S(1)} %get-tuple-element.125.refs_3_), channel_id=1, source_target_pairs={{10,0},{0,8},{8,1},{1,9},{9,3},{3,11},{11,2},{2,10},{14,4},{4,12},... | collective-permute-start | bytes 393224 | tf_op jit(solution)/shard_map/ppermute | solution.py:61
  65.9 27.3 %collective-permute-start.1 = (bf16[8,128,128]{2,1,0:T(8,128)(2,1)S(1)}, bf16[8,128,128]{2,1,0:T(8,128)(2,1)S(1)}, u32[]{:S(2)}, u32[]{:S(2)}) collective-permute-start(bf16[8,128,128]{2,1,0:T(8,128)(2,1)S(1)} %concatenate.64), channel_id=1, source_target_pairs={{8,0},{1,8},{9,1},{3,9},{11,3},{2,11},{10,2},{0,10},{12,4},{5,12},... | collective-permute-start | bytes 786440 | tf_op jit(solution)/shard_map/ppermute | solution.py:61
  80.2 20.4 %collective-permute-start.22 = (bf16[21,128,128]{2,1,0:T(8,128)(2,1)S(1)}, bf16[21,128,128]{2,1,0:T(8,128)(2,1)S(1)}, u32[]{:S(2)}, u32[]{:S(2)}) collective-permute-start(bf16[21,128,128]{2,1,0:T(8,128)(2,1)S(1)} %collective-permute-done.19.refs_2_), channel_id=1, source_target_pairs={{8,0},{1,8},{9,1},{3,9},{11,3},{2,11},{10,2},{0,10},{12,4},{5,12},... | collective-permute-start | bytes 2064392 | tf_op jit(solution)/shard_map/ppermute | solution.py:61
  90.4 17.6 %collective-permute-start.23 = (bf16[21,128,128]{2,1,0:T(8,128)(2,1)S(1)}, bf16[21,128,128]{2,1,0:T(8,128)(2,1)S(1)}, u32[]{:S(2)}, u32[]{:S(2)}) collective-permute-start(bf16[21,128,128]{2,1,0:T(8,128)(2,1)S(1)} %collective-permute-done.20.refs_3_), channel_id=1, source_target_pairs={{8,0},{1,8},{9,1},{3,9},{11,3},{2,11},{10,2},{0,10},{12,4},{5,12},... | collective-permute-start | bytes 2064392 | tf_op jit(solution)/shard_map/ppermute | solution.py:61
  93.3 5.9 %collective-permute-start.2 = (bf16[8,128,128]{2,1,0:T(8,128)(2,1)S(1)}, bf16[8,128,128]{2,1,0:T(8,128)(2,1)S(1)}, u32[]{:S(2)}, u32[]{:S(2)}) collective-permute-start(bf16[8,128,128]{2,1,0:T(8,128)(2,1)S(1)} %concatenate.64), channel_id=1, source_target_pairs={{10,0},{0,8},{8,1},{1,9},{9,3},{3,11},{11,2},{2,10},{14,4},{4,12},... | collective-permute-start | bytes 786440 | tf_op jit(solution)/shard_map/ppermute | solution.py:61
  93.4 18.8 %collective-permute-start.3 = (bf16[8,128,128]{2,1,0:T(8,128)(2,1)S(1)}, bf16[8,128,128]{2,1,0:T(8,128)(2,1)S(1)}, u32[]{:S(2)}, u32[]{:S(2)}) collective-permute-start(bf16[8,128,128]{2,1,0:T(8,128)(2,1)S(1)} %collective-permute-done.1), channel_id=1, source_target_pairs={{8,0},{1,8},{9,1},{3,9},{11,3},{2,11},{10,2},{0,10},{12,4},{5,12},... | collective-permute-start | bytes 786440 | tf_op jit(solution)/shard_map/ppermute | solution.py:61
  99.2 13.0 %collective-permute-start.15 = (bf16[4,128,128]{2,1,0:T(8,128)(2,1)S(1)}, bf16[4,128,128]{2,1,0:T(8,128)(2,1)S(1)}, u32[]{:S(2)}, u32[]{:S(2)}) collective-permute-start(bf16[4,128,128]{2,1,0:T(8,128)(2,1)S(1)} %get-tuple-element.125.refs_3_), channel_id=1, source_target_pairs={{8,0},{1,8},{9,1},{3,9},{11,3},{2,11},{10,2},{0,10},{12,4},{5,12},... | collective-permute-start | bytes 393224 | tf_op jit(solution)/shard_map/ppermute | solution.py:61
  100.6 13.6 %collective-permute-start.4 = (bf16[8,128,128]{2,1,0:T(8,128)(2,1)S(1)}, bf16[8,128,128]{2,1,0:T(8,128)(2,1)S(1)}, u32[]{:S(2)}, u32[]{:S(2)}) collective-permute-start(bf16[8,128,128]{2,1,0:T(8,128)(2,1)S(1)} %collective-permute-done.2), channel_id=1, source_target_pairs={{10,0},{0,8},{8,1},{1,9},{9,3},{3,11},{11,2},{2,10},{14,4},{4,12},... | collective-permute-start | bytes 786440 | tf_op jit(solution)/shard_map/ppermute | solution.py:61
  107.9 20.4 %collective-permute-start.24 = (bf16[21,128,128]{2,1,0:T(8,128)(2,1)S(1)}, bf16[21,128,128]{2,1,0:T(8,128)(2,1)S(1)}, u32[]{:S(2)}, u32[]{:S(2)}) collective-permute-start(bf16[21,128,128]{2,1,0:T(8,128)(2,1)S(1)} %collective-permute-done.22.refs_4_), channel_id=1, source_target_pairs={{8,0},{1,8},{9,1},{3,9},{11,3},{2,11},{10,2},{0,10},{12,4},{5,12},... | collective-permute-start | bytes 2064392 | tf_op jit(solution)/shard_map/ppermute | solution.py:61
  109.9 18.5 %collective-permute-start.25 = (bf16[21,128,128]{2,1,0:T(8,128)(2,1)S(1)}, bf16[21,128,128]{2,1,0:T(8,128)(2,1)S(1)}, u32[]{:S(2)}, u32[]{:S(2)}) collective-permute-start(bf16[21,128,128]{2,1,0:T(8,128)(2,1)S(1)} %collective-permute-done.23.refs_5_), channel_id=1, source_target_pairs={{8,0},{1,8},{9,1},{3,9},{11,3},{2,11},{10,2},{0,10},{12,4},{5,12},... | collective-permute-start | bytes 2064392 | tf_op jit(solution)/shard_map/ppermute | solution.py:61
  112.2 4.6 %collective-permute-start.18 = (bf16[4,128,128]{2,1,0:T(8,128)(2,1)S(1)}, bf16[4,128,128]{2,1,0:T(8,128)(2,1)S(1)}, u32[]{:S(2)}, u32[]{:S(2)}) collective-permute-start(bf16[4,128,128]{2,1,0:T(8,128)(2,1)S(1)} %collective-permute-done.16.refs_5_), channel_id=1, source_target_pairs={{10,0},{0,8},{8,1},{1,9},{9,3},{3,11},{11,2},{2,10},{14,4},{4,12},... | collective-permute-start | bytes 393224 | tf_op jit(solution)/shard_map/ppermute | solution.py:61
  112.2 16.1 %collective-permute-start.17 = (bf16[4,128,128]{2,1,0:T(8,128)(2,1)S(1)}, bf16[4,128,128]{2,1,0:T(8,128)(2,1)S(1)}, u32[]{:S(2)}, u32[]{:S(2)}) collective-permute-start(bf16[4,128,128]{2,1,0:T(8,128)(2,1)S(1)} %collective-permute-done.15.refs_4_), channel_id=1, source_target_pairs={{8,0},{1,8},{9,1},{3,9},{11,3},{2,11},{10,2},{0,10},{12,4},{5,12},... | collective-permute-start | bytes 393224 | tf_op jit(solution)/shard_map/ppermute | solution.py:61
  134.8 12.3 %collective-permute-start.41 = (bf16[21,128,128]{2,1,0:T(8,128)(2,1)S(1)}, bf16[21,128,128]{2,1,0:T(8,128)(2,1)S(1)}, u32[]{:S(2)}, u32[]{:S(2)}) collective-permute-start(bf16[21,128,128]{2,1,0:T(8,128)(2,1)S(1)} %fusion.17), channel_id=1, source_target_pairs={{10,0},{0,8},{8,1},{1,9},{9,3},{3,11},{11,2},{2,10},{14,4},{4,12},... | collective-permute-start | bytes 2064392 | tf_op jit(solution)/shard_map/ppermute | solution.py:61
  136.1 16.7 %collective-permute-start.38 = (bf16[21,128,128]{2,1,0:T(8,128)(2,1)S(1)}, bf16[21,128,128]{2,1,0:T(8,128)(2,1)S(1)}, u32[]{:S(2)}, u32[]{:S(2)}) collective-permute-start(bf16[21,128,128]{2,1,0:T(8,128)(2,1)S(1)} %fusion.16), channel_id=1, source_target_pairs={{10,0},{0,8},{8,1},{1,9},{9,3},{3,11},{11,2},{2,10},{14,4},{4,12},... | collective-permute-start | bytes 2064392 | tf_op jit(solution)/shard_map/ppermute | solution.py:61
  143.6 10.5 %collective-permute-start.26 = (bf16[21,128,128]{2,1,0:T(8,128)(2,1)S(1)}, bf16[21,128,128]{2,1,0:T(8,128)(2,1)S(1)}, u32[]{:S(2)}, u32[]{:S(2)}) collective-permute-start(bf16[21,128,128]{2,1,0:T(8,128)(2,1)S(1)} %get-tuple-element.88.refs_0_), channel_id=1, source_target_pairs={{8,0},{1,8},{9,1},{3,9},{11,3},{2,11},{10,2},{0,10},{12,4},{5,12},... | collective-permute-start | bytes 2064392 | tf_op jit(solution)/shard_map/ppermute | solution.py:61
  145.5 15.8 %collective-permute-start.27 = (bf16[21,128,128]{2,1,0:T(8,128)(2,1)S(1)}, bf16[21,128,128]{2,1,0:T(8,128)(2,1)S(1)}, u32[]{:S(2)}, u32[]{:S(2)}) collective-permute-start(bf16[21,128,128]{2,1,0:T(8,128)(2,1)S(1)} %get-tuple-element.89.refs_1_), channel_id=1, source_target_pairs={{8,0},{1,8},{9,1},{3,9},{11,3},{2,11},{10,2},{0,10},{12,4},{5,12},... | collective-permute-start | bytes 2064392 | tf_op jit(solution)/shard_map/ppermute | solution.py:61
  148.3 15.3 %collective-permute-start.42 = (bf16[21,128,128]{2,1,0:T(8,128)(2,1)S(1)}, bf16[21,128,128]{2,1,0:T(8,128)(2,1)S(1)}, u32[]{:S(2)}, u32[]{:S(2)}) collective-permute-start(bf16[21,128,128]{2,1,0:T(8,128)(2,1)S(1)} %fusion.12), channel_id=1, source_target_pairs={{10,0},{0,8},{8,1},{1,9},{9,3},{3,11},{11,2},{2,10},{14,4},{4,12},... | collective-permute-start | bytes 2064392 | tf_op jit(solution)/shard_map/ppermute | solution.py:61
  153.9 13.6 %collective-permute-start.39 = (bf16[21,128,128]{2,1,0:T(8,128)(2,1)S(1)}, bf16[21,128,128]{2,1,0:T(8,128)(2,1)S(1)}, u32[]{:S(2)}, u32[]{:S(2)}) collective-permute-start(bf16[21,128,128]{2,1,0:T(8,128)(2,1)S(1)} %fusion.14), channel_id=1, source_target_pairs={{10,0},{0,8},{8,1},{1,9},{9,3},{3,11},{11,2},{2,10},{14,4},{4,12},... | collective-permute-start | bytes 2064392 | tf_op jit(solution)/shard_map/ppermute | solution.py:61
  154.0 16.8 %collective-permute-start.28 = (bf16[21,128,128]{2,1,0:T(8,128)(2,1)S(1)}, bf16[21,128,128]{2,1,0:T(8,128)(2,1)S(1)}, u32[]{:S(2)}, u32[]{:S(2)}) collective-permute-start(bf16[21,128,128]{2,1,0:T(8,128)(2,1)S(1)} %collective-permute-done.26.refs_2_), channel_id=1, source_target_pairs={{8,0},{1,8},{9,1},{3,9},{11,3},{2,11},{10,2},{0,10},{12,4},{5,12},... | collective-permute-start | bytes 2064392 | tf_op jit(solution)/shard_map/ppermute | solution.py:61
  161.4 14.7 %collective-permute-start.29 = (bf16[21,128,128]{2,1,0:T(8,128)(2,1)S(1)}, bf16[21,128,128]{2,1,0:T(8,128)(2,1)S(1)}, u32[]{:S(2)}, u32[]{:S(2)}) collective-permute-start(bf16[21,128,128]{2,1,0:T(8,128)(2,1)S(1)} %collective-permute-done.27.refs_3_), channel_id=1, source_target_pairs={{8,0},{1,8},{9,1},{3,9},{11,3},{2,11},{10,2},{0,10},{12,4},{5,12},... | collective-permute-start | bytes 2064392 | tf_op jit(solution)/shard_map/ppermute | solution.py:61
  164.7 13.6 %collective-permute-start.43 = (bf16[21,128,128]{2,1,0:T(8,128)(2,1)S(1)}, bf16[21,128,128]{2,1,0:T(8,128)(2,1)S(1)}, u32[]{:S(2)}, u32[]{:S(2)}) collective-permute-start(bf16[21,128,128]{2,1,0:T(8,128)(2,1)S(1)} %fusion.13), channel_id=1, source_target_pairs={{10,0},{0,8},{8,1},{1,9},{9,3},{3,11},{11,2},{2,10},{14,4},{4,12},... | collective-permute-start | bytes 2064392 | tf_op jit(solution)/shard_map/ppermute | solution.py:61
  168.7 13.8 %collective-permute-start.40 = (bf16[21,128,128]{2,1,0:T(8,128)(2,1)S(1)}, bf16[21,128,128]{2,1,0:T(8,128)(2,1)S(1)}, u32[]{:S(2)}, u32[]{:S(2)}) collective-permute-start(bf16[21,128,128]{2,1,0:T(8,128)(2,1)S(1)} %fusion.15), channel_id=1, source_target_pairs={{10,0},{0,8},{8,1},{1,9},{9,3},{3,11},{11,2},{2,10},{14,4},{4,12},... | collective-permute-start | bytes 2064392 | tf_op jit(solution)/shard_map/ppermute | solution.py:61
  170.8 22.1 %collective-permute-start.30 = (bf16[21,128,128]{2,1,0:T(8,128)(2,1)S(1)}, bf16[21,128,128]{2,1,0:T(8,128)(2,1)S(1)}, u32[]{:S(2)}, u32[]{:S(2)}) collective-permute-start(bf16[21,128,128]{2,1,0:T(8,128)(2,1)S(1)} %collective-permute-done.28.refs_4_), channel_id=1, source_target_pairs={{8,0},{1,8},{9,1},{3,9},{11,3},{2,11},{10,2},{0,10},{12,4},{5,12},... | collective-permute-start | bytes 2064392 | tf_op jit(solution)/shard_map/ppermute | solution.py:61
  176.1 16.8 %collective-permute-start.31 = (bf16[21,128,128]{2,1,0:T(8,128)(2,1)S(1)}, bf16[21,128,128]{2,1,0:T(8,128)(2,1)S(1)}, u32[]{:S(2)}, u32[]{:S(2)}) collective-permute-start(bf16[21,128,128]{2,1,0:T(8,128)(2,1)S(1)} %collective-permute-done.29.refs_5_), channel_id=1, source_target_pairs={{8,0},{1,8},{9,1},{3,9},{11,3},{2,11},{10,2},{0,10},{12,4},{5,12},... | collective-permute-start | bytes 2064392 | tf_op jit(solution)/shard_map/ppermute | solution.py:61
  188.5 12.3 %collective-permute-start.47 = (bf16[21,128,128]{2,1,0:T(8,128)(2,1)S(1)}, bf16[21,128,128]{2,1,0:T(8,128)(2,1)S(1)}, u32[]{:S(2)}, u32[]{:S(2)}) collective-permute-start(bf16[21,128,128]{2,1,0:T(8,128)(2,1)S(1)} %fusion.19), channel_id=1, source_target_pairs={{10,0},{0,8},{8,1},{1,9},{9,3},{3,11},{11,2},{2,10},{14,4},{4,12},... | collective-permute-start | bytes 2064392 | tf_op jit(solution)/shard_map/ppermute | solution.py:61
  190.4 15.9 %collective-permute-start.44 = (bf16[21,128,128]{2,1,0:T(8,128)(2,1)S(1)}, bf16[21,128,128]{2,1,0:T(8,128)(2,1)S(1)}, u32[]{:S(2)}, u32[]{:S(2)}) collective-permute-start(bf16[21,128,128]{2,1,0:T(8,128)(2,1)S(1)} %fusion.18), channel_id=1, source_target_pairs={{10,0},{0,8},{8,1},{1,9},{9,3},{3,11},{11,2},{2,10},{14,4},{4,12},... | collective-permute-start | bytes 2064392 | tf_op jit(solution)/shard_map/ppermute | solution.py:61
  199.3 8.9 %collective-permute-start.32 = (bf16[21,128,128]{2,1,0:T(8,128)(2,1)S(1)}, bf16[21,128,128]{2,1,0:T(8,128)(2,1)S(1)}, u32[]{:S(2)}, u32[]{:S(2)}) collective-permute-start(bf16[21,128,128]{2,1,0:T(8,128)(2,1)S(1)} %get-tuple-element.92.refs_0_.refs_8_), channel_id=1, source_target_pairs={{8,0},{1,8},{9,1},{3,9},{11,3},{2,11},{10,2},{0,10},{12,4},{5,12},... | collective-permute-start | bytes 2064392 | tf_op jit(solution)/shard_map/ppermute | solution.py:61
  199.3 15.8 %collective-permute-start.33 = (bf16[21,128,128]{2,1,0:T(8,128)(2,1)S(1)}, bf16[21,128,128]{2,1,0:T(8,128)(2,1)S(1)}, u32[]{:S(2)}, u32[]{:S(2)}) collective-permute-start(bf16[21,128,128]{2,1,0:T(8,128)(2,1)S(1)} %get-tuple-element.93.refs_1_.refs_9_), channel_id=1, source_target_pairs={{8,0},{1,8},{9,1},{3,9},{11,3},{2,11},{10,2},{0,10},{12,4},{5,12},... | collective-permute-start | bytes 2064392 | tf_op jit(solution)/shard_map/ppermute | solution.py:61
  201.2 16.2 %collective-permute-start.48 = (bf16[21,128,128]{2,1,0:T(8,128)(2,1)S(1)}, bf16[21,128,128]{2,1,0:T(8,128)(2,1)S(1)}, u32[]{:S(2)}, u32[]{:S(2)}) collective-permute-start(bf16[21,128,128]{2,1,0:T(8,128)(2,1)S(1)} %fusion.8), channel_id=1, source_target_pairs={{10,0},{0,8},{8,1},{1,9},{9,3},{3,11},{11,2},{2,10},{14,4},{4,12},... | collective-permute-start | bytes 2064392 | tf_op jit(solution)/shard_map/ppermute | solution.py:61
  206.7 14.3 %collective-permute-start.45 = (bf16[21,128,128]{2,1,0:T(8,128)(2,1)S(1)}, bf16[21,128,128]{2,1,0:T(8,128)(2,1)S(1)}, u32[]{:S(2)}, u32[]{:S(2)}) collective-permute-start(bf16[21,128,128]{2,1,0:T(8,128)(2,1)S(1)} %fusion.10), channel_id=1, source_target_pairs={{10,0},{0,8},{8,1},{1,9},{9,3},{3,11},{11,2},{2,10},{14,4},{4,12},... | collective-permute-start | bytes 2064392 | tf_op jit(solution)/shard_map/ppermute | solution.py:61
  208.2 15.7 %collective-permute-start.34 = (bf16[21,128,128]{2,1,0:T(8,128)(2,1)S(1)}, bf16[21,128,128]{2,1,0:T(8,128)(2,1)}, u32[]{:S(2)}, u32[]{:S(2)}) collective-permute-start(bf16[21,128,128]{2,1,0:T(8,128)(2,1)S(1)} %collective-permute-done.32.refs_2_.refs_10_), channel_id=1, source_target_pairs={{8,0},{1,8},{9,1},{3,9},{11,3},{2,11},{10,2},{0,10},{12,4},{5,12},... | collective-permute-start | bytes 2064392 | tf_op jit(solution)/shard_map/ppermute | solution.py:61
  215.2 14.7 %collective-permute-start.35 = (bf16[21,128,128]{2,1,0:T(8,128)(2,1)S(1)}, bf16[21,128,128]{2,1,0:T(8,128)(2,1)}, u32[]{:S(2)}, u32[]{:S(2)}) collective-permute-start(bf16[21,128,128]{2,1,0:T(8,128)(2,1)S(1)} %collective-permute-done.33.refs_3_.refs_11_), channel_id=1, source_target_pairs={{8,0},{1,8},{9,1},{3,9},{11,3},{2,11},{10,2},{0,10},{12,4},{5,12},... | collective-permute-start | bytes 2064392 | tf_op jit(solution)/shard_map/ppermute | solution.py:61
  218.7 15.0 %collective-permute-start.49 = (bf16[21,128,128]{2,1,0:T(8,128)(2,1)}, bf16[21,128,128]{2,1,0:T(8,128)(2,1)S(1)}, u32[]{:S(2)}, u32[]{:S(2)}) collective-permute-start(bf16[21,128,128]{2,1,0:T(8,128)(2,1)} %fusion.9), channel_id=1, source_target_pairs={{10,0},{0,8},{8,1},{1,9},{9,3},{3,11},{11,2},{2,10},{14,4},{4,12},... | collective-permute-start | bytes 2064392 | tf_op jit(solution)/shard_map/ppermute | solution.py:61
  222.3 14.3 %collective-permute-start.46 = (bf16[21,128,128]{2,1,0:T(8,128)(2,1)}, bf16[21,128,128]{2,1,0:T(8,128)(2,1)S(1)}, u32[]{:S(2)}, u32[]{:S(2)}) collective-permute-start(bf16[21,128,128]{2,1,0:T(8,128)(2,1)} %fusion.11), channel_id=1, source_target_pairs={{10,0},{0,8},{8,1},{1,9},{9,3},{3,11},{11,2},{2,10},{14,4},{4,12},... | collective-permute-start | bytes 2064392 | tf_op jit(solution)/shard_map/ppermute | solution.py:61
  223.9 18.4 %collective-permute-start.36 = (bf16[21,128,128]{2,1,0:T(8,128)(2,1)}, bf16[21,128,128]{2,1,0:T(8,128)(2,1)}, u32[]{:S(2)}, u32[]{:S(2)}) collective-permute-start(bf16[21,128,128]{2,1,0:T(8,128)(2,1)} %collective-permute-done.34.refs_4_.refs_12_), channel_id=1, source_target_pairs={{8,0},{1,8},{9,1},{3,9},{11,3},{2,11},{10,2},{0,10},{12,4},{5,12},... | collective-permute-start | bytes 2064392 | tf_op jit(solution)/shard_map/ppermute | solution.py:61
  229.9 14.9 %collective-permute-start.37 = (bf16[21,128,128]{2,1,0:T(8,128)(2,1)}, bf16[21,128,128]{2,1,0:T(8,128)(2,1)}, u32[]{:S(2)}, u32[]{:S(2)}) collective-permute-start(bf16[21,128,128]{2,1,0:T(8,128)(2,1)} %collective-permute-done.35.refs_5_.refs_13_), channel_id=1, source_target_pairs={{8,0},{1,8},{9,1},{3,9},{11,3},{2,11},{10,2},{0,10},{12,4},{5,12},... | collective-permute-start | bytes 2064392 | tf_op jit(solution)/shard_map/ppermute | solution.py:61
  248.5 5.0 %collective-permute-start.50 = (f32[1,128]{1,0:T(1,128)S(1)}, f32[1,128]{1,0:T(1,128)S(1)}, u32[]{:S(2)}, u32[]{:S(2)}) collective-permute-start(f32[1,128]{1,0:T(1,128)S(1)} %get-tuple-element.131), channel_id=1, source_target_pairs={{8,0},{0,8},{9,1},{1,9},{11,3},{3,11},{10,2},{2,10},{12,4},{4,12},... | collective-permute-start | bytes 1544 | tf_op jit(solution)/shard_map/ppermute | solution.py:66
  253.6 5.5 %collective-permute-start.51 = (f32[2,128]{1,0:T(2,128)S(1)}, f32[2,128]{1,0:T(2,128)S(1)}, u32[]{:S(2)}, u32[]{:S(2)}) collective-permute-start(f32[2,128]{1,0:T(2,128)S(1)} %maximum_select_fusion.4), channel_id=1, source_target_pairs={{1,0},{9,8},{0,1},{8,9},{2,3},{10,11},{3,2},{11,10},{5,4},{13,12},... | collective-permute-start | bytes 3080 | tf_op jit(solution)/shard_map/ppermute | solution.py:66
  255.3 8.3 %collective-permute-start.56 = (bf16[528,128]{1,0:T(8,128)(2,1)S(1)}, bf16[528,128]{1,0:T(8,128)(2,1)}, u32[]{:S(2)}, u32[]{:S(2)}) collective-permute-start(bf16[528,128]{1,0:T(8,128)(2,1)S(1)} %get-tuple-element.133.refs_3_), channel_id=1, source_target_pairs={{2,0},{10,8},{0,1},{8,9},{1,3},{9,11},{3,2},{11,10},{6,4},{14,12},... | collective-permute-start | bytes 405512 | tf_op jit(solution)/shard_map/ppermute | solution.py:61
  255.6 8.1 %collective-permute-start.55 = (bf16[528,128]{1,0:T(8,128)(2,1)S(1)}, bf16[528,128]{1,0:T(8,128)(2,1)}, u32[]{:S(2)}, u32[]{:S(2)}) collective-permute-start(bf16[528,128]{1,0:T(8,128)(2,1)S(1)} %get-tuple-element.133.refs_3_), channel_id=1, source_target_pairs={{1,0},{9,8},{3,1},{11,9},{2,3},{10,11},{0,2},{8,10},{5,4},{13,12},... | collective-permute-start | bytes 405512 | tf_op jit(solution)/shard_map/ppermute | solution.py:61
  257.4 6.3 %collective-permute-start.54 = (bf16[528,128]{1,0:T(8,128)(2,1)S(1)}, bf16[528,128]{1,0:T(8,128)(2,1)}, u32[]{:S(2)}, u32[]{:S(2)}) collective-permute-start(bf16[528,128]{1,0:T(8,128)(2,1)S(1)} %get-tuple-element.133.refs_3_), channel_id=1, source_target_pairs={{10,0},{0,8},{8,1},{1,9},{9,3},{3,11},{11,2},{2,10},{14,4},{4,12},... | collective-permute-start | bytes 405512 | tf_op jit(solution)/shard_map/ppermute | solution.py:61
  257.4 6.3 %collective-permute-start.53 = (bf16[528,128]{1,0:T(8,128)(2,1)S(1)}, bf16[528,128]{1,0:T(8,128)(2,1)}, u32[]{:S(2)}, u32[]{:S(2)}) collective-permute-start(bf16[528,128]{1,0:T(8,128)(2,1)S(1)} %get-tuple-element.133.refs_3_), channel_id=1, source_target_pairs={{8,0},{1,8},{9,1},{3,9},{11,3},{2,11},{10,2},{0,10},{12,4},{5,12},... | collective-permute-start | bytes 405512 | tf_op jit(solution)/shard_map/ppermute | solution.py:61
  259.1 4.5 %collective-permute-start.52 = (f32[4,128]{1,0:T(4,128)S(1)}, f32[4,128]{1,0:T(4,128)S(1)}, u32[]{:S(2)}, u32[]{:S(2)}) collective-permute-start(f32[4,128]{1,0:T(4,128)S(1)} %maximum_select_fusion.2), channel_id=1, source_target_pairs={{3,0},{11,8},{2,1},{10,9},{0,3},{8,11},{1,2},{9,10},{7,4},{15,12},... | collective-permute-start | bytes 6152 | tf_op jit(solution)/shard_map/ppermute | solution.py:66
  278.5 8.8 %collective-permute-start.63 = (f32[2,128,128]{2,1,0:T(8,128)S(1)}, f32[2,128,128]{2,1,0:T(8,128)S(1)}, u32[]{:S(2)}, u32[]{:S(2)}) collective-permute-start(f32[2,128,128]{2,1,0:T(8,128)S(1)} %get-tuple-element.160), channel_id=1, source_target_pairs={{11,0},{2,8},{10,1},{0,9},{8,3},{1,11},{9,2},{3,10},{15,4},{6,12},... | collective-permute-start | bytes 393224 | tf_op jit(solution)/shard_map/ppermute | solution.py:61
  279.8 7.6 %collective-permute-start.62 = (f32[2,128,128]{2,1,0:T(8,128)S(1)}, f32[2,128,128]{2,1,0:T(8,128)S(1)}, u32[]{:S(2)}, u32[]{:S(2)}) collective-permute-start(f32[2,128,128]{2,1,0:T(8,128)S(1)} %get-tuple-element.161), channel_id=1, source_target_pairs={{2,0},{10,8},{0,1},{8,9},{1,3},{9,11},{3,2},{11,10},{6,4},{14,12},... | collective-permute-start | bytes 393224 | tf_op jit(solution)/shard_map/ppermute | solution.py:61
  280.4 8.4 %collective-permute-start.61 = (f32[2,128,128]{2,1,0:T(8,128)S(1)}, f32[2,128,128]{2,1,0:T(8,128)S(1)}, u32[]{:S(2)}, u32[]{:S(2)}) collective-permute-start(f32[2,128,128]{2,1,0:T(8,128)S(1)} %get-tuple-element.162), channel_id=1, source_target_pairs={{10,0},{0,8},{8,1},{1,9},{9,3},{3,11},{11,2},{2,10},{14,4},{4,12},... | collective-permute-start | bytes 393224 | tf_op jit(solution)/shard_map/ppermute | solution.py:61
  281.8 4.5 %collective-permute-start.59 = (f32[4,128]{1,0:T(4,128)S(1)}, f32[4,128]{1,0:T(4,128)S(1)}, u32[]{:S(2)}, u32[]{:S(2)}) collective-permute-start(f32[4,128]{1,0:T(4,128)S(1)} %maximum_select_fusion.3), channel_id=1, source_target_pairs={{3,0},{11,8},{2,1},{10,9},{0,3},{8,11},{1,2},{9,10},{7,4},{15,12},... | collective-permute-start | bytes 6152 | tf_op jit(solution)/shard_map/ppermute | solution.py:66
  295.0 10.6 %collective-permute-start.64 = (bf16[128,128]{1,0:T(8,128)(2,1)S(1)}, bf16[128,128]{1,0:T(8,128)(2,1)S(1)}, u32[]{:S(2)}, u32[]{:S(2)}) collective-permute-start(bf16[128,128]{1,0:T(8,128)(2,1)S(1)} %get-tuple-element.167), channel_id=1, source_target_pairs={{0,16},{8,17},{1,18},{9,19},{3,20},{11,21},{2,22},{10,23},{4,24},{... | collective-permute-start | bytes 98312 | tf_op jit(solution)/shard_map/ppermute | solution.py:56
  295.8 9.9 %collective-permute-start.67 = (bf16[128,128]{1,0:T(8,128)(2,1)S(1)}, bf16[128,128]{1,0:T(8,128)(2,1)S(1)}, u32[]{:S(2)}, u32[]{:S(2)}) collective-permute-start(bf16[128,128]{1,0:T(8,128)(2,1)S(1)} %get-tuple-element.168), channel_id=1, source_target_pairs={{0,21},{8,22},{1,23},{9,16},{3,17},{11,18},{2,19},{10,20},{4,29},{... | collective-permute-start | bytes 98312 | tf_op jit(solution)/shard_map/ppermute | solution.py:56
  303.1 5.0 %collective-permute-start.66 = (bf16[128,128]{1,0:T(8,128)(2,1)S(1)}, bf16[128,128]{1,0:T(8,128)(2,1)S(1)}, u32[]{:S(2)}, u32[]{:S(2)}) collective-permute-start(bf16[128,128]{1,0:T(8,128)(2,1)S(1)} %get-tuple-element.169), channel_id=1, source_target_pairs={{0,22},{8,23},{1,16},{9,17},{3,18},{11,19},{2,20},{10,21},{4,30},{... | collective-permute-start | bytes 98312 | tf_op jit(solution)/shard_map/ppermute | solution.py:56
  303.1 5.0 %collective-permute-start.65 = (bf16[128,128]{1,0:T(8,128)(2,1)S(1)}, bf16[128,128]{1,0:T(8,128)(2,1)S(1)}, u32[]{:S(2)}, u32[]{:S(2)}) collective-permute-start(bf16[128,128]{1,0:T(8,128)(2,1)S(1)} %get-tuple-element.170), channel_id=1, source_target_pairs={{0,23},{8,16},{1,17},{9,18},{3,19},{11,20},{2,21},{10,22},{4,31},{... | collective-permute-start | bytes 98312 | tf_op jit(solution)/shard_map/ppermute | solution.py:56
  (34 other events, 238.5 us)

commit v4 on v3

--- a/solution.py
+++ b/solution.py
@@ -751,7 +751,7 @@
     )
     half_vector = vector.astype(jnp.bfloat16)
     rolled_vector = (half_vector, *other_classes_of(places, half_vector))
-    right, (vector, weights) = after(right, (vector, weights))
+    right, weights = after(right, weights)
     centre_float = own_centre.astype(jnp.float32)
     centre_square = jnp.sum((centre_float * centre_float).reshape(-1, ROWS, block), axis=0)
 
@@ -763,7 +763,9 @@
                 left, envs[-1] = after(left, envs[-1])
             envs.append(ahead(envs[-1], 1))
         if step == 0:
-            (rolled, rolled_vector), envs = after((rolled, rolled_vector), envs)
+            rolled, envs = after(rolled, envs)
+        if step == 1:
+            rolled_vector, envs = after(rolled_vector, envs)
         right, square = right_whole(
             envs,
             right_isos[step],

time: 311 us -> 325 us (1.045)
  waiting for transfers between devices: 107 us -> 118 us
  starting transfers between devices: 109 us -> 114 us
    ppermute x52, starting transfers between devices: 65.9 us -> 81.2 us  [ahead(): lax.ppermute(x, BOTH, self.pairs(lambda g, k: self.slot(g + chain_by, k +...]
    ppermute x5, starting transfers between devices: 24.7 us -> 13.3 us  [fetch(): lax.ppermute(x, BOTH, self.pairs(lambda g, k: self.home(g + site_by, k +...]
    ppermute x52, waiting for transfers between devices: 93.4 us -> 103 us  [ahead(): lax.ppermute(x, BOTH, self.pairs(lambda g, k: self.slot(g + chain_by, k +...]
    ppermute x5, waiting for transfers between devices: 0.01 us -> 4.79 us  [fetch(): lax.ppermute(x, BOTH, self.pairs(lambda g, k: self.home(g + site_by, k +...]
  transfers between devices with their start and end apart: 68 -> 68, of which waited for: 29 -> 28; matrix products, arithmetic and copies ran while one was open for 7% -> 5% of each run, Pallas kernels for 10% -> 9%
where the time goes in v4:
time: 325 us; the launch traced here: 323 us
  waiting for transfers between devices  118 us (36%)
  starting transfers between devices  114 us (35%)
  Pallas kernels  54 us (17%)
  matrix products  11.1 us (3%)
  local copies, waits for them, and re-layouts  10.8 us (3%)
  blocking collectives  8.75 us (3%)
  other arithmetic  4.66 us (1%)
    ppermute x52, waiting for transfers between devices, ahead(): lax.ppermute(x, BOTH, self.pairs(lambda g, k: self.slot(g + chain_by, k +...  103 us
    ppermute x52, starting transfers between devices, ahead(): lax.ppermute(x, BOTH, self.pairs(lambda g, k: self.slot(g + chain_by, k +...  81.2 us
    pallas_call x19, Pallas kernels, call(): pl.pallas_call(kernel, out_shape=out_shape, scratch_shapes=scratch_shapes...  54 us
    ppermute x5, starting transfers between devices, send_home(): lax.ppermute(x, BOTH, self.pairs(self.slot, lambda g, k: self.home(g + si...  13.5 us
    ppermute x5, starting transfers between devices, fetch(): lax.ppermute(x, BOTH, self.pairs(lambda g, k: self.home(g + site_by, k +...  13.3 us
    dot_general x12, matrix products, local(): jnp.einsum('xy,vxz->vyz', left_isos[step][s], gathered[s][piece], preferr...  11 us
    all_gather x1, blocking collectives, local(): lax.all_gather(weight_matrices(mpo[0], pattern[0], secs), 'site')  8.75 us
    ppermute x6, waiting for transfers between devices, partner(): lax.ppermute(x, BOTH, self.pairs(lambda g, k: self.slot(g, k ^ bit), self...  7.85 us
  transfers between devices with their start and end apart: 68, of which 28 were waited for; matrix products, arithmetic and copies ran while one was open for 5% of the time, Pallas kernels for 9%

profile of v4, /device:TPU:0, one launch (start us, length us, event | category | flops | bytes accessed | tf_op | source)
XLA Modules:
  0.0 323.0 jit_solution(7004296040931124507)
XLA Ops:
  0.7 2.9 pad_maximum_fusion
  3.6 2.1 collective-permute-start.8
  5.7 6.3 %collective-permute-start.13 = (bf16[4,128,128]{2,1,0:T(8,128)(2,1)S(1)}, bf16[4,128,128]{2,1,0:T(8,128)(2,1)S(1)}, u32[]{:S(2)}, u32[]{:S(2)}) collective-permute-start(bf16[4,128,128]{2,1,0:T(8,128)(2,1)S(1)} %bitcast.191), channel_id=1, source_target_pairs={{8,0},{9,8},{10,1},{11,9},{12,3},{13,11},{14,2},{15,10},{16,4},{17... | collective-permute-start | bytes 393224 | tf_op jit(solution)/shard_map/ppermute | solution.py:51
  11.9 3.0 collective-permute-start.14
  16.0 8.8 %all-gather = bf16[8,168,168]{2,1,0:T(8,128)(2,1)S(1)} all-gather(bf16[2,168,168]{2,1,0:T(8,128)(2,1)S(1)} %pad_maximum_fusion.2), channel_id=2, replica_groups=mesh['site'=4,'sec'=8] {'site'}, dimensions={0}, use_global_device_ids=true | all-gather | bytes 564480 | tf_op jit(solution)/shard_map/all_gather | solution.py:736
  30.4 1.5 collective-permute-start.15
  32.9 2.9 collective-permute-done.16
  35.9 3.8 %collective-permute-start.17 = (bf16[8,128,128]{2,1,0:T(8,128)(2,1)S(1)}, bf16[8,128,128]{2,1,0:T(8,128)(2,1)S(1)}, u32[]{:S(2)}, u32[]{:S(2)}) collective-permute-start(bf16[8,128,128]{2,1,0:T(8,128)(2,1)S(1)} %collective-permute-done.15), channel_id=1, source_target_pairs={{8,0},{1,8},{9,1},{3,9},{11,3},{2,11},{10,2},{0,10},{12,4},{5,12},... | collective-permute-start | bytes 786440 | tf_op jit(solution)/shard_map/ppermute | solution.py:61
  40.9 21.7 %collective-permute-start.19 = (bf16[21,128,128]{2,1,0:T(8,128)(2,1)S(1)}, bf16[21,128,128]{2,1,0:T(8,128)(2,1)S(1)}, u32[]{:S(2)}, u32[]{:S(2)}) collective-permute-start(bf16[21,128,128]{2,1,0:T(8,128)(2,1)S(1)} %get-tuple-element.85.refs_0_), channel_id=1, source_target_pairs={{8,0},{1,8},{9,1},{3,9},{11,3},{2,11},{10,2},{0,10},{12,4},{5,12},... | collective-permute-start | bytes 2064392 | tf_op jit(solution)/shard_map/ppermute | solution.py:61
  64.4 14.2 %collective-permute-done.19.refs_2_ = bf16[21,128,128]{2,1,0:T(8,128)(2,1)S(1)} collective-permute-done((bf16[21,128,128]{2,1,0:T(8,128)(2,1)S(1)}, bf16[21,128,128]{2,1,0:T(8,128)(2,1)S(1)}, u32[]{:S(2)}, u32[]{:S(2)}) %collective-permute-start.19) | collective-permute-done | bytes 688160 | tf_op jit(solution)/shard_map/ppermute | solution.py:61
  78.5 2.2 collective-permute-start.22
  80.7 8.0 %collective-permute-done.20.refs_3_ = bf16[21,128,128]{2,1,0:T(8,128)(2,1)S(1)} collective-permute-done((bf16[21,128,128]{2,1,0:T(8,128)(2,1)S(1)}, bf16[21,128,128]{2,1,0:T(8,128)(2,1)S(1)}, u32[]{:S(2)}, u32[]{:S(2)}) %collective-permute-start.20) | collective-permute-done | bytes 688160 | tf_op jit(solution)/shard_map/ppermute | solution.py:61
  88.7 1.9 collective-permute-start.23
  91.6 1.8 collective-permute-start.11
  93.7 5.3 %collective-permute-done.22.refs_4_ = bf16[21,128,128]{2,1,0:T(8,128)(2,1)S(1)} collective-permute-done((bf16[21,128,128]{2,1,0:T(8,128)(2,1)S(1)}, bf16[21,128,128]{2,1,0:T(8,128)(2,1)S(1)}, u32[]{:S(2)}, u32[]{:S(2)}) %collective-permute-start.22) | collective-permute-done | bytes 688160 | tf_op jit(solution)/shard_map/ppermute | solution.py:61
  98.9 7.4 %collective-permute-done.23.refs_5_ = bf16[21,128,128]{2,1,0:T(8,128)(2,1)S(1)} collective-permute-done((bf16[21,128,128]{2,1,0:T(8,128)(2,1)S(1)}, bf16[21,128,128]{2,1,0:T(8,128)(2,1)S(1)}, u32[]{:S(2)}, u32[]{:S(2)}) %collective-permute-start.23) | collective-permute-done | bytes 688160 | tf_op jit(solution)/shard_map/ppermute | solution.py:61
  106.3 1.9 collective-permute-start.24
  109.3 7.4 %collective-permute-done.24.refs_6_ = bf16[21,128,128]{2,1,0:T(8,128)(2,1)S(1)} collective-permute-done((bf16[21,128,128]{2,1,0:T(8,128)(2,1)S(1)}, bf16[21,128,128]{2,1,0:T(8,128)(2,1)S(1)}, u32[]{:S(2)}, u32[]{:S(2)}) %collective-permute-start.24) | collective-permute-done | bytes 688160 | tf_op jit(solution)/shard_map/ppermute | solution.py:61
  116.7 7.4 %collective-permute-done.25.refs_7_ = bf16[21,128,128]{2,1,0:T(8,128)(2,1)S(1)} collective-permute-done((bf16[21,128,128]{2,1,0:T(8,128)(2,1)S(1)}, bf16[21,128,128]{2,1,0:T(8,128)(2,1)S(1)}, u32[]{:S(2)}, u32[]{:S(2)}) %collective-permute-start.25) | collective-permute-done | bytes 688160 | tf_op jit(solution)/shard_map/ppermute | solution.py:61
  124.2 5.2 %shard_map.147 = (bf16[21,128,128]{2,1,0:T(8,128)(2,1)S(1)}, bf16[21,128,128]{2,1,0:T(8,128)(2,1)S(1)}, bf16[21,128,128]{2,1,0:T(8,128)(2,1)S(1)}, bf16[21,128,1...) custom-call(bf16[21,128,128]{2,1,0:T(8,128)(2,1)S(1)} %get-tuple-ele, ...), custom_call_target="tpu_custom_call" | custom-call | flops 2334130176 | bytes 3076096 | tf_op jit(solution)/shard_map/pallas_call | solution.py:511
  132.9 6.3 %shard_map.145 = (bf16[21,128,128]{2,1,0:T(8,128)(2,1)S(1)}, bf16[21,128,128]{2,1,0:T(8,128)(2,1)S(1)}, f32[8,128]{1,0:T(8,128)S(1)}) custom-call(bf16[21,128,128]{2,1,0:T(8,128)(2,1)S(1)} %get-tuple-element.85.refs_0_, bf16[21,128,128]{2,1,0:T(8,128)(2,1)S(1)} %get-tuple-element.86.refs_1_, bf16[21,128,128]{2,1,0:T(8,128)(2,1)S(1)} %collective-permute-done.19.refs_2_, ...), custom_call_target="tpu_custom_call" | custom-call | flops 2334130176 | bytes 7335936 | tf_op jit(solution)/shard_map/pallas_call | solution.py:511
  139.2 2.0 collective-permute-start.26
  143.3 5.1 %collective-permute-done.38 = bf16[21,128,128]{2,1,0:T(8,128)(2,1)S(1)} collective-permute-done((bf16[21,128,128]{2,1,0:T(8,128)(2,1)S(1)}, bf16[21,128,128]{2,1,0:T(8,128)(2,1)S(1)}, u32[]{:S(2)}, u32[]{:S(2)}) %collective-permute-start.38) | collective-permute-done | bytes 688160 | tf_op jit(solution)/shard_map/ppermute | solution.py:61
  150.9 4.8 %collective-permute-done = bf16[5,128,128]{2,1,0:T(8,128)(2,1)S(1)} collective-permute-done((bf16[5,128,128]{2,1,0:T(8,128)(2,1)S(1)}, bf16[5,128,128]{2,1,0:T(8,128)(2,1)S(1)}, u32[]{:S(2)}, u32[]{:S(2)}) %collective-permute-start) | collective-permute-done | bytes 163872 | tf_op jit(solution)/shard_map/ppermute | solution.py:51
  155.7 3.7 %collective-permute-start.3 = (bf16[128,128]{1,0:T(8,128)(2,1)S(1)}, bf16[128,128]{1,0:T(8,128)(2,1)S(1)}, u32[]{:S(2)}, u32[]{:S(2)}) collective-permute-start(bf16[128,128]{1,0:T(8,128)(2,1)S(1)} %get-tuple-element.180.centre_ref), channel_id=1, source_target_pairs={{9,0},{3,8},{11,1},{2,9},{10,3},{0,11},{8,2},{1,10},{13,4},{7,12},... | collective-permute-start | bytes 98312 | tf_op jit(solution)/shard_map/ppermute | solution.py:61
  159.3 6.5 %collective-permute-start.2 = (bf16[128,128]{1,0:T(8,128)(2,1)S(1)}, bf16[128,128]{1,0:T(8,128)(2,1)S(1)}, u32[]{:S(2)}, u32[]{:S(2)}) collective-permute-start(bf16[128,128]{1,0:T(8,128)(2,1)S(1)} %get-tuple-element.180.centre_ref), channel_id=1, source_target_pairs={{1,0},{9,8},{3,1},{11,9},{2,3},{10,11},{0,2},{8,10},{5,4},{13,12},... | collective-permute-start | bytes 98312 | tf_op jit(solution)/shard_map/ppermute | solution.py:61
  168.9 1.7 collective-permute-start.40
  172.1 3.7 %collective-permute-done.28.refs_4_ = bf16[21,128,128]{2,1,0:T(8,128)(2,1)S(1)} collective-permute-done((bf16[21,128,128]{2,1,0:T(8,128)(2,1)S(1)}, bf16[21,128,128]{2,1,0:T(8,128)(2,1)S(1)}, u32[]{:S(2)}, u32[]{:S(2)}) %collective-permute-start.28) | collective-permute-done | bytes 688160 | tf_op jit(solution)/shard_map/ppermute | solution.py:61
  175.8 2.2 collective-permute-start.30
  178.0 5.2 %collective-permute-done.29.refs_5_ = bf16[21,128,128]{2,1,0:T(8,128)(2,1)S(1)} collective-permute-done((bf16[21,128,128]{2,1,0:T(8,128)(2,1)S(1)}, bf16[21,128,128]{2,1,0:T(8,128)(2,1)S(1)}, u32[]{:S(2)}, u32[]{:S(2)}) %collective-permute-start.29) | collective-permute-done | bytes 688160 | tf_op jit(solution)/shard_map/ppermute | solution.py:61
  183.2 2.2 collective-permute-start.31
  185.8 1.6 collective-permute-done.40.moved_ref
  187.8 5.2 %shard_map.150 = (bf16[21,128,128]{2,1,0:T(8,128)(2,1)S(1)}, bf16[21,128,128]{2,1,0:T(8,128)(2,1)S(1)}, bf16[21,128,128]{2,1,0:T(8,128)(2,1)S(1)}, bf16[21,128,1...) custom-call(bf16[21,128,128]{2,1,0:T(8,128)(2,1)S(1)} %get-tuple-ele, ...), custom_call_target="tpu_custom_call" | custom-call | flops 2334130176 | bytes 3076096 | tf_op jit(solution)/shard_map/pallas_call | solution.py:511
  193.5 1.7 collective-permute-start.4
  195.6 3.7 %collective-permute-done.4.refs_4_ = bf16[4,128,128]{2,1,0:T(8,128)(2,1)S(1)} collective-permute-done((bf16[4,128,128]{2,1,0:T(8,128)(2,1)S(1)}, bf16[4,128,128]{2,1,0:T(8,128)(2,1)S(1)}, u32[]{:S(2)}, u32[]{:S(2)}) %collective-permute-start.4) | collective-permute-done | bytes 131104 | tf_op jit(solution)/shard_map/ppermute | solution.py:61
  199.4 2.4 collective-permute-start.44
  201.7 3.5 %collective-permute-done.7.refs_7_ = bf16[4,128,128]{2,1,0:T(8,128)(2,1)S(1)} collective-permute-done((bf16[4,128,128]{2,1,0:T(8,128)(2,1)S(1)}, bf16[4,128,128]{2,1,0:T(8,128)(2,1)S(1)}, u32[]{:S(2)}, u32[]{:S(2)}) %collective-permute-start.7) | collective-permute-done | bytes 131104 | tf_op jit(solution)/shard_map/ppermute | solution.py:61
  205.3 2.5 collective-permute-done.6.refs_6_
  207.8 6.3 %shard_map.146 = (bf16[21,128,128]{2,1,0:T(8,128)(2,1)S(1)}, bf16[21,128,128]{2,1,0:T(8,128)(2,1)S(1)}, f32[8,128]{1,0:T(8,128)S(1)}) custom-call(bf16[21,128,128]{2,1,0:T(8,128)(2,1)S(1)} %get-tuple-element.97.refs_0_, bf16[21,128,128]{2,1,0:T(8,128)(2,1)S(1)} %get-tuple-element.98.refs_1_, bf16[21,128,128]{2,1,0:T(8,128)(2,1)S(1)} %collective-permute-done.26.refs_2_, ...), custom_call_target="tpu_custom_call" | custom-call | flops 2334130176 | bytes 7335936 | tf_op jit(solution)/shard_map/pallas_call | solution.py:511
  214.1 2.2 collective-permute-start.32
  218.2 6.6 %collective-permute-done.32.refs_2_.refs_10_ = bf16[21,128,128]{2,1,0:T(8,128)(2,1)S(1)} collective-permute-done((bf16[21,128,128]{2,1,0:T(8,128)(2,1)S(1)}, bf16[21,128,128]{2,1,0:T(8,128)(2,1)S(1)}, u32[]{:S(2)}, u32[]{:S(2)}) %collective-permute-start.32) | collective-permute-done | bytes 688160 | tf_op jit(solution)/shard_map/ppermute | solution.py:61
  224.8 2.2 collective-permute-start.34
  227.0 5.2 %collective-permute-done.33.refs_3_.refs_11_ = bf16[21,128,128]{2,1,0:T(8,128)(2,1)S(1)} collective-permute-done((bf16[21,128,128]{2,1,0:T(8,128)(2,1)S(1)}, bf16[21,128,128]{2,1,0:T(8,128)(2,1)S(1)}, u32[]{:S(2)}, u32[]{:S(2)}) %collective-permute-start.33) | collective-permute-done | bytes 688160 | tf_op jit(solution)/shard_map/ppermute | solution.py:61
  232.2 2.2 collective-permute-start.35
  234.4 1.3 fusion.9
  237.9 1.7 collective-permute-done.34.refs_4_.refs_12_
  239.6 2.2 collective-permute-start.36
  241.8 5.2 %collective-permute-done.35.refs_5_.refs_13_ = bf16[21,128,128]{2,1,0:T(8,128)(2,1)} collective-permute-done((bf16[21,128,128]{2,1,0:T(8,128)(2,1)S(1)}, bf16[21,128,128]{2,1,0:T(8,128)(2,1)}, u32[]{:S(2)}, u32[]{:S(2)}) %collective-permute-start.35) | collective-permute-done | bytes 688160 | tf_op jit(solution)/shard_map/ppermute | solution.py:61
  247.0 2.2 collective-permute-start.37
  251.2 2.5 collective-permute-done.46.moved_ref
  254.2 5.2 %shard_map.153.refs_13_ = bf16[21504,128]{1,0:T(8,128)(2,1)S(1)} custom-call(bf16[21,128,128]{2,1,0:T(8,128)(2,1)S(1)} %get-tuple-element.137.refs_0_, bf16[21,128,128]{2,1,0:T(8,128)(2,1)S(1)} %get-tuple-element.138.refs_1_, bf16[1360,384]{1,0:T(8,128)(2,1)S(1)} %copy-done.21, bf16[4,128,128]{2,1,0:T(8,128)(2,1)S(1)} %get-tuple-element.140.refs_3_, ...), custom_call_target="tpu_custom_call" | custom-call | flops 2334130176 | bytes 3076096 | tf_op jit(solution)/shard_map/pallas_call | solution.py:511
  259.4 2.4 collective-permute-done.37.refs_7_.refs_15_
  261.8 3.8 %shard_map.154 = (f32[4,128,128]{2,1,0:T(8,128)S(1)}, bf16[528,128]{1,0:T(8,128)(2,1)S(1)}, f32[1,128]{1,0:T(1,128)S(1)}) custom-call(bf16[21,128,128]{2,1,0:T(8,128)(2,1)S(1)} %copy-done.1, bf16[21,128,128]{2,1,0:T(8,128)(2,1)S(1)} %copy-done.3, bf16[21,128,128]{2,1,0:T(8,128)(2,1)S(1)} %copy-done.5, bf16[21,128,128]{2,1,0:T(8,128)(2,1)S(1)} %copy-done.7, ...), custom_call_target="tpu_custom_call" | custom-call | flops 704643072 | bytes 11292672 | tf_op jit(solution)/shard_map/pallas_call | solution.py:511
  270.8 1.7 collective-permute-start.53
  272.5 1.6 collective-permute-start.52
  274.1 3.0 collective-permute-done.52
  280.5 8.9 %shard_map.155 = (f32[4,128,128]{2,1,0:T(8,128)S(1)}, f32[1,128]{1,0:T(1,128)S(1)}) custom-call(bf16[21,128,128]{2,1,0:T(8,128)(2,1)S(1)} %copy-done.11, bf16[21,128,128]{2,1,0:T(8,128)(2,1)S(1)} %copy-done.9, bf16[1360,384]{1,0:T(8,128)(2,1)S(1)} %copy-done.22, bf16[528,128]{1,0:T(8,128)(2,1)S(1)} %get-tuple-element.147.refs_3_, ...), custom_call_target="tpu_custom_call" | custom-call | flops 3038773248 | bytes 8601600 | tf_op jit(solution)/shard_map/pallas_call | solution.py:511
  293.2 1.7 collective-permute-start.62
  295.2 1.6 collective-permute-start.59
  296.8 2.9 collective-permute-done.59
  301.0 1.5 collective-permute-done.61
  303.6 4.8 %shard_map.157 = bf16[4,128,128]{2,1,0:T(8,128)(2,1)S(1)} custom-call(f32[4,2,128,128]{3,2,1,0:T(8,128)S(1)} %pad_maximum_fusion.1.both_ref, f32[8,128]{1,0:T(8,128)S(1)} %maximum_select_fusion.1.table_ref, bf16[128,128]{1,0:T(8,128)(2,1)S(1)} %get-tuple-element.180.centre_ref), custom_call_target="tpu_custom_call" | custom-call | flops 1258291200 | bytes 561152 | tf_op jit(solution)/shard_map/pallas_call | solution.py:511
  309.5 8.0 %collective-permute-start.67 = (bf16[128,128]{1,0:T(8,128)(2,1)S(1)}, bf16[128,128]{1,0:T(8,128)(2,1)S(1)}, u32[]{:S(2)}, u32[]{:S(2)}) collective-permute-start(bf16[128,128]{1,0:T(8,128)(2,1)S(1)} %get-tuple-element.182), channel_id=1, source_target_pairs={{0,21},{8,22},{1,23},{9,16},{3,17},{11,18},{2,19},{10,20},{4,29},{... | collective-permute-start | bytes 98312 | tf_op jit(solution)/shard_map/ppermute | solution.py:56
  318.1 2.5 collective-permute-start.65
  (216 shorter events, 52.3 us)
Async XLA Ops:
  3.6 36.1 %collective-permute-start.8 = (bf16[50,128,128]{2,1,0:T(8,128)(2,1)}, bf16[50,128,128]{2,1,0:T(8,128)(2,1)S(1)}, u32[]{:S(2)}, u32[]{:S(2)}) collective-permute-start(bf16[50,128,128]{2,1,0:T(8,128)(2,1)} %pad_maximum_fusion), channel_id=1, source_target_pairs={{0,0},{1,8},{2,1},{3,9},{4,3},{5,11},{6,2},{7,10},{8,4},{9,12},{10... | collective-permute-start | bytes 4915208 | tf_op jit(solution)/shard_map/ppermute | solution.py:51
  5.7 24.3 %collective-permute-start.13 = (bf16[4,128,128]{2,1,0:T(8,128)(2,1)S(1)}, bf16[4,128,128]{2,1,0:T(8,128)(2,1)S(1)}, u32[]{:S(2)}, u32[]{:S(2)}) collective-permute-start(bf16[4,128,128]{2,1,0:T(8,128)(2,1)S(1)} %bitcast.191), channel_id=1, source_target_pairs={{8,0},{9,8},{10,1},{11,9},{12,3},{13,11},{14,2},{15,10},{16,4},{17... | collective-permute-start | bytes 393224 | tf_op jit(solution)/shard_map/ppermute | solution.py:51
  11.9 18.0 %collective-permute-start.14 = (bf16[4,128,128]{2,1,0:T(8,128)(2,1)}, bf16[4,128,128]{2,1,0:T(8,128)(2,1)S(1)}, u32[]{:S(2)}, u32[]{:S(2)}) collective-permute-start(bf16[4,128,128]{2,1,0:T(8,128)(2,1)} %bitcast.7), channel_id=1, source_target_pairs={{24,0},{25,8},{26,1},{27,9},{28,3},{29,11},{30,2},{31,10},{0,4},{1... | collective-permute-start | bytes 393224 | tf_op jit(solution)/shard_map/ppermute | solution.py:51
  30.0 5.9 %collective-permute-start.16 = (bf16[8,128,128]{2,1,0:T(8,128)(2,1)S(1)}, bf16[8,128,128]{2,1,0:T(8,128)(2,1)S(1)}, u32[]{:S(2)}, u32[]{:S(2)}) collective-permute-start(bf16[8,128,128]{2,1,0:T(8,128)(2,1)S(1)} %constant_dynamic-update-slice_fusion), channel_id=1, source_target_pairs={{10,0},{0,8},{8,1},{1,9},{9,3},{3,11},{11,2},{2,10},{14,4},{4,12},... | collective-permute-start | bytes 786440 | tf_op jit(solution)/shard_map/ppermute | solution.py:61
  30.4 5.5 %collective-permute-start.15 = (bf16[8,128,128]{2,1,0:T(8,128)(2,1)S(1)}, bf16[8,128,128]{2,1,0:T(8,128)(2,1)S(1)}, u32[]{:S(2)}, u32[]{:S(2)}) collective-permute-start(bf16[8,128,128]{2,1,0:T(8,128)(2,1)S(1)} %constant_dynamic-update-slice_fusion), channel_id=1, source_target_pairs={{8,0},{1,8},{9,1},{3,9},{11,3},{2,11},{10,2},{0,10},{12,4},{5,12},... | collective-permute-start | bytes 786440 | tf_op jit(solution)/shard_map/ppermute | solution.py:61
  35.9 28.0 %collective-permute-start.18 = (bf16[8,128,128]{2,1,0:T(8,128)(2,1)S(1)}, bf16[8,128,128]{2,1,0:T(8,128)(2,1)S(1)}, u32[]{:S(2)}, u32[]{:S(2)}) collective-permute-start(bf16[8,128,128]{2,1,0:T(8,128)(2,1)S(1)} %collective-permute-done.16), channel_id=1, source_target_pairs={{10,0},{0,8},{8,1},{1,9},{9,3},{3,11},{11,2},{2,10},{14,4},{4,12},... | collective-permute-start | bytes 786440 | tf_op jit(solution)/shard_map/ppermute | solution.py:61
  35.9 26.9 %collective-permute-start.17 = (bf16[8,128,128]{2,1,0:T(8,128)(2,1)S(1)}, bf16[8,128,128]{2,1,0:T(8,128)(2,1)S(1)}, u32[]{:S(2)}, u32[]{:S(2)}) collective-permute-start(bf16[8,128,128]{2,1,0:T(8,128)(2,1)S(1)} %collective-permute-done.15), channel_id=1, source_target_pairs={{8,0},{1,8},{9,1},{3,9},{11,3},{2,11},{10,2},{0,10},{12,4},{5,12},... | collective-permute-start | bytes 786440 | tf_op jit(solution)/shard_map/ppermute | solution.py:61
  39.8 53.7 %collective-permute-start.21 = (bf16[42,128,128]{2,1,0:T(8,128)(2,1)S(1)}, bf16[42,128,128]{2,1,0:T(8,128)(2,1)S(1)}, u32[]{:S(2)}, u32[]{:S(2)}) collective-permute-start(bf16[42,128,128]{2,1,0:T(8,128)(2,1)S(1)} %bitcast.203), channel_id=1, source_target_pairs={{0,0},{1,8},{2,1},{3,9},{4,3},{5,11},{6,2},{7,10},{8,4},{9,12},{10... | collective-permute-start | bytes 4128776 | tf_op jit(solution)/shard_map/ppermute | solution.py:51
  40.9 37.6 %collective-permute-start.19 = (bf16[21,128,128]{2,1,0:T(8,128)(2,1)S(1)}, bf16[21,128,128]{2,1,0:T(8,128)(2,1)S(1)}, u32[]{:S(2)}, u32[]{:S(2)}) collective-permute-start(bf16[21,128,128]{2,1,0:T(8,128)(2,1)S(1)} %get-tuple-element.85.refs_0_), channel_id=1, source_target_pairs={{8,0},{1,8},{9,1},{3,9},{11,3},{2,11},{10,2},{0,10},{12,4},{5,12},... | collective-permute-start | bytes 2064392 | tf_op jit(solution)/shard_map/ppermute | solution.py:61
  62.6 26.1 %collective-permute-start.20 = (bf16[21,128,128]{2,1,0:T(8,128)(2,1)S(1)}, bf16[21,128,128]{2,1,0:T(8,128)(2,1)S(1)}, u32[]{:S(2)}, u32[]{:S(2)}) collective-permute-start(bf16[21,128,128]{2,1,0:T(8,128)(2,1)S(1)} %get-tuple-element.86.refs_1_), channel_id=1, source_target_pairs={{8,0},{1,8},{9,1},{3,9},{11,3},{2,11},{10,2},{0,10},{12,4},{5,12},... | collective-permute-start | bytes 2064392 | tf_op jit(solution)/shard_map/ppermute | solution.py:61
  63.8 27.8 %collective-permute-start.9 = (bf16[8,128,128]{2,1,0:T(8,128)(2,1)S(1)}, bf16[8,128,128]{2,1,0:T(8,128)(2,1)S(1)}, u32[]{:S(2)}, u32[]{:S(2)}) collective-permute-start(bf16[8,128,128]{2,1,0:T(8,128)(2,1)S(1)} %concatenate.64), channel_id=1, source_target_pairs={{8,0},{1,8},{9,1},{3,9},{11,3},{2,11},{10,2},{0,10},{12,4},{5,12},... | collective-permute-start | bytes 786440 | tf_op jit(solution)/shard_map/ppermute | solution.py:61
  63.8 29.6 %collective-permute-start.10 = (bf16[8,128,128]{2,1,0:T(8,128)(2,1)S(1)}, bf16[8,128,128]{2,1,0:T(8,128)(2,1)S(1)}, u32[]{:S(2)}, u32[]{:S(2)}) collective-permute-start(bf16[8,128,128]{2,1,0:T(8,128)(2,1)S(1)} %concatenate.64), channel_id=1, source_target_pairs={{10,0},{0,8},{8,1},{1,9},{9,3},{3,11},{11,2},{2,10},{14,4},{4,12},... | collective-permute-start | bytes 786440 | tf_op jit(solution)/shard_map/ppermute | solution.py:61
  78.5 20.4 %collective-permute-start.22 = (bf16[21,128,128]{2,1,0:T(8,128)(2,1)S(1)}, bf16[21,128,128]{2,1,0:T(8,128)(2,1)S(1)}, u32[]{:S(2)}, u32[]{:S(2)}) collective-permute-start(bf16[21,128,128]{2,1,0:T(8,128)(2,1)S(1)} %collective-permute-done.19.refs_2_), channel_id=1, source_target_pairs={{8,0},{1,8},{9,1},{3,9},{11,3},{2,11},{10,2},{0,10},{12,4},{5,12},... | collective-permute-start | bytes 2064392 | tf_op jit(solution)/shard_map/ppermute | solution.py:61
  88.7 17.6 %collective-permute-start.23 = (bf16[21,128,128]{2,1,0:T(8,128)(2,1)S(1)}, bf16[21,128,128]{2,1,0:T(8,128)(2,1)S(1)}, u32[]{:S(2)}, u32[]{:S(2)}) collective-permute-start(bf16[21,128,128]{2,1,0:T(8,128)(2,1)S(1)} %collective-permute-done.20.refs_3_), channel_id=1, source_target_pairs={{8,0},{1,8},{9,1},{3,9},{11,3},{2,11},{10,2},{0,10},{12,4},{5,12},... | collective-permute-start | bytes 2064392 | tf_op jit(solution)/shard_map/ppermute | solution.py:61
  91.6 17.5 %collective-permute-start.11 = (bf16[8,128,128]{2,1,0:T(8,128)(2,1)S(1)}, bf16[8,128,128]{2,1,0:T(8,128)(2,1)S(1)}, u32[]{:S(2)}, u32[]{:S(2)}) collective-permute-start(bf16[8,128,128]{2,1,0:T(8,128)(2,1)S(1)} %collective-permute-done.9), channel_id=1, source_target_pairs={{8,0},{1,8},{9,1},{3,9},{11,3},{2,11},{10,2},{0,10},{12,4},{5,12},... | collective-permute-start | bytes 786440 | tf_op jit(solution)/shard_map/ppermute | solution.py:61
  93.5 15.7 %collective-permute-start.12 = (bf16[8,128,128]{2,1,0:T(8,128)(2,1)S(1)}, bf16[8,128,128]{2,1,0:T(8,128)(2,1)S(1)}, u32[]{:S(2)}, u32[]{:S(2)}) collective-permute-start(bf16[8,128,128]{2,1,0:T(8,128)(2,1)S(1)} %collective-permute-done.10), channel_id=1, source_target_pairs={{10,0},{0,8},{8,1},{1,9},{9,3},{3,11},{11,2},{2,10},{14,4},{4,12},... | collective-permute-start | bytes 786440 | tf_op jit(solution)/shard_map/ppermute | solution.py:61
  106.3 10.4 %collective-permute-start.24 = (bf16[21,128,128]{2,1,0:T(8,128)(2,1)S(1)}, bf16[21,128,128]{2,1,0:T(8,128)(2,1)S(1)}, u32[]{:S(2)}, u32[]{:S(2)}) collective-permute-start(bf16[21,128,128]{2,1,0:T(8,128)(2,1)S(1)} %collective-permute-done.22.refs_4_), channel_id=1, source_target_pairs={{8,0},{1,8},{9,1},{3,9},{11,3},{2,11},{10,2},{0,10},{12,4},{5,12},... | collective-permute-start | bytes 2064392 | tf_op jit(solution)/shard_map/ppermute | solution.py:61
  108.2 15.8 %collective-permute-start.25 = (bf16[21,128,128]{2,1,0:T(8,128)(2,1)S(1)}, bf16[21,128,128]{2,1,0:T(8,128)(2,1)S(1)}, u32[]{:S(2)}, u32[]{:S(2)}) collective-permute-start(bf16[21,128,128]{2,1,0:T(8,128)(2,1)S(1)} %collective-permute-done.23.refs_5_), channel_id=1, source_target_pairs={{8,0},{1,8},{9,1},{3,9},{11,3},{2,11},{10,2},{0,10},{12,4},{5,12},... | collective-permute-start | bytes 2064392 | tf_op jit(solution)/shard_map/ppermute | solution.py:61
  130.5 11.6 %collective-permute-start.41 = (bf16[21,128,128]{2,1,0:T(8,128)(2,1)S(1)}, bf16[21,128,128]{2,1,0:T(8,128)(2,1)S(1)}, u32[]{:S(2)}, u32[]{:S(2)}) collective-permute-start(bf16[21,128,128]{2,1,0:T(8,128)(2,1)S(1)} %fusion.17), channel_id=1, source_target_pairs={{10,0},{0,8},{8,1},{1,9},{9,3},{3,11},{11,2},{2,10},{14,4},{4,12},... | collective-permute-start | bytes 2064392 | tf_op jit(solution)/shard_map/ppermute | solution.py:61
  131.7 16.7 %collective-permute-start.38 = (bf16[21,128,128]{2,1,0:T(8,128)(2,1)S(1)}, bf16[21,128,128]{2,1,0:T(8,128)(2,1)S(1)}, u32[]{:S(2)}, u32[]{:S(2)}) collective-permute-start(bf16[21,128,128]{2,1,0:T(8,128)(2,1)S(1)} %fusion.16), channel_id=1, source_target_pairs={{10,0},{0,8},{8,1},{1,9},{9,3},{3,11},{11,2},{2,10},{14,4},{4,12},... | collective-permute-start | bytes 2064392 | tf_op jit(solution)/shard_map/ppermute | solution.py:61
  139.2 27.7 %collective-permute-start.26 = (bf16[21,128,128]{2,1,0:T(8,128)(2,1)S(1)}, bf16[21,128,128]{2,1,0:T(8,128)(2,1)S(1)}, u32[]{:S(2)}, u32[]{:S(2)}) collective-permute-start(bf16[21,128,128]{2,1,0:T(8,128)(2,1)S(1)} %get-tuple-element.97.refs_0_), channel_id=1, source_target_pairs={{8,0},{1,8},{9,1},{3,9},{11,3},{2,11},{10,2},{0,10},{12,4},{5,12},... | collective-permute-start | bytes 2064392 | tf_op jit(solution)/shard_map/ppermute | solution.py:61
  141.2 25.8 %collective-permute-start.27 = (bf16[21,128,128]{2,1,0:T(8,128)(2,1)S(1)}, bf16[21,128,128]{2,1,0:T(8,128)(2,1)S(1)}, u32[]{:S(2)}, u32[]{:S(2)}) collective-permute-start(bf16[21,128,128]{2,1,0:T(8,128)(2,1)S(1)} %get-tuple-element.98.refs_1_), channel_id=1, source_target_pairs={{8,0},{1,8},{9,1},{3,9},{11,3},{2,11},{10,2},{0,10},{12,4},{5,12},... | collective-permute-start | bytes 2064392 | tf_op jit(solution)/shard_map/ppermute | solution.py:61
  143.3 16.1 %collective-permute-start.42 = (bf16[21,128,128]{2,1,0:T(8,128)(2,1)S(1)}, bf16[21,128,128]{2,1,0:T(8,128)(2,1)S(1)}, u32[]{:S(2)}, u32[]{:S(2)}) collective-permute-start(bf16[21,128,128]{2,1,0:T(8,128)(2,1)S(1)} %fusion.12), channel_id=1, source_target_pairs={{10,0},{0,8},{8,1},{1,9},{9,3},{3,11},{11,2},{2,10},{14,4},{4,12},... | collective-permute-start | bytes 2064392 | tf_op jit(solution)/shard_map/ppermute | solution.py:61
  149.6 17.5 %collective-permute-start.39 = (bf16[21,128,128]{2,1,0:T(8,128)(2,1)S(1)}, bf16[21,128,128]{2,1,0:T(8,128)(2,1)S(1)}, u32[]{:S(2)}, u32[]{:S(2)}) collective-permute-start(bf16[21,128,128]{2,1,0:T(8,128)(2,1)S(1)} %fusion.14), channel_id=1, source_target_pairs={{10,0},{0,8},{8,1},{1,9},{9,3},{3,11},{11,2},{2,10},{14,4},{4,12},... | collective-permute-start | bytes 2064392 | tf_op jit(solution)/shard_map/ppermute | solution.py:61
  149.7 5.9 %collective-permute-start = (bf16[5,128,128]{2,1,0:T(8,128)(2,1)S(1)}, bf16[5,128,128]{2,1,0:T(8,128)(2,1)S(1)}, u32[]{:S(2)}, u32[]{:S(2)}) collective-permute-start(bf16[5,128,128]{2,1,0:T(8,128)(2,1)S(1)} %pad_maximum_fusion.3), channel_id=1, source_target_pairs={{16,0},{17,8},{18,1},{19,9},{20,3},{21,11},{22,2},{23,10},{24,4},{... | collective-permute-start | bytes 491528 | tf_op jit(solution)/shard_map/ppermute | solution.py:51
  155.7 13.0 %collective-permute-start.3 = (bf16[128,128]{1,0:T(8,128)(2,1)S(1)}, bf16[128,128]{1,0:T(8,128)(2,1)S(1)}, u32[]{:S(2)}, u32[]{:S(2)}) collective-permute-start(bf16[128,128]{1,0:T(8,128)(2,1)S(1)} %get-tuple-element.180.centre_ref), channel_id=1, source_target_pairs={{9,0},{3,8},{11,1},{2,9},{10,3},{0,11},{8,2},{1,10},{13,4},{7,12},... | collective-permute-start | bytes 98312 | tf_op jit(solution)/shard_map/ppermute | solution.py:61
  159.3 9.5 %collective-permute-start.2 = (bf16[128,128]{1,0:T(8,128)(2,1)S(1)}, bf16[128,128]{1,0:T(8,128)(2,1)S(1)}, u32[]{:S(2)}, u32[]{:S(2)}) collective-permute-start(bf16[128,128]{1,0:T(8,128)(2,1)S(1)} %get-tuple-element.180.centre_ref), channel_id=1, source_target_pairs={{1,0},{9,8},{3,1},{11,9},{2,3},{10,11},{0,2},{8,10},{5,4},{13,12},... | collective-permute-start | bytes 98312 | tf_op jit(solution)/shard_map/ppermute | solution.py:61
  167.0 8.8 %collective-permute-start.28 = (bf16[21,128,128]{2,1,0:T(8,128)(2,1)S(1)}, bf16[21,128,128]{2,1,0:T(8,128)(2,1)S(1)}, u32[]{:S(2)}, u32[]{:S(2)}) collective-permute-start(bf16[21,128,128]{2,1,0:T(8,128)(2,1)S(1)} %collective-permute-done.26.refs_2_), channel_id=1, source_target_pairs={{8,0},{1,8},{9,1},{3,9},{11,3},{2,11},{10,2},{0,10},{12,4},{5,12},... | collective-permute-start | bytes 2064392 | tf_op jit(solution)/shard_map/ppermute | solution.py:61
  167.1 16.1 %collective-permute-start.29 = (bf16[21,128,128]{2,1,0:T(8,128)(2,1)S(1)}, bf16[21,128,128]{2,1,0:T(8,128)(2,1)S(1)}, u32[]{:S(2)}, u32[]{:S(2)}) collective-permute-start(bf16[21,128,128]{2,1,0:T(8,128)(2,1)S(1)} %collective-permute-done.27.refs_3_), channel_id=1, source_target_pairs={{8,0},{1,8},{9,1},{3,9},{11,3},{2,11},{10,2},{0,10},{12,4},{5,12},... | collective-permute-start | bytes 2064392 | tf_op jit(solution)/shard_map/ppermute | solution.py:61
  168.7 16.8 %collective-permute-start.43 = (bf16[21,128,128]{2,1,0:T(8,128)(2,1)S(1)}, bf16[21,128,128]{2,1,0:T(8,128)(2,1)S(1)}, u32[]{:S(2)}, u32[]{:S(2)}) collective-permute-start(bf16[21,128,128]{2,1,0:T(8,128)(2,1)S(1)} %fusion.13), channel_id=1, source_target_pairs={{10,0},{0,8},{8,1},{1,9},{9,3},{3,11},{11,2},{2,10},{14,4},{4,12},... | collective-permute-start | bytes 2064392 | tf_op jit(solution)/shard_map/ppermute | solution.py:61
  168.9 18.5 %collective-permute-start.40 = (bf16[21,128,128]{2,1,0:T(8,128)(2,1)S(1)}, bf16[21,128,128]{2,1,0:T(8,128)(2,1)S(1)}, u32[]{:S(2)}, u32[]{:S(2)}) collective-permute-start(bf16[21,128,128]{2,1,0:T(8,128)(2,1)S(1)} %fusion.15), channel_id=1, source_target_pairs={{10,0},{0,8},{8,1},{1,9},{9,3},{3,11},{11,2},{2,10},{14,4},{4,12},... | collective-permute-start | bytes 2064392 | tf_op jit(solution)/shard_map/ppermute | solution.py:61
  170.8 24.5 %collective-permute-start.5 = (bf16[4,128,128]{2,1,0:T(8,128)(2,1)S(1)}, bf16[4,128,128]{2,1,0:T(8,128)(2,1)S(1)}, u32[]{:S(2)}, u32[]{:S(2)}) collective-permute-start(bf16[4,128,128]{2,1,0:T(8,128)(2,1)S(1)} %get-tuple-element.140.refs_3_), channel_id=1, source_target_pairs={{10,0},{0,8},{8,1},{1,9},{9,3},{3,11},{11,2},{2,10},{14,4},{4,12},... | collective-permute-start | bytes 393224 | tf_op jit(solution)/shard_map/ppermute | solution.py:61
  175.8 32.0 %collective-permute-start.30 = (bf16[21,128,128]{2,1,0:T(8,128)(2,1)S(1)}, bf16[21,128,128]{2,1,0:T(8,128)(2,1)S(1)}, u32[]{:S(2)}, u32[]{:S(2)}) collective-permute-start(bf16[21,128,128]{2,1,0:T(8,128)(2,1)S(1)} %collective-permute-done.28.refs_4_), channel_id=1, source_target_pairs={{8,0},{1,8},{9,1},{3,9},{11,3},{2,11},{10,2},{0,10},{12,4},{5,12},... | collective-permute-start | bytes 2064392 | tf_op jit(solution)/shard_map/ppermute | solution.py:61
  183.2 24.6 %collective-permute-start.31 = (bf16[21,128,128]{2,1,0:T(8,128)(2,1)S(1)}, bf16[21,128,128]{2,1,0:T(8,128)(2,1)S(1)}, u32[]{:S(2)}, u32[]{:S(2)}) collective-permute-start(bf16[21,128,128]{2,1,0:T(8,128)(2,1)S(1)} %collective-permute-done.29.refs_5_), channel_id=1, source_target_pairs={{8,0},{1,8},{9,1},{3,9},{11,3},{2,11},{10,2},{0,10},{12,4},{5,12},... | collective-permute-start | bytes 2064392 | tf_op jit(solution)/shard_map/ppermute | solution.py:61
  193.4 23.0 %collective-permute-start.47 = (bf16[21,128,128]{2,1,0:T(8,128)(2,1)S(1)}, bf16[21,128,128]{2,1,0:T(8,128)(2,1)S(1)}, u32[]{:S(2)}, u32[]{:S(2)}) collective-permute-start(bf16[21,128,128]{2,1,0:T(8,128)(2,1)S(1)} %fusion.19), channel_id=1, source_target_pairs={{10,0},{0,8},{8,1},{1,9},{9,3},{3,11},{11,2},{2,10},{14,4},{4,12},... | collective-permute-start | bytes 2064392 | tf_op jit(solution)/shard_map/ppermute | solution.py:61
  193.5 5.9 %collective-permute-start.4 = (bf16[4,128,128]{2,1,0:T(8,128)(2,1)S(1)}, bf16[4,128,128]{2,1,0:T(8,128)(2,1)S(1)}, u32[]{:S(2)}, u32[]{:S(2)}) collective-permute-start(bf16[4,128,128]{2,1,0:T(8,128)(2,1)S(1)} %get-tuple-element.140.refs_3_), channel_id=1, source_target_pairs={{8,0},{1,8},{9,1},{3,9},{11,3},{2,11},{10,2},{0,10},{12,4},{5,12},... | collective-permute-start | bytes 393224 | tf_op jit(solution)/shard_map/ppermute | solution.py:61
  195.2 10.0 %collective-permute-start.7 = (bf16[4,128,128]{2,1,0:T(8,128)(2,1)S(1)}, bf16[4,128,128]{2,1,0:T(8,128)(2,1)S(1)}, u32[]{:S(2)}, u32[]{:S(2)}) collective-permute-start(bf16[4,128,128]{2,1,0:T(8,128)(2,1)S(1)} %collective-permute-done.5.refs_5_), channel_id=1, source_target_pairs={{10,0},{0,8},{8,1},{1,9},{9,3},{3,11},{11,2},{2,10},{14,4},{4,12},... | collective-permute-start | bytes 393224 | tf_op jit(solution)/shard_map/ppermute | solution.py:61
  199.4 18.0 %collective-permute-start.44 = (bf16[21,128,128]{2,1,0:T(8,128)(2,1)S(1)}, bf16[21,128,128]{2,1,0:T(8,128)(2,1)S(1)}, u32[]{:S(2)}, u32[]{:S(2)}) collective-permute-start(bf16[21,128,128]{2,1,0:T(8,128)(2,1)S(1)} %fusion.18), channel_id=1, source_target_pairs={{10,0},{0,8},{8,1},{1,9},{9,3},{3,11},{11,2},{2,10},{14,4},{4,12},... | collective-permute-start | bytes 2064392 | tf_op jit(solution)/shard_map/ppermute | solution.py:61
  214.1 10.7 %collective-permute-start.32 = (bf16[21,128,128]{2,1,0:T(8,128)(2,1)S(1)}, bf16[21,128,128]{2,1,0:T(8,128)(2,1)S(1)}, u32[]{:S(2)}, u32[]{:S(2)}) collective-permute-start(bf16[21,128,128]{2,1,0:T(8,128)(2,1)S(1)} %get-tuple-element.107.refs_0_.refs_8_), channel_id=1, source_target_pairs={{8,0},{1,8},{9,1},{3,9},{11,3},{2,11},{10,2},{0,10},{12,4},{5,12},... | collective-permute-start | bytes 2064392 | tf_op jit(solution)/shard_map/ppermute | solution.py:61
  216.4 15.8 %collective-permute-start.33 = (bf16[21,128,128]{2,1,0:T(8,128)(2,1)S(1)}, bf16[21,128,128]{2,1,0:T(8,128)(2,1)S(1)}, u32[]{:S(2)}, u32[]{:S(2)}) collective-permute-start(bf16[21,128,128]{2,1,0:T(8,128)(2,1)S(1)} %get-tuple-element.108.refs_1_.refs_9_), channel_id=1, source_target_pairs={{8,0},{1,8},{9,1},{3,9},{11,3},{2,11},{10,2},{0,10},{12,4},{5,12},... | collective-permute-start | bytes 2064392 | tf_op jit(solution)/shard_map/ppermute | solution.py:61
  216.8 17.6 %collective-permute-start.48 = (bf16[21,128,128]{2,1,0:T(8,128)(2,1)S(1)}, bf16[21,128,128]{2,1,0:T(8,128)(2,1)S(1)}, u32[]{:S(2)}, u32[]{:S(2)}) collective-permute-start(bf16[21,128,128]{2,1,0:T(8,128)(2,1)S(1)} %fusion.8), channel_id=1, source_target_pairs={{10,0},{0,8},{8,1},{1,9},{9,3},{3,11},{11,2},{2,10},{14,4},{4,12},... | collective-permute-start | bytes 2064392 | tf_op jit(solution)/shard_map/ppermute | solution.py:61
  217.8 18.0 %collective-permute-start.45 = (bf16[21,128,128]{2,1,0:T(8,128)(2,1)S(1)}, bf16[21,128,128]{2,1,0:T(8,128)(2,1)S(1)}, u32[]{:S(2)}, u32[]{:S(2)}) collective-permute-start(bf16[21,128,128]{2,1,0:T(8,128)(2,1)S(1)} %fusion.10), channel_id=1, source_target_pairs={{10,0},{0,8},{8,1},{1,9},{9,3},{3,11},{11,2},{2,10},{14,4},{4,12},... | collective-permute-start | bytes 2064392 | tf_op jit(solution)/shard_map/ppermute | solution.py:61
  224.8 14.7 %collective-permute-start.34 = (bf16[21,128,128]{2,1,0:T(8,128)(2,1)S(1)}, bf16[21,128,128]{2,1,0:T(8,128)(2,1)}, u32[]{:S(2)}, u32[]{:S(2)}) collective-permute-start(bf16[21,128,128]{2,1,0:T(8,128)(2,1)S(1)} %collective-permute-done.32.refs_2_.refs_10_), channel_id=1, source_target_pairs={{8,0},{1,8},{9,1},{3,9},{11,3},{2,11},{10,2},{0,10},{12,4},{5,12},... | collective-permute-start | bytes 2064392 | tf_op jit(solution)/shard_map/ppermute | solution.py:61
  232.2 14.7 %collective-permute-start.35 = (bf16[21,128,128]{2,1,0:T(8,128)(2,1)S(1)}, bf16[21,128,128]{2,1,0:T(8,128)(2,1)}, u32[]{:S(2)}, u32[]{:S(2)}) collective-permute-start(bf16[21,128,128]{2,1,0:T(8,128)(2,1)S(1)} %collective-permute-done.33.refs_3_.refs_11_), channel_id=1, source_target_pairs={{8,0},{1,8},{9,1},{3,9},{11,3},{2,11},{10,2},{0,10},{12,4},{5,12},... | collective-permute-start | bytes 2064392 | tf_op jit(solution)/shard_map/ppermute | solution.py:61
  235.7 15.0 %collective-permute-start.49 = (bf16[21,128,128]{2,1,0:T(8,128)(2,1)}, bf16[21,128,128]{2,1,0:T(8,128)(2,1)S(1)}, u32[]{:S(2)}, u32[]{:S(2)}) collective-permute-start(bf16[21,128,128]{2,1,0:T(8,128)(2,1)} %fusion.9), channel_id=1, source_target_pairs={{10,0},{0,8},{8,1},{1,9},{9,3},{3,11},{11,2},{2,10},{14,4},{4,12},... | collective-permute-start | bytes 2064392 | tf_op jit(solution)/shard_map/ppermute | solution.py:61
  237.0 16.7 %collective-permute-start.46 = (bf16[21,128,128]{2,1,0:T(8,128)(2,1)}, bf16[21,128,128]{2,1,0:T(8,128)(2,1)S(1)}, u32[]{:S(2)}, u32[]{:S(2)}) collective-permute-start(bf16[21,128,128]{2,1,0:T(8,128)(2,1)} %fusion.11), channel_id=1, source_target_pairs={{10,0},{0,8},{8,1},{1,9},{9,3},{3,11},{11,2},{2,10},{14,4},{4,12},... | collective-permute-start | bytes 2064392 | tf_op jit(solution)/shard_map/ppermute | solution.py:61
  239.6 19.8 %collective-permute-start.36 = (bf16[21,128,128]{2,1,0:T(8,128)(2,1)}, bf16[21,128,128]{2,1,0:T(8,128)(2,1)}, u32[]{:S(2)}, u32[]{:S(2)}) collective-permute-start(bf16[21,128,128]{2,1,0:T(8,128)(2,1)} %collective-permute-done.34.refs_4_.refs_12_), channel_id=1, source_target_pairs={{8,0},{1,8},{9,1},{3,9},{11,3},{2,11},{10,2},{0,10},{12,4},{5,12},... | collective-permute-start | bytes 2064392 | tf_op jit(solution)/shard_map/ppermute | solution.py:61
  247.0 14.9 %collective-permute-start.37 = (bf16[21,128,128]{2,1,0:T(8,128)(2,1)}, bf16[21,128,128]{2,1,0:T(8,128)(2,1)}, u32[]{:S(2)}, u32[]{:S(2)}) collective-permute-start(bf16[21,128,128]{2,1,0:T(8,128)(2,1)} %collective-permute-done.35.refs_5_.refs_13_), channel_id=1, source_target_pairs={{8,0},{1,8},{9,1},{3,9},{11,3},{2,11},{10,2},{0,10},{12,4},{5,12},... | collective-permute-start | bytes 2064392 | tf_op jit(solution)/shard_map/ppermute | solution.py:61
  267.5 5.0 %collective-permute-start.51 = (f32[2,128]{1,0:T(2,128)S(1)}, f32[2,128]{1,0:T(2,128)S(1)}, u32[]{:S(2)}, u32[]{:S(2)}) collective-permute-start(f32[2,128]{1,0:T(2,128)S(1)} %maximum_select_fusion.4), channel_id=1, source_target_pairs={{1,0},{9,8},{0,1},{8,9},{2,3},{10,11},{3,2},{11,10},{5,4},{13,12},... | collective-permute-start | bytes 3080 | tf_op jit(solution)/shard_map/ppermute | solution.py:66
  268.7 8.3 %collective-permute-start.56 = (bf16[528,128]{1,0:T(8,128)(2,1)S(1)}, bf16[528,128]{1,0:T(8,128)(2,1)}, u32[]{:S(2)}, u32[]{:S(2)}) collective-permute-start(bf16[528,128]{1,0:T(8,128)(2,1)S(1)} %get-tuple-element.147.refs_3_), channel_id=1, source_target_pairs={{2,0},{10,8},{0,1},{8,9},{1,3},{9,11},{3,2},{11,10},{6,4},{14,12},... | collective-permute-start | bytes 405512 | tf_op jit(solution)/shard_map/ppermute | solution.py:61
  269.5 7.6 %collective-permute-start.55 = (bf16[528,128]{1,0:T(8,128)(2,1)S(1)}, bf16[528,128]{1,0:T(8,128)(2,1)}, u32[]{:S(2)}, u32[]{:S(2)}) collective-permute-start(bf16[528,128]{1,0:T(8,128)(2,1)S(1)} %get-tuple-element.147.refs_3_), channel_id=1, source_target_pairs={{1,0},{9,8},{3,1},{11,9},{2,3},{10,11},{0,2},{8,10},{5,4},{13,12},... | collective-permute-start | bytes 405512 | tf_op jit(solution)/shard_map/ppermute | solution.py:61
  270.8 6.3 %collective-permute-start.54 = (bf16[528,128]{1,0:T(8,128)(2,1)S(1)}, bf16[528,128]{1,0:T(8,128)(2,1)}, u32[]{:S(2)}, u32[]{:S(2)}) collective-permute-start(bf16[528,128]{1,0:T(8,128)(2,1)S(1)} %get-tuple-element.147.refs_3_), channel_id=1, source_target_pairs={{10,0},{0,8},{8,1},{1,9},{9,3},{3,11},{11,2},{2,10},{14,4},{4,12},... | collective-permute-start | bytes 405512 | tf_op jit(solution)/shard_map/ppermute | solution.py:61
  270.8 6.3 %collective-permute-start.53 = (bf16[528,128]{1,0:T(8,128)(2,1)S(1)}, bf16[528,128]{1,0:T(8,128)(2,1)}, u32[]{:S(2)}, u32[]{:S(2)}) collective-permute-start(bf16[528,128]{1,0:T(8,128)(2,1)S(1)} %get-tuple-element.147.refs_3_), channel_id=1, source_target_pairs={{8,0},{1,8},{9,1},{3,9},{11,3},{2,11},{10,2},{0,10},{12,4},{5,12},... | collective-permute-start | bytes 405512 | tf_op jit(solution)/shard_map/ppermute | solution.py:61
  272.5 4.5 %collective-permute-start.52 = (f32[4,128]{1,0:T(4,128)S(1)}, f32[4,128]{1,0:T(4,128)S(1)}, u32[]{:S(2)}, u32[]{:S(2)}) collective-permute-start(f32[4,128]{1,0:T(4,128)S(1)} %maximum_select_fusion.2), channel_id=1, source_target_pairs={{3,0},{11,8},{2,1},{10,9},{0,3},{8,11},{1,2},{9,10},{7,4},{15,12},... | collective-permute-start | bytes 6152 | tf_op jit(solution)/shard_map/ppermute | solution.py:66
  291.5 3.6 %collective-permute-start.58 = (f32[2,128]{1,0:T(2,128)S(1)}, f32[2,128]{1,0:T(2,128)S(1)}, u32[]{:S(2)}, u32[]{:S(2)}) collective-permute-start(f32[2,128]{1,0:T(2,128)S(1)} %maximum_select_fusion.5), channel_id=1, source_target_pairs={{1,0},{9,8},{0,1},{8,9},{2,3},{10,11},{3,2},{11,10},{5,4},{13,12},... | collective-permute-start | bytes 3080 | tf_op jit(solution)/shard_map/ppermute | solution.py:66
  292.4 8.6 %collective-permute-start.63 = (f32[2,128,128]{2,1,0:T(8,128)S(1)}, f32[2,128,128]{2,1,0:T(8,128)S(1)}, u32[]{:S(2)}, u32[]{:S(2)}) collective-permute-start(f32[2,128,128]{2,1,0:T(8,128)S(1)} %get-tuple-element.174), channel_id=1, source_target_pairs={{11,0},{2,8},{10,1},{0,9},{8,3},{1,11},{9,2},{3,10},{15,4},{6,12},... | collective-permute-start | bytes 393224 | tf_op jit(solution)/shard_map/ppermute | solution.py:61
  293.2 7.8 %collective-permute-start.62 = (f32[2,128,128]{2,1,0:T(8,128)S(1)}, f32[2,128,128]{2,1,0:T(8,128)S(1)}, u32[]{:S(2)}, u32[]{:S(2)}) collective-permute-start(f32[2,128,128]{2,1,0:T(8,128)S(1)} %get-tuple-element.175), channel_id=1, source_target_pairs={{2,0},{10,8},{0,1},{8,9},{1,3},{9,11},{3,2},{11,10},{6,4},{14,12},... | collective-permute-start | bytes 393224 | tf_op jit(solution)/shard_map/ppermute | solution.py:61
  294.9 7.6 %collective-permute-start.61 = (f32[2,128,128]{2,1,0:T(8,128)S(1)}, f32[2,128,128]{2,1,0:T(8,128)S(1)}, u32[]{:S(2)}, u32[]{:S(2)}) collective-permute-start(f32[2,128,128]{2,1,0:T(8,128)S(1)} %get-tuple-element.176), channel_id=1, source_target_pairs={{10,0},{0,8},{8,1},{1,9},{9,3},{3,11},{11,2},{2,10},{14,4},{4,12},... | collective-permute-start | bytes 393224 | tf_op jit(solution)/shard_map/ppermute | solution.py:61
  295.2 4.5 %collective-permute-start.59 = (f32[4,128]{1,0:T(4,128)S(1)}, f32[4,128]{1,0:T(4,128)S(1)}, u32[]{:S(2)}, u32[]{:S(2)}) collective-permute-start(f32[4,128]{1,0:T(4,128)S(1)} %maximum_select_fusion.3), channel_id=1, source_target_pairs={{3,0},{11,8},{2,1},{10,9},{0,3},{8,11},{1,2},{9,10},{7,4},{15,12},... | collective-permute-start | bytes 6152 | tf_op jit(solution)/shard_map/ppermute | solution.py:66
  299.7 3.9 %collective-permute-start.60 = (f32[8,128]{1,0:T(8,128)S(1)}, f32[8,128]{1,0:T(8,128)S(1)}, u32[]{:S(2)}, u32[]{:S(2)}) collective-permute-start(f32[8,128]{1,0:T(8,128)S(1)} %maximum_select_fusion.1.table_ref), channel_id=1, source_target_pairs={{0,16},{8,17},{1,18},{9,19},{3,20},{11,21},{2,22},{10,23},{4,24},{... | collective-permute-start | bytes 12296 | tf_op jit(solution)/shard_map/ppermute | solution.py:56
  308.4 12.9 %collective-permute-start.64 = (bf16[128,128]{1,0:T(8,128)(2,1)S(1)}, bf16[128,128]{1,0:T(8,128)(2,1)S(1)}, u32[]{:S(2)}, u32[]{:S(2)}) collective-permute-start(bf16[128,128]{1,0:T(8,128)(2,1)S(1)} %get-tuple-element.181), channel_id=1, source_target_pairs={{0,16},{8,17},{1,18},{9,19},{3,20},{11,21},{2,22},{10,23},{4,24},{... | collective-permute-start | bytes 98312 | tf_op jit(solution)/shard_map/ppermute | solution.py:56
  309.5 11.9 %collective-permute-start.67 = (bf16[128,128]{1,0:T(8,128)(2,1)S(1)}, bf16[128,128]{1,0:T(8,128)(2,1)S(1)}, u32[]{:S(2)}, u32[]{:S(2)}) collective-permute-start(bf16[128,128]{1,0:T(8,128)(2,1)S(1)} %get-tuple-element.182), channel_id=1, source_target_pairs={{0,21},{8,22},{1,23},{9,16},{3,17},{11,18},{2,19},{10,20},{4,29},{... | collective-permute-start | bytes 98312 | tf_op jit(solution)/shard_map/ppermute | solution.py:56
  317.5 4.8 %collective-permute-start.66 = (bf16[128,128]{1,0:T(8,128)(2,1)S(1)}, bf16[128,128]{1,0:T(8,128)(2,1)S(1)}, u32[]{:S(2)}, u32[]{:S(2)}) collective-permute-start(bf16[128,128]{1,0:T(8,128)(2,1)S(1)} %get-tuple-element.183), channel_id=1, source_target_pairs={{0,22},{8,23},{1,16},{9,17},{3,18},{11,19},{2,20},{10,21},{4,30},{... | collective-permute-start | bytes 98312 | tf_op jit(solution)/shard_map/ppermute | solution.py:56
  318.1 4.2 %collective-permute-start.65 = (bf16[128,128]{1,0:T(8,128)(2,1)S(1)}, bf16[128,128]{1,0:T(8,128)(2,1)S(1)}, u32[]{:S(2)}, u32[]{:S(2)}) collective-permute-start(bf16[128,128]{1,0:T(8,128)(2,1)S(1)} %get-tuple-element.184), channel_id=1, source_target_pairs={{0,23},{8,16},{1,17},{9,18},{3,19},{11,20},{2,21},{10,22},{4,31},{... | collective-permute-start | bytes 98312 | tf_op jit(solution)/shard_map/ppermute | solution.py:56
  (37 other events, 235.8 us)

commit v5 on v3

--- a/solution.py
+++ b/solution.py
@@ -12,7 +12,6 @@
 POLAR = 6
 
 TINY = 1e-06
-HIGHEST = lax.Precision.HIGHEST
 CHARGE_STEPS = (0, 1, -1, 2, -2)
 CLASSES = len(CHARGE_STEPS)
 BOTH = ("site", "sec")
@@ -477,10 +476,17 @@
     columns = lax.broadcasted_iota(jnp.int32, (block, block), 1)
     unit = (rows == columns).astype(jnp.float32)
 
+    def halves(x):
+        high = x.astype(jnp.bfloat16)
+        return high, (x - high.astype(jnp.float32)).astype(jnp.bfloat16)
+
     def product(x, y, contract=((1,), (0,))):
-        return lax.dot_general(
-            x, y, (contract, ((), ())), precision=HIGHEST, preferred_element_type=jnp.float32
-        )
+        (x_high, x_low), (y_high, y_low) = halves(x), halves(y)
+        parts = [
+            lax.dot_general(left, right, (contract, ((), ())), preferred_element_type=jnp.float32)
+            for left, right in ((x_high, y_low), (x_low, y_high), (x_high, y_high))
+        ]
+        return parts[0] + parts[1] + parts[2]
 
     scale, energy, factor, square, centre_sq = quotient(table_ref[...], entry_count)
     vector = updated(
@@ -761,9 +767,11 @@
         for t in range(1, states):
             if step == 0 and t == states - 1:
                 left, envs[-1] = after(left, envs[-1])
+            if step == 1 and t == states - 1:
+                rolled_vector, envs[-1] = after(rolled_vector, envs[-1])
             envs.append(ahead(envs[-1], 1))
         if step == 0:
-            (rolled, rolled_vector), envs = after((rolled, rolled_vector), envs)
+            rolled, envs = after(rolled, envs)
         right, square = right_whole(
             envs,
             right_isos[step],

time: 311 us -> 320 us (1.029)
  waiting for transfers between devices: 107 us -> 117 us
    ppermute x52, waiting for transfers between devices: 93.4 us -> 104 us  [ahead(): lax.ppermute(x, BOTH, self.pairs(lambda g, k: self.slot(g + chain_by, k +...]
  transfers between devices with their start and end apart: 68 -> 68, of which waited for: 29 -> 28; matrix products, arithmetic and copies ran while one was open for 7% -> 7% of each run, Pallas kernels for 10% -> 10%
where the time goes in v5:
time: 320 us; the launch traced here: 318 us
  waiting for transfers between devices  117 us (37%)
  starting transfers between devices  110 us (34%)
  Pallas kernels  52.7 us (16%)
  local copies, waits for them, and re-layouts  11.9 us (4%)
  matrix products  11.1 us (3%)
  blocking collectives  8.06 us (3%)
  other arithmetic  5.6 us (2%)
    ppermute x52, waiting for transfers between devices, ahead(): lax.ppermute(x, BOTH, self.pairs(lambda g, k: self.slot(g + chain_by, k +...  104 us
    ppermute x52, starting transfers between devices, ahead(): lax.ppermute(x, BOTH, self.pairs(lambda g, k: self.slot(g + chain_by, k +...  67.3 us
    pallas_call x19, Pallas kernels, call(): pl.pallas_call(kernel, out_shape=out_shape, scratch_shapes=scratch_shapes...  52.7 us
    ppermute x5, starting transfers between devices, fetch(): lax.ppermute(x, BOTH, self.pairs(lambda g, k: self.home(g + site_by, k +...  24.7 us
    ppermute x5, starting transfers between devices, send_home(): lax.ppermute(x, BOTH, self.pairs(self.slot, lambda g, k: self.home(g + si...  11.2 us
    dot_general x12, matrix products, local(): jnp.einsum('xy,vxz->vyz', left_isos[step][s], gathered[s][piece], preferr...  10.9 us
    ppermute x6, waiting for transfers between devices, partner(): lax.ppermute(x, BOTH, self.pairs(lambda g, k: self.slot(g, k ^ bit), self...  9.11 us
    all_gather x1, blocking collectives, local(): lax.all_gather(weight_matrices(mpo[0], pattern[0], secs), 'site')  8.06 us
  transfers between devices with their start and end apart: 68, of which 28 were waited for; matrix products, arithmetic and copies ran while one was open for 7% of the time, Pallas kernels for 10%

profile of v5, /device:TPU:0, one launch (start us, length us, event | category | flops | bytes accessed | tf_op | source)
XLA Modules:
  0.0 318.3 jit_solution(4307470920610980373)
XLA Ops:
  0.6 5.0 %collective-permute-start.5 = (bf16[4,128,128]{2,1,0:T(8,128)(2,1)}, bf16[4,128,128]{2,1,0:T(8,128)(2,1)S(1)}, u32[]{:S(2)}, u32[]{:S(2)}) collective-permute-start(bf16[4,128,128]{2,1,0:T(8,128)(2,1)} %bitcast.190), channel_id=1, source_target_pairs={{8,0},{9,8},{10,1},{11,9},{12,3},{13,11},{14,2},{15,10},{16,4},{17... | collective-permute-start | bytes 393224 | tf_op jit(solution)/shard_map/ppermute | solution.py:50
  5.7 4.4 %collective-permute-start.6 = (bf16[4,128,128]{2,1,0:T(8,128)(2,1)}, bf16[4,128,128]{2,1,0:T(8,128)(2,1)S(1)}, u32[]{:S(2)}, u32[]{:S(2)}) collective-permute-start(bf16[4,128,128]{2,1,0:T(8,128)(2,1)} %bitcast.193), channel_id=1, source_target_pairs={{24,0},{25,8},{26,1},{27,9},{28,3},{29,11},{30,2},{31,10},{0,4},{1... | collective-permute-start | bytes 393224 | tf_op jit(solution)/shard_map/ppermute | solution.py:50
  11.6 2.9 pad_maximum_fusion
  14.6 13.9 %collective-permute-start = (bf16[50,128,128]{2,1,0:T(8,128)(2,1)}, bf16[50,128,128]{2,1,0:T(8,128)(2,1)}, u32[]{:S(2)}, u32[]{:S(2)}) collective-permute-start(bf16[50,128,128]{2,1,0:T(8,128)(2,1)} %pad_maximum_fusion), channel_id=1, source_target_pairs={{0,0},{1,8},{2,1},{3,9},{4,3},{5,11},{6,2},{7,10},{8,4},{9,12},{10... | collective-permute-start | bytes 4915208 | tf_op jit(solution)/shard_map/ppermute | solution.py:50
  29.5 8.1 %all-gather = bf16[8,168,168]{2,1,0:T(8,128)(2,1)S(1)} all-gather(bf16[2,168,168]{2,1,0:T(8,128)(2,1)S(1)} %pad_maximum_fusion.2), channel_id=2, replica_groups=mesh['site'=4,'sec'=8] {'site'}, dimensions={0}, use_global_device_ids=true | all-gather | bytes 564480 | tf_op jit(solution)/shard_map/all_gather | solution.py:742
  45.8 1.5 collective-permute-done.14
  47.4 4.2 %collective-permute-done.13 = bf16[128,128]{1,0:T(8,128)(2,1)S(1)} collective-permute-done((bf16[128,128]{1,0:T(8,128)(2,1)S(1)}, bf16[128,128]{1,0:T(8,128)(2,1)S(1)}, u32[]{:S(2)}, u32[]{:S(2)}) %collective-permute-start.13) | collective-permute-done | bytes 32800 | tf_op jit(solution)/shard_map/ppermute | solution.py:60
  52.3 1.8 collective-permute-start.9
  56.4 7.9 %collective-permute-start.15 = (bf16[21,128,128]{2,1,0:T(8,128)(2,1)S(1)}, bf16[21,128,128]{2,1,0:T(8,128)(2,1)S(1)}, u32[]{:S(2)}, u32[]{:S(2)}) collective-permute-start(bf16[21,128,128]{2,1,0:T(8,128)(2,1)S(1)} %get-tuple-element.80.refs_0_), channel_id=1, source_target_pairs={{8,0},{1,8},{9,1},{3,9},{11,3},{2,11},{10,2},{0,10},{12,4},{5,12},... | collective-permute-start | bytes 2064392 | tf_op jit(solution)/shard_map/ppermute | solution.py:60
  66.0 14.1 %collective-permute-done.15.refs_2_ = bf16[21,128,128]{2,1,0:T(8,128)(2,1)S(1)} collective-permute-done((bf16[21,128,128]{2,1,0:T(8,128)(2,1)S(1)}, bf16[21,128,128]{2,1,0:T(8,128)(2,1)S(1)}, u32[]{:S(2)}, u32[]{:S(2)}) %collective-permute-start.15) | collective-permute-done | bytes 688160 | tf_op jit(solution)/shard_map/ppermute | solution.py:60
  80.2 2.2 collective-permute-start.18
  82.4 8.0 %collective-permute-done.16.refs_3_ = bf16[21,128,128]{2,1,0:T(8,128)(2,1)S(1)} collective-permute-done((bf16[21,128,128]{2,1,0:T(8,128)(2,1)S(1)}, bf16[21,128,128]{2,1,0:T(8,128)(2,1)S(1)}, u32[]{:S(2)}, u32[]{:S(2)}) %collective-permute-start.16) | collective-permute-done | bytes 688160 | tf_op jit(solution)/shard_map/ppermute | solution.py:60
  90.4 1.9 collective-permute-start.19
  93.3 1.8 collective-permute-start.3
  95.3 5.3 %collective-permute-done.18.refs_4_ = bf16[21,128,128]{2,1,0:T(8,128)(2,1)S(1)} collective-permute-done((bf16[21,128,128]{2,1,0:T(8,128)(2,1)S(1)}, bf16[21,128,128]{2,1,0:T(8,128)(2,1)S(1)}, u32[]{:S(2)}, u32[]{:S(2)}) %collective-permute-start.18) | collective-permute-done | bytes 688160 | tf_op jit(solution)/shard_map/ppermute | solution.py:60
  100.6 7.4 %collective-permute-done.19.refs_5_ = bf16[21,128,128]{2,1,0:T(8,128)(2,1)S(1)} collective-permute-done((bf16[21,128,128]{2,1,0:T(8,128)(2,1)S(1)}, bf16[21,128,128]{2,1,0:T(8,128)(2,1)S(1)}, u32[]{:S(2)}, u32[]{:S(2)}) %collective-permute-start.19) | collective-permute-done | bytes 688160 | tf_op jit(solution)/shard_map/ppermute | solution.py:60
  107.9 1.9 collective-permute-start.20
  109.8 1.6 collective-permute-start.21
  111.6 6.7 %collective-permute-done.20.refs_6_ = bf16[21,128,128]{2,1,0:T(8,128)(2,1)S(1)} collective-permute-done((bf16[21,128,128]{2,1,0:T(8,128)(2,1)S(1)}, bf16[21,128,128]{2,1,0:T(8,128)(2,1)S(1)}, u32[]{:S(2)}, u32[]{:S(2)}) %collective-permute-start.20) | collective-permute-done | bytes 688160 | tf_op jit(solution)/shard_map/ppermute | solution.py:60
  118.3 7.4 %collective-permute-done.21.refs_7_ = bf16[21,128,128]{2,1,0:T(8,128)(2,1)S(1)} collective-permute-done((bf16[21,128,128]{2,1,0:T(8,128)(2,1)S(1)}, bf16[21,128,128]{2,1,0:T(8,128)(2,1)S(1)}, u32[]{:S(2)}, u32[]{:S(2)}) %collective-permute-start.21) | collective-permute-done | bytes 688160 | tf_op jit(solution)/shard_map/ppermute | solution.py:60
  125.8 5.2 %shard_map.147 = (bf16[21,128,128]{2,1,0:T(8,128)(2,1)S(1)}, bf16[21,128,128]{2,1,0:T(8,128)(2,1)S(1)}, bf16[21,128,128]{2,1,0:T(8,128)(2,1)S(1)}, bf16[21,128,1...) custom-call(bf16[21,128,128]{2,1,0:T(8,128)(2,1)S(1)} %get-tuple-ele, ...), custom_call_target="tpu_custom_call" | custom-call | flops 2334130176 | bytes 3076096 | tf_op jit(solution)/shard_map/pallas_call | solution.py:517
  134.5 6.3 %shard_map.145 = (bf16[21,128,128]{2,1,0:T(8,128)(2,1)S(1)}, bf16[21,128,128]{2,1,0:T(8,128)(2,1)S(1)}, f32[8,128]{1,0:T(8,128)S(1)}) custom-call(bf16[21,128,128]{2,1,0:T(8,128)(2,1)S(1)} %get-tuple-element.80.refs_0_, bf16[21,128,128]{2,1,0:T(8,128)(2,1)S(1)} %get-tuple-element.81.refs_1_, bf16[21,128,128]{2,1,0:T(8,128)(2,1)S(1)} %collective-permute-done.15.refs_2_, ...), custom_call_target="tpu_custom_call" | custom-call | flops 2334130176 | bytes 7335936 | tf_op jit(solution)/shard_map/pallas_call | solution.py:517
  140.9 2.0 collective-permute-start.22
  142.9 1.6 collective-permute-start.23
  146.3 3.8 %collective-permute-done.38 = bf16[21,128,128]{2,1,0:T(8,128)(2,1)S(1)} collective-permute-done((bf16[21,128,128]{2,1,0:T(8,128)(2,1)S(1)}, bf16[21,128,128]{2,1,0:T(8,128)(2,1)S(1)}, u32[]{:S(2)}, u32[]{:S(2)}) %collective-permute-start.38) | collective-permute-done | bytes 688160 | tf_op jit(solution)/shard_map/ppermute | solution.py:60
  151.4 2.1 collective-permute-start.28
  153.5 5.2 %collective-permute-done.23.refs_3_ = bf16[21,128,128]{2,1,0:T(8,128)(2,1)S(1)} collective-permute-done((bf16[21,128,128]{2,1,0:T(8,128)(2,1)S(1)}, bf16[21,128,128]{2,1,0:T(8,128)(2,1)S(1)}, u32[]{:S(2)}, u32[]{:S(2)}) %collective-permute-start.23) | collective-permute-done | bytes 688160 | tf_op jit(solution)/shard_map/ppermute | solution.py:60
  158.7 2.2 collective-permute-start.29
  162.0 2.2 collective-permute-start.43
  167.8 7.0 %collective-permute-done.24.refs_4_ = bf16[4,128,128]{2,1,0:T(8,128)(2,1)S(1)} collective-permute-done((bf16[4,128,128]{2,1,0:T(8,128)(2,1)S(1)}, bf16[4,128,128]{2,1,0:T(8,128)(2,1)S(1)}, u32[]{:S(2)}, u32[]{:S(2)}) %collective-permute-start.24) | collective-permute-done | bytes 131104 | tf_op jit(solution)/shard_map/ppermute | solution.py:60
  174.8 4.3 %collective-permute-start.27 = (bf16[4,128,128]{2,1,0:T(8,128)(2,1)S(1)}, bf16[4,128,128]{2,1,0:T(8,128)(2,1)S(1)}, u32[]{:S(2)}, u32[]{:S(2)}) collective-permute-start(bf16[4,128,128]{2,1,0:T(8,128)(2,1)S(1)} %collective-permute-done.25.refs_5_), channel_id=1, source_target_pairs={{10,0},{0,8},{8,1},{1,9},{9,3},{3,11},{11,2},{2,10},{14,4},{4,12},... | collective-permute-start | bytes 393224 | tf_op jit(solution)/shard_map/ppermute | solution.py:60
  179.9 2.5 collective-permute-done.27.refs_7_
  182.6 2.4 collective-permute-done.26.refs_6_
  185.0 2.0 collective-permute-start.30
  187.0 1.5 collective-permute-start.31
  189.4 5.2 %shard_map.150 = (bf16[21,128,128]{2,1,0:T(8,128)(2,1)S(1)}, bf16[21,128,128]{2,1,0:T(8,128)(2,1)S(1)}, bf16[21,128,128]{2,1,0:T(8,128)(2,1)S(1)}, bf16[21,128,1...) custom-call(bf16[21,128,128]{2,1,0:T(8,128)(2,1)S(1)} %get-tuple-ele, ...), custom_call_target="tpu_custom_call" | custom-call | flops 2334130176 | bytes 3076096 | tf_op jit(solution)/shard_map/pallas_call | solution.py:517
  196.6 6.2 %collective-permute-done.31.refs_7_ = bf16[21,128,128]{2,1,0:T(8,128)(2,1)S(1)} collective-permute-done((bf16[21,128,128]{2,1,0:T(8,128)(2,1)S(1)}, bf16[21,128,128]{2,1,0:T(8,128)(2,1)S(1)}, u32[]{:S(2)}, u32[]{:S(2)}) %collective-permute-start.31) | collective-permute-done | bytes 688160 | tf_op jit(solution)/shard_map/ppermute | solution.py:60
  202.8 6.3 %shard_map.146 = (bf16[21,128,128]{2,1,0:T(8,128)(2,1)S(1)}, bf16[21,128,128]{2,1,0:T(8,128)(2,1)S(1)}, f32[8,128]{1,0:T(8,128)S(1)}) custom-call(bf16[21,128,128]{2,1,0:T(8,128)(2,1)S(1)} %get-tuple-element.90.refs_0_, bf16[21,128,128]{2,1,0:T(8,128)(2,1)S(1)} %get-tuple-element.91.refs_1_, bf16[21,128,128]{2,1,0:T(8,128)(2,1)S(1)} %collective-permute-done.22.refs_2_, ...), custom_call_target="tpu_custom_call" | custom-call | flops 2334130176 | bytes 7335936 | tf_op jit(solution)/shard_map/pallas_call | solution.py:517
  209.2 2.2 collective-permute-start.32
  213.5 1.5 collective-permute-start.45
  215.0 4.9 %collective-permute-done.32.refs_2_.refs_10_ = bf16[21,128,128]{2,1,0:T(8,128)(2,1)S(1)} collective-permute-done((bf16[21,128,128]{2,1,0:T(8,128)(2,1)S(1)}, bf16[21,128,128]{2,1,0:T(8,128)(2,1)S(1)}, u32[]{:S(2)}, u32[]{:S(2)}) %collective-permute-start.32) | collective-permute-done | bytes 688160 | tf_op jit(solution)/shard_map/ppermute | solution.py:60
  219.9 2.2 collective-permute-start.34
  222.1 5.2 %collective-permute-done.33.refs_3_.refs_11_ = bf16[21,128,128]{2,1,0:T(8,128)(2,1)S(1)} collective-permute-done((bf16[21,128,128]{2,1,0:T(8,128)(2,1)S(1)}, bf16[21,128,128]{2,1,0:T(8,128)(2,1)S(1)}, u32[]{:S(2)}, u32[]{:S(2)}) %collective-permute-start.33) | collective-permute-done | bytes 688160 | tf_op jit(solution)/shard_map/ppermute | solution.py:60
  227.3 2.2 collective-permute-start.35
  232.8 1.7 collective-permute-start.46
  234.6 2.0 collective-permute-start.36
  236.6 5.4 %collective-permute-done.35.refs_5_.refs_13_ = bf16[21,128,128]{2,1,0:T(8,128)(2,1)} collective-permute-done((bf16[21,128,128]{2,1,0:T(8,128)(2,1)S(1)}, bf16[21,128,128]{2,1,0:T(8,128)(2,1)}, u32[]{:S(2)}, u32[]{:S(2)}) %collective-permute-start.35) | collective-permute-done | bytes 688160 | tf_op jit(solution)/shard_map/ppermute | solution.py:60
  242.0 2.2 collective-permute-start.37
  246.2 2.5 collective-permute-done.46.moved_ref
  249.2 5.2 %shard_map.153.refs_13_ = bf16[21504,128]{1,0:T(8,128)(2,1)S(1)} custom-call(bf16[21,128,128]{2,1,0:T(8,128)(2,1)S(1)} %get-tuple-element.126.refs_0_, bf16[21,128,128]{2,1,0:T(8,128)(2,1)S(1)} %get-tuple-element.127.refs_1_, bf16[1360,384]{1,0:T(8,128)(2,1)S(1)} %copy-done.21, bf16[4,128,128]{2,1,0:T(8,128)(2,1)S(1)} %get-tuple-element.129.refs_3_, ...), custom_call_target="tpu_custom_call" | custom-call | flops 2334130176 | bytes 3076096 | tf_op jit(solution)/shard_map/pallas_call | solution.py:517
  254.5 2.4 collective-permute-done.37.refs_7_.refs_15_
  256.9 3.8 %shard_map.154 = (f32[4,128,128]{2,1,0:T(8,128)S(1)}, bf16[528,128]{1,0:T(8,128)(2,1)S(1)}, f32[1,128]{1,0:T(1,128)S(1)}) custom-call(bf16[21,128,128]{2,1,0:T(8,128)(2,1)S(1)} %copy-done.1, bf16[21,128,128]{2,1,0:T(8,128)(2,1)S(1)} %copy-done.3, bf16[21,128,128]{2,1,0:T(8,128)(2,1)S(1)} %copy-done.5, bf16[21,128,128]{2,1,0:T(8,128)(2,1)S(1)} %copy-done.7, ...), custom_call_target="tpu_custom_call" | custom-call | flops 704643072 | bytes 11292672 | tf_op jit(solution)/shard_map/pallas_call | solution.py:517
  260.6 2.8 collective-permute-start.50
  264.2 1.8 collective-permute-start.51
  266.3 1.7 collective-permute-start.55
  268.0 1.7 collective-permute-start.53
  270.5 3.9 %collective-permute-done.52 = f32[4,128]{1,0:T(4,128)S(1)} collective-permute-done((f32[4,128]{1,0:T(4,128)S(1)}, f32[4,128]{1,0:T(4,128)S(1)}, u32[]{:S(2)}, u32[]{:S(2)}) %collective-permute-start.52) | collective-permute-done | bytes 2080 | tf_op jit(solution)/shard_map/ppermute | solution.py:65
  277.8 8.9 %shard_map.155 = (f32[4,128,128]{2,1,0:T(8,128)S(1)}, f32[1,128]{1,0:T(1,128)S(1)}) custom-call(bf16[21,128,128]{2,1,0:T(8,128)(2,1)S(1)} %copy-done.11, bf16[21,128,128]{2,1,0:T(8,128)(2,1)S(1)} %copy-done.9, bf16[1360,384]{1,0:T(8,128)(2,1)S(1)} %copy-done.22, bf16[528,128]{1,0:T(8,128)(2,1)S(1)} %get-tuple-element.137.refs_3_, ...), custom_call_target="tpu_custom_call" | custom-call | flops 3038773248 | bytes 8601600 | tf_op jit(solution)/shard_map/pallas_call | solution.py:517
  293.9 3.1 collective-permute-done.59
  297.7 1.7 collective-permute-done.61
  300.6 3.5 %shard_map.157 = bf16[4,128,128]{2,1,0:T(8,128)(2,1)S(1)} custom-call(f32[4,2,128,128]{3,2,1,0:T(8,128)S(1)} %pad_maximum_fusion.1.both_ref, f32[8,128]{1,0:T(8,128)S(1)} %maximum_select_fusion.1.table_ref, bf16[128,128]{1,0:T(8,128)(2,1)S(1)} %get-tuple-element.170.centre_ref), custom_call_target="tpu_custom_call" | custom-call | flops 1258291200 | bytes 561152 | tf_op jit(solution)/shard_map/pallas_call | solution.py:517
  304.9 7.8 %collective-permute-start.67 = (bf16[128,128]{1,0:T(8,128)(2,1)S(1)}, bf16[128,128]{1,0:T(8,128)(2,1)S(1)}, u32[]{:S(2)}, u32[]{:S(2)}) collective-permute-start(bf16[128,128]{1,0:T(8,128)(2,1)S(1)} %get-tuple-element.172), channel_id=1, source_target_pairs={{0,21},{8,22},{1,23},{9,16},{3,17},{11,18},{2,19},{10,20},{4,29},{... | collective-permute-start | bytes 98312 | tf_op jit(solution)/shard_map/ppermute | solution.py:55
  312.8 1.8 collective-permute-start.65
  315.3 2.3 collective-permute-done.66
  (210 shorter events, 56.1 us)
Async XLA Ops:
  0.6 43.2 %collective-permute-start.5 = (bf16[4,128,128]{2,1,0:T(8,128)(2,1)}, bf16[4,128,128]{2,1,0:T(8,128)(2,1)S(1)}, u32[]{:S(2)}, u32[]{:S(2)}) collective-permute-start(bf16[4,128,128]{2,1,0:T(8,128)(2,1)} %bitcast.190), channel_id=1, source_target_pairs={{8,0},{9,8},{10,1},{11,9},{12,3},{13,11},{14,2},{15,10},{16,4},{17... | collective-permute-start | bytes 393224 | tf_op jit(solution)/shard_map/ppermute | solution.py:50
  5.7 38.3 %collective-permute-start.6 = (bf16[4,128,128]{2,1,0:T(8,128)(2,1)}, bf16[4,128,128]{2,1,0:T(8,128)(2,1)S(1)}, u32[]{:S(2)}, u32[]{:S(2)}) collective-permute-start(bf16[4,128,128]{2,1,0:T(8,128)(2,1)} %bitcast.193), channel_id=1, source_target_pairs={{24,0},{25,8},{26,1},{27,9},{28,3},{29,11},{30,2},{31,10},{0,4},{1... | collective-permute-start | bytes 393224 | tf_op jit(solution)/shard_map/ppermute | solution.py:50
  11.0 32.9 %collective-permute-start.11 = (bf16[5,128,128]{2,1,0:T(8,128)(2,1)S(1)}, bf16[5,128,128]{2,1,0:T(8,128)(2,1)S(1)}, u32[]{:S(2)}, u32[]{:S(2)}) collective-permute-start(bf16[5,128,128]{2,1,0:T(8,128)(2,1)S(1)} %pad_maximum_fusion.3), channel_id=1, source_target_pairs={{16,0},{17,8},{18,1},{19,9},{20,3},{21,11},{22,2},{23,10},{24,4},{... | collective-permute-start | bytes 491528 | tf_op jit(solution)/shard_map/ppermute | solution.py:50
  14.6 39.5 %collective-permute-start = (bf16[50,128,128]{2,1,0:T(8,128)(2,1)}, bf16[50,128,128]{2,1,0:T(8,128)(2,1)}, u32[]{:S(2)}, u32[]{:S(2)}) collective-permute-start(bf16[50,128,128]{2,1,0:T(8,128)(2,1)} %pad_maximum_fusion), channel_id=1, source_target_pairs={{0,0},{1,8},{2,1},{3,9},{4,3},{5,11},{6,2},{7,10},{8,4},{9,12},{10... | collective-permute-start | bytes 4915208 | tf_op jit(solution)/shard_map/ppermute | solution.py:50
  44.0 7.8 %collective-permute-start.8 = (bf16[8,128,128]{2,1,0:T(8,128)(2,1)S(1)}, bf16[8,128,128]{2,1,0:T(8,128)(2,1)S(1)}, u32[]{:S(2)}, u32[]{:S(2)}) collective-permute-start(bf16[8,128,128]{2,1,0:T(8,128)(2,1)S(1)} %constant_dynamic-update-slice_fusion), channel_id=1, source_target_pairs={{10,0},{0,8},{8,1},{1,9},{9,3},{3,11},{11,2},{2,10},{14,4},{4,12},... | collective-permute-start | bytes 786440 | tf_op jit(solution)/shard_map/ppermute | solution.py:60
  44.4 7.9 %collective-permute-start.7 = (bf16[8,128,128]{2,1,0:T(8,128)(2,1)S(1)}, bf16[8,128,128]{2,1,0:T(8,128)(2,1)S(1)}, u32[]{:S(2)}, u32[]{:S(2)}) collective-permute-start(bf16[8,128,128]{2,1,0:T(8,128)(2,1)S(1)} %constant_dynamic-update-slice_fusion), channel_id=1, source_target_pairs={{8,0},{1,8},{9,1},{3,9},{11,3},{2,11},{10,2},{0,10},{12,4},{5,12},... | collective-permute-start | bytes 786440 | tf_op jit(solution)/shard_map/ppermute | solution.py:60
  45.8 5.8 %collective-permute-start.13 = (bf16[128,128]{1,0:T(8,128)(2,1)S(1)}, bf16[128,128]{1,0:T(8,128)(2,1)S(1)}, u32[]{:S(2)}, u32[]{:S(2)}) collective-permute-start(bf16[128,128]{1,0:T(8,128)(2,1)S(1)} %get-tuple-element.170.centre_ref), channel_id=1, source_target_pairs={{1,0},{9,8},{3,1},{11,9},{2,3},{10,11},{0,2},{8,10},{5,4},{13,12},... | collective-permute-start | bytes 98312 | tf_op jit(solution)/shard_map/ppermute | solution.py:60
  47.3 4.3 %collective-permute-start.12 = (bf16[128,128]{1,0:T(8,128)(2,1)S(1)}, bf16[128,128]{1,0:T(8,128)(2,1)S(1)}, u32[]{:S(2)}, u32[]{:S(2)}) collective-permute-start(bf16[128,128]{1,0:T(8,128)(2,1)S(1)} %get-tuple-element.170.centre_ref), channel_id=1, source_target_pairs={{8,0},{1,8},{9,1},{3,9},{11,3},{2,11},{10,2},{0,10},{12,4},{5,12},... | collective-permute-start | bytes 98312 | tf_op jit(solution)/shard_map/ppermute | solution.py:60
  51.8 13.7 %collective-permute-start.10 = (bf16[8,128,128]{2,1,0:T(8,128)(2,1)S(1)}, bf16[8,128,128]{2,1,0:T(8,128)(2,1)S(1)}, u32[]{:S(2)}, u32[]{:S(2)}) collective-permute-start(bf16[8,128,128]{2,1,0:T(8,128)(2,1)S(1)} %collective-permute-done.8), channel_id=1, source_target_pairs={{10,0},{0,8},{8,1},{1,9},{9,3},{3,11},{11,2},{2,10},{14,4},{4,12},... | collective-permute-start | bytes 786440 | tf_op jit(solution)/shard_map/ppermute | solution.py:60
  52.3 12.1 %collective-permute-start.9 = (bf16[8,128,128]{2,1,0:T(8,128)(2,1)S(1)}, bf16[8,128,128]{2,1,0:T(8,128)(2,1)S(1)}, u32[]{:S(2)}, u32[]{:S(2)}) collective-permute-start(bf16[8,128,128]{2,1,0:T(8,128)(2,1)S(1)} %collective-permute-done.7), channel_id=1, source_target_pairs={{8,0},{1,8},{9,1},{3,9},{11,3},{2,11},{10,2},{0,10},{12,4},{5,12},... | collective-permute-start | bytes 786440 | tf_op jit(solution)/shard_map/ppermute | solution.py:60
  55.5 39.6 %collective-permute-start.17 = (bf16[42,128,128]{2,1,0:T(8,128)(2,1)S(1)}, bf16[42,128,128]{2,1,0:T(8,128)(2,1)S(1)}, u32[]{:S(2)}, u32[]{:S(2)}) collective-permute-start(bf16[42,128,128]{2,1,0:T(8,128)(2,1)S(1)} %bitcast.205), channel_id=1, source_target_pairs={{0,0},{1,8},{2,1},{3,9},{4,3},{5,11},{6,2},{7,10},{8,4},{9,12},{10... | collective-permute-start | bytes 4128776 | tf_op jit(solution)/shard_map/ppermute | solution.py:50
  56.4 23.8 %collective-permute-start.15 = (bf16[21,128,128]{2,1,0:T(8,128)(2,1)S(1)}, bf16[21,128,128]{2,1,0:T(8,128)(2,1)S(1)}, u32[]{:S(2)}, u32[]{:S(2)}) collective-permute-start(bf16[21,128,128]{2,1,0:T(8,128)(2,1)S(1)} %get-tuple-element.80.refs_0_), channel_id=1, source_target_pairs={{8,0},{1,8},{9,1},{3,9},{11,3},{2,11},{10,2},{0,10},{12,4},{5,12},... | collective-permute-start | bytes 2064392 | tf_op jit(solution)/shard_map/ppermute | solution.py:60
  64.3 26.1 %collective-permute-start.16 = (bf16[21,128,128]{2,1,0:T(8,128)(2,1)S(1)}, bf16[21,128,128]{2,1,0:T(8,128)(2,1)S(1)}, u32[]{:S(2)}, u32[]{:S(2)}) collective-permute-start(bf16[21,128,128]{2,1,0:T(8,128)(2,1)S(1)} %get-tuple-element.81.refs_1_), channel_id=1, source_target_pairs={{8,0},{1,8},{9,1},{3,9},{11,3},{2,11},{10,2},{0,10},{12,4},{5,12},... | collective-permute-start | bytes 2064392 | tf_op jit(solution)/shard_map/ppermute | solution.py:60
  65.4 27.8 %collective-permute-start.1 = (bf16[8,128,128]{2,1,0:T(8,128)(2,1)S(1)}, bf16[8,128,128]{2,1,0:T(8,128)(2,1)S(1)}, u32[]{:S(2)}, u32[]{:S(2)}) collective-permute-start(bf16[8,128,128]{2,1,0:T(8,128)(2,1)S(1)} %concatenate.64), channel_id=1, source_target_pairs={{8,0},{1,8},{9,1},{3,9},{11,3},{2,11},{10,2},{0,10},{12,4},{5,12},... | collective-permute-start | bytes 786440 | tf_op jit(solution)/shard_map/ppermute | solution.py:60
  65.5 29.6 %collective-permute-start.2 = (bf16[8,128,128]{2,1,0:T(8,128)(2,1)S(1)}, bf16[8,128,128]{2,1,0:T(8,128)(2,1)S(1)}, u32[]{:S(2)}, u32[]{:S(2)}) collective-permute-start(bf16[8,128,128]{2,1,0:T(8,128)(2,1)S(1)} %concatenate.64), channel_id=1, source_target_pairs={{10,0},{0,8},{8,1},{1,9},{9,3},{3,11},{11,2},{2,10},{14,4},{4,12},... | collective-permute-start | bytes 786440 | tf_op jit(solution)/shard_map/ppermute | solution.py:60
  80.2 20.4 %collective-permute-start.18 = (bf16[21,128,128]{2,1,0:T(8,128)(2,1)S(1)}, bf16[21,128,128]{2,1,0:T(8,128)(2,1)S(1)}, u32[]{:S(2)}, u32[]{:S(2)}) collective-permute-start(bf16[21,128,128]{2,1,0:T(8,128)(2,1)S(1)} %collective-permute-done.15.refs_2_), channel_id=1, source_target_pairs={{8,0},{1,8},{9,1},{3,9},{11,3},{2,11},{10,2},{0,10},{12,4},{5,12},... | collective-permute-start | bytes 2064392 | tf_op jit(solution)/shard_map/ppermute | solution.py:60
  90.4 17.6 %collective-permute-start.19 = (bf16[21,128,128]{2,1,0:T(8,128)(2,1)S(1)}, bf16[21,128,128]{2,1,0:T(8,128)(2,1)S(1)}, u32[]{:S(2)}, u32[]{:S(2)}) collective-permute-start(bf16[21,128,128]{2,1,0:T(8,128)(2,1)S(1)} %collective-permute-done.16.refs_3_), channel_id=1, source_target_pairs={{8,0},{1,8},{9,1},{3,9},{11,3},{2,11},{10,2},{0,10},{12,4},{5,12},... | collective-permute-start | bytes 2064392 | tf_op jit(solution)/shard_map/ppermute | solution.py:60
  93.3 18.2 %collective-permute-start.3 = (bf16[8,128,128]{2,1,0:T(8,128)(2,1)S(1)}, bf16[8,128,128]{2,1,0:T(8,128)(2,1)S(1)}, u32[]{:S(2)}, u32[]{:S(2)}) collective-permute-start(bf16[8,128,128]{2,1,0:T(8,128)(2,1)S(1)} %collective-permute-done.1), channel_id=1, source_target_pairs={{8,0},{1,8},{9,1},{3,9},{11,3},{2,11},{10,2},{0,10},{12,4},{5,12},... | collective-permute-start | bytes 786440 | tf_op jit(solution)/shard_map/ppermute | solution.py:60
  95.1 16.5 %collective-permute-start.4 = (bf16[8,128,128]{2,1,0:T(8,128)(2,1)S(1)}, bf16[8,128,128]{2,1,0:T(8,128)(2,1)S(1)}, u32[]{:S(2)}, u32[]{:S(2)}) collective-permute-start(bf16[8,128,128]{2,1,0:T(8,128)(2,1)S(1)} %collective-permute-done.2), channel_id=1, source_target_pairs={{10,0},{0,8},{8,1},{1,9},{9,3},{3,11},{11,2},{2,10},{14,4},{4,12},... | collective-permute-start | bytes 786440 | tf_op jit(solution)/shard_map/ppermute | solution.py:60
  107.9 10.4 %collective-permute-start.20 = (bf16[21,128,128]{2,1,0:T(8,128)(2,1)S(1)}, bf16[21,128,128]{2,1,0:T(8,128)(2,1)S(1)}, u32[]{:S(2)}, u32[]{:S(2)}) collective-permute-start(bf16[21,128,128]{2,1,0:T(8,128)(2,1)S(1)} %collective-permute-done.18.refs_4_), channel_id=1, source_target_pairs={{8,0},{1,8},{9,1},{3,9},{11,3},{2,11},{10,2},{0,10},{12,4},{5,12},... | collective-permute-start | bytes 2064392 | tf_op jit(solution)/shard_map/ppermute | solution.py:60
  109.8 15.8 %collective-permute-start.21 = (bf16[21,128,128]{2,1,0:T(8,128)(2,1)S(1)}, bf16[21,128,128]{2,1,0:T(8,128)(2,1)S(1)}, u32[]{:S(2)}, u32[]{:S(2)}) collective-permute-start(bf16[21,128,128]{2,1,0:T(8,128)(2,1)S(1)} %collective-permute-done.19.refs_5_), channel_id=1, source_target_pairs={{8,0},{1,8},{9,1},{3,9},{11,3},{2,11},{10,2},{0,10},{12,4},{5,12},... | collective-permute-start | bytes 2064392 | tf_op jit(solution)/shard_map/ppermute | solution.py:60
  132.2 12.3 %collective-permute-start.41 = (bf16[21,128,128]{2,1,0:T(8,128)(2,1)S(1)}, bf16[21,128,128]{2,1,0:T(8,128)(2,1)S(1)}, u32[]{:S(2)}, u32[]{:S(2)}) collective-permute-start(bf16[21,128,128]{2,1,0:T(8,128)(2,1)S(1)} %fusion.17), channel_id=1, source_target_pairs={{10,0},{0,8},{8,1},{1,9},{9,3},{3,11},{11,2},{2,10},{14,4},{4,12},... | collective-permute-start | bytes 2064392 | tf_op jit(solution)/shard_map/ppermute | solution.py:60
  133.4 16.7 %collective-permute-start.38 = (bf16[21,128,128]{2,1,0:T(8,128)(2,1)S(1)}, bf16[21,128,128]{2,1,0:T(8,128)(2,1)S(1)}, u32[]{:S(2)}, u32[]{:S(2)}) collective-permute-start(bf16[21,128,128]{2,1,0:T(8,128)(2,1)S(1)} %fusion.16), channel_id=1, source_target_pairs={{10,0},{0,8},{8,1},{1,9},{9,3},{3,11},{11,2},{2,10},{14,4},{4,12},... | collective-permute-start | bytes 2064392 | tf_op jit(solution)/shard_map/ppermute | solution.py:60
  140.9 10.5 %collective-permute-start.22 = (bf16[21,128,128]{2,1,0:T(8,128)(2,1)S(1)}, bf16[21,128,128]{2,1,0:T(8,128)(2,1)S(1)}, u32[]{:S(2)}, u32[]{:S(2)}) collective-permute-start(bf16[21,128,128]{2,1,0:T(8,128)(2,1)S(1)} %get-tuple-element.90.refs_0_), channel_id=1, source_target_pairs={{8,0},{1,8},{9,1},{3,9},{11,3},{2,11},{10,2},{0,10},{12,4},{5,12},... | collective-permute-start | bytes 2064392 | tf_op jit(solution)/shard_map/ppermute | solution.py:60
  142.9 15.8 %collective-permute-start.23 = (bf16[21,128,128]{2,1,0:T(8,128)(2,1)S(1)}, bf16[21,128,128]{2,1,0:T(8,128)(2,1)S(1)}, u32[]{:S(2)}, u32[]{:S(2)}) collective-permute-start(bf16[21,128,128]{2,1,0:T(8,128)(2,1)S(1)} %get-tuple-element.91.refs_1_), channel_id=1, source_target_pairs={{8,0},{1,8},{9,1},{3,9},{11,3},{2,11},{10,2},{0,10},{12,4},{5,12},... | collective-permute-start | bytes 2064392 | tf_op jit(solution)/shard_map/ppermute | solution.py:60
  145.6 15.3 %collective-permute-start.42 = (bf16[21,128,128]{2,1,0:T(8,128)(2,1)S(1)}, bf16[21,128,128]{2,1,0:T(8,128)(2,1)S(1)}, u32[]{:S(2)}, u32[]{:S(2)}) collective-permute-start(bf16[21,128,128]{2,1,0:T(8,128)(2,1)S(1)} %fusion.12), channel_id=1, source_target_pairs={{10,0},{0,8},{8,1},{1,9},{9,3},{3,11},{11,2},{2,10},{14,4},{4,12},... | collective-permute-start | bytes 2064392 | tf_op jit(solution)/shard_map/ppermute | solution.py:60
  151.3 13.6 %collective-permute-start.39 = (bf16[21,128,128]{2,1,0:T(8,128)(2,1)S(1)}, bf16[21,128,128]{2,1,0:T(8,128)(2,1)S(1)}, u32[]{:S(2)}, u32[]{:S(2)}) collective-permute-start(bf16[21,128,128]{2,1,0:T(8,128)(2,1)S(1)} %fusion.14), channel_id=1, source_target_pairs={{10,0},{0,8},{8,1},{1,9},{9,3},{3,11},{11,2},{2,10},{14,4},{4,12},... | collective-permute-start | bytes 2064392 | tf_op jit(solution)/shard_map/ppermute | solution.py:60
  151.3 15.8 %collective-permute-start.25 = (bf16[4,128,128]{2,1,0:T(8,128)(2,1)S(1)}, bf16[4,128,128]{2,1,0:T(8,128)(2,1)S(1)}, u32[]{:S(2)}, u32[]{:S(2)}) collective-permute-start(bf16[4,128,128]{2,1,0:T(8,128)(2,1)S(1)} %get-tuple-element.129.refs_3_), channel_id=1, source_target_pairs={{10,0},{0,8},{8,1},{1,9},{9,3},{3,11},{11,2},{2,10},{14,4},{4,12},... | collective-permute-start | bytes 393224 | tf_op jit(solution)/shard_map/ppermute | solution.py:60
  151.4 33.5 %collective-permute-start.28 = (bf16[21,128,128]{2,1,0:T(8,128)(2,1)S(1)}, bf16[21,128,128]{2,1,0:T(8,128)(2,1)S(1)}, u32[]{:S(2)}, u32[]{:S(2)}) collective-permute-start(bf16[21,128,128]{2,1,0:T(8,128)(2,1)S(1)} %collective-permute-done.22.refs_2_), channel_id=1, source_target_pairs={{8,0},{1,8},{9,1},{3,9},{11,3},{2,11},{10,2},{0,10},{12,4},{5,12},... | collective-permute-start | bytes 2064392 | tf_op jit(solution)/shard_map/ppermute | solution.py:60
  158.7 26.3 %collective-permute-start.29 = (bf16[21,128,128]{2,1,0:T(8,128)(2,1)S(1)}, bf16[21,128,128]{2,1,0:T(8,128)(2,1)S(1)}, u32[]{:S(2)}, u32[]{:S(2)}) collective-permute-start(bf16[21,128,128]{2,1,0:T(8,128)(2,1)S(1)} %collective-permute-done.23.refs_3_), channel_id=1, source_target_pairs={{8,0},{1,8},{9,1},{3,9},{11,3},{2,11},{10,2},{0,10},{12,4},{5,12},... | collective-permute-start | bytes 2064392 | tf_op jit(solution)/shard_map/ppermute | solution.py:60
  162.0 26.5 %collective-permute-start.43 = (bf16[21,128,128]{2,1,0:T(8,128)(2,1)S(1)}, bf16[21,128,128]{2,1,0:T(8,128)(2,1)S(1)}, u32[]{:S(2)}, u32[]{:S(2)}) collective-permute-start(bf16[21,128,128]{2,1,0:T(8,128)(2,1)S(1)} %fusion.13), channel_id=1, source_target_pairs={{10,0},{0,8},{8,1},{1,9},{9,3},{3,11},{11,2},{2,10},{14,4},{4,12},... | collective-permute-start | bytes 2064392 | tf_op jit(solution)/shard_map/ppermute | solution.py:60
  166.0 22.9 %collective-permute-start.40 = (bf16[21,128,128]{2,1,0:T(8,128)(2,1)S(1)}, bf16[21,128,128]{2,1,0:T(8,128)(2,1)S(1)}, u32[]{:S(2)}, u32[]{:S(2)}) collective-permute-start(bf16[21,128,128]{2,1,0:T(8,128)(2,1)S(1)} %fusion.15), channel_id=1, source_target_pairs={{10,0},{0,8},{8,1},{1,9},{9,3},{3,11},{11,2},{2,10},{14,4},{4,12},... | collective-permute-start | bytes 2064392 | tf_op jit(solution)/shard_map/ppermute | solution.py:60
  167.2 7.7 %collective-permute-start.24 = (bf16[4,128,128]{2,1,0:T(8,128)(2,1)S(1)}, bf16[4,128,128]{2,1,0:T(8,128)(2,1)S(1)}, u32[]{:S(2)}, u32[]{:S(2)}) collective-permute-start(bf16[4,128,128]{2,1,0:T(8,128)(2,1)S(1)} %get-tuple-element.129.refs_3_), channel_id=1, source_target_pairs={{8,0},{1,8},{9,1},{3,9},{11,3},{2,11},{10,2},{0,10},{12,4},{5,12},... | collective-permute-start | bytes 393224 | tf_op jit(solution)/shard_map/ppermute | solution.py:60
  174.8 7.6 %collective-permute-start.27 = (bf16[4,128,128]{2,1,0:T(8,128)(2,1)S(1)}, bf16[4,128,128]{2,1,0:T(8,128)(2,1)S(1)}, u32[]{:S(2)}, u32[]{:S(2)}) collective-permute-start(bf16[4,128,128]{2,1,0:T(8,128)(2,1)S(1)} %collective-permute-done.25.refs_5_), channel_id=1, source_target_pairs={{10,0},{0,8},{8,1},{1,9},{9,3},{3,11},{11,2},{2,10},{14,4},{4,12},... | collective-permute-start | bytes 393224 | tf_op jit(solution)/shard_map/ppermute | solution.py:60
  185.0 11.6 %collective-permute-start.30 = (bf16[21,128,128]{2,1,0:T(8,128)(2,1)S(1)}, bf16[21,128,128]{2,1,0:T(8,128)(2,1)S(1)}, u32[]{:S(2)}, u32[]{:S(2)}) collective-permute-start(bf16[21,128,128]{2,1,0:T(8,128)(2,1)S(1)} %collective-permute-done.28.refs_4_), channel_id=1, source_target_pairs={{8,0},{1,8},{9,1},{3,9},{11,3},{2,11},{10,2},{0,10},{12,4},{5,12},... | collective-permute-start | bytes 2064392 | tf_op jit(solution)/shard_map/ppermute | solution.py:60
  187.0 15.8 %collective-permute-start.31 = (bf16[21,128,128]{2,1,0:T(8,128)(2,1)S(1)}, bf16[21,128,128]{2,1,0:T(8,128)(2,1)S(1)}, u32[]{:S(2)}, u32[]{:S(2)}) collective-permute-start(bf16[21,128,128]{2,1,0:T(8,128)(2,1)S(1)} %collective-permute-done.29.refs_5_), channel_id=1, source_target_pairs={{8,0},{1,8},{9,1},{3,9},{11,3},{2,11},{10,2},{0,10},{12,4},{5,12},... | collective-permute-start | bytes 2064392 | tf_op jit(solution)/shard_map/ppermute | solution.py:60
  195.0 17.7 %collective-permute-start.47 = (bf16[21,128,128]{2,1,0:T(8,128)(2,1)S(1)}, bf16[21,128,128]{2,1,0:T(8,128)(2,1)S(1)}, u32[]{:S(2)}, u32[]{:S(2)}) collective-permute-start(bf16[21,128,128]{2,1,0:T(8,128)(2,1)S(1)} %fusion.19), channel_id=1, source_target_pairs={{10,0},{0,8},{8,1},{1,9},{9,3},{3,11},{11,2},{2,10},{14,4},{4,12},... | collective-permute-start | bytes 2064392 | tf_op jit(solution)/shard_map/ppermute | solution.py:60
  195.4 17.7 %collective-permute-start.44 = (bf16[21,128,128]{2,1,0:T(8,128)(2,1)S(1)}, bf16[21,128,128]{2,1,0:T(8,128)(2,1)S(1)}, u32[]{:S(2)}, u32[]{:S(2)}) collective-permute-start(bf16[21,128,128]{2,1,0:T(8,128)(2,1)S(1)} %fusion.18), channel_id=1, source_target_pairs={{10,0},{0,8},{8,1},{1,9},{9,3},{3,11},{11,2},{2,10},{14,4},{4,12},... | collective-permute-start | bytes 2064392 | tf_op jit(solution)/shard_map/ppermute | solution.py:60
  209.2 10.7 %collective-permute-start.32 = (bf16[21,128,128]{2,1,0:T(8,128)(2,1)S(1)}, bf16[21,128,128]{2,1,0:T(8,128)(2,1)S(1)}, u32[]{:S(2)}, u32[]{:S(2)}) collective-permute-start(bf16[21,128,128]{2,1,0:T(8,128)(2,1)S(1)} %get-tuple-element.96.refs_0_.refs_8_), channel_id=1, source_target_pairs={{8,0},{1,8},{9,1},{3,9},{11,3},{2,11},{10,2},{0,10},{12,4},{5,12},... | collective-permute-start | bytes 2064392 | tf_op jit(solution)/shard_map/ppermute | solution.py:60
  211.4 15.8 %collective-permute-start.33 = (bf16[21,128,128]{2,1,0:T(8,128)(2,1)S(1)}, bf16[21,128,128]{2,1,0:T(8,128)(2,1)S(1)}, u32[]{:S(2)}, u32[]{:S(2)}) collective-permute-start(bf16[21,128,128]{2,1,0:T(8,128)(2,1)S(1)} %get-tuple-element.97.refs_1_.refs_9_), channel_id=1, source_target_pairs={{8,0},{1,8},{9,1},{3,9},{11,3},{2,11},{10,2},{0,10},{12,4},{5,12},... | collective-permute-start | bytes 2064392 | tf_op jit(solution)/shard_map/ppermute | solution.py:60
  213.0 16.4 %collective-permute-start.48 = (bf16[21,128,128]{2,1,0:T(8,128)(2,1)S(1)}, bf16[21,128,128]{2,1,0:T(8,128)(2,1)S(1)}, u32[]{:S(2)}, u32[]{:S(2)}) collective-permute-start(bf16[21,128,128]{2,1,0:T(8,128)(2,1)S(1)} %fusion.8), channel_id=1, source_target_pairs={{10,0},{0,8},{8,1},{1,9},{9,3},{3,11},{11,2},{2,10},{14,4},{4,12},... | collective-permute-start | bytes 2064392 | tf_op jit(solution)/shard_map/ppermute | solution.py:60
  213.5 18.1 %collective-permute-start.45 = (bf16[21,128,128]{2,1,0:T(8,128)(2,1)S(1)}, bf16[21,128,128]{2,1,0:T(8,128)(2,1)S(1)}, u32[]{:S(2)}, u32[]{:S(2)}) collective-permute-start(bf16[21,128,128]{2,1,0:T(8,128)(2,1)S(1)} %fusion.10), channel_id=1, source_target_pairs={{10,0},{0,8},{8,1},{1,9},{9,3},{3,11},{11,2},{2,10},{14,4},{4,12},... | collective-permute-start | bytes 2064392 | tf_op jit(solution)/shard_map/ppermute | solution.py:60
  219.9 14.7 %collective-permute-start.34 = (bf16[21,128,128]{2,1,0:T(8,128)(2,1)S(1)}, bf16[21,128,128]{2,1,0:T(8,128)(2,1)}, u32[]{:S(2)}, u32[]{:S(2)}) collective-permute-start(bf16[21,128,128]{2,1,0:T(8,128)(2,1)S(1)} %collective-permute-done.32.refs_2_.refs_10_), channel_id=1, source_target_pairs={{8,0},{1,8},{9,1},{3,9},{11,3},{2,11},{10,2},{0,10},{12,4},{5,12},... | collective-permute-start | bytes 2064392 | tf_op jit(solution)/shard_map/ppermute | solution.py:60
  227.3 14.7 %collective-permute-start.35 = (bf16[21,128,128]{2,1,0:T(8,128)(2,1)S(1)}, bf16[21,128,128]{2,1,0:T(8,128)(2,1)}, u32[]{:S(2)}, u32[]{:S(2)}) collective-permute-start(bf16[21,128,128]{2,1,0:T(8,128)(2,1)S(1)} %collective-permute-done.33.refs_3_.refs_11_), channel_id=1, source_target_pairs={{8,0},{1,8},{9,1},{3,9},{11,3},{2,11},{10,2},{0,10},{12,4},{5,12},... | collective-permute-start | bytes 2064392 | tf_op jit(solution)/shard_map/ppermute | solution.py:60
  230.8 15.0 %collective-permute-start.49 = (bf16[21,128,128]{2,1,0:T(8,128)(2,1)}, bf16[21,128,128]{2,1,0:T(8,128)(2,1)S(1)}, u32[]{:S(2)}, u32[]{:S(2)}) collective-permute-start(bf16[21,128,128]{2,1,0:T(8,128)(2,1)} %fusion.9), channel_id=1, source_target_pairs={{10,0},{0,8},{8,1},{1,9},{9,3},{3,11},{11,2},{2,10},{14,4},{4,12},... | collective-permute-start | bytes 2064392 | tf_op jit(solution)/shard_map/ppermute | solution.py:60
  232.8 15.9 %collective-permute-start.46 = (bf16[21,128,128]{2,1,0:T(8,128)(2,1)}, bf16[21,128,128]{2,1,0:T(8,128)(2,1)S(1)}, u32[]{:S(2)}, u32[]{:S(2)}) collective-permute-start(bf16[21,128,128]{2,1,0:T(8,128)(2,1)} %fusion.11), channel_id=1, source_target_pairs={{10,0},{0,8},{8,1},{1,9},{9,3},{3,11},{11,2},{2,10},{14,4},{4,12},... | collective-permute-start | bytes 2064392 | tf_op jit(solution)/shard_map/ppermute | solution.py:60
  234.6 19.8 %collective-permute-start.36 = (bf16[21,128,128]{2,1,0:T(8,128)(2,1)}, bf16[21,128,128]{2,1,0:T(8,128)(2,1)}, u32[]{:S(2)}, u32[]{:S(2)}) collective-permute-start(bf16[21,128,128]{2,1,0:T(8,128)(2,1)} %collective-permute-done.34.refs_4_.refs_12_), channel_id=1, source_target_pairs={{8,0},{1,8},{9,1},{3,9},{11,3},{2,11},{10,2},{0,10},{12,4},{5,12},... | collective-permute-start | bytes 2064392 | tf_op jit(solution)/shard_map/ppermute | solution.py:60
  242.0 14.9 %collective-permute-start.37 = (bf16[21,128,128]{2,1,0:T(8,128)(2,1)}, bf16[21,128,128]{2,1,0:T(8,128)(2,1)}, u32[]{:S(2)}, u32[]{:S(2)}) collective-permute-start(bf16[21,128,128]{2,1,0:T(8,128)(2,1)} %collective-permute-done.35.refs_5_.refs_13_), channel_id=1, source_target_pairs={{8,0},{1,8},{9,1},{3,9},{11,3},{2,11},{10,2},{0,10},{12,4},{5,12},... | collective-permute-start | bytes 2064392 | tf_op jit(solution)/shard_map/ppermute | solution.py:60
  264.2 5.5 %collective-permute-start.51 = (f32[2,128]{1,0:T(2,128)S(1)}, f32[2,128]{1,0:T(2,128)S(1)}, u32[]{:S(2)}, u32[]{:S(2)}) collective-permute-start(f32[2,128]{1,0:T(2,128)S(1)} %maximum_select_fusion.4), channel_id=1, source_target_pairs={{1,0},{9,8},{0,1},{8,9},{2,3},{10,11},{3,2},{11,10},{5,4},{13,12},... | collective-permute-start | bytes 3080 | tf_op jit(solution)/shard_map/ppermute | solution.py:65
  266.0 8.3 %collective-permute-start.56 = (bf16[528,128]{1,0:T(8,128)(2,1)S(1)}, bf16[528,128]{1,0:T(8,128)(2,1)}, u32[]{:S(2)}, u32[]{:S(2)}) collective-permute-start(bf16[528,128]{1,0:T(8,128)(2,1)S(1)} %get-tuple-element.137.refs_3_), channel_id=1, source_target_pairs={{2,0},{10,8},{0,1},{8,9},{1,3},{9,11},{3,2},{11,10},{6,4},{14,12},... | collective-permute-start | bytes 405512 | tf_op jit(solution)/shard_map/ppermute | solution.py:60
  266.3 8.1 %collective-permute-start.55 = (bf16[528,128]{1,0:T(8,128)(2,1)S(1)}, bf16[528,128]{1,0:T(8,128)(2,1)}, u32[]{:S(2)}, u32[]{:S(2)}) collective-permute-start(bf16[528,128]{1,0:T(8,128)(2,1)S(1)} %get-tuple-element.137.refs_3_), channel_id=1, source_target_pairs={{1,0},{9,8},{3,1},{11,9},{2,3},{10,11},{0,2},{8,10},{5,4},{13,12},... | collective-permute-start | bytes 405512 | tf_op jit(solution)/shard_map/ppermute | solution.py:60
  268.0 6.3 %collective-permute-start.54 = (bf16[528,128]{1,0:T(8,128)(2,1)S(1)}, bf16[528,128]{1,0:T(8,128)(2,1)}, u32[]{:S(2)}, u32[]{:S(2)}) collective-permute-start(bf16[528,128]{1,0:T(8,128)(2,1)S(1)} %get-tuple-element.137.refs_3_), channel_id=1, source_target_pairs={{10,0},{0,8},{8,1},{1,9},{9,3},{3,11},{11,2},{2,10},{14,4},{4,12},... | collective-permute-start | bytes 405512 | tf_op jit(solution)/shard_map/ppermute | solution.py:60
  268.0 6.3 %collective-permute-start.53 = (bf16[528,128]{1,0:T(8,128)(2,1)S(1)}, bf16[528,128]{1,0:T(8,128)(2,1)}, u32[]{:S(2)}, u32[]{:S(2)}) collective-permute-start(bf16[528,128]{1,0:T(8,128)(2,1)S(1)} %get-tuple-element.137.refs_3_), channel_id=1, source_target_pairs={{8,0},{1,8},{9,1},{3,9},{11,3},{2,11},{10,2},{0,10},{12,4},{5,12},... | collective-permute-start | bytes 405512 | tf_op jit(solution)/shard_map/ppermute | solution.py:60
  269.8 4.5 %collective-permute-start.52 = (f32[4,128]{1,0:T(4,128)S(1)}, f32[4,128]{1,0:T(4,128)S(1)}, u32[]{:S(2)}, u32[]{:S(2)}) collective-permute-start(f32[4,128]{1,0:T(4,128)S(1)} %maximum_select_fusion.2), channel_id=1, source_target_pairs={{3,0},{11,8},{2,1},{10,9},{0,3},{8,11},{1,2},{9,10},{7,4},{15,12},... | collective-permute-start | bytes 6152 | tf_op jit(solution)/shard_map/ppermute | solution.py:65
  288.8 3.6 %collective-permute-start.58 = (f32[2,128]{1,0:T(2,128)S(1)}, f32[2,128]{1,0:T(2,128)S(1)}, u32[]{:S(2)}, u32[]{:S(2)}) collective-permute-start(f32[2,128]{1,0:T(2,128)S(1)} %maximum_select_fusion.5), channel_id=1, source_target_pairs={{1,0},{9,8},{0,1},{8,9},{2,3},{10,11},{3,2},{11,10},{5,4},{13,12},... | collective-permute-start | bytes 3080 | tf_op jit(solution)/shard_map/ppermute | solution.py:65
  289.1 8.6 %collective-permute-start.63 = (f32[2,128,128]{2,1,0:T(8,128)S(1)}, f32[2,128,128]{2,1,0:T(8,128)S(1)}, u32[]{:S(2)}, u32[]{:S(2)}) collective-permute-start(f32[2,128,128]{2,1,0:T(8,128)S(1)} %get-tuple-element.164), channel_id=1, source_target_pairs={{11,0},{2,8},{10,1},{0,9},{8,3},{1,11},{9,2},{3,10},{15,4},{6,12},... | collective-permute-start | bytes 393224 | tf_op jit(solution)/shard_map/ppermute | solution.py:60
  290.4 7.3 %collective-permute-start.62 = (f32[2,128,128]{2,1,0:T(8,128)S(1)}, f32[2,128,128]{2,1,0:T(8,128)S(1)}, u32[]{:S(2)}, u32[]{:S(2)}) collective-permute-start(f32[2,128,128]{2,1,0:T(8,128)S(1)} %get-tuple-element.165), channel_id=1, source_target_pairs={{2,0},{10,8},{0,1},{8,9},{1,3},{9,11},{3,2},{11,10},{6,4},{14,12},... | collective-permute-start | bytes 393224 | tf_op jit(solution)/shard_map/ppermute | solution.py:60
  291.5 7.9 %collective-permute-start.61 = (f32[2,128,128]{2,1,0:T(8,128)S(1)}, f32[2,128,128]{2,1,0:T(8,128)S(1)}, u32[]{:S(2)}, u32[]{:S(2)}) collective-permute-start(f32[2,128,128]{2,1,0:T(8,128)S(1)} %get-tuple-element.166), channel_id=1, source_target_pairs={{10,0},{0,8},{8,1},{1,9},{9,3},{3,11},{11,2},{2,10},{14,4},{4,12},... | collective-permute-start | bytes 393224 | tf_op jit(solution)/shard_map/ppermute | solution.py:60
  292.4 4.5 %collective-permute-start.59 = (f32[4,128]{1,0:T(4,128)S(1)}, f32[4,128]{1,0:T(4,128)S(1)}, u32[]{:S(2)}, u32[]{:S(2)}) collective-permute-start(f32[4,128]{1,0:T(4,128)S(1)} %maximum_select_fusion.3), channel_id=1, source_target_pairs={{3,0},{11,8},{2,1},{10,9},{0,3},{8,11},{1,2},{9,10},{7,4},{15,12},... | collective-permute-start | bytes 6152 | tf_op jit(solution)/shard_map/ppermute | solution.py:65
  297.0 3.7 %collective-permute-start.60 = (f32[8,128]{1,0:T(8,128)S(1)}, f32[8,128]{1,0:T(8,128)S(1)}, u32[]{:S(2)}, u32[]{:S(2)}) collective-permute-start(f32[8,128]{1,0:T(8,128)S(1)} %maximum_select_fusion.1.table_ref), channel_id=1, source_target_pairs={{0,16},{8,17},{1,18},{9,19},{3,20},{11,21},{2,22},{10,23},{4,24},{... | collective-permute-start | bytes 12296 | tf_op jit(solution)/shard_map/ppermute | solution.py:55
  304.1 11.2 %collective-permute-start.64 = (bf16[128,128]{1,0:T(8,128)(2,1)S(1)}, bf16[128,128]{1,0:T(8,128)(2,1)S(1)}, u32[]{:S(2)}, u32[]{:S(2)}) collective-permute-start(bf16[128,128]{1,0:T(8,128)(2,1)S(1)} %get-tuple-element.171), channel_id=1, source_target_pairs={{0,16},{8,17},{1,18},{9,19},{3,20},{11,21},{2,22},{10,23},{4,24},{... | collective-permute-start | bytes 98312 | tf_op jit(solution)/shard_map/ppermute | solution.py:55
  304.9 10.4 %collective-permute-start.67 = (bf16[128,128]{1,0:T(8,128)(2,1)S(1)}, bf16[128,128]{1,0:T(8,128)(2,1)S(1)}, u32[]{:S(2)}, u32[]{:S(2)}) collective-permute-start(bf16[128,128]{1,0:T(8,128)(2,1)S(1)} %get-tuple-element.172), channel_id=1, source_target_pairs={{0,21},{8,22},{1,23},{9,16},{3,17},{11,18},{2,19},{10,20},{4,29},{... | collective-permute-start | bytes 98312 | tf_op jit(solution)/shard_map/ppermute | solution.py:55
  312.7 4.9 %collective-permute-start.66 = (bf16[128,128]{1,0:T(8,128)(2,1)S(1)}, bf16[128,128]{1,0:T(8,128)(2,1)S(1)}, u32[]{:S(2)}, u32[]{:S(2)}) collective-permute-start(bf16[128,128]{1,0:T(8,128)(2,1)S(1)} %get-tuple-element.173), channel_id=1, source_target_pairs={{0,22},{8,23},{1,16},{9,17},{3,18},{11,19},{2,20},{10,21},{4,30},{... | collective-permute-start | bytes 98312 | tf_op jit(solution)/shard_map/ppermute | solution.py:55
  312.8 4.8 %collective-permute-start.65 = (bf16[128,128]{1,0:T(8,128)(2,1)S(1)}, bf16[128,128]{1,0:T(8,128)(2,1)S(1)}, u32[]{:S(2)}, u32[]{:S(2)}) collective-permute-start(bf16[128,128]{1,0:T(8,128)(2,1)S(1)} %get-tuple-element.174), channel_id=1, source_target_pairs={{0,23},{8,16},{1,17},{9,18},{3,19},{11,20},{2,21},{10,22},{4,31},{... | collective-permute-start | bytes 98312 | tf_op jit(solution)/shard_map/ppermute | solution.py:55
  (34 other events, 224.3 us)

commit v6 on v5

--- a/solution.py
+++ b/solution.py
@@ -767,11 +767,20 @@
         for t in range(1, states):
             if step == 0 and t == states - 1:
                 left, envs[-1] = after(left, envs[-1])
-            if step == 1 and t == states - 1:
-                rolled_vector, envs[-1] = after(rolled_vector, envs[-1])
             envs.append(ahead(envs[-1], 1))
+        gathered = left_front(left, rolled[step][:, :states], weights[0][step], left_groups)
+
+        def left_part(s, piece):
+            return jnp.einsum(
+                "xy,vxz->vyz",
+                left_isos[step][s],
+                gathered[s][piece],
+                preferred_element_type=jnp.float32,
+            )
+
+        sent = [left_part(states - 1, piece).astype(jnp.bfloat16) for piece in range(pieces)]
         if step == 0:
-            rolled, envs = after(rolled, envs)
+            (rolled, rolled_vector, sent), envs = after((rolled, rolled_vector, sent), envs)
         right, square = right_whole(
             envs,
             right_isos[step],
@@ -781,18 +790,10 @@
         )
         right_squares.append(square)
 
-        gathered = left_front(left, rolled[step][:, :states], weights[0][step], left_groups)
-        moved = [None] * pieces
-        for s in reversed(range(1, states)):
+        moved = [places.ahead(chunk, -1) for chunk in sent]
+        for s in reversed(range(1, states - 1)):
             for piece in range(pieces):
-                part = jnp.einsum(
-                    "xy,vxz->vyz",
-                    left_isos[step][s],
-                    gathered[s][piece],
-                    preferred_element_type=jnp.float32,
-                )
-                if moved[piece] is not None:
-                    part = part + moved[piece].astype(jnp.float32)
+                part = left_part(s, piece) + moved[piece].astype(jnp.float32)
                 moved[piece] = places.ahead(part.astype(jnp.bfloat16), -1)
         closed = [
             left_close(left_isos[step][0], gathered[0][piece], moved[piece])

time: 320 us -> 312 us (0.975)
  waiting for transfers between devices: 117 us -> 87.3 us
  starting transfers between devices: 110 us -> 130 us
    ppermute x52, waiting for transfers between devices: 104 us -> 72.5 us  [ahead(): lax.ppermute(x, BOTH, self.pairs(lambda g, k: self.slot(g + chain_by, k +...]
    ppermute x52, starting transfers between devices: 67.3 us -> 88.4 us  [ahead(): lax.ppermute(x, BOTH, self.pairs(lambda g, k: self.slot(g + chain_by, k +...]
  transfers between devices with their start and end apart: 68 -> 68, of which waited for: 28 -> 29; matrix products, arithmetic and copies ran while one was open for 7% -> 8% of each run, Pallas kernels for 10% -> 12%
where the time goes in v6:
time: 312 us; the launch traced here: 309 us
  starting transfers between devices  130 us (42%)
  waiting for transfers between devices  87.3 us (28%)
  Pallas kernels  52.7 us (17%)
  local copies, waits for them, and re-layouts  12.1 us (4%)
  matrix products  11.1 us (4%)
  blocking collectives  7.9 us (3%)
  other arithmetic  5.6 us (2%)
    ppermute x52, starting transfers between devices, ahead(): lax.ppermute(x, BOTH, self.pairs(lambda g, k: self.slot(g + chain_by, k +...  88.4 us
    ppermute x52, waiting for transfers between devices, ahead(): lax.ppermute(x, BOTH, self.pairs(lambda g, k: self.slot(g + chain_by, k +...  72.5 us
    pallas_call x19, Pallas kernels, call(): pl.pallas_call(kernel, out_shape=out_shape, scratch_shapes=scratch_shapes...  52.7 us
    ppermute x5, starting transfers between devices, fetch(): lax.ppermute(x, BOTH, self.pairs(lambda g, k: self.home(g + site_by, k +...  24.1 us
    dot_general x12, matrix products, left_part(): jnp.einsum('xy,vxz->vyz', left_isos[step][s], gathered[s][piece], preferr...  10.9 us
    ppermute x5, starting transfers between devices, send_home(): lax.ppermute(x, BOTH, self.pairs(self.slot, lambda g, k: self.home(g + si...  10.3 us
    ppermute x6, waiting for transfers between devices, partner(): lax.ppermute(x, BOTH, self.pairs(lambda g, k: self.slot(g, k ^ bit), self...  8.9 us
    all_gather x1, blocking collectives, local(): lax.all_gather(weight_matrices(mpo[0], pattern[0], secs), 'site')  7.9 us
  transfers between devices with their start and end apart: 68, of which 29 were waited for; matrix products, arithmetic and copies ran while one was open for 8% of the time, Pallas kernels for 12%

profile of v6, /device:TPU:0, one launch (start us, length us, event | category | flops | bytes accessed | tf_op | source)
XLA Modules:
  0.0 308.8 jit_solution(102243917770697838)
XLA Ops:
  0.6 5.0 %collective-permute-start.5 = (bf16[4,128,128]{2,1,0:T(8,128)(2,1)}, bf16[4,128,128]{2,1,0:T(8,128)(2,1)S(1)}, u32[]{:S(2)}, u32[]{:S(2)}) collective-permute-start(bf16[4,128,128]{2,1,0:T(8,128)(2,1)} %bitcast.190), channel_id=1, source_target_pairs={{8,0},{9,8},{10,1},{11,9},{12,3},{13,11},{14,2},{15,10},{16,4},{17... | collective-permute-start | bytes 393224 | tf_op jit(solution)/shard_map/ppermute | solution.py:50
  7.2 3.9 %collective-permute-start.6 = (bf16[4,128,128]{2,1,0:T(8,128)(2,1)}, bf16[4,128,128]{2,1,0:T(8,128)(2,1)S(1)}, u32[]{:S(2)}, u32[]{:S(2)}) collective-permute-start(bf16[4,128,128]{2,1,0:T(8,128)(2,1)} %bitcast.193), channel_id=1, source_target_pairs={{24,0},{25,8},{26,1},{27,9},{28,3},{29,11},{30,2},{31,10},{0,4},{1... | collective-permute-start | bytes 393224 | tf_op jit(solution)/shard_map/ppermute | solution.py:50
  11.2 2.9 pad_maximum_fusion
  14.1 13.8 %collective-permute-start = (bf16[50,128,128]{2,1,0:T(8,128)(2,1)}, bf16[50,128,128]{2,1,0:T(8,128)(2,1)}, u32[]{:S(2)}, u32[]{:S(2)}) collective-permute-start(bf16[50,128,128]{2,1,0:T(8,128)(2,1)} %pad_maximum_fusion), channel_id=1, source_target_pairs={{0,0},{1,8},{2,1},{3,9},{4,3},{5,11},{6,2},{7,10},{8,4},{9,12},{10... | collective-permute-start | bytes 4915208 | tf_op jit(solution)/shard_map/ppermute | solution.py:50
  28.8 7.9 %all-gather = bf16[8,168,168]{2,1,0:T(8,128)(2,1)S(1)} all-gather(bf16[2,168,168]{2,1,0:T(8,128)(2,1)S(1)} %pad_maximum_fusion.2), channel_id=2, replica_groups=mesh['site'=4,'sec'=8] {'site'}, dimensions={0}, use_global_device_ids=true | all-gather | bytes 564480 | tf_op jit(solution)/shard_map/all_gather | solution.py:742
  43.2 3.2 %collective-permute-start.14 = (bf16[128,128]{1,0:T(8,128)(2,1)S(1)}, bf16[128,128]{1,0:T(8,128)(2,1)S(1)}, u32[]{:S(2)}, u32[]{:S(2)}) collective-permute-start(bf16[128,128]{1,0:T(8,128)(2,1)S(1)} %get-tuple-element.168.centre_ref), channel_id=1, source_target_pairs={{9,0},{3,8},{11,1},{2,9},{10,3},{0,11},{8,2},{1,10},{13,4},{7,12},... | collective-permute-start | bytes 98312 | tf_op jit(solution)/shard_map/ppermute | solution.py:60
  47.9 2.5 collective-permute-start.8
  51.2 3.6 %collective-permute-start.15 = (bf16[4,128,128]{2,1,0:T(8,128)(2,1)S(1)}, bf16[4,128,128]{2,1,0:T(8,128)(2,1)S(1)}, u32[]{:S(2)}, u32[]{:S(2)}) collective-permute-start(bf16[4,128,128]{2,1,0:T(8,128)(2,1)S(1)} %get-tuple-element.129.refs_3_), channel_id=1, source_target_pairs={{8,0},{1,8},{9,1},{3,9},{11,3},{2,11},{10,2},{0,10},{12,4},{5,12},... | collective-permute-start | bytes 393224 | tf_op jit(solution)/shard_map/ppermute | solution.py:60
  54.8 2.4 collective-permute-start.9
  57.4 3.7 %collective-permute-done.9 = bf16[8,128,128]{2,1,0:T(8,128)(2,1)S(1)} collective-permute-done((bf16[8,128,128]{2,1,0:T(8,128)(2,1)S(1)}, bf16[8,128,128]{2,1,0:T(8,128)(2,1)S(1)}, u32[]{:S(2)}, u32[]{:S(2)}) %collective-permute-start.9) | collective-permute-done | bytes 262176 | tf_op jit(solution)/shard_map/ppermute | solution.py:60
  61.2 1.6 fusion.32
  64.6 3.1 %collective-permute-start.1 = (bf16[8,128,128]{2,1,0:T(8,128)(2,1)S(1)}, bf16[8,128,128]{2,1,0:T(8,128)(2,1)S(1)}, u32[]{:S(2)}, u32[]{:S(2)}) collective-permute-start(bf16[8,128,128]{2,1,0:T(8,128)(2,1)S(1)} %concatenate.64), channel_id=1, source_target_pairs={{8,0},{1,8},{9,1},{3,9},{11,3},{2,11},{10,2},{0,10},{12,4},{5,12},... | collective-permute-start | bytes 786440 | tf_op jit(solution)/shard_map/ppermute | solution.py:60
  67.9 1.7 collective-permute-start.20
  71.9 2.6 collective-permute-done.1
  74.5 2.2 collective-permute-start.3
  76.8 5.8 %collective-permute-start.4 = (bf16[8,128,128]{2,1,0:T(8,128)(2,1)S(1)}, bf16[8,128,128]{2,1,0:T(8,128)(2,1)S(1)}, u32[]{:S(2)}, u32[]{:S(2)}) collective-permute-start(bf16[8,128,128]{2,1,0:T(8,128)(2,1)S(1)} %collective-permute-done.2), channel_id=1, source_target_pairs={{10,0},{0,8},{8,1},{1,9},{9,3},{3,11},{11,2},{2,10},{14,4},{4,12},... | collective-permute-start | bytes 786440 | tf_op jit(solution)/shard_map/ppermute | solution.py:60
  82.6 14.6 %collective-permute-done.3 = bf16[8,128,128]{2,1,0:T(8,128)(2,1)S(1)} collective-permute-done((bf16[8,128,128]{2,1,0:T(8,128)(2,1)S(1)}, bf16[8,128,128]{2,1,0:T(8,128)(2,1)S(1)}, u32[]{:S(2)}, u32[]{:S(2)}) %collective-permute-start.3) | collective-permute-done | bytes 262176 | tf_op jit(solution)/shard_map/ppermute | solution.py:60
  97.2 2.5 collective-permute-start.16
  99.7 6.6 %collective-permute-start.23 = (bf16[21,128,128]{2,1,0:T(8,128)(2,1)S(1)}, bf16[21,128,128]{2,1,0:T(8,128)(2,1)S(1)}, u32[]{:S(2)}, u32[]{:S(2)}) collective-permute-start(bf16[21,128,128]{2,1,0:T(8,128)(2,1)S(1)} %collective-permute-done.22.refs_3_), channel_id=1, source_target_pairs={{8,0},{1,8},{9,1},{3,9},{11,3},{2,11},{10,2},{0,10},{12,4},{5,12},... | collective-permute-start | bytes 2064392 | tf_op jit(solution)/shard_map/ppermute | solution.py:60
  106.4 2.0 collective-permute-start.17
  108.6 6.9 %collective-permute-done.23.refs_5_ = bf16[21,128,128]{2,1,0:T(8,128)(2,1)S(1)} collective-permute-done((bf16[21,128,128]{2,1,0:T(8,128)(2,1)S(1)}, bf16[21,128,128]{2,1,0:T(8,128)(2,1)S(1)}, u32[]{:S(2)}, u32[]{:S(2)}) %collective-permute-start.23) | collective-permute-done | bytes 688160 | tf_op jit(solution)/shard_map/ppermute | solution.py:60
  115.5 1.9 collective-permute-start.24
  117.4 6.6 %collective-permute-start.25 = (bf16[21,128,128]{2,1,0:T(8,128)(2,1)S(1)}, bf16[21,128,128]{2,1,0:T(8,128)(2,1)S(1)}, u32[]{:S(2)}, u32[]{:S(2)}) collective-permute-start(bf16[21,128,128]{2,1,0:T(8,128)(2,1)S(1)} %collective-permute-done.23.refs_5_), channel_id=1, source_target_pairs={{8,0},{1,8},{9,1},{3,9},{11,3},{2,11},{10,2},{0,10},{12,4},{5,12},... | collective-permute-start | bytes 2064392 | tf_op jit(solution)/shard_map/ppermute | solution.py:60
  124.0 5.2 %shard_map.145 = (bf16[21,128,128]{2,1,0:T(8,128)(2,1)S(1)}, bf16[21,128,128]{2,1,0:T(8,128)(2,1)S(1)}, bf16[21,128,128]{2,1,0:T(8,128)(2,1)S(1)}, bf16[21,128,1...) custom-call(bf16[21,128,128]{2,1,0:T(8,128)(2,1)S(1)} %get-tuple-ele, ...), custom_call_target="tpu_custom_call" | custom-call | flops 2334130176 | bytes 3076096 | tf_op jit(solution)/shard_map/pallas_call | solution.py:517
  131.5 1.7 collective-permute-done.25.refs_7_
  133.3 7.8 %collective-permute-start.41 = (bf16[21,128,128]{2,1,0:T(8,128)(2,1)S(1)}, bf16[21,128,128]{2,1,0:T(8,128)(2,1)S(1)}, u32[]{:S(2)}, u32[]{:S(2)}) collective-permute-start(bf16[21,128,128]{2,1,0:T(8,128)(2,1)S(1)} %fusion.17), channel_id=1, source_target_pairs={{10,0},{0,8},{8,1},{1,9},{9,3},{3,11},{11,2},{2,10},{14,4},{4,12},... | collective-permute-start | bytes 2064392 | tf_op jit(solution)/shard_map/ppermute | solution.py:60
  142.1 6.3 %shard_map.146 = (bf16[21,128,128]{2,1,0:T(8,128)(2,1)S(1)}, bf16[21,128,128]{2,1,0:T(8,128)(2,1)S(1)}, f32[8,128]{1,0:T(8,128)S(1)}) custom-call(bf16[21,128,128]{2,1,0:T(8,128)(2,1)S(1)} %get-tuple-element.85.refs_0_, bf16[21,128,128]{2,1,0:T(8,128)(2,1)S(1)} %get-tuple-element.86.refs_1_, bf16[21,128,128]{2,1,0:T(8,128)(2,1)S(1)} %collective-permute-done.20.refs_2_, ...), custom_call_target="tpu_custom_call" | custom-call | flops 2334130176 | bytes 7335936 | tf_op jit(solution)/shard_map/pallas_call | solution.py:517
  148.4 1.8 collective-permute-start.26
  153.1 4.4 %collective-permute-start.39 = (bf16[21,128,128]{2,1,0:T(8,128)(2,1)S(1)}, bf16[21,128,128]{2,1,0:T(8,128)(2,1)S(1)}, u32[]{:S(2)}, u32[]{:S(2)}) collective-permute-start(bf16[21,128,128]{2,1,0:T(8,128)(2,1)S(1)} %fusion.14), channel_id=1, source_target_pairs={{10,0},{0,8},{8,1},{1,9},{9,3},{3,11},{11,2},{2,10},{14,4},{4,12},... | collective-permute-start | bytes 2064392 | tf_op jit(solution)/shard_map/ppermute | solution.py:60
  158.7 2.2 collective-permute-start.28
  160.9 5.2 %collective-permute-done.27.refs_3_ = bf16[21,128,128]{2,1,0:T(8,128)(2,1)S(1)} collective-permute-done((bf16[21,128,128]{2,1,0:T(8,128)(2,1)S(1)}, bf16[21,128,128]{2,1,0:T(8,128)(2,1)S(1)}, u32[]{:S(2)}, u32[]{:S(2)}) %collective-permute-start.27) | collective-permute-done | bytes 688160 | tf_op jit(solution)/shard_map/ppermute | solution.py:60
  166.1 2.2 collective-permute-start.29
  170.6 1.6 collective-permute-start.40
  173.4 2.2 collective-permute-start.30
  175.6 5.2 %collective-permute-done.29.refs_5_ = bf16[21,128,128]{2,1,0:T(8,128)(2,1)S(1)} collective-permute-done((bf16[21,128,128]{2,1,0:T(8,128)(2,1)S(1)}, bf16[21,128,128]{2,1,0:T(8,128)(2,1)S(1)}, u32[]{:S(2)}, u32[]{:S(2)}) %collective-permute-start.29) | collective-permute-done | bytes 688160 | tf_op jit(solution)/shard_map/ppermute | solution.py:60
  180.8 2.2 collective-permute-start.31
  183.4 3.8 %collective-permute-done.40.moved_ref = bf16[21,128,128]{2,1,0:T(8,128)(2,1)S(1)} collective-permute-done((bf16[21,128,128]{2,1,0:T(8,128)(2,1)S(1)}, bf16[21,128,128]{2,1,0:T(8,128)(2,1)S(1)}, u32[]{:S(2)}, u32[]{:S(2)}) %collective-permute-start.40) | collective-permute-done | bytes 688160 | tf_op jit(solution)/shard_map/ppermute | solution.py:60
  187.6 5.2 %shard_map.150 = (bf16[21,128,128]{2,1,0:T(8,128)(2,1)S(1)}, bf16[21,128,128]{2,1,0:T(8,128)(2,1)S(1)}, bf16[21,128,128]{2,1,0:T(8,128)(2,1)S(1)}, bf16[21,128,1...) custom-call(bf16[21,128,128]{2,1,0:T(8,128)(2,1)S(1)} %get-tuple-ele, ...), custom_call_target="tpu_custom_call" | custom-call | flops 2334130176 | bytes 3076096 | tf_op jit(solution)/shard_map/pallas_call | solution.py:517
  195.6 6.3 %shard_map.147 = (bf16[21,128,128]{2,1,0:T(8,128)(2,1)S(1)}, bf16[21,128,128]{2,1,0:T(8,128)(2,1)S(1)}, f32[8,128]{1,0:T(8,128)S(1)}) custom-call(bf16[21,128,128]{2,1,0:T(8,128)(2,1)S(1)} %get-tuple-element.95.refs_0_, bf16[21,128,128]{2,1,0:T(8,128)(2,1)S(1)} %get-tuple-element.96.refs_1_, bf16[21,128,128]{2,1,0:T(8,128)(2,1)S(1)} %collective-permute-done.26.refs_2_, ...), custom_call_target="tpu_custom_call" | custom-call | flops 2334130176 | bytes 7335936 | tf_op jit(solution)/shard_map/pallas_call | solution.py:517
  201.9 2.0 collective-permute-start.32
  204.8 6.2 %collective-permute-done.44 = bf16[21,128,128]{2,1,0:T(8,128)(2,1)S(1)} collective-permute-done((bf16[21,128,128]{2,1,0:T(8,128)(2,1)S(1)}, bf16[21,128,128]{2,1,0:T(8,128)(2,1)S(1)}, u32[]{:S(2)}, u32[]{:S(2)}) %collective-permute-start.44) | collective-permute-done | bytes 688160 | tf_op jit(solution)/shard_map/ppermute | solution.py:60
  212.3 2.2 collective-permute-start.34
  214.5 5.2 %collective-permute-done.33.refs_3_.refs_11_ = bf16[21,128,128]{2,1,0:T(8,128)(2,1)S(1)} collective-permute-done((bf16[21,128,128]{2,1,0:T(8,128)(2,1)S(1)}, bf16[21,128,128]{2,1,0:T(8,128)(2,1)S(1)}, u32[]{:S(2)}, u32[]{:S(2)}) %collective-permute-start.33) | collective-permute-done | bytes 688160 | tf_op jit(solution)/shard_map/ppermute | solution.py:60
  219.7 2.2 collective-permute-start.35
  223.2 2.5 collective-permute-done.45
  227.1 2.2 collective-permute-start.36
  229.3 5.2 %collective-permute-done.35.refs_5_.refs_13_ = bf16[21,128,128]{2,1,0:T(8,128)(2,1)} collective-permute-done((bf16[21,128,128]{2,1,0:T(8,128)(2,1)S(1)}, bf16[21,128,128]{2,1,0:T(8,128)(2,1)}, u32[]{:S(2)}, u32[]{:S(2)}) %collective-permute-start.35) | collective-permute-done | bytes 688160 | tf_op jit(solution)/shard_map/ppermute | solution.py:60
  234.5 2.2 collective-permute-start.37
  238.7 2.5 collective-permute-done.46.moved_ref
  241.7 5.2 %shard_map.153.refs_13_ = bf16[21504,128]{1,0:T(8,128)(2,1)S(1)} custom-call(bf16[21,128,128]{2,1,0:T(8,128)(2,1)S(1)} %get-tuple-element.126.refs_0_, bf16[21,128,128]{2,1,0:T(8,128)(2,1)S(1)} %get-tuple-element.127.refs_1_, bf16[1360,384]{1,0:T(8,128)(2,1)S(1)} %copy-done.21, bf16[4,128,128]{2,1,0:T(8,128)(2,1)S(1)} %get-tuple-element.129.refs_3_, ...), custom_call_target="tpu_custom_call" | custom-call | flops 2334130176 | bytes 3076096 | tf_op jit(solution)/shard_map/pallas_call | solution.py:517
  246.9 2.4 collective-permute-done.37.refs_7_.refs_15_
  249.3 3.8 %shard_map.154 = (f32[4,128,128]{2,1,0:T(8,128)S(1)}, bf16[528,128]{1,0:T(8,128)(2,1)S(1)}, f32[1,128]{1,0:T(1,128)S(1)}) custom-call(bf16[21,128,128]{2,1,0:T(8,128)(2,1)S(1)} %copy-done.1, bf16[21,128,128]{2,1,0:T(8,128)(2,1)S(1)} %copy-done.3, bf16[21,128,128]{2,1,0:T(8,128)(2,1)S(1)} %copy-done.5, bf16[21,128,128]{2,1,0:T(8,128)(2,1)S(1)} %copy-done.7, ...), custom_call_target="tpu_custom_call" | custom-call | flops 704643072 | bytes 11292672 | tf_op jit(solution)/shard_map/pallas_call | solution.py:517
  253.1 1.9 collective-permute-start.50
  255.8 1.6 collective-permute-start.51
  258.0 1.9 collective-permute-start.56
  261.1 3.9 %collective-permute-done.52 = f32[4,128]{1,0:T(4,128)S(1)} collective-permute-done((f32[4,128]{1,0:T(4,128)S(1)}, f32[4,128]{1,0:T(4,128)S(1)}, u32[]{:S(2)}, u32[]{:S(2)}) %collective-permute-start.52) | collective-permute-done | bytes 2080 | tf_op jit(solution)/shard_map/ppermute | solution.py:65
  268.5 8.9 %shard_map.155 = (f32[4,128,128]{2,1,0:T(8,128)S(1)}, f32[1,128]{1,0:T(1,128)S(1)}) custom-call(bf16[21,128,128]{2,1,0:T(8,128)(2,1)S(1)} %copy-done.11, bf16[21,128,128]{2,1,0:T(8,128)(2,1)S(1)} %copy-done.9, bf16[1360,384]{1,0:T(8,128)(2,1)S(1)} %copy-done.22, bf16[528,128]{1,0:T(8,128)(2,1)S(1)} %get-tuple-element.137.refs_3_, ...), custom_call_target="tpu_custom_call" | custom-call | flops 3038773248 | bytes 8601600 | tf_op jit(solution)/shard_map/pallas_call | solution.py:517
  283.1 1.5 collective-permute-start.59
  284.7 3.0 collective-permute-done.59
  288.4 2.9 collective-permute-done.60.table_ref
  291.4 3.5 %shard_map.157 = bf16[4,128,128]{2,1,0:T(8,128)(2,1)S(1)} custom-call(f32[4,2,128,128]{3,2,1,0:T(8,128)S(1)} %pad_maximum_fusion.1.both_ref, f32[8,128]{1,0:T(8,128)S(1)} %maximum_select_fusion.1.table_ref, bf16[128,128]{1,0:T(8,128)(2,1)S(1)} %get-tuple-element.168.centre_ref), custom_call_target="tpu_custom_call" | custom-call | flops 1258291200 | bytes 561152 | tf_op jit(solution)/shard_map/pallas_call | solution.py:517
  295.6 6.5 %collective-permute-start.65 = (bf16[128,128]{1,0:T(8,128)(2,1)S(1)}, bf16[128,128]{1,0:T(8,128)(2,1)S(1)}, u32[]{:S(2)}, u32[]{:S(2)}) collective-permute-start(bf16[128,128]{1,0:T(8,128)(2,1)S(1)} %get-tuple-element.172), channel_id=1, source_target_pairs={{0,23},{8,16},{1,17},{9,18},{3,19},{11,20},{2,21},{10,22},{4,31},{... | collective-permute-start | bytes 98312 | tf_op jit(solution)/shard_map/ppermute | solution.py:55
  302.1 2.3 collective-permute-start.67
  305.2 2.9 collective-permute-done.66
  (211 shorter events, 52.1 us)
Async XLA Ops:
  0.6 42.3 %collective-permute-start.5 = (bf16[4,128,128]{2,1,0:T(8,128)(2,1)}, bf16[4,128,128]{2,1,0:T(8,128)(2,1)S(1)}, u32[]{:S(2)}, u32[]{:S(2)}) collective-permute-start(bf16[4,128,128]{2,1,0:T(8,128)(2,1)} %bitcast.190), channel_id=1, source_target_pairs={{8,0},{9,8},{10,1},{11,9},{12,3},{13,11},{14,2},{15,10},{16,4},{17... | collective-permute-start | bytes 393224 | tf_op jit(solution)/shard_map/ppermute | solution.py:50
  6.6 36.4 %collective-permute-start.11 = (bf16[5,128,128]{2,1,0:T(8,128)(2,1)S(1)}, bf16[5,128,128]{2,1,0:T(8,128)(2,1)S(1)}, u32[]{:S(2)}, u32[]{:S(2)}) collective-permute-start(bf16[5,128,128]{2,1,0:T(8,128)(2,1)S(1)} %pad_maximum_fusion.3), channel_id=1, source_target_pairs={{16,0},{17,8},{18,1},{19,9},{20,3},{21,11},{22,2},{23,10},{24,4},{... | collective-permute-start | bytes 491528 | tf_op jit(solution)/shard_map/ppermute | solution.py:50
  7.2 35.7 %collective-permute-start.6 = (bf16[4,128,128]{2,1,0:T(8,128)(2,1)}, bf16[4,128,128]{2,1,0:T(8,128)(2,1)S(1)}, u32[]{:S(2)}, u32[]{:S(2)}) collective-permute-start(bf16[4,128,128]{2,1,0:T(8,128)(2,1)} %bitcast.193), channel_id=1, source_target_pairs={{24,0},{25,8},{26,1},{27,9},{28,3},{29,11},{30,2},{31,10},{0,4},{1... | collective-permute-start | bytes 393224 | tf_op jit(solution)/shard_map/ppermute | solution.py:50
  14.1 47.1 %collective-permute-start = (bf16[50,128,128]{2,1,0:T(8,128)(2,1)}, bf16[50,128,128]{2,1,0:T(8,128)(2,1)}, u32[]{:S(2)}, u32[]{:S(2)}) collective-permute-start(bf16[50,128,128]{2,1,0:T(8,128)(2,1)} %pad_maximum_fusion), channel_id=1, source_target_pairs={{0,0},{1,8},{2,1},{3,9},{4,3},{5,11},{6,2},{7,10},{8,4},{9,12},{10... | collective-permute-start | bytes 4915208 | tf_op jit(solution)/shard_map/ppermute | solution.py:50
  43.0 11.8 %collective-permute-start.7 = (bf16[8,128,128]{2,1,0:T(8,128)(2,1)S(1)}, bf16[8,128,128]{2,1,0:T(8,128)(2,1)S(1)}, u32[]{:S(2)}, u32[]{:S(2)}) collective-permute-start(bf16[8,128,128]{2,1,0:T(8,128)(2,1)S(1)} %constant_dynamic-update-slice_fusion), channel_id=1, source_target_pairs={{8,0},{1,8},{9,1},{3,9},{11,3},{2,11},{10,2},{0,10},{12,4},{5,12},... | collective-permute-start | bytes 786440 | tf_op jit(solution)/shard_map/ppermute | solution.py:60
  43.1 4.9 %collective-permute-start.12 = (bf16[128,128]{1,0:T(8,128)(2,1)S(1)}, bf16[128,128]{1,0:T(8,128)(2,1)S(1)}, u32[]{:S(2)}, u32[]{:S(2)}) collective-permute-start(bf16[128,128]{1,0:T(8,128)(2,1)S(1)} %get-tuple-element.168.centre_ref), channel_id=1, source_target_pairs={{8,0},{1,8},{9,1},{3,9},{11,3},{2,11},{10,2},{0,10},{12,4},{5,12},... | collective-permute-start | bytes 98312 | tf_op jit(solution)/shard_map/ppermute | solution.py:60
  43.1 7.9 %collective-permute-start.13 = (bf16[128,128]{1,0:T(8,128)(2,1)S(1)}, bf16[128,128]{1,0:T(8,128)(2,1)S(1)}, u32[]{:S(2)}, u32[]{:S(2)}) collective-permute-start(bf16[128,128]{1,0:T(8,128)(2,1)S(1)} %get-tuple-element.168.centre_ref), channel_id=1, source_target_pairs={{1,0},{9,8},{3,1},{11,9},{2,3},{10,11},{0,2},{8,10},{5,4},{13,12},... | collective-permute-start | bytes 98312 | tf_op jit(solution)/shard_map/ppermute | solution.py:60
  43.2 7.8 %collective-permute-start.14 = (bf16[128,128]{1,0:T(8,128)(2,1)S(1)}, bf16[128,128]{1,0:T(8,128)(2,1)S(1)}, u32[]{:S(2)}, u32[]{:S(2)}) collective-permute-start(bf16[128,128]{1,0:T(8,128)(2,1)S(1)} %get-tuple-element.168.centre_ref), channel_id=1, source_target_pairs={{9,0},{3,8},{11,1},{2,9},{10,3},{0,11},{8,2},{1,10},{13,4},{7,12},... | collective-permute-start | bytes 98312 | tf_op jit(solution)/shard_map/ppermute | solution.py:60
  47.9 9.3 %collective-permute-start.8 = (bf16[8,128,128]{2,1,0:T(8,128)(2,1)S(1)}, bf16[8,128,128]{2,1,0:T(8,128)(2,1)S(1)}, u32[]{:S(2)}, u32[]{:S(2)}) collective-permute-start(bf16[8,128,128]{2,1,0:T(8,128)(2,1)S(1)} %constant_dynamic-update-slice_fusion), channel_id=1, source_target_pairs={{10,0},{0,8},{8,1},{1,9},{9,3},{3,11},{11,2},{2,10},{14,4},{4,12},... | collective-permute-start | bytes 786440 | tf_op jit(solution)/shard_map/ppermute | solution.py:60
  51.2 18.4 %collective-permute-start.15 = (bf16[4,128,128]{2,1,0:T(8,128)(2,1)S(1)}, bf16[4,128,128]{2,1,0:T(8,128)(2,1)S(1)}, u32[]{:S(2)}, u32[]{:S(2)}) collective-permute-start(bf16[4,128,128]{2,1,0:T(8,128)(2,1)S(1)} %get-tuple-element.129.refs_3_), channel_id=1, source_target_pairs={{8,0},{1,8},{9,1},{3,9},{11,3},{2,11},{10,2},{0,10},{12,4},{5,12},... | collective-permute-start | bytes 393224 | tf_op jit(solution)/shard_map/ppermute | solution.py:60
  54.8 6.3 %collective-permute-start.9 = (bf16[8,128,128]{2,1,0:T(8,128)(2,1)S(1)}, bf16[8,128,128]{2,1,0:T(8,128)(2,1)S(1)}, u32[]{:S(2)}, u32[]{:S(2)}) collective-permute-start(bf16[8,128,128]{2,1,0:T(8,128)(2,1)S(1)} %collective-permute-done.7), channel_id=1, source_target_pairs={{8,0},{1,8},{9,1},{3,9},{11,3},{2,11},{10,2},{0,10},{12,4},{5,12},... | collective-permute-start | bytes 786440 | tf_op jit(solution)/shard_map/ppermute | solution.py:60
  57.3 10.5 %collective-permute-start.10 = (bf16[8,128,128]{2,1,0:T(8,128)(2,1)S(1)}, bf16[8,128,128]{2,1,0:T(8,128)(2,1)S(1)}, u32[]{:S(2)}, u32[]{:S(2)}) collective-permute-start(bf16[8,128,128]{2,1,0:T(8,128)(2,1)S(1)} %collective-permute-done.8), channel_id=1, source_target_pairs={{10,0},{0,8},{8,1},{1,9},{9,3},{3,11},{11,2},{2,10},{14,4},{4,12},... | collective-permute-start | bytes 786440 | tf_op jit(solution)/shard_map/ppermute | solution.py:60
  62.9 45.5 %collective-permute-start.19 = (bf16[42,128,128]{2,1,0:T(8,128)(2,1)S(1)}, bf16[42,128,128]{2,1,0:T(8,128)(2,1)S(1)}, u32[]{:S(2)}, u32[]{:S(2)}) collective-permute-start(bf16[42,128,128]{2,1,0:T(8,128)(2,1)S(1)} %bitcast.205), channel_id=1, source_target_pairs={{0,0},{1,8},{2,1},{3,9},{4,3},{5,11},{6,2},{7,10},{8,4},{9,12},{10... | collective-permute-start | bytes 4128776 | tf_op jit(solution)/shard_map/ppermute | solution.py:50
  64.6 9.9 %collective-permute-start.1 = (bf16[8,128,128]{2,1,0:T(8,128)(2,1)S(1)}, bf16[8,128,128]{2,1,0:T(8,128)(2,1)S(1)}, u32[]{:S(2)}, u32[]{:S(2)}) collective-permute-start(bf16[8,128,128]{2,1,0:T(8,128)(2,1)S(1)} %concatenate.64), channel_id=1, source_target_pairs={{8,0},{1,8},{9,1},{3,9},{11,3},{2,11},{10,2},{0,10},{12,4},{5,12},... | collective-permute-start | bytes 786440 | tf_op jit(solution)/shard_map/ppermute | solution.py:60
  67.8 9.0 %collective-permute-start.2 = (bf16[8,128,128]{2,1,0:T(8,128)(2,1)S(1)}, bf16[8,128,128]{2,1,0:T(8,128)(2,1)S(1)}, u32[]{:S(2)}, u32[]{:S(2)}) collective-permute-start(bf16[8,128,128]{2,1,0:T(8,128)(2,1)S(1)} %concatenate.64), channel_id=1, source_target_pairs={{10,0},{0,8},{8,1},{1,9},{9,3},{3,11},{11,2},{2,10},{14,4},{4,12},... | collective-permute-start | bytes 786440 | tf_op jit(solution)/shard_map/ppermute | solution.py:60
  67.9 31.8 %collective-permute-start.20 = (bf16[21,128,128]{2,1,0:T(8,128)(2,1)S(1)}, bf16[21,128,128]{2,1,0:T(8,128)(2,1)S(1)}, u32[]{:S(2)}, u32[]{:S(2)}) collective-permute-start(bf16[21,128,128]{2,1,0:T(8,128)(2,1)S(1)} %get-tuple-element.85.refs_0_), channel_id=1, source_target_pairs={{8,0},{1,8},{9,1},{3,9},{11,3},{2,11},{10,2},{0,10},{12,4},{5,12},... | collective-permute-start | bytes 2064392 | tf_op jit(solution)/shard_map/ppermute | solution.py:60
  69.6 30.1 %collective-permute-start.22 = (bf16[21,128,128]{2,1,0:T(8,128)(2,1)S(1)}, bf16[21,128,128]{2,1,0:T(8,128)(2,1)S(1)}, u32[]{:S(2)}, u32[]{:S(2)}) collective-permute-start(bf16[21,128,128]{2,1,0:T(8,128)(2,1)S(1)} %get-tuple-element.86.refs_1_), channel_id=1, source_target_pairs={{8,0},{1,8},{9,1},{3,9},{11,3},{2,11},{10,2},{0,10},{12,4},{5,12},... | collective-permute-start | bytes 2064392 | tf_op jit(solution)/shard_map/ppermute | solution.py:60
  74.5 22.6 %collective-permute-start.3 = (bf16[8,128,128]{2,1,0:T(8,128)(2,1)S(1)}, bf16[8,128,128]{2,1,0:T(8,128)(2,1)S(1)}, u32[]{:S(2)}, u32[]{:S(2)}) collective-permute-start(bf16[8,128,128]{2,1,0:T(8,128)(2,1)S(1)} %collective-permute-done.1), channel_id=1, source_target_pairs={{8,0},{1,8},{9,1},{3,9},{11,3},{2,11},{10,2},{0,10},{12,4},{5,12},... | collective-permute-start | bytes 786440 | tf_op jit(solution)/shard_map/ppermute | solution.py:60
  76.8 31.5 %collective-permute-start.4 = (bf16[8,128,128]{2,1,0:T(8,128)(2,1)S(1)}, bf16[8,128,128]{2,1,0:T(8,128)(2,1)S(1)}, u32[]{:S(2)}, u32[]{:S(2)}) collective-permute-start(bf16[8,128,128]{2,1,0:T(8,128)(2,1)S(1)} %collective-permute-done.2), channel_id=1, source_target_pairs={{10,0},{0,8},{8,1},{1,9},{9,3},{3,11},{11,2},{2,10},{14,4},{4,12},... | collective-permute-start | bytes 786440 | tf_op jit(solution)/shard_map/ppermute | solution.py:60
  97.2 9.2 %collective-permute-start.16 = (bf16[4,128,128]{2,1,0:T(8,128)(2,1)S(1)}, bf16[4,128,128]{2,1,0:T(8,128)(2,1)S(1)}, u32[]{:S(2)}, u32[]{:S(2)}) collective-permute-start(bf16[4,128,128]{2,1,0:T(8,128)(2,1)S(1)} %get-tuple-element.129.refs_3_), channel_id=1, source_target_pairs={{10,0},{0,8},{8,1},{1,9},{9,3},{3,11},{11,2},{2,10},{14,4},{4,12},... | collective-permute-start | bytes 393224 | tf_op jit(solution)/shard_map/ppermute | solution.py:60
  99.7 8.9 %collective-permute-start.21 = (bf16[21,128,128]{2,1,0:T(8,128)(2,1)S(1)}, bf16[21,128,128]{2,1,0:T(8,128)(2,1)S(1)}, u32[]{:S(2)}, u32[]{:S(2)}) collective-permute-start(bf16[21,128,128]{2,1,0:T(8,128)(2,1)S(1)} %collective-permute-done.20.refs_2_), channel_id=1, source_target_pairs={{8,0},{1,8},{9,1},{3,9},{11,3},{2,11},{10,2},{0,10},{12,4},{5,12},... | collective-permute-start | bytes 2064392 | tf_op jit(solution)/shard_map/ppermute | solution.py:60
  99.7 15.8 %collective-permute-start.23 = (bf16[21,128,128]{2,1,0:T(8,128)(2,1)S(1)}, bf16[21,128,128]{2,1,0:T(8,128)(2,1)S(1)}, u32[]{:S(2)}, u32[]{:S(2)}) collective-permute-start(bf16[21,128,128]{2,1,0:T(8,128)(2,1)S(1)} %collective-permute-done.22.refs_3_), channel_id=1, source_target_pairs={{8,0},{1,8},{9,1},{3,9},{11,3},{2,11},{10,2},{0,10},{12,4},{5,12},... | collective-permute-start | bytes 2064392 | tf_op jit(solution)/shard_map/ppermute | solution.py:60
  106.4 25.1 %collective-permute-start.17 = (bf16[4,128,128]{2,1,0:T(8,128)(2,1)S(1)}, bf16[4,128,128]{2,1,0:T(8,128)(2,1)S(1)}, u32[]{:S(2)}, u32[]{:S(2)}) collective-permute-start(bf16[4,128,128]{2,1,0:T(8,128)(2,1)S(1)} %collective-permute-done.15.refs_4_), channel_id=1, source_target_pairs={{8,0},{1,8},{9,1},{3,9},{11,3},{2,11},{10,2},{0,10},{12,4},{5,12},... | collective-permute-start | bytes 393224 | tf_op jit(solution)/shard_map/ppermute | solution.py:60
  108.3 23.2 %collective-permute-start.18 = (bf16[4,128,128]{2,1,0:T(8,128)(2,1)S(1)}, bf16[4,128,128]{2,1,0:T(8,128)(2,1)S(1)}, u32[]{:S(2)}, u32[]{:S(2)}) collective-permute-start(bf16[4,128,128]{2,1,0:T(8,128)(2,1)S(1)} %collective-permute-done.16.refs_5_), channel_id=1, source_target_pairs={{10,0},{0,8},{8,1},{1,9},{9,3},{3,11},{11,2},{2,10},{14,4},{4,12},... | collective-permute-start | bytes 393224 | tf_op jit(solution)/shard_map/ppermute | solution.py:60
  115.5 16.0 %collective-permute-start.24 = (bf16[21,128,128]{2,1,0:T(8,128)(2,1)S(1)}, bf16[21,128,128]{2,1,0:T(8,128)(2,1)S(1)}, u32[]{:S(2)}, u32[]{:S(2)}) collective-permute-start(bf16[21,128,128]{2,1,0:T(8,128)(2,1)S(1)} %collective-permute-done.21.refs_4_), channel_id=1, source_target_pairs={{8,0},{1,8},{9,1},{3,9},{11,3},{2,11},{10,2},{0,10},{12,4},{5,12},... | collective-permute-start | bytes 2064392 | tf_op jit(solution)/shard_map/ppermute | solution.py:60
  117.4 15.8 %collective-permute-start.25 = (bf16[21,128,128]{2,1,0:T(8,128)(2,1)S(1)}, bf16[21,128,128]{2,1,0:T(8,128)(2,1)S(1)}, u32[]{:S(2)}, u32[]{:S(2)}) collective-permute-start(bf16[21,128,128]{2,1,0:T(8,128)(2,1)S(1)} %collective-permute-done.23.refs_5_), channel_id=1, source_target_pairs={{8,0},{1,8},{9,1},{3,9},{11,3},{2,11},{10,2},{0,10},{12,4},{5,12},... | collective-permute-start | bytes 2064392 | tf_op jit(solution)/shard_map/ppermute | solution.py:60
  133.3 17.0 %collective-permute-start.41 = (bf16[21,128,128]{2,1,0:T(8,128)(2,1)S(1)}, bf16[21,128,128]{2,1,0:T(8,128)(2,1)S(1)}, u32[]{:S(2)}, u32[]{:S(2)}) collective-permute-start(bf16[21,128,128]{2,1,0:T(8,128)(2,1)S(1)} %fusion.17), channel_id=1, source_target_pairs={{10,0},{0,8},{8,1},{1,9},{9,3},{3,11},{11,2},{2,10},{14,4},{4,12},... | collective-permute-start | bytes 2064392 | tf_op jit(solution)/shard_map/ppermute | solution.py:60
  141.1 10.9 %collective-permute-start.38 = (bf16[21,128,128]{2,1,0:T(8,128)(2,1)S(1)}, bf16[21,128,128]{2,1,0:T(8,128)(2,1)S(1)}, u32[]{:S(2)}, u32[]{:S(2)}) collective-permute-start(bf16[21,128,128]{2,1,0:T(8,128)(2,1)S(1)} %fusion.16), channel_id=1, source_target_pairs={{10,0},{0,8},{8,1},{1,9},{9,3},{3,11},{11,2},{2,10},{14,4},{4,12},... | collective-permute-start | bytes 2064392 | tf_op jit(solution)/shard_map/ppermute | solution.py:60
  148.4 10.3 %collective-permute-start.26 = (bf16[21,128,128]{2,1,0:T(8,128)(2,1)S(1)}, bf16[21,128,128]{2,1,0:T(8,128)(2,1)S(1)}, u32[]{:S(2)}, u32[]{:S(2)}) collective-permute-start(bf16[21,128,128]{2,1,0:T(8,128)(2,1)S(1)} %get-tuple-element.95.refs_0_), channel_id=1, source_target_pairs={{8,0},{1,8},{9,1},{3,9},{11,3},{2,11},{10,2},{0,10},{12,4},{5,12},... | collective-permute-start | bytes 2064392 | tf_op jit(solution)/shard_map/ppermute | solution.py:60
  150.2 15.8 %collective-permute-start.27 = (bf16[21,128,128]{2,1,0:T(8,128)(2,1)S(1)}, bf16[21,128,128]{2,1,0:T(8,128)(2,1)S(1)}, u32[]{:S(2)}, u32[]{:S(2)}) collective-permute-start(bf16[21,128,128]{2,1,0:T(8,128)(2,1)S(1)} %get-tuple-element.96.refs_1_), channel_id=1, source_target_pairs={{8,0},{1,8},{9,1},{3,9},{11,3},{2,11},{10,2},{0,10},{12,4},{5,12},... | collective-permute-start | bytes 2064392 | tf_op jit(solution)/shard_map/ppermute | solution.py:60
  151.5 16.8 %collective-permute-start.42 = (bf16[21,128,128]{2,1,0:T(8,128)(2,1)S(1)}, bf16[21,128,128]{2,1,0:T(8,128)(2,1)S(1)}, u32[]{:S(2)}, u32[]{:S(2)}) collective-permute-start(bf16[21,128,128]{2,1,0:T(8,128)(2,1)S(1)} %fusion.12), channel_id=1, source_target_pairs={{10,0},{0,8},{8,1},{1,9},{9,3},{3,11},{11,2},{2,10},{14,4},{4,12},... | collective-permute-start | bytes 2064392 | tf_op jit(solution)/shard_map/ppermute | solution.py:60
  153.1 16.4 %collective-permute-start.39 = (bf16[21,128,128]{2,1,0:T(8,128)(2,1)S(1)}, bf16[21,128,128]{2,1,0:T(8,128)(2,1)S(1)}, u32[]{:S(2)}, u32[]{:S(2)}) collective-permute-start(bf16[21,128,128]{2,1,0:T(8,128)(2,1)S(1)} %fusion.14), channel_id=1, source_target_pairs={{10,0},{0,8},{8,1},{1,9},{9,3},{3,11},{11,2},{2,10},{14,4},{4,12},... | collective-permute-start | bytes 2064392 | tf_op jit(solution)/shard_map/ppermute | solution.py:60
  158.7 14.7 %collective-permute-start.28 = (bf16[21,128,128]{2,1,0:T(8,128)(2,1)S(1)}, bf16[21,128,128]{2,1,0:T(8,128)(2,1)S(1)}, u32[]{:S(2)}, u32[]{:S(2)}) collective-permute-start(bf16[21,128,128]{2,1,0:T(8,128)(2,1)S(1)} %collective-permute-done.26.refs_2_), channel_id=1, source_target_pairs={{8,0},{1,8},{9,1},{3,9},{11,3},{2,11},{10,2},{0,10},{12,4},{5,12},... | collective-permute-start | bytes 2064392 | tf_op jit(solution)/shard_map/ppermute | solution.py:60
  166.1 14.7 %collective-permute-start.29 = (bf16[21,128,128]{2,1,0:T(8,128)(2,1)S(1)}, bf16[21,128,128]{2,1,0:T(8,128)(2,1)S(1)}, u32[]{:S(2)}, u32[]{:S(2)}) collective-permute-start(bf16[21,128,128]{2,1,0:T(8,128)(2,1)S(1)} %collective-permute-done.27.refs_3_), channel_id=1, source_target_pairs={{8,0},{1,8},{9,1},{3,9},{11,3},{2,11},{10,2},{0,10},{12,4},{5,12},... | collective-permute-start | bytes 2064392 | tf_op jit(solution)/shard_map/ppermute | solution.py:60
  169.4 13.6 %collective-permute-start.43 = (bf16[21,128,128]{2,1,0:T(8,128)(2,1)S(1)}, bf16[21,128,128]{2,1,0:T(8,128)(2,1)S(1)}, u32[]{:S(2)}, u32[]{:S(2)}) collective-permute-start(bf16[21,128,128]{2,1,0:T(8,128)(2,1)S(1)} %fusion.13), channel_id=1, source_target_pairs={{10,0},{0,8},{8,1},{1,9},{9,3},{3,11},{11,2},{2,10},{14,4},{4,12},... | collective-permute-start | bytes 2064392 | tf_op jit(solution)/shard_map/ppermute | solution.py:60
  170.6 16.6 %collective-permute-start.40 = (bf16[21,128,128]{2,1,0:T(8,128)(2,1)S(1)}, bf16[21,128,128]{2,1,0:T(8,128)(2,1)S(1)}, u32[]{:S(2)}, u32[]{:S(2)}) collective-permute-start(bf16[21,128,128]{2,1,0:T(8,128)(2,1)S(1)} %fusion.15), channel_id=1, source_target_pairs={{10,0},{0,8},{8,1},{1,9},{9,3},{3,11},{11,2},{2,10},{14,4},{4,12},... | collective-permute-start | bytes 2064392 | tf_op jit(solution)/shard_map/ppermute | solution.py:60
  173.4 21.7 %collective-permute-start.30 = (bf16[21,128,128]{2,1,0:T(8,128)(2,1)S(1)}, bf16[21,128,128]{2,1,0:T(8,128)(2,1)S(1)}, u32[]{:S(2)}, u32[]{:S(2)}) collective-permute-start(bf16[21,128,128]{2,1,0:T(8,128)(2,1)S(1)} %collective-permute-done.28.refs_4_), channel_id=1, source_target_pairs={{8,0},{1,8},{9,1},{3,9},{11,3},{2,11},{10,2},{0,10},{12,4},{5,12},... | collective-permute-start | bytes 2064392 | tf_op jit(solution)/shard_map/ppermute | solution.py:60
  180.8 14.7 %collective-permute-start.31 = (bf16[21,128,128]{2,1,0:T(8,128)(2,1)S(1)}, bf16[21,128,128]{2,1,0:T(8,128)(2,1)S(1)}, u32[]{:S(2)}, u32[]{:S(2)}) collective-permute-start(bf16[21,128,128]{2,1,0:T(8,128)(2,1)S(1)} %collective-permute-done.29.refs_5_), channel_id=1, source_target_pairs={{8,0},{1,8},{9,1},{3,9},{11,3},{2,11},{10,2},{0,10},{12,4},{5,12},... | collective-permute-start | bytes 2064392 | tf_op jit(solution)/shard_map/ppermute | solution.py:60
  193.2 10.7 %collective-permute-start.47 = (bf16[21,128,128]{2,1,0:T(8,128)(2,1)S(1)}, bf16[21,128,128]{2,1,0:T(8,128)(2,1)S(1)}, u32[]{:S(2)}, u32[]{:S(2)}) collective-permute-start(bf16[21,128,128]{2,1,0:T(8,128)(2,1)S(1)} %fusion.19), channel_id=1, source_target_pairs={{10,0},{0,8},{8,1},{1,9},{9,3},{3,11},{11,2},{2,10},{14,4},{4,12},... | collective-permute-start | bytes 2064392 | tf_op jit(solution)/shard_map/ppermute | solution.py:60
  193.7 17.3 %collective-permute-start.44 = (bf16[21,128,128]{2,1,0:T(8,128)(2,1)S(1)}, bf16[21,128,128]{2,1,0:T(8,128)(2,1)S(1)}, u32[]{:S(2)}, u32[]{:S(2)}) collective-permute-start(bf16[21,128,128]{2,1,0:T(8,128)(2,1)S(1)} %fusion.18), channel_id=1, source_target_pairs={{10,0},{0,8},{8,1},{1,9},{9,3},{3,11},{11,2},{2,10},{14,4},{4,12},... | collective-permute-start | bytes 2064392 | tf_op jit(solution)/shard_map/ppermute | solution.py:60
  201.9 10.4 %collective-permute-start.32 = (bf16[21,128,128]{2,1,0:T(8,128)(2,1)S(1)}, bf16[21,128,128]{2,1,0:T(8,128)(2,1)S(1)}, u32[]{:S(2)}, u32[]{:S(2)}) collective-permute-start(bf16[21,128,128]{2,1,0:T(8,128)(2,1)S(1)} %get-tuple-element.99.refs_0_.refs_8_), channel_id=1, source_target_pairs={{8,0},{1,8},{9,1},{3,9},{11,3},{2,11},{10,2},{0,10},{12,4},{5,12},... | collective-permute-start | bytes 2064392 | tf_op jit(solution)/shard_map/ppermute | solution.py:60
  203.9 15.8 %collective-permute-start.33 = (bf16[21,128,128]{2,1,0:T(8,128)(2,1)S(1)}, bf16[21,128,128]{2,1,0:T(8,128)(2,1)S(1)}, u32[]{:S(2)}, u32[]{:S(2)}) collective-permute-start(bf16[21,128,128]{2,1,0:T(8,128)(2,1)S(1)} %get-tuple-element.100.refs_1_.refs_9_), channel_id=1, source_target_pairs={{8,0},{1,8},{9,1},{3,9},{11,3},{2,11},{10,2},{0,10},{12,4},{5,12},... | collective-permute-start | bytes 2064392 | tf_op jit(solution)/shard_map/ppermute | solution.py:60
  204.3 17.6 %collective-permute-start.48 = (bf16[21,128,128]{2,1,0:T(8,128)(2,1)S(1)}, bf16[21,128,128]{2,1,0:T(8,128)(2,1)S(1)}, u32[]{:S(2)}, u32[]{:S(2)}) collective-permute-start(bf16[21,128,128]{2,1,0:T(8,128)(2,1)S(1)} %fusion.8), channel_id=1, source_target_pairs={{10,0},{0,8},{8,1},{1,9},{9,3},{3,11},{11,2},{2,10},{14,4},{4,12},... | collective-permute-start | bytes 2064392 | tf_op jit(solution)/shard_map/ppermute | solution.py:60
  211.4 14.3 %collective-permute-start.45 = (bf16[21,128,128]{2,1,0:T(8,128)(2,1)S(1)}, bf16[21,128,128]{2,1,0:T(8,128)(2,1)S(1)}, u32[]{:S(2)}, u32[]{:S(2)}) collective-permute-start(bf16[21,128,128]{2,1,0:T(8,128)(2,1)S(1)} %fusion.10), channel_id=1, source_target_pairs={{10,0},{0,8},{8,1},{1,9},{9,3},{3,11},{11,2},{2,10},{14,4},{4,12},... | collective-permute-start | bytes 2064392 | tf_op jit(solution)/shard_map/ppermute | solution.py:60
  212.3 14.7 %collective-permute-start.34 = (bf16[21,128,128]{2,1,0:T(8,128)(2,1)S(1)}, bf16[21,128,128]{2,1,0:T(8,128)(2,1)}, u32[]{:S(2)}, u32[]{:S(2)}) collective-permute-start(bf16[21,128,128]{2,1,0:T(8,128)(2,1)S(1)} %collective-permute-done.32.refs_2_.refs_10_), channel_id=1, source_target_pairs={{8,0},{1,8},{9,1},{3,9},{11,3},{2,11},{10,2},{0,10},{12,4},{5,12},... | collective-permute-start | bytes 2064392 | tf_op jit(solution)/shard_map/ppermute | solution.py:60
  219.7 14.7 %collective-permute-start.35 = (bf16[21,128,128]{2,1,0:T(8,128)(2,1)S(1)}, bf16[21,128,128]{2,1,0:T(8,128)(2,1)}, u32[]{:S(2)}, u32[]{:S(2)}) collective-permute-start(bf16[21,128,128]{2,1,0:T(8,128)(2,1)S(1)} %collective-permute-done.33.refs_3_.refs_11_), channel_id=1, source_target_pairs={{8,0},{1,8},{9,1},{3,9},{11,3},{2,11},{10,2},{0,10},{12,4},{5,12},... | collective-permute-start | bytes 2064392 | tf_op jit(solution)/shard_map/ppermute | solution.py:60
  223.2 15.0 %collective-permute-start.49 = (bf16[21,128,128]{2,1,0:T(8,128)(2,1)}, bf16[21,128,128]{2,1,0:T(8,128)(2,1)S(1)}, u32[]{:S(2)}, u32[]{:S(2)}) collective-permute-start(bf16[21,128,128]{2,1,0:T(8,128)(2,1)} %fusion.9), channel_id=1, source_target_pairs={{10,0},{0,8},{8,1},{1,9},{9,3},{3,11},{11,2},{2,10},{14,4},{4,12},... | collective-permute-start | bytes 2064392 | tf_op jit(solution)/shard_map/ppermute | solution.py:60
  227.0 14.2 %collective-permute-start.46 = (bf16[21,128,128]{2,1,0:T(8,128)(2,1)}, bf16[21,128,128]{2,1,0:T(8,128)(2,1)S(1)}, u32[]{:S(2)}, u32[]{:S(2)}) collective-permute-start(bf16[21,128,128]{2,1,0:T(8,128)(2,1)} %fusion.11), channel_id=1, source_target_pairs={{10,0},{0,8},{8,1},{1,9},{9,3},{3,11},{11,2},{2,10},{14,4},{4,12},... | collective-permute-start | bytes 2064392 | tf_op jit(solution)/shard_map/ppermute | solution.py:60
  227.1 19.8 %collective-permute-start.36 = (bf16[21,128,128]{2,1,0:T(8,128)(2,1)}, bf16[21,128,128]{2,1,0:T(8,128)(2,1)}, u32[]{:S(2)}, u32[]{:S(2)}) collective-permute-start(bf16[21,128,128]{2,1,0:T(8,128)(2,1)} %collective-permute-done.34.refs_4_.refs_12_), channel_id=1, source_target_pairs={{8,0},{1,8},{9,1},{3,9},{11,3},{2,11},{10,2},{0,10},{12,4},{5,12},... | collective-permute-start | bytes 2064392 | tf_op jit(solution)/shard_map/ppermute | solution.py:60
  234.5 14.9 %collective-permute-start.37 = (bf16[21,128,128]{2,1,0:T(8,128)(2,1)}, bf16[21,128,128]{2,1,0:T(8,128)(2,1)}, u32[]{:S(2)}, u32[]{:S(2)}) collective-permute-start(bf16[21,128,128]{2,1,0:T(8,128)(2,1)} %collective-permute-done.35.refs_5_.refs_13_), channel_id=1, source_target_pairs={{8,0},{1,8},{9,1},{3,9},{11,3},{2,11},{10,2},{0,10},{12,4},{5,12},... | collective-permute-start | bytes 2064392 | tf_op jit(solution)/shard_map/ppermute | solution.py:60
  255.8 4.1 %collective-permute-start.51 = (f32[2,128]{1,0:T(2,128)S(1)}, f32[2,128]{1,0:T(2,128)S(1)}, u32[]{:S(2)}, u32[]{:S(2)}) collective-permute-start(f32[2,128]{1,0:T(2,128)S(1)} %maximum_select_fusion.4), channel_id=1, source_target_pairs={{1,0},{9,8},{0,1},{8,9},{2,3},{10,11},{3,2},{11,10},{5,4},{13,12},... | collective-permute-start | bytes 3080 | tf_op jit(solution)/shard_map/ppermute | solution.py:65
  257.4 7.6 %collective-permute-start.53 = (bf16[528,128]{1,0:T(8,128)(2,1)S(1)}, bf16[528,128]{1,0:T(8,128)(2,1)}, u32[]{:S(2)}, u32[]{:S(2)}) collective-permute-start(bf16[528,128]{1,0:T(8,128)(2,1)S(1)} %get-tuple-element.137.refs_3_), channel_id=1, source_target_pairs={{8,0},{1,8},{9,1},{3,9},{11,3},{2,11},{10,2},{0,10},{12,4},{5,12},... | collective-permute-start | bytes 405512 | tf_op jit(solution)/shard_map/ppermute | solution.py:60
  257.4 7.6 %collective-permute-start.54 = (bf16[528,128]{1,0:T(8,128)(2,1)S(1)}, bf16[528,128]{1,0:T(8,128)(2,1)}, u32[]{:S(2)}, u32[]{:S(2)}) collective-permute-start(bf16[528,128]{1,0:T(8,128)(2,1)S(1)} %get-tuple-element.137.refs_3_), channel_id=1, source_target_pairs={{10,0},{0,8},{8,1},{1,9},{9,3},{3,11},{11,2},{2,10},{14,4},{4,12},... | collective-permute-start | bytes 405512 | tf_op jit(solution)/shard_map/ppermute | solution.py:60
  257.9 7.2 %collective-permute-start.55 = (bf16[528,128]{1,0:T(8,128)(2,1)S(1)}, bf16[528,128]{1,0:T(8,128)(2,1)}, u32[]{:S(2)}, u32[]{:S(2)}) collective-permute-start(bf16[528,128]{1,0:T(8,128)(2,1)S(1)} %get-tuple-element.137.refs_3_), channel_id=1, source_target_pairs={{1,0},{9,8},{3,1},{11,9},{2,3},{10,11},{0,2},{8,10},{5,4},{13,12},... | collective-permute-start | bytes 405512 | tf_op jit(solution)/shard_map/ppermute | solution.py:60
  258.0 7.1 %collective-permute-start.56 = (bf16[528,128]{1,0:T(8,128)(2,1)S(1)}, bf16[528,128]{1,0:T(8,128)(2,1)}, u32[]{:S(2)}, u32[]{:S(2)}) collective-permute-start(bf16[528,128]{1,0:T(8,128)(2,1)S(1)} %get-tuple-element.137.refs_3_), channel_id=1, source_target_pairs={{2,0},{10,8},{0,1},{8,9},{1,3},{9,11},{3,2},{11,10},{6,4},{14,12},... | collective-permute-start | bytes 405512 | tf_op jit(solution)/shard_map/ppermute | solution.py:60
  259.9 5.1 %collective-permute-start.52 = (f32[4,128]{1,0:T(4,128)S(1)}, f32[4,128]{1,0:T(4,128)S(1)}, u32[]{:S(2)}, u32[]{:S(2)}) collective-permute-start(f32[4,128]{1,0:T(4,128)S(1)} %maximum_select_fusion.2), channel_id=1, source_target_pairs={{3,0},{11,8},{2,1},{10,9},{0,3},{8,11},{1,2},{9,10},{7,4},{15,12},... | collective-permute-start | bytes 6152 | tf_op jit(solution)/shard_map/ppermute | solution.py:65
  281.0 7.3 %collective-permute-start.61 = (f32[2,128,128]{2,1,0:T(8,128)S(1)}, f32[2,128,128]{2,1,0:T(8,128)S(1)}, u32[]{:S(2)}, u32[]{:S(2)}) collective-permute-start(f32[2,128,128]{2,1,0:T(8,128)S(1)} %get-tuple-element.164), channel_id=1, source_target_pairs={{10,0},{0,8},{8,1},{1,9},{9,3},{3,11},{11,2},{2,10},{14,4},{4,12},... | collective-permute-start | bytes 393224 | tf_op jit(solution)/shard_map/ppermute | solution.py:60
  281.1 7.3 %collective-permute-start.62 = (f32[2,128,128]{2,1,0:T(8,128)S(1)}, f32[2,128,128]{2,1,0:T(8,128)S(1)}, u32[]{:S(2)}, u32[]{:S(2)}) collective-permute-start(f32[2,128,128]{2,1,0:T(8,128)S(1)} %get-tuple-element.163), channel_id=1, source_target_pairs={{2,0},{10,8},{0,1},{8,9},{1,3},{9,11},{3,2},{11,10},{6,4},{14,12},... | collective-permute-start | bytes 393224 | tf_op jit(solution)/shard_map/ppermute | solution.py:60
  281.7 6.6 %collective-permute-start.63 = (f32[2,128,128]{2,1,0:T(8,128)S(1)}, f32[2,128,128]{2,1,0:T(8,128)S(1)}, u32[]{:S(2)}, u32[]{:S(2)}) collective-permute-start(f32[2,128,128]{2,1,0:T(8,128)S(1)} %get-tuple-element.162), channel_id=1, source_target_pairs={{11,0},{2,8},{10,1},{0,9},{8,3},{1,11},{9,2},{3,10},{15,4},{6,12},... | collective-permute-start | bytes 393224 | tf_op jit(solution)/shard_map/ppermute | solution.py:60
  283.1 4.5 %collective-permute-start.59 = (f32[4,128]{1,0:T(4,128)S(1)}, f32[4,128]{1,0:T(4,128)S(1)}, u32[]{:S(2)}, u32[]{:S(2)}) collective-permute-start(f32[4,128]{1,0:T(4,128)S(1)} %maximum_select_fusion.3), channel_id=1, source_target_pairs={{3,0},{11,8},{2,1},{10,9},{0,3},{8,11},{1,2},{9,10},{7,4},{15,12},... | collective-permute-start | bytes 6152 | tf_op jit(solution)/shard_map/ppermute | solution.py:65
  294.9 10.3 %collective-permute-start.64 = (bf16[128,128]{1,0:T(8,128)(2,1)S(1)}, bf16[128,128]{1,0:T(8,128)(2,1)S(1)}, u32[]{:S(2)}, u32[]{:S(2)}) collective-permute-start(bf16[128,128]{1,0:T(8,128)(2,1)S(1)} %get-tuple-element.169), channel_id=1, source_target_pairs={{0,16},{8,17},{1,18},{9,19},{3,20},{11,21},{2,22},{10,23},{4,24},{... | collective-permute-start | bytes 98312 | tf_op jit(solution)/shard_map/ppermute | solution.py:55
  295.6 9.6 %collective-permute-start.65 = (bf16[128,128]{1,0:T(8,128)(2,1)S(1)}, bf16[128,128]{1,0:T(8,128)(2,1)S(1)}, u32[]{:S(2)}, u32[]{:S(2)}) collective-permute-start(bf16[128,128]{1,0:T(8,128)(2,1)S(1)} %get-tuple-element.172), channel_id=1, source_target_pairs={{0,23},{8,16},{1,17},{9,18},{3,19},{11,20},{2,21},{10,22},{4,31},{... | collective-permute-start | bytes 98312 | tf_op jit(solution)/shard_map/ppermute | solution.py:55
  302.1 6.0 %collective-permute-start.66 = (bf16[128,128]{1,0:T(8,128)(2,1)S(1)}, bf16[128,128]{1,0:T(8,128)(2,1)S(1)}, u32[]{:S(2)}, u32[]{:S(2)}) collective-permute-start(bf16[128,128]{1,0:T(8,128)(2,1)S(1)} %get-tuple-element.171), channel_id=1, source_target_pairs={{0,22},{8,23},{1,16},{9,17},{3,18},{11,19},{2,20},{10,21},{4,30},{... | collective-permute-start | bytes 98312 | tf_op jit(solution)/shard_map/ppermute | solution.py:55
  302.1 6.0 %collective-permute-start.67 = (bf16[128,128]{1,0:T(8,128)(2,1)S(1)}, bf16[128,128]{1,0:T(8,128)(2,1)S(1)}, u32[]{:S(2)}, u32[]{:S(2)}) collective-permute-start(bf16[128,128]{1,0:T(8,128)(2,1)S(1)} %get-tuple-element.170), channel_id=1, source_target_pairs={{0,21},{8,22},{1,23},{9,16},{3,17},{11,18},{2,19},{10,20},{4,29},{... | collective-permute-start | bytes 98312 | tf_op jit(solution)/shard_map/ppermute | solution.py:55
  (34 other events, 267.9 us)

commit v7 on v6

--- a/solution.py
+++ b/solution.py
@@ -695,10 +695,6 @@
     return one, minus, places.ahead(one, 1), places.ahead(minus, -1)
 
 
-def classes_of(places, x):
-    return jnp.stack([x, *other_classes_of(places, x)])
-
-
 def other_classes_at_once(places, x):
     return tuple(places.ahead(x, charge) for charge in CHARGE_STEPS[1:])
 
@@ -732,10 +728,11 @@
     right = jnp.split(first[:channels], pieces)
     right, left_env = after(right, left_env)
     left = jnp.split(places.fetch(left_env[0, :, 0]), pieces)
-    rolled = [
-        classes_of(places, jnp.concatenate([left_isos[step], right_isos[step]]))
-        for step in range(ENV_STEPS)
-    ]
+    rolled = []
+    for step in range(ENV_STEPS):
+        isos = jnp.concatenate([left_isos[step], right_isos[step]])
+        others = other_classes_at_once if step == 0 else other_classes_of
+        rolled.append(jnp.stack([isos, *others(places, isos)]))
     own_iso, own_centre = own_tensors[:states], own_tensors[states]
     centres = [own_centre] + [places.ahead(own_centre, s) for s in range(1, states)]
 

time: 312 us -> 317 us (1.016)
  waiting for transfers between devices: 87.3 us -> 97.3 us
  starting transfers between devices: 130 us -> 124 us
    ppermute x52, waiting for transfers between devices: 72.5 us -> 82.2 us  [ahead(): lax.ppermute(x, BOTH, self.pairs(lambda g, k: self.slot(g + chain_by, k +...]
    ppermute x52, starting transfers between devices: 88.4 us -> 84.8 us  [ahead(): lax.ppermute(x, BOTH, self.pairs(lambda g, k: self.slot(g + chain_by, k +...]
  transfers between devices with their start and end apart: 68 -> 68, of which waited for: 29 -> 31; matrix products, arithmetic and copies ran while one was open for 8% -> 7% of each run, Pallas kernels for 12% -> 11%
where the time goes in v7:
time: 317 us; the launch traced here: 313 us
  starting transfers between devices  124 us (39%)
  waiting for transfers between devices  97.3 us (31%)
  Pallas kernels  52.7 us (17%)
  local copies, waits for them, and re-layouts  12.1 us (4%)
  matrix products  11.1 us (4%)
  blocking collectives  7.9 us (2%)
  other arithmetic  5.6 us (2%)
    ppermute x52, starting transfers between devices, ahead(): lax.ppermute(x, BOTH, self.pairs(lambda g, k: self.slot(g + chain_by, k +...  84.8 us
    ppermute x52, waiting for transfers between devices, ahead(): lax.ppermute(x, BOTH, self.pairs(lambda g, k: self.slot(g + chain_by, k +...  82.2 us
    pallas_call x19, Pallas kernels, call(): pl.pallas_call(kernel, out_shape=out_shape, scratch_shapes=scratch_shapes...  52.7 us
    ppermute x5, starting transfers between devices, fetch(): lax.ppermute(x, BOTH, self.pairs(lambda g, k: self.home(g + site_by, k +...  24.1 us
    dot_general x12, matrix products, left_part(): jnp.einsum('xy,vxz->vyz', left_isos[step][s], gathered[s][piece], preferr...  10.9 us
    ppermute x5, starting transfers between devices, send_home(): lax.ppermute(x, BOTH, self.pairs(self.slot, lambda g, k: self.home(g + si...  9.84 us
    ppermute x6, waiting for transfers between devices, partner(): lax.ppermute(x, BOTH, self.pairs(lambda g, k: self.slot(g, k ^ bit), self...  9.42 us
    all_gather x1, blocking collectives, local(): lax.all_gather(weight_matrices(mpo[0], pattern[0], secs), 'site')  7.9 us
  transfers between devices with their start and end apart: 68, of which 31 were waited for; matrix products, arithmetic and copies ran while one was open for 7% of the time, Pallas kernels for 11%

profile of v7, /device:TPU:0, one launch (start us, length us, event | category | flops | bytes accessed | tf_op | source)
XLA Modules:
  0.0 312.7 jit_solution(13183262639951857466)
XLA Ops:
  0.6 5.0 %collective-permute-start.5 = (bf16[4,128,128]{2,1,0:T(8,128)(2,1)}, bf16[4,128,128]{2,1,0:T(8,128)(2,1)S(1)}, u32[]{:S(2)}, u32[]{:S(2)}) collective-permute-start(bf16[4,128,128]{2,1,0:T(8,128)(2,1)} %bitcast.190), channel_id=1, source_target_pairs={{8,0},{9,8},{10,1},{11,9},{12,3},{13,11},{14,2},{15,10},{16,4},{17... | collective-permute-start | bytes 393224 | tf_op jit(solution)/shard_map/ppermute | solution.py:50
  7.2 3.9 %collective-permute-start.6 = (bf16[4,128,128]{2,1,0:T(8,128)(2,1)}, bf16[4,128,128]{2,1,0:T(8,128)(2,1)S(1)}, u32[]{:S(2)}, u32[]{:S(2)}) collective-permute-start(bf16[4,128,128]{2,1,0:T(8,128)(2,1)} %bitcast.193), channel_id=1, source_target_pairs={{24,0},{25,8},{26,1},{27,9},{28,3},{29,11},{30,2},{31,10},{0,4},{1... | collective-permute-start | bytes 393224 | tf_op jit(solution)/shard_map/ppermute | solution.py:50
  11.2 2.9 pad_maximum_fusion
  14.1 13.8 %collective-permute-start = (bf16[50,128,128]{2,1,0:T(8,128)(2,1)}, bf16[50,128,128]{2,1,0:T(8,128)(2,1)}, u32[]{:S(2)}, u32[]{:S(2)}) collective-permute-start(bf16[50,128,128]{2,1,0:T(8,128)(2,1)} %pad_maximum_fusion), channel_id=1, source_target_pairs={{0,0},{1,8},{2,1},{3,9},{4,3},{5,11},{6,2},{7,10},{8,4},{9,12},{10... | collective-permute-start | bytes 4915208 | tf_op jit(solution)/shard_map/ppermute | solution.py:50
  28.8 7.9 %all-gather = bf16[8,168,168]{2,1,0:T(8,128)(2,1)S(1)} all-gather(bf16[2,168,168]{2,1,0:T(8,128)(2,1)S(1)} %pad_maximum_fusion.2), channel_id=2, replica_groups=mesh['site'=4,'sec'=8] {'site'}, dimensions={0}, use_global_device_ids=true | all-gather | bytes 564480 | tf_op jit(solution)/shard_map/all_gather | solution.py:739
  43.2 3.2 %collective-permute-start.14 = (bf16[128,128]{1,0:T(8,128)(2,1)S(1)}, bf16[128,128]{1,0:T(8,128)(2,1)S(1)}, u32[]{:S(2)}, u32[]{:S(2)}) collective-permute-start(bf16[128,128]{1,0:T(8,128)(2,1)S(1)} %get-tuple-element.168.centre_ref), channel_id=1, source_target_pairs={{9,0},{3,8},{11,1},{2,9},{10,3},{0,11},{8,2},{1,10},{13,4},{7,12},... | collective-permute-start | bytes 98312 | tf_op jit(solution)/shard_map/ppermute | solution.py:60
  46.4 1.5 collective-permute-done.12
  47.9 2.5 collective-permute-start.8
  51.2 3.6 %collective-permute-start.15 = (bf16[4,128,128]{2,1,0:T(8,128)(2,1)S(1)}, bf16[4,128,128]{2,1,0:T(8,128)(2,1)S(1)}, u32[]{:S(2)}, u32[]{:S(2)}) collective-permute-start(bf16[4,128,128]{2,1,0:T(8,128)(2,1)S(1)} %get-tuple-element.129.refs_3_), channel_id=1, source_target_pairs={{8,0},{1,8},{9,1},{3,9},{11,3},{2,11},{10,2},{0,10},{12,4},{5,12},... | collective-permute-start | bytes 393224 | tf_op jit(solution)/shard_map/ppermute | solution.py:60
  54.8 2.4 collective-permute-start.9
  57.4 3.7 %collective-permute-done.9 = bf16[8,128,128]{2,1,0:T(8,128)(2,1)S(1)} collective-permute-done((bf16[8,128,128]{2,1,0:T(8,128)(2,1)S(1)}, bf16[8,128,128]{2,1,0:T(8,128)(2,1)S(1)}, u32[]{:S(2)}, u32[]{:S(2)}) %collective-permute-start.9) | collective-permute-done | bytes 262176 | tf_op jit(solution)/shard_map/ppermute | solution.py:60
  61.2 1.6 fusion.32
  64.6 3.1 %collective-permute-start.1 = (bf16[8,128,128]{2,1,0:T(8,128)(2,1)S(1)}, bf16[8,128,128]{2,1,0:T(8,128)(2,1)S(1)}, u32[]{:S(2)}, u32[]{:S(2)}) collective-permute-start(bf16[8,128,128]{2,1,0:T(8,128)(2,1)S(1)} %concatenate.64), channel_id=1, source_target_pairs={{8,0},{1,8},{9,1},{3,9},{11,3},{2,11},{10,2},{0,10},{12,4},{5,12},... | collective-permute-start | bytes 786440 | tf_op jit(solution)/shard_map/ppermute | solution.py:60
  67.9 1.7 collective-permute-start.20
  71.9 2.7 collective-permute-done.1
  74.5 1.6 collective-permute-start.3
  76.5 5.4 %collective-permute-start.4 = (bf16[8,128,128]{2,1,0:T(8,128)(2,1)S(1)}, bf16[8,128,128]{2,1,0:T(8,128)(2,1)S(1)}, u32[]{:S(2)}, u32[]{:S(2)}) collective-permute-start(bf16[8,128,128]{2,1,0:T(8,128)(2,1)S(1)} %concatenate.64), channel_id=1, source_target_pairs={{2,0},{10,8},{0,1},{8,9},{1,3},{9,11},{3,2},{11,10},{6,4},{14,12},... | collective-permute-start | bytes 786440 | tf_op jit(solution)/shard_map/ppermute | solution.py:60
  82.0 20.7 %collective-permute-done.3 = bf16[8,128,128]{2,1,0:T(8,128)(2,1)S(1)} collective-permute-done((bf16[8,128,128]{2,1,0:T(8,128)(2,1)S(1)}, bf16[8,128,128]{2,1,0:T(8,128)(2,1)S(1)}, u32[]{:S(2)}, u32[]{:S(2)}) %collective-permute-start.3) | collective-permute-done | bytes 262176 | tf_op jit(solution)/shard_map/ppermute | solution.py:60
  102.7 1.7 collective-permute-start.21
  104.4 4.7 %collective-permute-start.23 = (bf16[21,128,128]{2,1,0:T(8,128)(2,1)S(1)}, bf16[21,128,128]{2,1,0:T(8,128)(2,1)S(1)}, u32[]{:S(2)}, u32[]{:S(2)}) collective-permute-start(bf16[21,128,128]{2,1,0:T(8,128)(2,1)S(1)} %collective-permute-done.22.refs_3_), channel_id=1, source_target_pairs={{8,0},{1,8},{9,1},{3,9},{11,3},{2,11},{10,2},{0,10},{12,4},{5,12},... | collective-permute-start | bytes 2064392 | tf_op jit(solution)/shard_map/ppermute | solution.py:60
  109.2 1.8 collective-permute-start.17
  112.9 7.4 %collective-permute-done.23.refs_5_ = bf16[21,128,128]{2,1,0:T(8,128)(2,1)S(1)} collective-permute-done((bf16[21,128,128]{2,1,0:T(8,128)(2,1)S(1)}, bf16[21,128,128]{2,1,0:T(8,128)(2,1)S(1)}, u32[]{:S(2)}, u32[]{:S(2)}) %collective-permute-start.23) | collective-permute-done | bytes 688160 | tf_op jit(solution)/shard_map/ppermute | solution.py:60
  120.3 1.9 collective-permute-start.24
  122.2 4.5 %collective-permute-start.25 = (bf16[21,128,128]{2,1,0:T(8,128)(2,1)S(1)}, bf16[21,128,128]{2,1,0:T(8,128)(2,1)S(1)}, u32[]{:S(2)}, u32[]{:S(2)}) collective-permute-start(bf16[21,128,128]{2,1,0:T(8,128)(2,1)S(1)} %collective-permute-done.23.refs_5_), channel_id=1, source_target_pairs={{8,0},{1,8},{9,1},{3,9},{11,3},{2,11},{10,2},{0,10},{12,4},{5,12},... | collective-permute-start | bytes 2064392 | tf_op jit(solution)/shard_map/ppermute | solution.py:60
  126.7 5.2 %shard_map.145 = (bf16[21,128,128]{2,1,0:T(8,128)(2,1)S(1)}, bf16[21,128,128]{2,1,0:T(8,128)(2,1)S(1)}, bf16[21,128,128]{2,1,0:T(8,128)(2,1)S(1)}, bf16[21,128,1...) custom-call(bf16[21,128,128]{2,1,0:T(8,128)(2,1)S(1)} %get-tuple-ele, ...), custom_call_target="tpu_custom_call" | custom-call | flops 2334130176 | bytes 3076096 | tf_op jit(solution)/shard_map/pallas_call | solution.py:517
  134.2 3.8 %collective-permute-done.25.refs_7_ = bf16[21,128,128]{2,1,0:T(8,128)(2,1)S(1)} collective-permute-done((bf16[21,128,128]{2,1,0:T(8,128)(2,1)S(1)}, bf16[21,128,128]{2,1,0:T(8,128)(2,1)S(1)}, u32[]{:S(2)}, u32[]{:S(2)}) %collective-permute-start.25) | collective-permute-done | bytes 688160 | tf_op jit(solution)/shard_map/ppermute | solution.py:60
  138.0 7.8 %collective-permute-start.41 = (bf16[21,128,128]{2,1,0:T(8,128)(2,1)S(1)}, bf16[21,128,128]{2,1,0:T(8,128)(2,1)S(1)}, u32[]{:S(2)}, u32[]{:S(2)}) collective-permute-start(bf16[21,128,128]{2,1,0:T(8,128)(2,1)S(1)} %fusion.17), channel_id=1, source_target_pairs={{10,0},{0,8},{8,1},{1,9},{9,3},{3,11},{11,2},{2,10},{14,4},{4,12},... | collective-permute-start | bytes 2064392 | tf_op jit(solution)/shard_map/ppermute | solution.py:60
  146.8 6.3 %shard_map.146 = (bf16[21,128,128]{2,1,0:T(8,128)(2,1)S(1)}, bf16[21,128,128]{2,1,0:T(8,128)(2,1)S(1)}, f32[8,128]{1,0:T(8,128)S(1)}) custom-call(bf16[21,128,128]{2,1,0:T(8,128)(2,1)S(1)} %get-tuple-element.85.refs_0_, bf16[21,128,128]{2,1,0:T(8,128)(2,1)S(1)} %get-tuple-element.86.refs_1_, bf16[21,128,128]{2,1,0:T(8,128)(2,1)S(1)} %collective-permute-done.20.refs_2_, ...), custom_call_target="tpu_custom_call" | custom-call | flops 2334130176 | bytes 7335936 | tf_op jit(solution)/shard_map/pallas_call | solution.py:517
  153.2 1.8 collective-permute-start.26
  157.9 4.4 %collective-permute-start.39 = (bf16[21,128,128]{2,1,0:T(8,128)(2,1)S(1)}, bf16[21,128,128]{2,1,0:T(8,128)(2,1)S(1)}, u32[]{:S(2)}, u32[]{:S(2)}) collective-permute-start(bf16[21,128,128]{2,1,0:T(8,128)(2,1)S(1)} %fusion.14), channel_id=1, source_target_pairs={{10,0},{0,8},{8,1},{1,9},{9,3},{3,11},{11,2},{2,10},{14,4},{4,12},... | collective-permute-start | bytes 2064392 | tf_op jit(solution)/shard_map/ppermute | solution.py:60
  163.4 2.2 collective-permute-start.28
  165.6 5.2 %collective-permute-done.27.refs_3_ = bf16[21,128,128]{2,1,0:T(8,128)(2,1)S(1)} collective-permute-done((bf16[21,128,128]{2,1,0:T(8,128)(2,1)S(1)}, bf16[21,128,128]{2,1,0:T(8,128)(2,1)S(1)}, u32[]{:S(2)}, u32[]{:S(2)}) %collective-permute-start.27) | collective-permute-done | bytes 688160 | tf_op jit(solution)/shard_map/ppermute | solution.py:60
  170.8 2.2 collective-permute-start.29
  175.4 1.6 collective-permute-start.40
  178.2 2.2 collective-permute-start.30
  180.4 5.2 %collective-permute-done.29.refs_5_ = bf16[21,128,128]{2,1,0:T(8,128)(2,1)S(1)} collective-permute-done((bf16[21,128,128]{2,1,0:T(8,128)(2,1)S(1)}, bf16[21,128,128]{2,1,0:T(8,128)(2,1)S(1)}, u32[]{:S(2)}, u32[]{:S(2)}) %collective-permute-start.29) | collective-permute-done | bytes 688160 | tf_op jit(solution)/shard_map/ppermute | solution.py:60
  185.6 2.2 collective-permute-start.31
  188.2 3.8 %collective-permute-done.40.moved_ref = bf16[21,128,128]{2,1,0:T(8,128)(2,1)S(1)} collective-permute-done((bf16[21,128,128]{2,1,0:T(8,128)(2,1)S(1)}, bf16[21,128,128]{2,1,0:T(8,128)(2,1)S(1)}, u32[]{:S(2)}, u32[]{:S(2)}) %collective-permute-start.40) | collective-permute-done | bytes 688160 | tf_op jit(solution)/shard_map/ppermute | solution.py:60
  192.4 5.2 %shard_map.150 = (bf16[21,128,128]{2,1,0:T(8,128)(2,1)S(1)}, bf16[21,128,128]{2,1,0:T(8,128)(2,1)S(1)}, bf16[21,128,128]{2,1,0:T(8,128)(2,1)S(1)}, bf16[21,128,1...) custom-call(bf16[21,128,128]{2,1,0:T(8,128)(2,1)S(1)} %get-tuple-ele, ...), custom_call_target="tpu_custom_call" | custom-call | flops 2334130176 | bytes 3076096 | tf_op jit(solution)/shard_map/pallas_call | solution.py:517
  200.3 6.3 %shard_map.147 = (bf16[21,128,128]{2,1,0:T(8,128)(2,1)S(1)}, bf16[21,128,128]{2,1,0:T(8,128)(2,1)S(1)}, f32[8,128]{1,0:T(8,128)S(1)}) custom-call(bf16[21,128,128]{2,1,0:T(8,128)(2,1)S(1)} %get-tuple-element.95.refs_0_, bf16[21,128,128]{2,1,0:T(8,128)(2,1)S(1)} %get-tuple-element.96.refs_1_, bf16[21,128,128]{2,1,0:T(8,128)(2,1)S(1)} %collective-permute-done.26.refs_2_, ...), custom_call_target="tpu_custom_call" | custom-call | flops 2334130176 | bytes 7335936 | tf_op jit(solution)/shard_map/pallas_call | solution.py:517
  206.7 2.2 collective-permute-start.32
  209.9 5.9 %collective-permute-done.44 = bf16[21,128,128]{2,1,0:T(8,128)(2,1)S(1)} collective-permute-done((bf16[21,128,128]{2,1,0:T(8,128)(2,1)S(1)}, bf16[21,128,128]{2,1,0:T(8,128)(2,1)S(1)}, u32[]{:S(2)}, u32[]{:S(2)}) %collective-permute-start.44) | collective-permute-done | bytes 688160 | tf_op jit(solution)/shard_map/ppermute | solution.py:60
  217.4 2.2 collective-permute-start.34
  219.6 5.2 %collective-permute-done.33.refs_3_.refs_11_ = bf16[21,128,128]{2,1,0:T(8,128)(2,1)S(1)} collective-permute-done((bf16[21,128,128]{2,1,0:T(8,128)(2,1)S(1)}, bf16[21,128,128]{2,1,0:T(8,128)(2,1)S(1)}, u32[]{:S(2)}, u32[]{:S(2)}) %collective-permute-start.33) | collective-permute-done | bytes 688160 | tf_op jit(solution)/shard_map/ppermute | solution.py:60
  224.7 2.2 collective-permute-start.35
  228.3 2.3 collective-permute-done.45
  232.1 2.2 collective-permute-start.36
  234.3 5.2 %collective-permute-done.35.refs_5_.refs_13_ = bf16[21,128,128]{2,1,0:T(8,128)(2,1)} collective-permute-done((bf16[21,128,128]{2,1,0:T(8,128)(2,1)S(1)}, bf16[21,128,128]{2,1,0:T(8,128)(2,1)}, u32[]{:S(2)}, u32[]{:S(2)}) %collective-permute-start.35) | collective-permute-done | bytes 688160 | tf_op jit(solution)/shard_map/ppermute | solution.py:60
  239.5 2.2 collective-permute-start.37
  243.7 2.5 collective-permute-done.46.moved_ref
  246.7 5.2 %shard_map.153.refs_13_ = bf16[21504,128]{1,0:T(8,128)(2,1)S(1)} custom-call(bf16[21,128,128]{2,1,0:T(8,128)(2,1)S(1)} %get-tuple-element.126.refs_0_, bf16[21,128,128]{2,1,0:T(8,128)(2,1)S(1)} %get-tuple-element.127.refs_1_, bf16[1360,384]{1,0:T(8,128)(2,1)S(1)} %copy-done.21, bf16[4,128,128]{2,1,0:T(8,128)(2,1)S(1)} %get-tuple-element.129.refs_3_, ...), custom_call_target="tpu_custom_call" | custom-call | flops 2334130176 | bytes 3076096 | tf_op jit(solution)/shard_map/pallas_call | solution.py:517
  251.9 2.4 collective-permute-done.37.refs_7_.refs_15_
  254.3 3.8 %shard_map.154 = (f32[4,128,128]{2,1,0:T(8,128)S(1)}, bf16[528,128]{1,0:T(8,128)(2,1)S(1)}, f32[1,128]{1,0:T(1,128)S(1)}) custom-call(bf16[21,128,128]{2,1,0:T(8,128)(2,1)S(1)} %copy-done.1, bf16[21,128,128]{2,1,0:T(8,128)(2,1)S(1)} %copy-done.3, bf16[21,128,128]{2,1,0:T(8,128)(2,1)S(1)} %copy-done.5, bf16[21,128,128]{2,1,0:T(8,128)(2,1)S(1)} %copy-done.7, ...), custom_call_target="tpu_custom_call" | custom-call | flops 704643072 | bytes 11292672 | tf_op jit(solution)/shard_map/pallas_call | solution.py:517
  261.3 1.7 collective-permute-start.55
  264.0 1.7 collective-permute-start.52
  265.7 3.8 %collective-permute-done.52 = f32[4,128]{1,0:T(4,128)S(1)} collective-permute-done((f32[4,128]{1,0:T(4,128)S(1)}, f32[4,128]{1,0:T(4,128)S(1)}, u32[]{:S(2)}, u32[]{:S(2)}) %collective-permute-start.52) | collective-permute-done | bytes 2080 | tf_op jit(solution)/shard_map/ppermute | solution.py:65
  273.0 8.9 %shard_map.155 = (f32[4,128,128]{2,1,0:T(8,128)S(1)}, f32[1,128]{1,0:T(1,128)S(1)}) custom-call(bf16[21,128,128]{2,1,0:T(8,128)(2,1)S(1)} %copy-done.11, bf16[21,128,128]{2,1,0:T(8,128)(2,1)S(1)} %copy-done.9, bf16[1360,384]{1,0:T(8,128)(2,1)S(1)} %copy-done.22, bf16[528,128]{1,0:T(8,128)(2,1)S(1)} %get-tuple-element.137.refs_3_, ...), custom_call_target="tpu_custom_call" | custom-call | flops 3038773248 | bytes 8601600 | tf_op jit(solution)/shard_map/pallas_call | solution.py:517
  287.6 1.5 collective-permute-start.59
  289.2 3.0 collective-permute-done.59
  292.9 2.9 collective-permute-done.60.table_ref
  295.8 3.5 %shard_map.157 = bf16[4,128,128]{2,1,0:T(8,128)(2,1)S(1)} custom-call(f32[4,2,128,128]{3,2,1,0:T(8,128)S(1)} %pad_maximum_fusion.1.both_ref, f32[8,128]{1,0:T(8,128)S(1)} %maximum_select_fusion.1.table_ref, bf16[128,128]{1,0:T(8,128)(2,1)S(1)} %get-tuple-element.168.centre_ref), custom_call_target="tpu_custom_call" | custom-call | flops 1258291200 | bytes 561152 | tf_op jit(solution)/shard_map/pallas_call | solution.py:517
  300.1 5.9 %collective-permute-start.65 = (bf16[128,128]{1,0:T(8,128)(2,1)S(1)}, bf16[128,128]{1,0:T(8,128)(2,1)S(1)}, u32[]{:S(2)}, u32[]{:S(2)}) collective-permute-start(bf16[128,128]{1,0:T(8,128)(2,1)S(1)} %get-tuple-element.172), channel_id=1, source_target_pairs={{0,23},{8,16},{1,17},{9,18},{3,19},{11,20},{2,21},{10,22},{4,31},{... | collective-permute-start | bytes 98312 | tf_op jit(solution)/shard_map/ppermute | solution.py:55
  306.6 1.9 collective-permute-start.67
  309.3 1.7 collective-permute-done.66
  (211 shorter events, 56.4 us)
Async XLA Ops:
  0.6 42.3 %collective-permute-start.5 = (bf16[4,128,128]{2,1,0:T(8,128)(2,1)}, bf16[4,128,128]{2,1,0:T(8,128)(2,1)S(1)}, u32[]{:S(2)}, u32[]{:S(2)}) collective-permute-start(bf16[4,128,128]{2,1,0:T(8,128)(2,1)} %bitcast.190), channel_id=1, source_target_pairs={{8,0},{9,8},{10,1},{11,9},{12,3},{13,11},{14,2},{15,10},{16,4},{17... | collective-permute-start | bytes 393224 | tf_op jit(solution)/shard_map/ppermute | solution.py:50
  6.6 36.4 %collective-permute-start.11 = (bf16[5,128,128]{2,1,0:T(8,128)(2,1)S(1)}, bf16[5,128,128]{2,1,0:T(8,128)(2,1)S(1)}, u32[]{:S(2)}, u32[]{:S(2)}) collective-permute-start(bf16[5,128,128]{2,1,0:T(8,128)(2,1)S(1)} %pad_maximum_fusion.3), channel_id=1, source_target_pairs={{16,0},{17,8},{18,1},{19,9},{20,3},{21,11},{22,2},{23,10},{24,4},{... | collective-permute-start | bytes 491528 | tf_op jit(solution)/shard_map/ppermute | solution.py:50
  7.2 35.7 %collective-permute-start.6 = (bf16[4,128,128]{2,1,0:T(8,128)(2,1)}, bf16[4,128,128]{2,1,0:T(8,128)(2,1)S(1)}, u32[]{:S(2)}, u32[]{:S(2)}) collective-permute-start(bf16[4,128,128]{2,1,0:T(8,128)(2,1)} %bitcast.193), channel_id=1, source_target_pairs={{24,0},{25,8},{26,1},{27,9},{28,3},{29,11},{30,2},{31,10},{0,4},{1... | collective-permute-start | bytes 393224 | tf_op jit(solution)/shard_map/ppermute | solution.py:50
  14.1 47.1 %collective-permute-start = (bf16[50,128,128]{2,1,0:T(8,128)(2,1)}, bf16[50,128,128]{2,1,0:T(8,128)(2,1)}, u32[]{:S(2)}, u32[]{:S(2)}) collective-permute-start(bf16[50,128,128]{2,1,0:T(8,128)(2,1)} %pad_maximum_fusion), channel_id=1, source_target_pairs={{0,0},{1,8},{2,1},{3,9},{4,3},{5,11},{6,2},{7,10},{8,4},{9,12},{10... | collective-permute-start | bytes 4915208 | tf_op jit(solution)/shard_map/ppermute | solution.py:50
  43.0 11.8 %collective-permute-start.7 = (bf16[8,128,128]{2,1,0:T(8,128)(2,1)S(1)}, bf16[8,128,128]{2,1,0:T(8,128)(2,1)S(1)}, u32[]{:S(2)}, u32[]{:S(2)}) collective-permute-start(bf16[8,128,128]{2,1,0:T(8,128)(2,1)S(1)} %constant_dynamic-update-slice_fusion), channel_id=1, source_target_pairs={{8,0},{1,8},{9,1},{3,9},{11,3},{2,11},{10,2},{0,10},{12,4},{5,12},... | collective-permute-start | bytes 786440 | tf_op jit(solution)/shard_map/ppermute | solution.py:60
  43.1 4.9 %collective-permute-start.12 = (bf16[128,128]{1,0:T(8,128)(2,1)S(1)}, bf16[128,128]{1,0:T(8,128)(2,1)S(1)}, u32[]{:S(2)}, u32[]{:S(2)}) collective-permute-start(bf16[128,128]{1,0:T(8,128)(2,1)S(1)} %get-tuple-element.168.centre_ref), channel_id=1, source_target_pairs={{8,0},{1,8},{9,1},{3,9},{11,3},{2,11},{10,2},{0,10},{12,4},{5,12},... | collective-permute-start | bytes 98312 | tf_op jit(solution)/shard_map/ppermute | solution.py:60
  43.1 7.9 %collective-permute-start.13 = (bf16[128,128]{1,0:T(8,128)(2,1)S(1)}, bf16[128,128]{1,0:T(8,128)(2,1)S(1)}, u32[]{:S(2)}, u32[]{:S(2)}) collective-permute-start(bf16[128,128]{1,0:T(8,128)(2,1)S(1)} %get-tuple-element.168.centre_ref), channel_id=1, source_target_pairs={{1,0},{9,8},{3,1},{11,9},{2,3},{10,11},{0,2},{8,10},{5,4},{13,12},... | collective-permute-start | bytes 98312 | tf_op jit(solution)/shard_map/ppermute | solution.py:60
  43.2 7.8 %collective-permute-start.14 = (bf16[128,128]{1,0:T(8,128)(2,1)S(1)}, bf16[128,128]{1,0:T(8,128)(2,1)S(1)}, u32[]{:S(2)}, u32[]{:S(2)}) collective-permute-start(bf16[128,128]{1,0:T(8,128)(2,1)S(1)} %get-tuple-element.168.centre_ref), channel_id=1, source_target_pairs={{9,0},{3,8},{11,1},{2,9},{10,3},{0,11},{8,2},{1,10},{13,4},{7,12},... | collective-permute-start | bytes 98312 | tf_op jit(solution)/shard_map/ppermute | solution.py:60
  47.9 9.4 %collective-permute-start.8 = (bf16[8,128,128]{2,1,0:T(8,128)(2,1)S(1)}, bf16[8,128,128]{2,1,0:T(8,128)(2,1)S(1)}, u32[]{:S(2)}, u32[]{:S(2)}) collective-permute-start(bf16[8,128,128]{2,1,0:T(8,128)(2,1)S(1)} %constant_dynamic-update-slice_fusion), channel_id=1, source_target_pairs={{10,0},{0,8},{8,1},{1,9},{9,3},{3,11},{11,2},{2,10},{14,4},{4,12},... | collective-permute-start | bytes 786440 | tf_op jit(solution)/shard_map/ppermute | solution.py:60
  51.2 18.4 %collective-permute-start.15 = (bf16[4,128,128]{2,1,0:T(8,128)(2,1)S(1)}, bf16[4,128,128]{2,1,0:T(8,128)(2,1)S(1)}, u32[]{:S(2)}, u32[]{:S(2)}) collective-permute-start(bf16[4,128,128]{2,1,0:T(8,128)(2,1)S(1)} %get-tuple-element.129.refs_3_), channel_id=1, source_target_pairs={{8,0},{1,8},{9,1},{3,9},{11,3},{2,11},{10,2},{0,10},{12,4},{5,12},... | collective-permute-start | bytes 393224 | tf_op jit(solution)/shard_map/ppermute | solution.py:60
  54.8 6.3 %collective-permute-start.9 = (bf16[8,128,128]{2,1,0:T(8,128)(2,1)S(1)}, bf16[8,128,128]{2,1,0:T(8,128)(2,1)S(1)}, u32[]{:S(2)}, u32[]{:S(2)}) collective-permute-start(bf16[8,128,128]{2,1,0:T(8,128)(2,1)S(1)} %collective-permute-done.7), channel_id=1, source_target_pairs={{8,0},{1,8},{9,1},{3,9},{11,3},{2,11},{10,2},{0,10},{12,4},{5,12},... | collective-permute-start | bytes 786440 | tf_op jit(solution)/shard_map/ppermute | solution.py:60
  57.3 10.5 %collective-permute-start.10 = (bf16[8,128,128]{2,1,0:T(8,128)(2,1)S(1)}, bf16[8,128,128]{2,1,0:T(8,128)(2,1)S(1)}, u32[]{:S(2)}, u32[]{:S(2)}) collective-permute-start(bf16[8,128,128]{2,1,0:T(8,128)(2,1)S(1)} %collective-permute-done.8), channel_id=1, source_target_pairs={{10,0},{0,8},{8,1},{1,9},{9,3},{3,11},{11,2},{2,10},{14,4},{4,12},... | collective-permute-start | bytes 786440 | tf_op jit(solution)/shard_map/ppermute | solution.py:60
  62.9 49.2 %collective-permute-start.19 = (bf16[42,128,128]{2,1,0:T(8,128)(2,1)S(1)}, bf16[42,128,128]{2,1,0:T(8,128)(2,1)S(1)}, u32[]{:S(2)}, u32[]{:S(2)}) collective-permute-start(bf16[42,128,128]{2,1,0:T(8,128)(2,1)S(1)} %bitcast.205), channel_id=1, source_target_pairs={{0,0},{1,8},{2,1},{3,9},{4,3},{5,11},{6,2},{7,10},{8,4},{9,12},{10... | collective-permute-start | bytes 4128776 | tf_op jit(solution)/shard_map/ppermute | solution.py:50
  64.6 9.9 %collective-permute-start.1 = (bf16[8,128,128]{2,1,0:T(8,128)(2,1)S(1)}, bf16[8,128,128]{2,1,0:T(8,128)(2,1)S(1)}, u32[]{:S(2)}, u32[]{:S(2)}) collective-permute-start(bf16[8,128,128]{2,1,0:T(8,128)(2,1)S(1)} %concatenate.64), channel_id=1, source_target_pairs={{8,0},{1,8},{9,1},{3,9},{11,3},{2,11},{10,2},{0,10},{12,4},{5,12},... | collective-permute-start | bytes 786440 | tf_op jit(solution)/shard_map/ppermute | solution.py:60
  67.8 8.7 %collective-permute-start.2 = (bf16[8,128,128]{2,1,0:T(8,128)(2,1)S(1)}, bf16[8,128,128]{2,1,0:T(8,128)(2,1)S(1)}, u32[]{:S(2)}, u32[]{:S(2)}) collective-permute-start(bf16[8,128,128]{2,1,0:T(8,128)(2,1)S(1)} %concatenate.64), channel_id=1, source_target_pairs={{10,0},{0,8},{8,1},{1,9},{9,3},{3,11},{11,2},{2,10},{14,4},{4,12},... | collective-permute-start | bytes 786440 | tf_op jit(solution)/shard_map/ppermute | solution.py:60
  67.9 34.8 %collective-permute-start.20 = (bf16[21,128,128]{2,1,0:T(8,128)(2,1)S(1)}, bf16[21,128,128]{2,1,0:T(8,128)(2,1)S(1)}, u32[]{:S(2)}, u32[]{:S(2)}) collective-permute-start(bf16[21,128,128]{2,1,0:T(8,128)(2,1)S(1)} %get-tuple-element.85.refs_0_), channel_id=1, source_target_pairs={{8,0},{1,8},{9,1},{3,9},{11,3},{2,11},{10,2},{0,10},{12,4},{5,12},... | collective-permute-start | bytes 2064392 | tf_op jit(solution)/shard_map/ppermute | solution.py:60
  69.6 34.8 %collective-permute-start.22 = (bf16[21,128,128]{2,1,0:T(8,128)(2,1)S(1)}, bf16[21,128,128]{2,1,0:T(8,128)(2,1)S(1)}, u32[]{:S(2)}, u32[]{:S(2)}) collective-permute-start(bf16[21,128,128]{2,1,0:T(8,128)(2,1)S(1)} %get-tuple-element.86.refs_1_), channel_id=1, source_target_pairs={{8,0},{1,8},{9,1},{3,9},{11,3},{2,11},{10,2},{0,10},{12,4},{5,12},... | collective-permute-start | bytes 2064392 | tf_op jit(solution)/shard_map/ppermute | solution.py:60
  74.5 28.2 %collective-permute-start.3 = (bf16[8,128,128]{2,1,0:T(8,128)(2,1)S(1)}, bf16[8,128,128]{2,1,0:T(8,128)(2,1)S(1)}, u32[]{:S(2)}, u32[]{:S(2)}) collective-permute-start(bf16[8,128,128]{2,1,0:T(8,128)(2,1)S(1)} %concatenate.64), channel_id=1, source_target_pairs={{1,0},{9,8},{3,1},{11,9},{2,3},{10,11},{0,2},{8,10},{5,4},{13,12},... | collective-permute-start | bytes 786440 | tf_op jit(solution)/shard_map/ppermute | solution.py:60
  76.5 34.4 %collective-permute-start.4 = (bf16[8,128,128]{2,1,0:T(8,128)(2,1)S(1)}, bf16[8,128,128]{2,1,0:T(8,128)(2,1)S(1)}, u32[]{:S(2)}, u32[]{:S(2)}) collective-permute-start(bf16[8,128,128]{2,1,0:T(8,128)(2,1)S(1)} %concatenate.64), channel_id=1, source_target_pairs={{2,0},{10,8},{0,1},{8,9},{1,3},{9,11},{3,2},{11,10},{6,4},{14,12},... | collective-permute-start | bytes 786440 | tf_op jit(solution)/shard_map/ppermute | solution.py:60
  102.7 6.5 %collective-permute-start.16 = (bf16[4,128,128]{2,1,0:T(8,128)(2,1)S(1)}, bf16[4,128,128]{2,1,0:T(8,128)(2,1)S(1)}, u32[]{:S(2)}, u32[]{:S(2)}) collective-permute-start(bf16[4,128,128]{2,1,0:T(8,128)(2,1)S(1)} %get-tuple-element.129.refs_3_), channel_id=1, source_target_pairs={{10,0},{0,8},{8,1},{1,9},{9,3},{3,11},{11,2},{2,10},{14,4},{4,12},... | collective-permute-start | bytes 393224 | tf_op jit(solution)/shard_map/ppermute | solution.py:60
  102.7 10.2 %collective-permute-start.21 = (bf16[21,128,128]{2,1,0:T(8,128)(2,1)S(1)}, bf16[21,128,128]{2,1,0:T(8,128)(2,1)S(1)}, u32[]{:S(2)}, u32[]{:S(2)}) collective-permute-start(bf16[21,128,128]{2,1,0:T(8,128)(2,1)S(1)} %collective-permute-done.20.refs_2_), channel_id=1, source_target_pairs={{8,0},{1,8},{9,1},{3,9},{11,3},{2,11},{10,2},{0,10},{12,4},{5,12},... | collective-permute-start | bytes 2064392 | tf_op jit(solution)/shard_map/ppermute | solution.py:60
  104.4 15.8 %collective-permute-start.23 = (bf16[21,128,128]{2,1,0:T(8,128)(2,1)S(1)}, bf16[21,128,128]{2,1,0:T(8,128)(2,1)S(1)}, u32[]{:S(2)}, u32[]{:S(2)}) collective-permute-start(bf16[21,128,128]{2,1,0:T(8,128)(2,1)S(1)} %collective-permute-done.22.refs_3_), channel_id=1, source_target_pairs={{8,0},{1,8},{9,1},{3,9},{11,3},{2,11},{10,2},{0,10},{12,4},{5,12},... | collective-permute-start | bytes 2064392 | tf_op jit(solution)/shard_map/ppermute | solution.py:60
  109.2 25.0 %collective-permute-start.17 = (bf16[4,128,128]{2,1,0:T(8,128)(2,1)S(1)}, bf16[4,128,128]{2,1,0:T(8,128)(2,1)S(1)}, u32[]{:S(2)}, u32[]{:S(2)}) collective-permute-start(bf16[4,128,128]{2,1,0:T(8,128)(2,1)S(1)} %collective-permute-done.15.refs_4_), channel_id=1, source_target_pairs={{8,0},{1,8},{9,1},{3,9},{11,3},{2,11},{10,2},{0,10},{12,4},{5,12},... | collective-permute-start | bytes 393224 | tf_op jit(solution)/shard_map/ppermute | solution.py:60
  111.0 23.2 %collective-permute-start.18 = (bf16[4,128,128]{2,1,0:T(8,128)(2,1)S(1)}, bf16[4,128,128]{2,1,0:T(8,128)(2,1)S(1)}, u32[]{:S(2)}, u32[]{:S(2)}) collective-permute-start(bf16[4,128,128]{2,1,0:T(8,128)(2,1)S(1)} %collective-permute-done.16.refs_5_), channel_id=1, source_target_pairs={{10,0},{0,8},{8,1},{1,9},{9,3},{3,11},{11,2},{2,10},{14,4},{4,12},... | collective-permute-start | bytes 393224 | tf_op jit(solution)/shard_map/ppermute | solution.py:60
  120.3 13.9 %collective-permute-start.24 = (bf16[21,128,128]{2,1,0:T(8,128)(2,1)S(1)}, bf16[21,128,128]{2,1,0:T(8,128)(2,1)S(1)}, u32[]{:S(2)}, u32[]{:S(2)}) collective-permute-start(bf16[21,128,128]{2,1,0:T(8,128)(2,1)S(1)} %collective-permute-done.21.refs_4_), channel_id=1, source_target_pairs={{8,0},{1,8},{9,1},{3,9},{11,3},{2,11},{10,2},{0,10},{12,4},{5,12},... | collective-permute-start | bytes 2064392 | tf_op jit(solution)/shard_map/ppermute | solution.py:60
  122.2 15.8 %collective-permute-start.25 = (bf16[21,128,128]{2,1,0:T(8,128)(2,1)S(1)}, bf16[21,128,128]{2,1,0:T(8,128)(2,1)S(1)}, u32[]{:S(2)}, u32[]{:S(2)}) collective-permute-start(bf16[21,128,128]{2,1,0:T(8,128)(2,1)S(1)} %collective-permute-done.23.refs_5_), channel_id=1, source_target_pairs={{8,0},{1,8},{9,1},{3,9},{11,3},{2,11},{10,2},{0,10},{12,4},{5,12},... | collective-permute-start | bytes 2064392 | tf_op jit(solution)/shard_map/ppermute | solution.py:60
  138.0 17.1 %collective-permute-start.41 = (bf16[21,128,128]{2,1,0:T(8,128)(2,1)S(1)}, bf16[21,128,128]{2,1,0:T(8,128)(2,1)S(1)}, u32[]{:S(2)}, u32[]{:S(2)}) collective-permute-start(bf16[21,128,128]{2,1,0:T(8,128)(2,1)S(1)} %fusion.17), channel_id=1, source_target_pairs={{10,0},{0,8},{8,1},{1,9},{9,3},{3,11},{11,2},{2,10},{14,4},{4,12},... | collective-permute-start | bytes 2064392 | tf_op jit(solution)/shard_map/ppermute | solution.py:60
  145.8 10.9 %collective-permute-start.38 = (bf16[21,128,128]{2,1,0:T(8,128)(2,1)S(1)}, bf16[21,128,128]{2,1,0:T(8,128)(2,1)S(1)}, u32[]{:S(2)}, u32[]{:S(2)}) collective-permute-start(bf16[21,128,128]{2,1,0:T(8,128)(2,1)S(1)} %fusion.16), channel_id=1, source_target_pairs={{10,0},{0,8},{8,1},{1,9},{9,3},{3,11},{11,2},{2,10},{14,4},{4,12},... | collective-permute-start | bytes 2064392 | tf_op jit(solution)/shard_map/ppermute | solution.py:60
  153.2 10.3 %collective-permute-start.26 = (bf16[21,128,128]{2,1,0:T(8,128)(2,1)S(1)}, bf16[21,128,128]{2,1,0:T(8,128)(2,1)S(1)}, u32[]{:S(2)}, u32[]{:S(2)}) collective-permute-start(bf16[21,128,128]{2,1,0:T(8,128)(2,1)S(1)} %get-tuple-element.95.refs_0_), channel_id=1, source_target_pairs={{8,0},{1,8},{9,1},{3,9},{11,3},{2,11},{10,2},{0,10},{12,4},{5,12},... | collective-permute-start | bytes 2064392 | tf_op jit(solution)/shard_map/ppermute | solution.py:60
  155.0 15.8 %collective-permute-start.27 = (bf16[21,128,128]{2,1,0:T(8,128)(2,1)S(1)}, bf16[21,128,128]{2,1,0:T(8,128)(2,1)S(1)}, u32[]{:S(2)}, u32[]{:S(2)}) collective-permute-start(bf16[21,128,128]{2,1,0:T(8,128)(2,1)S(1)} %get-tuple-element.96.refs_1_), channel_id=1, source_target_pairs={{8,0},{1,8},{9,1},{3,9},{11,3},{2,11},{10,2},{0,10},{12,4},{5,12},... | collective-permute-start | bytes 2064392 | tf_op jit(solution)/shard_map/ppermute | solution.py:60
  156.2 16.8 %collective-permute-start.42 = (bf16[21,128,128]{2,1,0:T(8,128)(2,1)S(1)}, bf16[21,128,128]{2,1,0:T(8,128)(2,1)S(1)}, u32[]{:S(2)}, u32[]{:S(2)}) collective-permute-start(bf16[21,128,128]{2,1,0:T(8,128)(2,1)S(1)} %fusion.12), channel_id=1, source_target_pairs={{10,0},{0,8},{8,1},{1,9},{9,3},{3,11},{11,2},{2,10},{14,4},{4,12},... | collective-permute-start | bytes 2064392 | tf_op jit(solution)/shard_map/ppermute | solution.py:60
  157.9 16.4 %collective-permute-start.39 = (bf16[21,128,128]{2,1,0:T(8,128)(2,1)S(1)}, bf16[21,128,128]{2,1,0:T(8,128)(2,1)S(1)}, u32[]{:S(2)}, u32[]{:S(2)}) collective-permute-start(bf16[21,128,128]{2,1,0:T(8,128)(2,1)S(1)} %fusion.14), channel_id=1, source_target_pairs={{10,0},{0,8},{8,1},{1,9},{9,3},{3,11},{11,2},{2,10},{14,4},{4,12},... | collective-permute-start | bytes 2064392 | tf_op jit(solution)/shard_map/ppermute | solution.py:60
  163.4 14.7 %collective-permute-start.28 = (bf16[21,128,128]{2,1,0:T(8,128)(2,1)S(1)}, bf16[21,128,128]{2,1,0:T(8,128)(2,1)S(1)}, u32[]{:S(2)}, u32[]{:S(2)}) collective-permute-start(bf16[21,128,128]{2,1,0:T(8,128)(2,1)S(1)} %collective-permute-done.26.refs_2_), channel_id=1, source_target_pairs={{8,0},{1,8},{9,1},{3,9},{11,3},{2,11},{10,2},{0,10},{12,4},{5,12},... | collective-permute-start | bytes 2064392 | tf_op jit(solution)/shard_map/ppermute | solution.py:60
  170.8 14.7 %collective-permute-start.29 = (bf16[21,128,128]{2,1,0:T(8,128)(2,1)S(1)}, bf16[21,128,128]{2,1,0:T(8,128)(2,1)S(1)}, u32[]{:S(2)}, u32[]{:S(2)}) collective-permute-start(bf16[21,128,128]{2,1,0:T(8,128)(2,1)S(1)} %collective-permute-done.27.refs_3_), channel_id=1, source_target_pairs={{8,0},{1,8},{9,1},{3,9},{11,3},{2,11},{10,2},{0,10},{12,4},{5,12},... | collective-permute-start | bytes 2064392 | tf_op jit(solution)/shard_map/ppermute | solution.py:60
  174.2 13.6 %collective-permute-start.43 = (bf16[21,128,128]{2,1,0:T(8,128)(2,1)S(1)}, bf16[21,128,128]{2,1,0:T(8,128)(2,1)S(1)}, u32[]{:S(2)}, u32[]{:S(2)}) collective-permute-start(bf16[21,128,128]{2,1,0:T(8,128)(2,1)S(1)} %fusion.13), channel_id=1, source_target_pairs={{10,0},{0,8},{8,1},{1,9},{9,3},{3,11},{11,2},{2,10},{14,4},{4,12},... | collective-permute-start | bytes 2064392 | tf_op jit(solution)/shard_map/ppermute | solution.py:60
  175.4 16.6 %collective-permute-start.40 = (bf16[21,128,128]{2,1,0:T(8,128)(2,1)S(1)}, bf16[21,128,128]{2,1,0:T(8,128)(2,1)S(1)}, u32[]{:S(2)}, u32[]{:S(2)}) collective-permute-start(bf16[21,128,128]{2,1,0:T(8,128)(2,1)S(1)} %fusion.15), channel_id=1, source_target_pairs={{10,0},{0,8},{8,1},{1,9},{9,3},{3,11},{11,2},{2,10},{14,4},{4,12},... | collective-permute-start | bytes 2064392 | tf_op jit(solution)/shard_map/ppermute | solution.py:60
  178.2 21.6 %collective-permute-start.30 = (bf16[21,128,128]{2,1,0:T(8,128)(2,1)S(1)}, bf16[21,128,128]{2,1,0:T(8,128)(2,1)S(1)}, u32[]{:S(2)}, u32[]{:S(2)}) collective-permute-start(bf16[21,128,128]{2,1,0:T(8,128)(2,1)S(1)} %collective-permute-done.28.refs_4_), channel_id=1, source_target_pairs={{8,0},{1,8},{9,1},{3,9},{11,3},{2,11},{10,2},{0,10},{12,4},{5,12},... | collective-permute-start | bytes 2064392 | tf_op jit(solution)/shard_map/ppermute | solution.py:60
  185.6 14.7 %collective-permute-start.31 = (bf16[21,128,128]{2,1,0:T(8,128)(2,1)S(1)}, bf16[21,128,128]{2,1,0:T(8,128)(2,1)S(1)}, u32[]{:S(2)}, u32[]{:S(2)}) collective-permute-start(bf16[21,128,128]{2,1,0:T(8,128)(2,1)S(1)} %collective-permute-done.29.refs_5_), channel_id=1, source_target_pairs={{8,0},{1,8},{9,1},{3,9},{11,3},{2,11},{10,2},{0,10},{12,4},{5,12},... | collective-permute-start | bytes 2064392 | tf_op jit(solution)/shard_map/ppermute | solution.py:60
  198.0 11.0 %collective-permute-start.47 = (bf16[21,128,128]{2,1,0:T(8,128)(2,1)S(1)}, bf16[21,128,128]{2,1,0:T(8,128)(2,1)S(1)}, u32[]{:S(2)}, u32[]{:S(2)}) collective-permute-start(bf16[21,128,128]{2,1,0:T(8,128)(2,1)S(1)} %fusion.19), channel_id=1, source_target_pairs={{10,0},{0,8},{8,1},{1,9},{9,3},{3,11},{11,2},{2,10},{14,4},{4,12},... | collective-permute-start | bytes 2064392 | tf_op jit(solution)/shard_map/ppermute | solution.py:60
  198.4 17.3 %collective-permute-start.44 = (bf16[21,128,128]{2,1,0:T(8,128)(2,1)S(1)}, bf16[21,128,128]{2,1,0:T(8,128)(2,1)S(1)}, u32[]{:S(2)}, u32[]{:S(2)}) collective-permute-start(bf16[21,128,128]{2,1,0:T(8,128)(2,1)S(1)} %fusion.18), channel_id=1, source_target_pairs={{10,0},{0,8},{8,1},{1,9},{9,3},{3,11},{11,2},{2,10},{14,4},{4,12},... | collective-permute-start | bytes 2064392 | tf_op jit(solution)/shard_map/ppermute | solution.py:60
  206.7 10.7 %collective-permute-start.32 = (bf16[21,128,128]{2,1,0:T(8,128)(2,1)S(1)}, bf16[21,128,128]{2,1,0:T(8,128)(2,1)S(1)}, u32[]{:S(2)}, u32[]{:S(2)}) collective-permute-start(bf16[21,128,128]{2,1,0:T(8,128)(2,1)S(1)} %get-tuple-element.99.refs_0_.refs_8_), channel_id=1, source_target_pairs={{8,0},{1,8},{9,1},{3,9},{11,3},{2,11},{10,2},{0,10},{12,4},{5,12},... | collective-permute-start | bytes 2064392 | tf_op jit(solution)/shard_map/ppermute | solution.py:60
  208.9 15.8 %collective-permute-start.33 = (bf16[21,128,128]{2,1,0:T(8,128)(2,1)S(1)}, bf16[21,128,128]{2,1,0:T(8,128)(2,1)S(1)}, u32[]{:S(2)}, u32[]{:S(2)}) collective-permute-start(bf16[21,128,128]{2,1,0:T(8,128)(2,1)S(1)} %get-tuple-element.100.refs_1_.refs_9_), channel_id=1, source_target_pairs={{8,0},{1,8},{9,1},{3,9},{11,3},{2,11},{10,2},{0,10},{12,4},{5,12},... | collective-permute-start | bytes 2064392 | tf_op jit(solution)/shard_map/ppermute | solution.py:60
  209.4 17.6 %collective-permute-start.48 = (bf16[21,128,128]{2,1,0:T(8,128)(2,1)S(1)}, bf16[21,128,128]{2,1,0:T(8,128)(2,1)S(1)}, u32[]{:S(2)}, u32[]{:S(2)}) collective-permute-start(bf16[21,128,128]{2,1,0:T(8,128)(2,1)S(1)} %fusion.8), channel_id=1, source_target_pairs={{10,0},{0,8},{8,1},{1,9},{9,3},{3,11},{11,2},{2,10},{14,4},{4,12},... | collective-permute-start | bytes 2064392 | tf_op jit(solution)/shard_map/ppermute | solution.py:60
  216.2 14.3 %collective-permute-start.45 = (bf16[21,128,128]{2,1,0:T(8,128)(2,1)S(1)}, bf16[21,128,128]{2,1,0:T(8,128)(2,1)S(1)}, u32[]{:S(2)}, u32[]{:S(2)}) collective-permute-start(bf16[21,128,128]{2,1,0:T(8,128)(2,1)S(1)} %fusion.10), channel_id=1, source_target_pairs={{10,0},{0,8},{8,1},{1,9},{9,3},{3,11},{11,2},{2,10},{14,4},{4,12},... | collective-permute-start | bytes 2064392 | tf_op jit(solution)/shard_map/ppermute | solution.py:60
  217.4 14.7 %collective-permute-start.34 = (bf16[21,128,128]{2,1,0:T(8,128)(2,1)S(1)}, bf16[21,128,128]{2,1,0:T(8,128)(2,1)}, u32[]{:S(2)}, u32[]{:S(2)}) collective-permute-start(bf16[21,128,128]{2,1,0:T(8,128)(2,1)S(1)} %collective-permute-done.32.refs_2_.refs_10_), channel_id=1, source_target_pairs={{8,0},{1,8},{9,1},{3,9},{11,3},{2,11},{10,2},{0,10},{12,4},{5,12},... | collective-permute-start | bytes 2064392 | tf_op jit(solution)/shard_map/ppermute | solution.py:60
  224.7 14.7 %collective-permute-start.35 = (bf16[21,128,128]{2,1,0:T(8,128)(2,1)S(1)}, bf16[21,128,128]{2,1,0:T(8,128)(2,1)}, u32[]{:S(2)}, u32[]{:S(2)}) collective-permute-start(bf16[21,128,128]{2,1,0:T(8,128)(2,1)S(1)} %collective-permute-done.33.refs_3_.refs_11_), channel_id=1, source_target_pairs={{8,0},{1,8},{9,1},{3,9},{11,3},{2,11},{10,2},{0,10},{12,4},{5,12},... | collective-permute-start | bytes 2064392 | tf_op jit(solution)/shard_map/ppermute | solution.py:60
  228.3 15.0 %collective-permute-start.49 = (bf16[21,128,128]{2,1,0:T(8,128)(2,1)}, bf16[21,128,128]{2,1,0:T(8,128)(2,1)S(1)}, u32[]{:S(2)}, u32[]{:S(2)}) collective-permute-start(bf16[21,128,128]{2,1,0:T(8,128)(2,1)} %fusion.9), channel_id=1, source_target_pairs={{10,0},{0,8},{8,1},{1,9},{9,3},{3,11},{11,2},{2,10},{14,4},{4,12},... | collective-permute-start | bytes 2064392 | tf_op jit(solution)/shard_map/ppermute | solution.py:60
  231.7 14.4 %collective-permute-start.46 = (bf16[21,128,128]{2,1,0:T(8,128)(2,1)}, bf16[21,128,128]{2,1,0:T(8,128)(2,1)S(1)}, u32[]{:S(2)}, u32[]{:S(2)}) collective-permute-start(bf16[21,128,128]{2,1,0:T(8,128)(2,1)} %fusion.11), channel_id=1, source_target_pairs={{10,0},{0,8},{8,1},{1,9},{9,3},{3,11},{11,2},{2,10},{14,4},{4,12},... | collective-permute-start | bytes 2064392 | tf_op jit(solution)/shard_map/ppermute | solution.py:60
  232.1 19.8 %collective-permute-start.36 = (bf16[21,128,128]{2,1,0:T(8,128)(2,1)}, bf16[21,128,128]{2,1,0:T(8,128)(2,1)}, u32[]{:S(2)}, u32[]{:S(2)}) collective-permute-start(bf16[21,128,128]{2,1,0:T(8,128)(2,1)} %collective-permute-done.34.refs_4_.refs_12_), channel_id=1, source_target_pairs={{8,0},{1,8},{9,1},{3,9},{11,3},{2,11},{10,2},{0,10},{12,4},{5,12},... | collective-permute-start | bytes 2064392 | tf_op jit(solution)/shard_map/ppermute | solution.py:60
  239.5 14.9 %collective-permute-start.37 = (bf16[21,128,128]{2,1,0:T(8,128)(2,1)}, bf16[21,128,128]{2,1,0:T(8,128)(2,1)}, u32[]{:S(2)}, u32[]{:S(2)}) collective-permute-start(bf16[21,128,128]{2,1,0:T(8,128)(2,1)} %collective-permute-done.35.refs_5_.refs_13_), channel_id=1, source_target_pairs={{8,0},{1,8},{9,1},{3,9},{11,3},{2,11},{10,2},{0,10},{12,4},{5,12},... | collective-permute-start | bytes 2064392 | tf_op jit(solution)/shard_map/ppermute | solution.py:60
  260.5 9.0 %collective-permute-start.53 = (bf16[528,128]{1,0:T(8,128)(2,1)S(1)}, bf16[528,128]{1,0:T(8,128)(2,1)}, u32[]{:S(2)}, u32[]{:S(2)}) collective-permute-start(bf16[528,128]{1,0:T(8,128)(2,1)S(1)} %get-tuple-element.137.refs_3_), channel_id=1, source_target_pairs={{8,0},{1,8},{9,1},{3,9},{11,3},{2,11},{10,2},{0,10},{12,4},{5,12},... | collective-permute-start | bytes 405512 | tf_op jit(solution)/shard_map/ppermute | solution.py:60
  261.3 8.3 %collective-permute-start.54 = (bf16[528,128]{1,0:T(8,128)(2,1)S(1)}, bf16[528,128]{1,0:T(8,128)(2,1)}, u32[]{:S(2)}, u32[]{:S(2)}) collective-permute-start(bf16[528,128]{1,0:T(8,128)(2,1)S(1)} %get-tuple-element.137.refs_3_), channel_id=1, source_target_pairs={{10,0},{0,8},{8,1},{1,9},{9,3},{3,11},{11,2},{2,10},{14,4},{4,12},... | collective-permute-start | bytes 405512 | tf_op jit(solution)/shard_map/ppermute | solution.py:60
  261.3 8.3 %collective-permute-start.55 = (bf16[528,128]{1,0:T(8,128)(2,1)S(1)}, bf16[528,128]{1,0:T(8,128)(2,1)}, u32[]{:S(2)}, u32[]{:S(2)}) collective-permute-start(bf16[528,128]{1,0:T(8,128)(2,1)S(1)} %get-tuple-element.137.refs_3_), channel_id=1, source_target_pairs={{1,0},{9,8},{3,1},{11,9},{2,3},{10,11},{0,2},{8,10},{5,4},{13,12},... | collective-permute-start | bytes 405512 | tf_op jit(solution)/shard_map/ppermute | solution.py:60
  263.0 6.6 %collective-permute-start.56 = (bf16[528,128]{1,0:T(8,128)(2,1)S(1)}, bf16[528,128]{1,0:T(8,128)(2,1)}, u32[]{:S(2)}, u32[]{:S(2)}) collective-permute-start(bf16[528,128]{1,0:T(8,128)(2,1)S(1)} %get-tuple-element.137.refs_3_), channel_id=1, source_target_pairs={{2,0},{10,8},{0,1},{8,9},{1,3},{9,11},{3,2},{11,10},{6,4},{14,12},... | collective-permute-start | bytes 405512 | tf_op jit(solution)/shard_map/ppermute | solution.py:60
  264.0 5.5 %collective-permute-start.52 = (f32[4,128]{1,0:T(4,128)S(1)}, f32[4,128]{1,0:T(4,128)S(1)}, u32[]{:S(2)}, u32[]{:S(2)}) collective-permute-start(f32[4,128]{1,0:T(4,128)S(1)} %maximum_select_fusion.2), channel_id=1, source_target_pairs={{3,0},{11,8},{2,1},{10,9},{0,3},{8,11},{1,2},{9,10},{7,4},{15,12},... | collective-permute-start | bytes 6152 | tf_op jit(solution)/shard_map/ppermute | solution.py:65
  284.7 8.2 %collective-permute-start.61 = (f32[2,128,128]{2,1,0:T(8,128)S(1)}, f32[2,128,128]{2,1,0:T(8,128)S(1)}, u32[]{:S(2)}, u32[]{:S(2)}) collective-permute-start(f32[2,128,128]{2,1,0:T(8,128)S(1)} %get-tuple-element.164), channel_id=1, source_target_pairs={{10,0},{0,8},{8,1},{1,9},{9,3},{3,11},{11,2},{2,10},{14,4},{4,12},... | collective-permute-start | bytes 393224 | tf_op jit(solution)/shard_map/ppermute | solution.py:60
  284.8 8.1 %collective-permute-start.62 = (f32[2,128,128]{2,1,0:T(8,128)S(1)}, f32[2,128,128]{2,1,0:T(8,128)S(1)}, u32[]{:S(2)}, u32[]{:S(2)}) collective-permute-start(f32[2,128,128]{2,1,0:T(8,128)S(1)} %get-tuple-element.163), channel_id=1, source_target_pairs={{2,0},{10,8},{0,1},{8,9},{1,3},{9,11},{3,2},{11,10},{6,4},{14,12},... | collective-permute-start | bytes 393224 | tf_op jit(solution)/shard_map/ppermute | solution.py:60
  286.2 6.7 %collective-permute-start.63 = (f32[2,128,128]{2,1,0:T(8,128)S(1)}, f32[2,128,128]{2,1,0:T(8,128)S(1)}, u32[]{:S(2)}, u32[]{:S(2)}) collective-permute-start(f32[2,128,128]{2,1,0:T(8,128)S(1)} %get-tuple-element.162), channel_id=1, source_target_pairs={{11,0},{2,8},{10,1},{0,9},{8,3},{1,11},{9,2},{3,10},{15,4},{6,12},... | collective-permute-start | bytes 393224 | tf_op jit(solution)/shard_map/ppermute | solution.py:60
  287.6 4.5 %collective-permute-start.59 = (f32[4,128]{1,0:T(4,128)S(1)}, f32[4,128]{1,0:T(4,128)S(1)}, u32[]{:S(2)}, u32[]{:S(2)}) collective-permute-start(f32[4,128]{1,0:T(4,128)S(1)} %maximum_select_fusion.3), channel_id=1, source_target_pairs={{3,0},{11,8},{2,1},{10,9},{0,3},{8,11},{1,2},{9,10},{7,4},{15,12},... | collective-permute-start | bytes 6152 | tf_op jit(solution)/shard_map/ppermute | solution.py:65
  292.2 3.7 %collective-permute-start.60 = (f32[8,128]{1,0:T(8,128)S(1)}, f32[8,128]{1,0:T(8,128)S(1)}, u32[]{:S(2)}, u32[]{:S(2)}) collective-permute-start(f32[8,128]{1,0:T(8,128)S(1)} %maximum_select_fusion.1.table_ref), channel_id=1, source_target_pairs={{0,16},{8,17},{1,18},{9,19},{3,20},{11,21},{2,22},{10,23},{4,24},{... | collective-permute-start | bytes 12296 | tf_op jit(solution)/shard_map/ppermute | solution.py:55
  299.4 9.9 %collective-permute-start.64 = (bf16[128,128]{1,0:T(8,128)(2,1)S(1)}, bf16[128,128]{1,0:T(8,128)(2,1)S(1)}, u32[]{:S(2)}, u32[]{:S(2)}) collective-permute-start(bf16[128,128]{1,0:T(8,128)(2,1)S(1)} %get-tuple-element.169), channel_id=1, source_target_pairs={{0,16},{8,17},{1,18},{9,19},{3,20},{11,21},{2,22},{10,23},{4,24},{... | collective-permute-start | bytes 98312 | tf_op jit(solution)/shard_map/ppermute | solution.py:55
  300.1 9.2 %collective-permute-start.65 = (bf16[128,128]{1,0:T(8,128)(2,1)S(1)}, bf16[128,128]{1,0:T(8,128)(2,1)S(1)}, u32[]{:S(2)}, u32[]{:S(2)}) collective-permute-start(bf16[128,128]{1,0:T(8,128)(2,1)S(1)} %get-tuple-element.172), channel_id=1, source_target_pairs={{0,23},{8,16},{1,17},{9,18},{3,19},{11,20},{2,21},{10,22},{4,31},{... | collective-permute-start | bytes 98312 | tf_op jit(solution)/shard_map/ppermute | solution.py:55
  306.0 5.0 %collective-permute-start.66 = (bf16[128,128]{1,0:T(8,128)(2,1)S(1)}, bf16[128,128]{1,0:T(8,128)(2,1)S(1)}, u32[]{:S(2)}, u32[]{:S(2)}) collective-permute-start(bf16[128,128]{1,0:T(8,128)(2,1)S(1)} %get-tuple-element.171), channel_id=1, source_target_pairs={{0,22},{8,23},{1,16},{9,17},{3,18},{11,19},{2,20},{10,21},{4,30},{... | collective-permute-start | bytes 98312 | tf_op jit(solution)/shard_map/ppermute | solution.py:55
  306.6 5.4 %collective-permute-start.67 = (bf16[128,128]{1,0:T(8,128)(2,1)S(1)}, bf16[128,128]{1,0:T(8,128)(2,1)S(1)}, u32[]{:S(2)}, u32[]{:S(2)}) collective-permute-start(bf16[128,128]{1,0:T(8,128)(2,1)S(1)} %get-tuple-element.170), channel_id=1, source_target_pairs={{0,21},{8,22},{1,23},{9,16},{3,17},{11,18},{2,19},{10,20},{4,29},{... | collective-permute-start | bytes 98312 | tf_op jit(solution)/shard_map/ppermute | solution.py:55
  (34 other events, 256.6 us)

commit v8 on v5

--- a/solution.py
+++ b/solution.py
@@ -767,11 +767,9 @@
         for t in range(1, states):
             if step == 0 and t == states - 1:
                 left, envs[-1] = after(left, envs[-1])
-            if step == 1 and t == states - 1:
-                rolled_vector, envs[-1] = after(rolled_vector, envs[-1])
             envs.append(ahead(envs[-1], 1))
         if step == 0:
-            rolled, envs = after(rolled, envs)
+            (rolled, rolled_vector), envs = after((rolled, rolled_vector), envs)
         right, square = right_whole(
             envs,
             right_isos[step],

time: 320 us -> 310 us (0.969)
  waiting for transfers between devices: 117 us -> 107 us
    ppermute x52, waiting for transfers between devices: 104 us -> 93.6 us  [ahead(): lax.ppermute(x, BOTH, self.pairs(lambda g, k: self.slot(g + chain_by, k +...]
  transfers between devices with their start and end apart: 68 -> 68, of which waited for: 28 -> 29; matrix products, arithmetic and copies ran while one was open for 7% -> 7% of each run, Pallas kernels for 10% -> 10%
where the time goes in v8:
time: 310 us; the launch traced here: 307 us
  starting transfers between devices  109 us (35%)
  waiting for transfers between devices  107 us (35%)
  Pallas kernels  52.7 us (17%)
  local copies, waits for them, and re-layouts  11.9 us (4%)
  matrix products  11.1 us (4%)
  blocking collectives  8.06 us (3%)
  other arithmetic  5.6 us (2%)
    ppermute x52, waiting for transfers between devices, ahead(): lax.ppermute(x, BOTH, self.pairs(lambda g, k: self.slot(g + chain_by, k +...  93.6 us
    ppermute x52, starting transfers between devices, ahead(): lax.ppermute(x, BOTH, self.pairs(lambda g, k: self.slot(g + chain_by, k +...  65.9 us
    pallas_call x19, Pallas kernels, call(): pl.pallas_call(kernel, out_shape=out_shape, scratch_shapes=scratch_shapes...  52.7 us
    ppermute x5, starting transfers between devices, fetch(): lax.ppermute(x, BOTH, self.pairs(lambda g, k: self.home(g + site_by, k +...  24.7 us
    dot_general x12, matrix products, local(): jnp.einsum('xy,vxz->vyz', left_isos[step][s], gathered[s][piece], preferr...  10.9 us
    ppermute x5, starting transfers between devices, send_home(): lax.ppermute(x, BOTH, self.pairs(self.slot, lambda g, k: self.home(g + si...  10.6 us
    ppermute x6, waiting for transfers between devices, partner(): lax.ppermute(x, BOTH, self.pairs(lambda g, k: self.slot(g, k ^ bit), self...  9.76 us
    all_gather x1, blocking collectives, local(): lax.all_gather(weight_matrices(mpo[0], pattern[0], secs), 'site')  8.06 us
  transfers between devices with their start and end apart: 68, of which 29 were waited for; matrix products, arithmetic and copies ran while one was open for 7% of the time, Pallas kernels for 10%

profile of v8, /device:TPU:0, one launch (start us, length us, event | category | flops | bytes accessed | tf_op | source)
XLA Modules:
  0.0 307.2 jit_solution(9852861148528456648)
XLA Ops:
  0.6 5.0 %collective-permute-start.5 = (bf16[4,128,128]{2,1,0:T(8,128)(2,1)}, bf16[4,128,128]{2,1,0:T(8,128)(2,1)S(1)}, u32[]{:S(2)}, u32[]{:S(2)}) collective-permute-start(bf16[4,128,128]{2,1,0:T(8,128)(2,1)} %bitcast.190), channel_id=1, source_target_pairs={{8,0},{9,8},{10,1},{11,9},{12,3},{13,11},{14,2},{15,10},{16,4},{17... | collective-permute-start | bytes 393224 | tf_op jit(solution)/shard_map/ppermute | solution.py:50
  5.7 4.4 %collective-permute-start.6 = (bf16[4,128,128]{2,1,0:T(8,128)(2,1)}, bf16[4,128,128]{2,1,0:T(8,128)(2,1)S(1)}, u32[]{:S(2)}, u32[]{:S(2)}) collective-permute-start(bf16[4,128,128]{2,1,0:T(8,128)(2,1)} %bitcast.193), channel_id=1, source_target_pairs={{24,0},{25,8},{26,1},{27,9},{28,3},{29,11},{30,2},{31,10},{0,4},{1... | collective-permute-start | bytes 393224 | tf_op jit(solution)/shard_map/ppermute | solution.py:50
  11.6 2.9 pad_maximum_fusion
  14.6 13.9 %collective-permute-start = (bf16[50,128,128]{2,1,0:T(8,128)(2,1)}, bf16[50,128,128]{2,1,0:T(8,128)(2,1)}, u32[]{:S(2)}, u32[]{:S(2)}) collective-permute-start(bf16[50,128,128]{2,1,0:T(8,128)(2,1)} %pad_maximum_fusion), channel_id=1, source_target_pairs={{0,0},{1,8},{2,1},{3,9},{4,3},{5,11},{6,2},{7,10},{8,4},{9,12},{10... | collective-permute-start | bytes 4915208 | tf_op jit(solution)/shard_map/ppermute | solution.py:50
  29.5 8.1 %all-gather = bf16[8,168,168]{2,1,0:T(8,128)(2,1)S(1)} all-gather(bf16[2,168,168]{2,1,0:T(8,128)(2,1)S(1)} %pad_maximum_fusion.2), channel_id=2, replica_groups=mesh['site'=4,'sec'=8] {'site'}, dimensions={0}, use_global_device_ids=true | all-gather | bytes 564480 | tf_op jit(solution)/shard_map/all_gather | solution.py:742
  45.8 1.5 collective-permute-done.14
  47.4 4.2 %collective-permute-done.13 = bf16[128,128]{1,0:T(8,128)(2,1)S(1)} collective-permute-done((bf16[128,128]{1,0:T(8,128)(2,1)S(1)}, bf16[128,128]{1,0:T(8,128)(2,1)S(1)}, u32[]{:S(2)}, u32[]{:S(2)}) %collective-permute-start.13) | collective-permute-done | bytes 32800 | tf_op jit(solution)/shard_map/ppermute | solution.py:60
  52.3 1.8 collective-permute-start.9
  54.1 1.4 fusion.32
  56.4 7.9 %collective-permute-start.19 = (bf16[21,128,128]{2,1,0:T(8,128)(2,1)S(1)}, bf16[21,128,128]{2,1,0:T(8,128)(2,1)S(1)}, u32[]{:S(2)}, u32[]{:S(2)}) collective-permute-start(bf16[21,128,128]{2,1,0:T(8,128)(2,1)S(1)} %get-tuple-element.78.refs_0_), channel_id=1, source_target_pairs={{8,0},{1,8},{9,1},{3,9},{11,3},{2,11},{10,2},{0,10},{12,4},{5,12},... | collective-permute-start | bytes 2064392 | tf_op jit(solution)/shard_map/ppermute | solution.py:60
  67.3 12.9 %collective-permute-done.19.refs_2_ = bf16[21,128,128]{2,1,0:T(8,128)(2,1)S(1)} collective-permute-done((bf16[21,128,128]{2,1,0:T(8,128)(2,1)S(1)}, bf16[21,128,128]{2,1,0:T(8,128)(2,1)S(1)}, u32[]{:S(2)}, u32[]{:S(2)}) %collective-permute-start.19) | collective-permute-done | bytes 688160 | tf_op jit(solution)/shard_map/ppermute | solution.py:60
  80.2 1.9 collective-permute-start.22
  82.1 8.3 %collective-permute-done.20.refs_3_ = bf16[21,128,128]{2,1,0:T(8,128)(2,1)S(1)} collective-permute-done((bf16[21,128,128]{2,1,0:T(8,128)(2,1)S(1)}, bf16[21,128,128]{2,1,0:T(8,128)(2,1)S(1)}, u32[]{:S(2)}, u32[]{:S(2)}) %collective-permute-start.20) | collective-permute-done | bytes 688160 | tf_op jit(solution)/shard_map/ppermute | solution.py:60
  90.4 1.9 collective-permute-start.23
  93.4 1.8 collective-permute-start.3
  95.4 3.8 %collective-permute-done.2 = bf16[8,128,128]{2,1,0:T(8,128)(2,1)S(1)} collective-permute-done((bf16[8,128,128]{2,1,0:T(8,128)(2,1)S(1)}, bf16[8,128,128]{2,1,0:T(8,128)(2,1)S(1)}, u32[]{:S(2)}, u32[]{:S(2)}) %collective-permute-start.2) | collective-permute-done | bytes 262176 | tf_op jit(solution)/shard_map/ppermute | solution.py:60
  100.6 7.4 %collective-permute-done.23.refs_5_ = bf16[21,128,128]{2,1,0:T(8,128)(2,1)S(1)} collective-permute-done((bf16[21,128,128]{2,1,0:T(8,128)(2,1)S(1)}, bf16[21,128,128]{2,1,0:T(8,128)(2,1)S(1)}, u32[]{:S(2)}, u32[]{:S(2)}) %collective-permute-start.23) | collective-permute-done | bytes 688160 | tf_op jit(solution)/shard_map/ppermute | solution.py:60
  107.9 1.9 collective-permute-start.24
  109.9 1.6 collective-permute-start.25
  112.2 2.0 collective-permute-start.17
  114.2 2.5 collective-permute-done.18.refs_7_
  116.7 11.6 %collective-permute-done.17.refs_6_ = bf16[4,128,128]{2,1,0:T(8,128)(2,1)S(1)} collective-permute-done((bf16[4,128,128]{2,1,0:T(8,128)(2,1)S(1)}, bf16[4,128,128]{2,1,0:T(8,128)(2,1)S(1)}, u32[]{:S(2)}, u32[]{:S(2)}) %collective-permute-start.17) | collective-permute-done | bytes 131104 | tf_op jit(solution)/shard_map/ppermute | solution.py:60
  128.5 5.2 %shard_map.147 = (bf16[21,128,128]{2,1,0:T(8,128)(2,1)S(1)}, bf16[21,128,128]{2,1,0:T(8,128)(2,1)S(1)}, bf16[21,128,128]{2,1,0:T(8,128)(2,1)S(1)}, bf16[21,128,1...) custom-call(bf16[21,128,128]{2,1,0:T(8,128)(2,1)S(1)} %get-tuple-ele, ...), custom_call_target="tpu_custom_call" | custom-call | flops 2334130176 | bytes 3076096 | tf_op jit(solution)/shard_map/pallas_call | solution.py:517
  137.2 6.3 %shard_map.145 = (bf16[21,128,128]{2,1,0:T(8,128)(2,1)S(1)}, bf16[21,128,128]{2,1,0:T(8,128)(2,1)S(1)}, f32[8,128]{1,0:T(8,128)S(1)}) custom-call(bf16[21,128,128]{2,1,0:T(8,128)(2,1)S(1)} %get-tuple-element.78.refs_0_, bf16[21,128,128]{2,1,0:T(8,128)(2,1)S(1)} %get-tuple-element.79.refs_1_, bf16[21,128,128]{2,1,0:T(8,128)(2,1)S(1)} %collective-permute-done.19.refs_2_, ...), custom_call_target="tpu_custom_call" | custom-call | flops 2334130176 | bytes 7335936 | tf_op jit(solution)/shard_map/pallas_call | solution.py:517
  143.6 2.0 collective-permute-start.26
  145.5 1.6 collective-permute-start.27
  149.0 3.8 %collective-permute-done.38 = bf16[21,128,128]{2,1,0:T(8,128)(2,1)S(1)} collective-permute-done((bf16[21,128,128]{2,1,0:T(8,128)(2,1)S(1)}, bf16[21,128,128]{2,1,0:T(8,128)(2,1)S(1)}, u32[]{:S(2)}, u32[]{:S(2)}) %collective-permute-start.38) | collective-permute-done | bytes 688160 | tf_op jit(solution)/shard_map/ppermute | solution.py:60
  154.0 2.2 collective-permute-start.28
  156.2 5.2 %collective-permute-done.27.refs_3_ = bf16[21,128,128]{2,1,0:T(8,128)(2,1)S(1)} collective-permute-done((bf16[21,128,128]{2,1,0:T(8,128)(2,1)S(1)}, bf16[21,128,128]{2,1,0:T(8,128)(2,1)S(1)}, u32[]{:S(2)}, u32[]{:S(2)}) %collective-permute-start.27) | collective-permute-done | bytes 688160 | tf_op jit(solution)/shard_map/ppermute | solution.py:60
  161.4 2.2 collective-permute-start.29
  164.7 2.2 collective-permute-start.43
  171.4 4.6 %collective-permute-done.29.refs_5_ = bf16[21,128,128]{2,1,0:T(8,128)(2,1)S(1)} collective-permute-done((bf16[21,128,128]{2,1,0:T(8,128)(2,1)S(1)}, bf16[21,128,128]{2,1,0:T(8,128)(2,1)S(1)}, u32[]{:S(2)}, u32[]{:S(2)}) %collective-permute-start.29) | collective-permute-done | bytes 688160 | tf_op jit(solution)/shard_map/ppermute | solution.py:60
  176.1 2.2 collective-permute-start.31
  178.7 3.8 %collective-permute-done.40.moved_ref = bf16[21,128,128]{2,1,0:T(8,128)(2,1)S(1)} collective-permute-done((bf16[21,128,128]{2,1,0:T(8,128)(2,1)S(1)}, bf16[21,128,128]{2,1,0:T(8,128)(2,1)S(1)}, u32[]{:S(2)}, u32[]{:S(2)}) %collective-permute-start.40) | collective-permute-done | bytes 688160 | tf_op jit(solution)/shard_map/ppermute | solution.py:60
  182.9 5.2 %shard_map.150 = (bf16[21,128,128]{2,1,0:T(8,128)(2,1)S(1)}, bf16[21,128,128]{2,1,0:T(8,128)(2,1)S(1)}, bf16[21,128,128]{2,1,0:T(8,128)(2,1)S(1)}, bf16[21,128,1...) custom-call(bf16[21,128,128]{2,1,0:T(8,128)(2,1)S(1)} %get-tuple-ele, ...), custom_call_target="tpu_custom_call" | custom-call | flops 2334130176 | bytes 3076096 | tf_op jit(solution)/shard_map/pallas_call | solution.py:517
  188.5 1.5 collective-permute-start.47
  190.4 2.5 collective-permute-start.44
  192.9 6.3 %shard_map.146 = (bf16[21,128,128]{2,1,0:T(8,128)(2,1)S(1)}, bf16[21,128,128]{2,1,0:T(8,128)(2,1)S(1)}, f32[8,128]{1,0:T(8,128)S(1)}) custom-call(bf16[21,128,128]{2,1,0:T(8,128)(2,1)S(1)} %get-tuple-element.88.refs_0_, bf16[21,128,128]{2,1,0:T(8,128)(2,1)S(1)} %get-tuple-element.89.refs_1_, bf16[21,128,128]{2,1,0:T(8,128)(2,1)S(1)} %collective-permute-done.26.refs_2_, ...), custom_call_target="tpu_custom_call" | custom-call | flops 2334130176 | bytes 7335936 | tf_op jit(solution)/shard_map/pallas_call | solution.py:517
  199.3 1.4 collective-permute-start.33
  202.1 4.2 %collective-permute-done.44 = bf16[21,128,128]{2,1,0:T(8,128)(2,1)S(1)} collective-permute-done((bf16[21,128,128]{2,1,0:T(8,128)(2,1)S(1)}, bf16[21,128,128]{2,1,0:T(8,128)(2,1)S(1)}, u32[]{:S(2)}, u32[]{:S(2)}) %collective-permute-start.44) | collective-permute-done | bytes 688160 | tf_op jit(solution)/shard_map/ppermute | solution.py:60
  206.7 1.5 collective-permute-start.45
  208.2 1.8 collective-permute-start.34
  210.0 5.2 %collective-permute-done.33.refs_3_.refs_11_ = bf16[21,128,128]{2,1,0:T(8,128)(2,1)S(1)} collective-permute-done((bf16[21,128,128]{2,1,0:T(8,128)(2,1)S(1)}, bf16[21,128,128]{2,1,0:T(8,128)(2,1)S(1)}, u32[]{:S(2)}, u32[]{:S(2)}) %collective-permute-start.33) | collective-permute-done | bytes 688160 | tf_op jit(solution)/shard_map/ppermute | solution.py:60
  215.2 2.2 collective-permute-start.35
  218.7 2.3 collective-permute-start.49
  222.3 1.6 collective-permute-start.46
  224.5 5.4 %collective-permute-done.35.refs_5_.refs_13_ = bf16[21,128,128]{2,1,0:T(8,128)(2,1)} collective-permute-done((bf16[21,128,128]{2,1,0:T(8,128)(2,1)S(1)}, bf16[21,128,128]{2,1,0:T(8,128)(2,1)}, u32[]{:S(2)}, u32[]{:S(2)}) %collective-permute-start.35) | collective-permute-done | bytes 688160 | tf_op jit(solution)/shard_map/ppermute | solution.py:60
  229.9 2.2 collective-permute-start.37
  234.1 2.5 collective-permute-done.46.moved_ref
  237.1 5.2 %shard_map.153.refs_13_ = bf16[21504,128]{1,0:T(8,128)(2,1)S(1)} custom-call(bf16[21,128,128]{2,1,0:T(8,128)(2,1)S(1)} %get-tuple-element.122.refs_0_, bf16[21,128,128]{2,1,0:T(8,128)(2,1)S(1)} %get-tuple-element.123.refs_1_, bf16[1360,384]{1,0:T(8,128)(2,1)S(1)} %copy-done.21, bf16[4,128,128]{2,1,0:T(8,128)(2,1)S(1)} %get-tuple-element.125.refs_3_, ...), custom_call_target="tpu_custom_call" | custom-call | flops 2334130176 | bytes 3076096 | tf_op jit(solution)/shard_map/pallas_call | solution.py:517
  242.3 2.4 collective-permute-done.37.refs_7_.refs_15_
  244.8 3.8 %shard_map.154 = (f32[4,128,128]{2,1,0:T(8,128)S(1)}, bf16[528,128]{1,0:T(8,128)(2,1)S(1)}, f32[1,128]{1,0:T(1,128)S(1)}) custom-call(bf16[21,128,128]{2,1,0:T(8,128)(2,1)S(1)} %copy-done.1, bf16[21,128,128]{2,1,0:T(8,128)(2,1)S(1)} %copy-done.3, bf16[21,128,128]{2,1,0:T(8,128)(2,1)S(1)} %copy-done.5, bf16[21,128,128]{2,1,0:T(8,128)(2,1)S(1)} %copy-done.7, ...), custom_call_target="tpu_custom_call" | custom-call | flops 704643072 | bytes 11292672 | tf_op jit(solution)/shard_map/pallas_call | solution.py:517
  248.5 4.2 %collective-permute-start.50 = (f32[1,128]{1,0:T(1,128)S(1)}, f32[1,128]{1,0:T(1,128)S(1)}, u32[]{:S(2)}, u32[]{:S(2)}) collective-permute-start(f32[1,128]{1,0:T(1,128)S(1)} %get-tuple-element.131), channel_id=1, source_target_pairs={{8,0},{0,8},{9,1},{1,9},{11,3},{3,11},{10,2},{2,10},{12,4},{4,12},... | collective-permute-start | bytes 1544 | tf_op jit(solution)/shard_map/ppermute | solution.py:65
  253.6 1.8 collective-permute-start.51
  255.6 1.8 collective-permute-start.55
  257.4 1.7 collective-permute-start.53
  259.2 4.5 %collective-permute-done.52 = f32[4,128]{1,0:T(4,128)S(1)} collective-permute-done((f32[4,128]{1,0:T(4,128)S(1)}, f32[4,128]{1,0:T(4,128)S(1)}, u32[]{:S(2)}, u32[]{:S(2)}) %collective-permute-start.52) | collective-permute-done | bytes 2080 | tf_op jit(solution)/shard_map/ppermute | solution.py:65
  267.1 8.9 %shard_map.155 = (f32[4,128,128]{2,1,0:T(8,128)S(1)}, f32[1,128]{1,0:T(1,128)S(1)}) custom-call(bf16[21,128,128]{2,1,0:T(8,128)(2,1)S(1)} %copy-done.11, bf16[21,128,128]{2,1,0:T(8,128)(2,1)S(1)} %copy-done.9, bf16[1360,384]{1,0:T(8,128)(2,1)S(1)} %copy-done.22, bf16[528,128]{1,0:T(8,128)(2,1)S(1)} %get-tuple-element.133.refs_3_, ...), custom_call_target="tpu_custom_call" | custom-call | flops 3038773248 | bytes 8601600 | tf_op jit(solution)/shard_map/pallas_call | solution.py:517
  283.2 3.1 %collective-permute-done.59 = f32[4,128]{1,0:T(4,128)S(1)} collective-permute-done((f32[4,128]{1,0:T(4,128)S(1)}, f32[4,128]{1,0:T(4,128)S(1)}, u32[]{:S(2)}, u32[]{:S(2)}) %collective-permute-start.59) | collective-permute-done | bytes 2080 | tf_op jit(solution)/shard_map/ppermute | solution.py:65
  287.1 1.7 collective-permute-done.61
  290.0 3.5 %shard_map.157 = bf16[4,128,128]{2,1,0:T(8,128)(2,1)S(1)} custom-call(f32[4,2,128,128]{3,2,1,0:T(8,128)S(1)} %pad_maximum_fusion.1.both_ref, f32[8,128]{1,0:T(8,128)S(1)} %maximum_select_fusion.1.table_ref, bf16[128,128]{1,0:T(8,128)(2,1)S(1)} %get-tuple-element.166.centre_ref), custom_call_target="tpu_custom_call" | custom-call | flops 1258291200 | bytes 561152 | tf_op jit(solution)/shard_map/pallas_call | solution.py:517
  294.2 7.3 %collective-permute-start.67 = (bf16[128,128]{1,0:T(8,128)(2,1)S(1)}, bf16[128,128]{1,0:T(8,128)(2,1)S(1)}, u32[]{:S(2)}, u32[]{:S(2)}) collective-permute-start(bf16[128,128]{1,0:T(8,128)(2,1)S(1)} %get-tuple-element.168), channel_id=1, source_target_pairs={{0,21},{8,22},{1,23},{9,16},{3,17},{11,18},{2,19},{10,20},{4,29},{... | collective-permute-start | bytes 98312 | tf_op jit(solution)/shard_map/ppermute | solution.py:55
  301.6 1.8 collective-permute-start.65
  304.1 2.4 collective-permute-done.66
  (210 shorter events, 55.7 us)
Async XLA Ops:
  0.6 43.2 %collective-permute-start.5 = (bf16[4,128,128]{2,1,0:T(8,128)(2,1)}, bf16[4,128,128]{2,1,0:T(8,128)(2,1)S(1)}, u32[]{:S(2)}, u32[]{:S(2)}) collective-permute-start(bf16[4,128,128]{2,1,0:T(8,128)(2,1)} %bitcast.190), channel_id=1, source_target_pairs={{8,0},{9,8},{10,1},{11,9},{12,3},{13,11},{14,2},{15,10},{16,4},{17... | collective-permute-start | bytes 393224 | tf_op jit(solution)/shard_map/ppermute | solution.py:50
  5.7 38.3 %collective-permute-start.6 = (bf16[4,128,128]{2,1,0:T(8,128)(2,1)}, bf16[4,128,128]{2,1,0:T(8,128)(2,1)S(1)}, u32[]{:S(2)}, u32[]{:S(2)}) collective-permute-start(bf16[4,128,128]{2,1,0:T(8,128)(2,1)} %bitcast.193), channel_id=1, source_target_pairs={{24,0},{25,8},{26,1},{27,9},{28,3},{29,11},{30,2},{31,10},{0,4},{1... | collective-permute-start | bytes 393224 | tf_op jit(solution)/shard_map/ppermute | solution.py:50
  11.0 32.9 %collective-permute-start.11 = (bf16[5,128,128]{2,1,0:T(8,128)(2,1)S(1)}, bf16[5,128,128]{2,1,0:T(8,128)(2,1)S(1)}, u32[]{:S(2)}, u32[]{:S(2)}) collective-permute-start(bf16[5,128,128]{2,1,0:T(8,128)(2,1)S(1)} %pad_maximum_fusion.3), channel_id=1, source_target_pairs={{16,0},{17,8},{18,1},{19,9},{20,3},{21,11},{22,2},{23,10},{24,4},{... | collective-permute-start | bytes 491528 | tf_op jit(solution)/shard_map/ppermute | solution.py:50
  14.6 39.5 %collective-permute-start = (bf16[50,128,128]{2,1,0:T(8,128)(2,1)}, bf16[50,128,128]{2,1,0:T(8,128)(2,1)}, u32[]{:S(2)}, u32[]{:S(2)}) collective-permute-start(bf16[50,128,128]{2,1,0:T(8,128)(2,1)} %pad_maximum_fusion), channel_id=1, source_target_pairs={{0,0},{1,8},{2,1},{3,9},{4,3},{5,11},{6,2},{7,10},{8,4},{9,12},{10... | collective-permute-start | bytes 4915208 | tf_op jit(solution)/shard_map/ppermute | solution.py:50
  44.0 7.8 %collective-permute-start.8 = (bf16[8,128,128]{2,1,0:T(8,128)(2,1)S(1)}, bf16[8,128,128]{2,1,0:T(8,128)(2,1)S(1)}, u32[]{:S(2)}, u32[]{:S(2)}) collective-permute-start(bf16[8,128,128]{2,1,0:T(8,128)(2,1)S(1)} %constant_dynamic-update-slice_fusion), channel_id=1, source_target_pairs={{10,0},{0,8},{8,1},{1,9},{9,3},{3,11},{11,2},{2,10},{14,4},{4,12},... | collective-permute-start | bytes 786440 | tf_op jit(solution)/shard_map/ppermute | solution.py:60
  44.4 7.9 %collective-permute-start.7 = (bf16[8,128,128]{2,1,0:T(8,128)(2,1)S(1)}, bf16[8,128,128]{2,1,0:T(8,128)(2,1)S(1)}, u32[]{:S(2)}, u32[]{:S(2)}) collective-permute-start(bf16[8,128,128]{2,1,0:T(8,128)(2,1)S(1)} %constant_dynamic-update-slice_fusion), channel_id=1, source_target_pairs={{8,0},{1,8},{9,1},{3,9},{11,3},{2,11},{10,2},{0,10},{12,4},{5,12},... | collective-permute-start | bytes 786440 | tf_op jit(solution)/shard_map/ppermute | solution.py:60
  45.8 5.8 %collective-permute-start.13 = (bf16[128,128]{1,0:T(8,128)(2,1)S(1)}, bf16[128,128]{1,0:T(8,128)(2,1)S(1)}, u32[]{:S(2)}, u32[]{:S(2)}) collective-permute-start(bf16[128,128]{1,0:T(8,128)(2,1)S(1)} %get-tuple-element.166.centre_ref), channel_id=1, source_target_pairs={{1,0},{9,8},{3,1},{11,9},{2,3},{10,11},{0,2},{8,10},{5,4},{13,12},... | collective-permute-start | bytes 98312 | tf_op jit(solution)/shard_map/ppermute | solution.py:60
  47.3 4.3 %collective-permute-start.12 = (bf16[128,128]{1,0:T(8,128)(2,1)S(1)}, bf16[128,128]{1,0:T(8,128)(2,1)S(1)}, u32[]{:S(2)}, u32[]{:S(2)}) collective-permute-start(bf16[128,128]{1,0:T(8,128)(2,1)S(1)} %get-tuple-element.166.centre_ref), channel_id=1, source_target_pairs={{8,0},{1,8},{9,1},{3,9},{11,3},{2,11},{10,2},{0,10},{12,4},{5,12},... | collective-permute-start | bytes 98312 | tf_op jit(solution)/shard_map/ppermute | solution.py:60
  51.8 14.1 %collective-permute-start.10 = (bf16[8,128,128]{2,1,0:T(8,128)(2,1)S(1)}, bf16[8,128,128]{2,1,0:T(8,128)(2,1)S(1)}, u32[]{:S(2)}, u32[]{:S(2)}) collective-permute-start(bf16[8,128,128]{2,1,0:T(8,128)(2,1)S(1)} %collective-permute-done.8), channel_id=1, source_target_pairs={{10,0},{0,8},{8,1},{1,9},{9,3},{3,11},{11,2},{2,10},{14,4},{4,12},... | collective-permute-start | bytes 786440 | tf_op jit(solution)/shard_map/ppermute | solution.py:60
  52.3 12.1 %collective-permute-start.9 = (bf16[8,128,128]{2,1,0:T(8,128)(2,1)S(1)}, bf16[8,128,128]{2,1,0:T(8,128)(2,1)S(1)}, u32[]{:S(2)}, u32[]{:S(2)}) collective-permute-start(bf16[8,128,128]{2,1,0:T(8,128)(2,1)S(1)} %collective-permute-done.7), channel_id=1, source_target_pairs={{8,0},{1,8},{9,1},{3,9},{11,3},{2,11},{10,2},{0,10},{12,4},{5,12},... | collective-permute-start | bytes 786440 | tf_op jit(solution)/shard_map/ppermute | solution.py:60
  55.5 37.8 %collective-permute-start.21 = (bf16[42,128,128]{2,1,0:T(8,128)(2,1)S(1)}, bf16[42,128,128]{2,1,0:T(8,128)(2,1)S(1)}, u32[]{:S(2)}, u32[]{:S(2)}) collective-permute-start(bf16[42,128,128]{2,1,0:T(8,128)(2,1)S(1)} %bitcast.205), channel_id=1, source_target_pairs={{0,0},{1,8},{2,1},{3,9},{4,3},{5,11},{6,2},{7,10},{8,4},{9,12},{10... | collective-permute-start | bytes 4128776 | tf_op jit(solution)/shard_map/ppermute | solution.py:50
  56.4 23.8 %collective-permute-start.19 = (bf16[21,128,128]{2,1,0:T(8,128)(2,1)S(1)}, bf16[21,128,128]{2,1,0:T(8,128)(2,1)S(1)}, u32[]{:S(2)}, u32[]{:S(2)}) collective-permute-start(bf16[21,128,128]{2,1,0:T(8,128)(2,1)S(1)} %get-tuple-element.78.refs_0_), channel_id=1, source_target_pairs={{8,0},{1,8},{9,1},{3,9},{11,3},{2,11},{10,2},{0,10},{12,4},{5,12},... | collective-permute-start | bytes 2064392 | tf_op jit(solution)/shard_map/ppermute | solution.py:60
  64.3 26.1 %collective-permute-start.20 = (bf16[21,128,128]{2,1,0:T(8,128)(2,1)S(1)}, bf16[21,128,128]{2,1,0:T(8,128)(2,1)S(1)}, u32[]{:S(2)}, u32[]{:S(2)}) collective-permute-start(bf16[21,128,128]{2,1,0:T(8,128)(2,1)S(1)} %get-tuple-element.79.refs_1_), channel_id=1, source_target_pairs={{8,0},{1,8},{9,1},{3,9},{11,3},{2,11},{10,2},{0,10},{12,4},{5,12},... | collective-permute-start | bytes 2064392 | tf_op jit(solution)/shard_map/ppermute | solution.py:60
  64.4 45.4 %collective-permute-start.16 = (bf16[4,128,128]{2,1,0:T(8,128)(2,1)S(1)}, bf16[4,128,128]{2,1,0:T(8,128)(2,1)S(1)}, u32[]{:S(2)}, u32[]{:S(2)}) collective-permute-start(bf16[4,128,128]{2,1,0:T(8,128)(2,1)S(1)} %get-tuple-element.125.refs_3_), channel_id=1, source_target_pairs={{10,0},{0,8},{8,1},{1,9},{9,3},{3,11},{11,2},{2,10},{14,4},{4,12},... | collective-permute-start | bytes 393224 | tf_op jit(solution)/shard_map/ppermute | solution.py:60
  65.9 27.3 %collective-permute-start.1 = (bf16[8,128,128]{2,1,0:T(8,128)(2,1)S(1)}, bf16[8,128,128]{2,1,0:T(8,128)(2,1)S(1)}, u32[]{:S(2)}, u32[]{:S(2)}) collective-permute-start(bf16[8,128,128]{2,1,0:T(8,128)(2,1)S(1)} %concatenate.64), channel_id=1, source_target_pairs={{8,0},{1,8},{9,1},{3,9},{11,3},{2,11},{10,2},{0,10},{12,4},{5,12},... | collective-permute-start | bytes 786440 | tf_op jit(solution)/shard_map/ppermute | solution.py:60
  80.2 20.4 %collective-permute-start.22 = (bf16[21,128,128]{2,1,0:T(8,128)(2,1)S(1)}, bf16[21,128,128]{2,1,0:T(8,128)(2,1)S(1)}, u32[]{:S(2)}, u32[]{:S(2)}) collective-permute-start(bf16[21,128,128]{2,1,0:T(8,128)(2,1)S(1)} %collective-permute-done.19.refs_2_), channel_id=1, source_target_pairs={{8,0},{1,8},{9,1},{3,9},{11,3},{2,11},{10,2},{0,10},{12,4},{5,12},... | collective-permute-start | bytes 2064392 | tf_op jit(solution)/shard_map/ppermute | solution.py:60
  90.4 17.6 %collective-permute-start.23 = (bf16[21,128,128]{2,1,0:T(8,128)(2,1)S(1)}, bf16[21,128,128]{2,1,0:T(8,128)(2,1)S(1)}, u32[]{:S(2)}, u32[]{:S(2)}) collective-permute-start(bf16[21,128,128]{2,1,0:T(8,128)(2,1)S(1)} %collective-permute-done.20.refs_3_), channel_id=1, source_target_pairs={{8,0},{1,8},{9,1},{3,9},{11,3},{2,11},{10,2},{0,10},{12,4},{5,12},... | collective-permute-start | bytes 2064392 | tf_op jit(solution)/shard_map/ppermute | solution.py:60
  93.3 5.9 %collective-permute-start.2 = (bf16[8,128,128]{2,1,0:T(8,128)(2,1)S(1)}, bf16[8,128,128]{2,1,0:T(8,128)(2,1)S(1)}, u32[]{:S(2)}, u32[]{:S(2)}) collective-permute-start(bf16[8,128,128]{2,1,0:T(8,128)(2,1)S(1)} %concatenate.64), channel_id=1, source_target_pairs={{10,0},{0,8},{8,1},{1,9},{9,3},{3,11},{11,2},{2,10},{14,4},{4,12},... | collective-permute-start | bytes 786440 | tf_op jit(solution)/shard_map/ppermute | solution.py:60
  93.4 18.8 %collective-permute-start.3 = (bf16[8,128,128]{2,1,0:T(8,128)(2,1)S(1)}, bf16[8,128,128]{2,1,0:T(8,128)(2,1)S(1)}, u32[]{:S(2)}, u32[]{:S(2)}) collective-permute-start(bf16[8,128,128]{2,1,0:T(8,128)(2,1)S(1)} %collective-permute-done.1), channel_id=1, source_target_pairs={{8,0},{1,8},{9,1},{3,9},{11,3},{2,11},{10,2},{0,10},{12,4},{5,12},... | collective-permute-start | bytes 786440 | tf_op jit(solution)/shard_map/ppermute | solution.py:60
  99.2 13.0 %collective-permute-start.15 = (bf16[4,128,128]{2,1,0:T(8,128)(2,1)S(1)}, bf16[4,128,128]{2,1,0:T(8,128)(2,1)S(1)}, u32[]{:S(2)}, u32[]{:S(2)}) collective-permute-start(bf16[4,128,128]{2,1,0:T(8,128)(2,1)S(1)} %get-tuple-element.125.refs_3_), channel_id=1, source_target_pairs={{8,0},{1,8},{9,1},{3,9},{11,3},{2,11},{10,2},{0,10},{12,4},{5,12},... | collective-permute-start | bytes 393224 | tf_op jit(solution)/shard_map/ppermute | solution.py:60
  100.6 13.6 %collective-permute-start.4 = (bf16[8,128,128]{2,1,0:T(8,128)(2,1)S(1)}, bf16[8,128,128]{2,1,0:T(8,128)(2,1)S(1)}, u32[]{:S(2)}, u32[]{:S(2)}) collective-permute-start(bf16[8,128,128]{2,1,0:T(8,128)(2,1)S(1)} %collective-permute-done.2), channel_id=1, source_target_pairs={{10,0},{0,8},{8,1},{1,9},{9,3},{3,11},{11,2},{2,10},{14,4},{4,12},... | collective-permute-start | bytes 786440 | tf_op jit(solution)/shard_map/ppermute | solution.py:60
  107.9 20.4 %collective-permute-start.24 = (bf16[21,128,128]{2,1,0:T(8,128)(2,1)S(1)}, bf16[21,128,128]{2,1,0:T(8,128)(2,1)S(1)}, u32[]{:S(2)}, u32[]{:S(2)}) collective-permute-start(bf16[21,128,128]{2,1,0:T(8,128)(2,1)S(1)} %collective-permute-done.22.refs_4_), channel_id=1, source_target_pairs={{8,0},{1,8},{9,1},{3,9},{11,3},{2,11},{10,2},{0,10},{12,4},{5,12},... | collective-permute-start | bytes 2064392 | tf_op jit(solution)/shard_map/ppermute | solution.py:60
  109.9 18.5 %collective-permute-start.25 = (bf16[21,128,128]{2,1,0:T(8,128)(2,1)S(1)}, bf16[21,128,128]{2,1,0:T(8,128)(2,1)S(1)}, u32[]{:S(2)}, u32[]{:S(2)}) collective-permute-start(bf16[21,128,128]{2,1,0:T(8,128)(2,1)S(1)} %collective-permute-done.23.refs_5_), channel_id=1, source_target_pairs={{8,0},{1,8},{9,1},{3,9},{11,3},{2,11},{10,2},{0,10},{12,4},{5,12},... | collective-permute-start | bytes 2064392 | tf_op jit(solution)/shard_map/ppermute | solution.py:60
  112.2 4.6 %collective-permute-start.18 = (bf16[4,128,128]{2,1,0:T(8,128)(2,1)S(1)}, bf16[4,128,128]{2,1,0:T(8,128)(2,1)S(1)}, u32[]{:S(2)}, u32[]{:S(2)}) collective-permute-start(bf16[4,128,128]{2,1,0:T(8,128)(2,1)S(1)} %collective-permute-done.16.refs_5_), channel_id=1, source_target_pairs={{10,0},{0,8},{8,1},{1,9},{9,3},{3,11},{11,2},{2,10},{14,4},{4,12},... | collective-permute-start | bytes 393224 | tf_op jit(solution)/shard_map/ppermute | solution.py:60
  112.2 16.1 %collective-permute-start.17 = (bf16[4,128,128]{2,1,0:T(8,128)(2,1)S(1)}, bf16[4,128,128]{2,1,0:T(8,128)(2,1)S(1)}, u32[]{:S(2)}, u32[]{:S(2)}) collective-permute-start(bf16[4,128,128]{2,1,0:T(8,128)(2,1)S(1)} %collective-permute-done.15.refs_4_), channel_id=1, source_target_pairs={{8,0},{1,8},{9,1},{3,9},{11,3},{2,11},{10,2},{0,10},{12,4},{5,12},... | collective-permute-start | bytes 393224 | tf_op jit(solution)/shard_map/ppermute | solution.py:60
  134.8 12.3 %collective-permute-start.41 = (bf16[21,128,128]{2,1,0:T(8,128)(2,1)S(1)}, bf16[21,128,128]{2,1,0:T(8,128)(2,1)S(1)}, u32[]{:S(2)}, u32[]{:S(2)}) collective-permute-start(bf16[21,128,128]{2,1,0:T(8,128)(2,1)S(1)} %fusion.17), channel_id=1, source_target_pairs={{10,0},{0,8},{8,1},{1,9},{9,3},{3,11},{11,2},{2,10},{14,4},{4,12},... | collective-permute-start | bytes 2064392 | tf_op jit(solution)/shard_map/ppermute | solution.py:60
  136.1 16.7 %collective-permute-start.38 = (bf16[21,128,128]{2,1,0:T(8,128)(2,1)S(1)}, bf16[21,128,128]{2,1,0:T(8,128)(2,1)S(1)}, u32[]{:S(2)}, u32[]{:S(2)}) collective-permute-start(bf16[21,128,128]{2,1,0:T(8,128)(2,1)S(1)} %fusion.16), channel_id=1, source_target_pairs={{10,0},{0,8},{8,1},{1,9},{9,3},{3,11},{11,2},{2,10},{14,4},{4,12},... | collective-permute-start | bytes 2064392 | tf_op jit(solution)/shard_map/ppermute | solution.py:60
  143.6 10.5 %collective-permute-start.26 = (bf16[21,128,128]{2,1,0:T(8,128)(2,1)S(1)}, bf16[21,128,128]{2,1,0:T(8,128)(2,1)S(1)}, u32[]{:S(2)}, u32[]{:S(2)}) collective-permute-start(bf16[21,128,128]{2,1,0:T(8,128)(2,1)S(1)} %get-tuple-element.88.refs_0_), channel_id=1, source_target_pairs={{8,0},{1,8},{9,1},{3,9},{11,3},{2,11},{10,2},{0,10},{12,4},{5,12},... | collective-permute-start | bytes 2064392 | tf_op jit(solution)/shard_map/ppermute | solution.py:60
  145.5 15.8 %collective-permute-start.27 = (bf16[21,128,128]{2,1,0:T(8,128)(2,1)S(1)}, bf16[21,128,128]{2,1,0:T(8,128)(2,1)S(1)}, u32[]{:S(2)}, u32[]{:S(2)}) collective-permute-start(bf16[21,128,128]{2,1,0:T(8,128)(2,1)S(1)} %get-tuple-element.89.refs_1_), channel_id=1, source_target_pairs={{8,0},{1,8},{9,1},{3,9},{11,3},{2,11},{10,2},{0,10},{12,4},{5,12},... | collective-permute-start | bytes 2064392 | tf_op jit(solution)/shard_map/ppermute | solution.py:60
  148.3 15.3 %collective-permute-start.42 = (bf16[21,128,128]{2,1,0:T(8,128)(2,1)S(1)}, bf16[21,128,128]{2,1,0:T(8,128)(2,1)S(1)}, u32[]{:S(2)}, u32[]{:S(2)}) collective-permute-start(bf16[21,128,128]{2,1,0:T(8,128)(2,1)S(1)} %fusion.12), channel_id=1, source_target_pairs={{10,0},{0,8},{8,1},{1,9},{9,3},{3,11},{11,2},{2,10},{14,4},{4,12},... | collective-permute-start | bytes 2064392 | tf_op jit(solution)/shard_map/ppermute | solution.py:60
  153.9 13.6 %collective-permute-start.39 = (bf16[21,128,128]{2,1,0:T(8,128)(2,1)S(1)}, bf16[21,128,128]{2,1,0:T(8,128)(2,1)S(1)}, u32[]{:S(2)}, u32[]{:S(2)}) collective-permute-start(bf16[21,128,128]{2,1,0:T(8,128)(2,1)S(1)} %fusion.14), channel_id=1, source_target_pairs={{10,0},{0,8},{8,1},{1,9},{9,3},{3,11},{11,2},{2,10},{14,4},{4,12},... | collective-permute-start | bytes 2064392 | tf_op jit(solution)/shard_map/ppermute | solution.py:60
  154.0 16.8 %collective-permute-start.28 = (bf16[21,128,128]{2,1,0:T(8,128)(2,1)S(1)}, bf16[21,128,128]{2,1,0:T(8,128)(2,1)S(1)}, u32[]{:S(2)}, u32[]{:S(2)}) collective-permute-start(bf16[21,128,128]{2,1,0:T(8,128)(2,1)S(1)} %collective-permute-done.26.refs_2_), channel_id=1, source_target_pairs={{8,0},{1,8},{9,1},{3,9},{11,3},{2,11},{10,2},{0,10},{12,4},{5,12},... | collective-permute-start | bytes 2064392 | tf_op jit(solution)/shard_map/ppermute | solution.py:60
  161.4 14.7 %collective-permute-start.29 = (bf16[21,128,128]{2,1,0:T(8,128)(2,1)S(1)}, bf16[21,128,128]{2,1,0:T(8,128)(2,1)S(1)}, u32[]{:S(2)}, u32[]{:S(2)}) collective-permute-start(bf16[21,128,128]{2,1,0:T(8,128)(2,1)S(1)} %collective-permute-done.27.refs_3_), channel_id=1, source_target_pairs={{8,0},{1,8},{9,1},{3,9},{11,3},{2,11},{10,2},{0,10},{12,4},{5,12},... | collective-permute-start | bytes 2064392 | tf_op jit(solution)/shard_map/ppermute | solution.py:60
  164.7 13.6 %collective-permute-start.43 = (bf16[21,128,128]{2,1,0:T(8,128)(2,1)S(1)}, bf16[21,128,128]{2,1,0:T(8,128)(2,1)S(1)}, u32[]{:S(2)}, u32[]{:S(2)}) collective-permute-start(bf16[21,128,128]{2,1,0:T(8,128)(2,1)S(1)} %fusion.13), channel_id=1, source_target_pairs={{10,0},{0,8},{8,1},{1,9},{9,3},{3,11},{11,2},{2,10},{14,4},{4,12},... | collective-permute-start | bytes 2064392 | tf_op jit(solution)/shard_map/ppermute | solution.py:60
  168.7 13.8 %collective-permute-start.40 = (bf16[21,128,128]{2,1,0:T(8,128)(2,1)S(1)}, bf16[21,128,128]{2,1,0:T(8,128)(2,1)S(1)}, u32[]{:S(2)}, u32[]{:S(2)}) collective-permute-start(bf16[21,128,128]{2,1,0:T(8,128)(2,1)S(1)} %fusion.15), channel_id=1, source_target_pairs={{10,0},{0,8},{8,1},{1,9},{9,3},{3,11},{11,2},{2,10},{14,4},{4,12},... | collective-permute-start | bytes 2064392 | tf_op jit(solution)/shard_map/ppermute | solution.py:60
  170.8 22.1 %collective-permute-start.30 = (bf16[21,128,128]{2,1,0:T(8,128)(2,1)S(1)}, bf16[21,128,128]{2,1,0:T(8,128)(2,1)S(1)}, u32[]{:S(2)}, u32[]{:S(2)}) collective-permute-start(bf16[21,128,128]{2,1,0:T(8,128)(2,1)S(1)} %collective-permute-done.28.refs_4_), channel_id=1, source_target_pairs={{8,0},{1,8},{9,1},{3,9},{11,3},{2,11},{10,2},{0,10},{12,4},{5,12},... | collective-permute-start | bytes 2064392 | tf_op jit(solution)/shard_map/ppermute | solution.py:60
  176.1 16.8 %collective-permute-start.31 = (bf16[21,128,128]{2,1,0:T(8,128)(2,1)S(1)}, bf16[21,128,128]{2,1,0:T(8,128)(2,1)S(1)}, u32[]{:S(2)}, u32[]{:S(2)}) collective-permute-start(bf16[21,128,128]{2,1,0:T(8,128)(2,1)S(1)} %collective-permute-done.29.refs_5_), channel_id=1, source_target_pairs={{8,0},{1,8},{9,1},{3,9},{11,3},{2,11},{10,2},{0,10},{12,4},{5,12},... | collective-permute-start | bytes 2064392 | tf_op jit(solution)/shard_map/ppermute | solution.py:60
  188.5 12.3 %collective-permute-start.47 = (bf16[21,128,128]{2,1,0:T(8,128)(2,1)S(1)}, bf16[21,128,128]{2,1,0:T(8,128)(2,1)S(1)}, u32[]{:S(2)}, u32[]{:S(2)}) collective-permute-start(bf16[21,128,128]{2,1,0:T(8,128)(2,1)S(1)} %fusion.19), channel_id=1, source_target_pairs={{10,0},{0,8},{8,1},{1,9},{9,3},{3,11},{11,2},{2,10},{14,4},{4,12},... | collective-permute-start | bytes 2064392 | tf_op jit(solution)/shard_map/ppermute | solution.py:60
  190.4 15.9 %collective-permute-start.44 = (bf16[21,128,128]{2,1,0:T(8,128)(2,1)S(1)}, bf16[21,128,128]{2,1,0:T(8,128)(2,1)S(1)}, u32[]{:S(2)}, u32[]{:S(2)}) collective-permute-start(bf16[21,128,128]{2,1,0:T(8,128)(2,1)S(1)} %fusion.18), channel_id=1, source_target_pairs={{10,0},{0,8},{8,1},{1,9},{9,3},{3,11},{11,2},{2,10},{14,4},{4,12},... | collective-permute-start | bytes 2064392 | tf_op jit(solution)/shard_map/ppermute | solution.py:60
  199.3 8.9 %collective-permute-start.32 = (bf16[21,128,128]{2,1,0:T(8,128)(2,1)S(1)}, bf16[21,128,128]{2,1,0:T(8,128)(2,1)S(1)}, u32[]{:S(2)}, u32[]{:S(2)}) collective-permute-start(bf16[21,128,128]{2,1,0:T(8,128)(2,1)S(1)} %get-tuple-element.92.refs_0_.refs_8_), channel_id=1, source_target_pairs={{8,0},{1,8},{9,1},{3,9},{11,3},{2,11},{10,2},{0,10},{12,4},{5,12},... | collective-permute-start | bytes 2064392 | tf_op jit(solution)/shard_map/ppermute | solution.py:60
  199.3 15.8 %collective-permute-start.33 = (bf16[21,128,128]{2,1,0:T(8,128)(2,1)S(1)}, bf16[21,128,128]{2,1,0:T(8,128)(2,1)S(1)}, u32[]{:S(2)}, u32[]{:S(2)}) collective-permute-start(bf16[21,128,128]{2,1,0:T(8,128)(2,1)S(1)} %get-tuple-element.93.refs_1_.refs_9_), channel_id=1, source_target_pairs={{8,0},{1,8},{9,1},{3,9},{11,3},{2,11},{10,2},{0,10},{12,4},{5,12},... | collective-permute-start | bytes 2064392 | tf_op jit(solution)/shard_map/ppermute | solution.py:60
  201.2 16.2 %collective-permute-start.48 = (bf16[21,128,128]{2,1,0:T(8,128)(2,1)S(1)}, bf16[21,128,128]{2,1,0:T(8,128)(2,1)S(1)}, u32[]{:S(2)}, u32[]{:S(2)}) collective-permute-start(bf16[21,128,128]{2,1,0:T(8,128)(2,1)S(1)} %fusion.8), channel_id=1, source_target_pairs={{10,0},{0,8},{8,1},{1,9},{9,3},{3,11},{11,2},{2,10},{14,4},{4,12},... | collective-permute-start | bytes 2064392 | tf_op jit(solution)/shard_map/ppermute | solution.py:60
  206.7 14.3 %collective-permute-start.45 = (bf16[21,128,128]{2,1,0:T(8,128)(2,1)S(1)}, bf16[21,128,128]{2,1,0:T(8,128)(2,1)S(1)}, u32[]{:S(2)}, u32[]{:S(2)}) collective-permute-start(bf16[21,128,128]{2,1,0:T(8,128)(2,1)S(1)} %fusion.10), channel_id=1, source_target_pairs={{10,0},{0,8},{8,1},{1,9},{9,3},{3,11},{11,2},{2,10},{14,4},{4,12},... | collective-permute-start | bytes 2064392 | tf_op jit(solution)/shard_map/ppermute | solution.py:60
  208.2 15.7 %collective-permute-start.34 = (bf16[21,128,128]{2,1,0:T(8,128)(2,1)S(1)}, bf16[21,128,128]{2,1,0:T(8,128)(2,1)}, u32[]{:S(2)}, u32[]{:S(2)}) collective-permute-start(bf16[21,128,128]{2,1,0:T(8,128)(2,1)S(1)} %collective-permute-done.32.refs_2_.refs_10_), channel_id=1, source_target_pairs={{8,0},{1,8},{9,1},{3,9},{11,3},{2,11},{10,2},{0,10},{12,4},{5,12},... | collective-permute-start | bytes 2064392 | tf_op jit(solution)/shard_map/ppermute | solution.py:60
  215.2 14.7 %collective-permute-start.35 = (bf16[21,128,128]{2,1,0:T(8,128)(2,1)S(1)}, bf16[21,128,128]{2,1,0:T(8,128)(2,1)}, u32[]{:S(2)}, u32[]{:S(2)}) collective-permute-start(bf16[21,128,128]{2,1,0:T(8,128)(2,1)S(1)} %collective-permute-done.33.refs_3_.refs_11_), channel_id=1, source_target_pairs={{8,0},{1,8},{9,1},{3,9},{11,3},{2,11},{10,2},{0,10},{12,4},{5,12},... | collective-permute-start | bytes 2064392 | tf_op jit(solution)/shard_map/ppermute | solution.py:60
  218.7 15.0 %collective-permute-start.49 = (bf16[21,128,128]{2,1,0:T(8,128)(2,1)}, bf16[21,128,128]{2,1,0:T(8,128)(2,1)S(1)}, u32[]{:S(2)}, u32[]{:S(2)}) collective-permute-start(bf16[21,128,128]{2,1,0:T(8,128)(2,1)} %fusion.9), channel_id=1, source_target_pairs={{10,0},{0,8},{8,1},{1,9},{9,3},{3,11},{11,2},{2,10},{14,4},{4,12},... | collective-permute-start | bytes 2064392 | tf_op jit(solution)/shard_map/ppermute | solution.py:60
  222.3 14.3 %collective-permute-start.46 = (bf16[21,128,128]{2,1,0:T(8,128)(2,1)}, bf16[21,128,128]{2,1,0:T(8,128)(2,1)S(1)}, u32[]{:S(2)}, u32[]{:S(2)}) collective-permute-start(bf16[21,128,128]{2,1,0:T(8,128)(2,1)} %fusion.11), channel_id=1, source_target_pairs={{10,0},{0,8},{8,1},{1,9},{9,3},{3,11},{11,2},{2,10},{14,4},{4,12},... | collective-permute-start | bytes 2064392 | tf_op jit(solution)/shard_map/ppermute | solution.py:60
  223.9 18.4 %collective-permute-start.36 = (bf16[21,128,128]{2,1,0:T(8,128)(2,1)}, bf16[21,128,128]{2,1,0:T(8,128)(2,1)}, u32[]{:S(2)}, u32[]{:S(2)}) collective-permute-start(bf16[21,128,128]{2,1,0:T(8,128)(2,1)} %collective-permute-done.34.refs_4_.refs_12_), channel_id=1, source_target_pairs={{8,0},{1,8},{9,1},{3,9},{11,3},{2,11},{10,2},{0,10},{12,4},{5,12},... | collective-permute-start | bytes 2064392 | tf_op jit(solution)/shard_map/ppermute | solution.py:60
  229.9 14.9 %collective-permute-start.37 = (bf16[21,128,128]{2,1,0:T(8,128)(2,1)}, bf16[21,128,128]{2,1,0:T(8,128)(2,1)}, u32[]{:S(2)}, u32[]{:S(2)}) collective-permute-start(bf16[21,128,128]{2,1,0:T(8,128)(2,1)} %collective-permute-done.35.refs_5_.refs_13_), channel_id=1, source_target_pairs={{8,0},{1,8},{9,1},{3,9},{11,3},{2,11},{10,2},{0,10},{12,4},{5,12},... | collective-permute-start | bytes 2064392 | tf_op jit(solution)/shard_map/ppermute | solution.py:60
  248.5 5.0 %collective-permute-start.50 = (f32[1,128]{1,0:T(1,128)S(1)}, f32[1,128]{1,0:T(1,128)S(1)}, u32[]{:S(2)}, u32[]{:S(2)}) collective-permute-start(f32[1,128]{1,0:T(1,128)S(1)} %get-tuple-element.131), channel_id=1, source_target_pairs={{8,0},{0,8},{9,1},{1,9},{11,3},{3,11},{10,2},{2,10},{12,4},{4,12},... | collective-permute-start | bytes 1544 | tf_op jit(solution)/shard_map/ppermute | solution.py:65
  253.6 5.5 %collective-permute-start.51 = (f32[2,128]{1,0:T(2,128)S(1)}, f32[2,128]{1,0:T(2,128)S(1)}, u32[]{:S(2)}, u32[]{:S(2)}) collective-permute-start(f32[2,128]{1,0:T(2,128)S(1)} %maximum_select_fusion.4), channel_id=1, source_target_pairs={{1,0},{9,8},{0,1},{8,9},{2,3},{10,11},{3,2},{11,10},{5,4},{13,12},... | collective-permute-start | bytes 3080 | tf_op jit(solution)/shard_map/ppermute | solution.py:65
  255.3 8.3 %collective-permute-start.56 = (bf16[528,128]{1,0:T(8,128)(2,1)S(1)}, bf16[528,128]{1,0:T(8,128)(2,1)}, u32[]{:S(2)}, u32[]{:S(2)}) collective-permute-start(bf16[528,128]{1,0:T(8,128)(2,1)S(1)} %get-tuple-element.133.refs_3_), channel_id=1, source_target_pairs={{2,0},{10,8},{0,1},{8,9},{1,3},{9,11},{3,2},{11,10},{6,4},{14,12},... | collective-permute-start | bytes 405512 | tf_op jit(solution)/shard_map/ppermute | solution.py:60
  255.6 8.1 %collective-permute-start.55 = (bf16[528,128]{1,0:T(8,128)(2,1)S(1)}, bf16[528,128]{1,0:T(8,128)(2,1)}, u32[]{:S(2)}, u32[]{:S(2)}) collective-permute-start(bf16[528,128]{1,0:T(8,128)(2,1)S(1)} %get-tuple-element.133.refs_3_), channel_id=1, source_target_pairs={{1,0},{9,8},{3,1},{11,9},{2,3},{10,11},{0,2},{8,10},{5,4},{13,12},... | collective-permute-start | bytes 405512 | tf_op jit(solution)/shard_map/ppermute | solution.py:60
  257.4 6.3 %collective-permute-start.54 = (bf16[528,128]{1,0:T(8,128)(2,1)S(1)}, bf16[528,128]{1,0:T(8,128)(2,1)}, u32[]{:S(2)}, u32[]{:S(2)}) collective-permute-start(bf16[528,128]{1,0:T(8,128)(2,1)S(1)} %get-tuple-element.133.refs_3_), channel_id=1, source_target_pairs={{10,0},{0,8},{8,1},{1,9},{9,3},{3,11},{11,2},{2,10},{14,4},{4,12},... | collective-permute-start | bytes 405512 | tf_op jit(solution)/shard_map/ppermute | solution.py:60
  257.4 6.3 %collective-permute-start.53 = (bf16[528,128]{1,0:T(8,128)(2,1)S(1)}, bf16[528,128]{1,0:T(8,128)(2,1)}, u32[]{:S(2)}, u32[]{:S(2)}) collective-permute-start(bf16[528,128]{1,0:T(8,128)(2,1)S(1)} %get-tuple-element.133.refs_3_), channel_id=1, source_target_pairs={{8,0},{1,8},{9,1},{3,9},{11,3},{2,11},{10,2},{0,10},{12,4},{5,12},... | collective-permute-start | bytes 405512 | tf_op jit(solution)/shard_map/ppermute | solution.py:60
  259.1 4.5 %collective-permute-start.52 = (f32[4,128]{1,0:T(4,128)S(1)}, f32[4,128]{1,0:T(4,128)S(1)}, u32[]{:S(2)}, u32[]{:S(2)}) collective-permute-start(f32[4,128]{1,0:T(4,128)S(1)} %maximum_select_fusion.2), channel_id=1, source_target_pairs={{3,0},{11,8},{2,1},{10,9},{0,3},{8,11},{1,2},{9,10},{7,4},{15,12},... | collective-permute-start | bytes 6152 | tf_op jit(solution)/shard_map/ppermute | solution.py:65
  278.5 8.6 %collective-permute-start.63 = (f32[2,128,128]{2,1,0:T(8,128)S(1)}, f32[2,128,128]{2,1,0:T(8,128)S(1)}, u32[]{:S(2)}, u32[]{:S(2)}) collective-permute-start(f32[2,128,128]{2,1,0:T(8,128)S(1)} %get-tuple-element.160), channel_id=1, source_target_pairs={{11,0},{2,8},{10,1},{0,9},{8,3},{1,11},{9,2},{3,10},{15,4},{6,12},... | collective-permute-start | bytes 393224 | tf_op jit(solution)/shard_map/ppermute | solution.py:60
  279.8 7.3 %collective-permute-start.62 = (f32[2,128,128]{2,1,0:T(8,128)S(1)}, f32[2,128,128]{2,1,0:T(8,128)S(1)}, u32[]{:S(2)}, u32[]{:S(2)}) collective-permute-start(f32[2,128,128]{2,1,0:T(8,128)S(1)} %get-tuple-element.161), channel_id=1, source_target_pairs={{2,0},{10,8},{0,1},{8,9},{1,3},{9,11},{3,2},{11,10},{6,4},{14,12},... | collective-permute-start | bytes 393224 | tf_op jit(solution)/shard_map/ppermute | solution.py:60
  280.4 8.4 %collective-permute-start.61 = (f32[2,128,128]{2,1,0:T(8,128)S(1)}, f32[2,128,128]{2,1,0:T(8,128)S(1)}, u32[]{:S(2)}, u32[]{:S(2)}) collective-permute-start(f32[2,128,128]{2,1,0:T(8,128)S(1)} %get-tuple-element.162), channel_id=1, source_target_pairs={{10,0},{0,8},{8,1},{1,9},{9,3},{3,11},{11,2},{2,10},{14,4},{4,12},... | collective-permute-start | bytes 393224 | tf_op jit(solution)/shard_map/ppermute | solution.py:60
  281.8 4.5 %collective-permute-start.59 = (f32[4,128]{1,0:T(4,128)S(1)}, f32[4,128]{1,0:T(4,128)S(1)}, u32[]{:S(2)}, u32[]{:S(2)}) collective-permute-start(f32[4,128]{1,0:T(4,128)S(1)} %maximum_select_fusion.3), channel_id=1, source_target_pairs={{3,0},{11,8},{2,1},{10,9},{0,3},{8,11},{1,2},{9,10},{7,4},{15,12},... | collective-permute-start | bytes 6152 | tf_op jit(solution)/shard_map/ppermute | solution.py:65
  293.5 10.6 %collective-permute-start.64 = (bf16[128,128]{1,0:T(8,128)(2,1)S(1)}, bf16[128,128]{1,0:T(8,128)(2,1)S(1)}, u32[]{:S(2)}, u32[]{:S(2)}) collective-permute-start(bf16[128,128]{1,0:T(8,128)(2,1)S(1)} %get-tuple-element.167), channel_id=1, source_target_pairs={{0,16},{8,17},{1,18},{9,19},{3,20},{11,21},{2,22},{10,23},{4,24},{... | collective-permute-start | bytes 98312 | tf_op jit(solution)/shard_map/ppermute | solution.py:55
  294.2 9.9 %collective-permute-start.67 = (bf16[128,128]{1,0:T(8,128)(2,1)S(1)}, bf16[128,128]{1,0:T(8,128)(2,1)S(1)}, u32[]{:S(2)}, u32[]{:S(2)}) collective-permute-start(bf16[128,128]{1,0:T(8,128)(2,1)S(1)} %get-tuple-element.168), channel_id=1, source_target_pairs={{0,21},{8,22},{1,23},{9,16},{3,17},{11,18},{2,19},{10,20},{4,29},{... | collective-permute-start | bytes 98312 | tf_op jit(solution)/shard_map/ppermute | solution.py:55
  301.5 5.0 %collective-permute-start.66 = (bf16[128,128]{1,0:T(8,128)(2,1)S(1)}, bf16[128,128]{1,0:T(8,128)(2,1)S(1)}, u32[]{:S(2)}, u32[]{:S(2)}) collective-permute-start(bf16[128,128]{1,0:T(8,128)(2,1)S(1)} %get-tuple-element.169), channel_id=1, source_target_pairs={{0,22},{8,23},{1,16},{9,17},{3,18},{11,19},{2,20},{10,21},{4,30},{... | collective-permute-start | bytes 98312 | tf_op jit(solution)/shard_map/ppermute | solution.py:55
  301.6 5.0 %collective-permute-start.65 = (bf16[128,128]{1,0:T(8,128)(2,1)S(1)}, bf16[128,128]{1,0:T(8,128)(2,1)S(1)}, u32[]{:S(2)}, u32[]{:S(2)}) collective-permute-start(bf16[128,128]{1,0:T(8,128)(2,1)S(1)} %get-tuple-element.170), channel_id=1, source_target_pairs={{0,23},{8,16},{1,17},{9,18},{3,19},{11,20},{2,21},{10,22},{4,31},{... | collective-permute-start | bytes 98312 | tf_op jit(solution)/shard_map/ppermute | solution.py:55
  (34 other events, 238.3 us)
